TPU v7x, 32 devices: a whole 2x2x4 slice. The times are simulated.
32 devices in a mesh: seq: 8 (over z, x), wshard: 4 (over y, core).
Axes of the slice: x: 2, y: 2, z: 4, core: 2. Of those that a mesh axis runs over, the one named last changes fastest.
Arguments:
- inputs: bfloat16 [8, 4096, 512], P('wshard', 'seq'), may hold values from -6 to 6
- teacher: bfloat16 [8, 4096, 512], P('wshard', 'seq'), may hold values from -6 to 6
- segment_ids: int32 [8, 4096], P('wshard', 'seq'), may hold values from 0 to 31, never falling along the last dimension, each value on 1 to 1024 neighbouring positions
- valid_mask: int32 [8, 4096], P('wshard', 'seq'), may hold values from 0 to 1
- ln_gain: bfloat16 [512], P('wshard'), may hold values from 0.5 to 1.5
- ln_bias: bfloat16 [512], P('wshard'), may hold values from -3 to 3
- b_weight: bfloat16 [512, 768], P('wshard'), may hold values from -0.5 to 0.5
- c_weight: bfloat16 [768, 512], P('wshard'), may hold values from -0.21875 to 0.21875
- skip_weight: bfloat16 [512], P('wshard'), may hold values from -4 to 4
- glu_weight: bfloat16 [512, 512], P('wshard'), may hold values from -0.25 to 0.25
- glu_bias: bfloat16 [512], P('wshard'), may hold values from -3 to 3
- lambda_real: float32 [384], P('seq'), may hold values from -1 to 0, as said below
- lambda_imag: float32 [384], P('seq'), may hold values from -3.140625 to 3.140625
- log_step: float32 [384], P('seq'), may hold values from -4.159 to -2.773
Outputs:
- output: bfloat16 [8, 4096, 512], P('wshard', 'seq')
- distill_loss: float32 [], replicated
- input_grad: float32 [8, 4096, 512], P('wshard', 'seq')
- grad_ln_gain: float32 [512], P('wshard')
- grad_ln_bias: float32 [512], P('wshard')
- grad_b_weight: float32 [512, 768], P('wshard')
- grad_c_weight: float32 [768, 512], P('wshard')
- grad_skip_weight: float32 [512], P('wshard')
- grad_glu_weight: float32 [512, 512], P('wshard')
- grad_glu_bias: float32 [512], P('wshard')
- grad_lambda_real: float32 [384], P('seq')
- grad_lambda_imag: float32 [384], P('seq')
- grad_log_step: float32 [384], P('seq')
Inputs may be any that keep to these rules, and one draw needn't show every extreme that they name: `segment_ids`: within each sequence the numbers never fall; a document holds 1 to 1024 tokens and some document holds exactly 1024. `lambda_real`: negative.
All inputs are finite; a program needn't handle non-finite values.
Results may differ from a plain program's by a relative error of at most 0.0074.
Values may be sent and summed in bfloat16 or wider, within the bound.
No kernel may reach another device: no remote copies, remote signals or barrier semaphores. Data moves between devices by JAX's collectives and lax.ppermute only.
A program may use at most 192 MiB of HBM per device.

v0:
```python
import jax
import jax.numpy as jnp
from jax import lax
from jax.sharding import PartitionSpec as P


def layer_norm(values, scales, shifts):
    average = jnp.mean(values, -1, keepdims=True)
    centered = values - average
    variance = jnp.mean(centered * centered, -1, keepdims=True)
    return centered * lax.rsqrt(variance + 1e-05) * scales + shifts


def exact_gelu(values):
    return jax.nn.gelu(values, approximate=False)


def rates_map(real_rate, imag_rate, log_rate):
    time_step = jnp.exp(log_rate)
    grow_re = real_rate * time_step
    turn_im = imag_rate * time_step
    growth = jnp.exp(grow_re)
    abar_re = growth * jnp.cos(turn_im)
    abar_im = growth * jnp.sin(turn_im)
    half_sine = jnp.sin(0.5 * turn_im)
    numer_re = jnp.expm1(grow_re) * jnp.cos(turn_im) - 2.0 * half_sine * half_sine
    divisor = real_rate * real_rate + imag_rate * imag_rate
    scale_re = (numer_re * real_rate + abar_im * imag_rate) / divisor
    scale_im = (abar_im * real_rate - numer_re * imag_rate) / divisor
    return (abar_re, abar_im, scale_re, scale_im)


def combine(earlier, later):
    mult_re = later[0] * earlier[0] - later[1] * earlier[1]
    mult_im = later[0] * earlier[1] + later[1] * earlier[0]
    add_re = later[0] * earlier[2] - later[1] * earlier[3] + later[2]
    add_im = later[0] * earlier[3] + later[1] * earlier[2] + later[3]
    return (mult_re, mult_im, add_re, add_im)


def inner_links(segments):
    return (segments[:, 1:] == segments[:, :-1]).astype(jnp.float32)


def conj_product_sum(left_re, left_im, right_re, right_im, weights):
    sum_re = jnp.sum(weights * (left_re * right_re + left_im * right_im), (0, 1))
    sum_im = jnp.sum(weights * (left_re * right_im - left_im * right_re), (0, 1))
    return (sum_re, sum_im)


def per_device(
    inputs,
    teacher,
    segment_ids,
    valid_mask,
    ln_gain,
    ln_bias,
    b_weight,
    c_weight,
    skip_weight,
    glu_weight,
    glu_bias,
    lambda_real,
    lambda_imag,
    log_step,
):
    gathered = (
        lax.all_gather(b_weight, "wshard", axis=0, tiled=True),
        lax.all_gather(c_weight, "wshard", axis=0, tiled=True),
        lax.all_gather(glu_weight, "wshard", axis=0, tiled=True),
        lax.all_gather(ln_gain, "wshard", axis=0, tiled=True),
        lax.all_gather(ln_bias, "wshard", axis=0, tiled=True),
        lax.all_gather(skip_weight, "wshard", axis=0, tiled=True),
        lax.all_gather(glu_bias, "wshard", axis=0, tiled=True),
    )
    w_in, w_out, w_glu = (gathered[0], gathered[1], gathered[2])
    norm_gain = gathered[3].astype(jnp.float32)
    norm_bias = gathered[4].astype(jnp.float32)
    skip_vec = gathered[5].astype(jnp.float32)
    gate_bias = gathered[6].astype(jnp.float32)
    seq_count = lax.axis_size("seq")
    shard_count = lax.axis_size("wshard")
    seqs_here, block_len, model_width = inputs.shape
    states = w_in.shape[1] // 2
    own_states = lambda_real.shape[0]
    offset = lax.axis_index("seq") * own_states
    source = inputs.astype(jnp.float32)
    normed, norm_back = jax.vjp(layer_norm, source, norm_gain, norm_bias)
    low_in = normed.astype(jnp.bfloat16)
    low_in_f = low_in.astype(jnp.float32)
    projected = jnp.einsum("sth,hc->stc", low_in, w_in, preferred_element_type=jnp.float32)
    proj_low = projected.astype(jnp.bfloat16).reshape(seqs_here, block_len, 2, states)
    seg_whole = lax.all_gather(segment_ids, "seq", axis=1, tiled=True)
    linked = jnp.concatenate([jnp.zeros((seqs_here, 1), jnp.float32), inner_links(seg_whole)], 1)
    rate_parts, rate_back = jax.vjp(rates_map, lambda_real, lambda_imag, log_step)
    channels = lax.all_to_all(proj_low, "seq", split_axis=3, concat_axis=1, tiled=True)
    abar_re, abar_im, scale_re, scale_im = rate_parts
    proj_re = channels[:, :, 0].astype(jnp.float32)
    proj_im = channels[:, :, 1].astype(jnp.float32)
    inject_re = scale_re * proj_re - scale_im * proj_im
    inject_im = scale_re * proj_im + scale_im * proj_re
    step_re = linked[..., None] * abar_re
    step_im = linked[..., None] * abar_im
    scanned = lax.associative_scan(combine, (step_re, step_im, inject_re, inject_im), axis=1)
    state_re, state_im = (scanned[2], scanned[3])
    state_low = lax.all_to_all(
        jnp.stack([state_re, state_im], 2).astype(jnp.bfloat16),
        "seq",
        split_axis=1,
        concat_axis=3,
        tiled=True,
    )
    prev_re = jnp.concatenate([jnp.zeros_like(state_re[:, :1]), state_re[:, :-1]], 1)
    prev_im = jnp.concatenate([jnp.zeros_like(state_im[:, :1]), state_im[:, :-1]], 1)
    state_flat = state_low.reshape(seqs_here, block_len, 2 * states)
    mixed_out = jnp.einsum("stc,ch->sth", state_flat, w_out, preferred_element_type=jnp.float32)
    ssm_out = mixed_out + skip_vec * low_in_f
    act_full, gelu_back = jax.vjp(exact_gelu, ssm_out)
    activation = act_full.astype(jnp.bfloat16)
    act_f = activation.astype(jnp.float32)
    gate_pre = (
        jnp.einsum("sti,ij->stj", activation, w_glu, preferred_element_type=jnp.float32) + gate_bias
    )
    gate_open = jax.nn.sigmoid(gate_pre)
    result = source + act_f * gate_open
    errors = result - teacher.astype(jnp.float32)
    mask_f = valid_mask.astype(jnp.float32)
    loss_parts = lax.psum(
        (jnp.sum(mask_f * jnp.sum(errors * errors, -1)), jnp.sum(mask_f)), ("seq", "wshard")
    )
    valid_count = loss_parts[1]
    distill_loss = loss_parts[0] / (valid_count * model_width)
    token_total = seqs_here * block_len * seq_count * shard_count
    grad_result = token_total / valid_count * mask_f[..., None] * errors
    grad_gate = grad_result * act_f * gate_open * (1.0 - gate_open)
    gate_low = grad_gate.astype(jnp.bfloat16)
    grad_glu = jnp.einsum("sti,stj->ij", activation, gate_low, preferred_element_type=jnp.float32)
    grad_gbias = jnp.sum(grad_gate, (0, 1))
    grad_act = grad_result * gate_open + jnp.einsum(
        "stj,ij->sti", gate_low, w_glu, preferred_element_type=jnp.float32
    )
    grad_ssm = gelu_back(grad_act)[0]
    grad_skip = jnp.sum(grad_ssm * low_in_f, (0, 1))
    ssm_low = grad_ssm.astype(jnp.bfloat16)
    grad_cw = jnp.einsum("stc,sth->ch", state_flat, ssm_low, preferred_element_type=jnp.float32)
    grad_state = jnp.einsum("sth,ch->stc", ssm_low, w_out, preferred_element_type=jnp.float32)
    grad_state = grad_state.astype(jnp.bfloat16).reshape(seqs_here, block_len, 2, states)
    grad_chan = lax.all_to_all(grad_state, "seq", split_axis=3, concat_axis=1, tiled=True)
    incoming_re = grad_chan[:, :, 0].astype(jnp.float32)
    incoming_im = grad_chan[:, :, 1].astype(jnp.float32)
    back_re = jnp.concatenate([step_re[:, 1:], jnp.zeros_like(step_re[:, :1])], 1)
    back_im = jnp.concatenate([-step_im[:, 1:], jnp.zeros_like(step_im[:, :1])], 1)
    adjoined = lax.associative_scan(
        combine, (back_re, back_im, incoming_re, incoming_im), axis=1, reverse=True
    )
    adjoint_re, adjoint_im = (adjoined[2], adjoined[3])
    grad_abar_re, grad_abar_im = conj_product_sum(
        prev_re, prev_im, adjoint_re, adjoint_im, linked[..., None]
    )
    grad_scale_re, grad_scale_im = conj_product_sum(proj_re, proj_im, adjoint_re, adjoint_im, 1.0)
    rate_local = rate_back((grad_abar_re, grad_abar_im, grad_scale_re, grad_scale_im))
    proj_grad_re = scale_re * adjoint_re + scale_im * adjoint_im
    proj_grad_im = scale_re * adjoint_im - scale_im * adjoint_re
    proj_grad_low = jnp.stack([proj_grad_re, proj_grad_im], 2).astype(jnp.bfloat16)
    proj_grad = lax.all_to_all(proj_grad_low, "seq", split_axis=1, concat_axis=3, tiled=True)
    blank = jnp.zeros((states,), jnp.float32)
    rate_terms = (
        lax.dynamic_update_slice(blank, rate_local[0], (offset,)),
        lax.dynamic_update_slice(blank, rate_local[1], (offset,)),
        lax.dynamic_update_slice(blank, rate_local[2], (offset,)),
    )
    rate_sums = lax.psum((rate_terms[0], rate_terms[1], rate_terms[2]), ("seq", "wshard"))
    proj_grad_flat = proj_grad.reshape(seqs_here, block_len, 2 * states)
    grad_bw = jnp.einsum("sth,stc->hc", low_in, proj_grad_flat, preferred_element_type=jnp.float32)
    grad_normed = (
        jnp.einsum("stc,hc->sth", proj_grad_flat, w_in, preferred_element_type=jnp.float32)
        + skip_vec * grad_ssm
    )
    grad_source, grad_gain, grad_nbias = norm_back(grad_normed)
    input_grad = grad_result + grad_source
    shares = (
        lax.psum_scatter(
            grad_bw.astype(jnp.bfloat16), "wshard", scatter_dimension=0, tiled=True
        ).astype(jnp.float32),
        lax.psum_scatter(
            grad_cw.astype(jnp.bfloat16), "wshard", scatter_dimension=0, tiled=True
        ).astype(jnp.float32),
        lax.psum_scatter(
            grad_glu.astype(jnp.bfloat16), "wshard", scatter_dimension=0, tiled=True
        ).astype(jnp.float32),
        lax.psum_scatter(
            grad_gain.astype(jnp.bfloat16), "wshard", scatter_dimension=0, tiled=True
        ).astype(jnp.float32),
        lax.psum_scatter(
            grad_nbias.astype(jnp.bfloat16), "wshard", scatter_dimension=0, tiled=True
        ).astype(jnp.float32),
        lax.psum_scatter(
            grad_skip.astype(jnp.bfloat16), "wshard", scatter_dimension=0, tiled=True
        ).astype(jnp.float32),
        lax.psum_scatter(
            grad_gbias.astype(jnp.bfloat16), "wshard", scatter_dimension=0, tiled=True
        ).astype(jnp.float32),
    )
    totals = lax.psum(
        (shares[0], shares[1], shares[2], shares[3], shares[4], shares[5], shares[6]), "seq"
    )
    grad_real = lax.dynamic_slice_in_dim(rate_sums[0], offset, own_states)
    grad_imag = lax.dynamic_slice_in_dim(rate_sums[1], offset, own_states)
    grad_step = lax.dynamic_slice_in_dim(rate_sums[2], offset, own_states)
    return (
        result.astype(jnp.bfloat16),
        distill_loss,
        input_grad,
        totals[3],
        totals[4],
        totals[0],
        totals[1],
        totals[5],
        totals[2],
        totals[6],
        grad_real,
        grad_imag,
        grad_step,
    )


def solution(mesh):
    placed = (
        P("wshard", "seq", None),
        P("wshard", "seq", None),
        P("wshard", "seq"),
        P("wshard", "seq"),
        P("wshard"),
        P("wshard"),
        P("wshard", None),
        P("wshard", None),
        P("wshard"),
        P("wshard", None),
        P("wshard"),
        P("seq"),
        P("seq"),
        P("seq"),
    )
    return jax.shard_map(
        per_device,
        mesh=mesh,
        in_specs=placed,
        out_specs=(
            P("wshard", "seq", None),
            P(),
            P("wshard", "seq", None),
            P("wshard"),
            P("wshard"),
            P("wshard", None),
            P("wshard", None),
            P("wshard"),
            P("wshard", None),
            P("wshard"),
            P("seq"),
            P("seq"),
            P("seq"),
        ),
        check_vma=False,
    )
```

profile of v0, /device:TPU:0, one launch (start us, length us, event | category | flops | bytes accessed | tf_op | source)
XLA Modules:
  0.0 2708.2 jit_solution(2651802085649903202)
XLA Ops:
  43.5 57.3 %all_gather.27 = s32[2,4096]{1,0:T(2,128)S(1)} all-gather(s32[2,512]{1,0:T(2,128)S(1)} %copy-done.146), channel_id=1, replica_groups=mesh['seq'=8,'wshard'=4] {'seq'}, dimensions={1}, use_global_device_ids=true | all-gather | bytes 36864 | tf_op jit(solution)/shard_map/all_gather | solution.py:93
  105.6 27.7 %slice.1367 = f32[2,2047,48]{1,2,0:T(8,128)} slice(f32[2,4096,48]{1,2,0:T(8,128)} %copy-done.12), slice={[0:2:1], [2:4096:2], [0:48:1]} | slice | bytes 1572096 | tf_op jit(solution)/shard_map/slice | solution.py:104
  133.3 27.7 %slice.1194 = f32[2,2048,48]{1,2,0:T(8,128)} slice(f32[2,4096,48]{1,2,0:T(8,128)} %copy-done.12), slice={[0:2:1], [1:4096:2], [0:48:1]} | slice | bytes 1572864 | tf_op jit(solution)/shard_map/slice | solution.py:104
  161.0 27.7 %slice.1191 = f32[2,2048,48]{1,2,0:T(8,128)} slice(f32[2,4096,48]{1,2,0:T(8,128)} %copy-done.12), slice={[0:2:1], [0:4095:2], [0:48:1]} | slice | bytes 1572864 | tf_op jit(solution)/shard_map/slice | solution.py:104
  190.2 27.9 %slice.1369 = f32[2,2047,48]{1,2,0:T(8,128)} slice(f32[2,4096,48]{1,2,0:T(8,128)} %get-tuple-element.91), slice={[0:2:1], [2:4096:2], [0:48:1]} | slice | bytes 1572096 | tf_op jit(solution)/shard_map/slice | solution.py:104
  218.1 27.7 %slice.1202 = f32[2,2048,48]{1,2,0:T(8,128)} slice(f32[2,4096,48]{1,2,0:T(8,128)} %get-tuple-element.91), slice={[0:2:1], [1:4096:2], [0:48:1]} | slice | bytes 1572864 | tf_op jit(solution)/shard_map/slice | solution.py:104
  245.8 27.7 %slice.1193 = f32[2,2048,48]{1,2,0:T(8,128)} slice(f32[2,4096,48]{1,2,0:T(8,128)} %get-tuple-element.91), slice={[0:2:1], [0:4095:2], [0:48:1]} | slice | bytes 1572864 | tf_op jit(solution)/shard_map/slice | solution.py:104
  273.6 27.3 %slice.1363 = f32[2,2047,48]{1,2,0:T(8,128)} slice(f32[2,4096,48]{1,2,0:T(8,128)S(1)} %get-tuple-element.260), slice={[0:2:1], [2:4096:2], [0:48:1]} | slice | bytes 1572096 | tf_op jit(solution)/shard_map/slice | solution.py:104
  300.8 26.9 slice.1197
  327.7 26.9 slice.1192
  354.6 27.1 %slice.1196 = f32[2,2048,48]{1,2,0:T(8,128)} slice(f32[2,4096,48]{1,2,0:T(8,128)S(1)} %get-tuple-element.261), slice={[0:2:1], [0:4095:2], [0:48:1]} | slice | bytes 1572864 | tf_op jit(solution)/shard_map/slice | solution.py:104
  381.7 26.9 slice.1190
  413.9 14.9 slice.1206
  443.4 15.1 slice.1198
  504.0 14.9 slice.1361
  533.6 15.1 slice.1200
  579.5 14.9 slice.1203
  878.2 26.9 slice.1189
  1053.7 15.5 pad.338
  1084.0 15.6 pad.339
  1099.6 15.6 pad.341
  1117.6 29.3 %pad.345 = f32[2,4096,48]{1,2,0:T(8,128)} pad(f32[2,2048,48]{1,2,0:T(8,128)} %add.1040, f32[]{:T(128)} %constant.44.clone.1), padding=0_0_0x1_0_1x0_0_0 | pad | bytes 2359300 | tf_op jit(solution)/shard_map/pad | solution.py:104
  1149.2 29.1 %pad.343 = f32[2,4096,48]{1,2,0:T(8,128)} pad(f32[2,2048,48]{1,2,0:T(8,128)} %add.1037, f32[]{:T(128)} %constant.44.clone.1), padding=0_0_0x1_0_1x0_0_0 | pad | bytes 2359300 | tf_op jit(solution)/shard_map/pad | solution.py:104
  1184.0 29.0 %pad.344 = f32[2,4096,48]{1,2,0:T(8,128)} pad(f32[2,2048,48]{1,2,0:T(8,128)} %pad_maximum_fusion.3, f32[]{:T(128)} %constant.44.clone.1), padding=0_0_0x0_1_1x0_0_0 | pad | bytes 2359300 | tf_op jit(solution)/shard_map/pad | solution.py:104
  1213.1 29.3 %pad.342 = f32[2,4096,48]{1,2,0:T(8,128)} pad(f32[2,2048,48]{1,2,0:T(8,128)} %pad_maximum_fusion.2, f32[]{:T(128)} %constant.44.clone.1), padding=0_0_0x0_1_1x0_0_0 | pad | bytes 2359300 | tf_op jit(solution)/shard_map/pad | solution.py:104
  1270.7 51.5 %psum.85 = f32[]{:T(128)} all-reduce(f32[]{:T(128)} %convert_reduce_fusion.1), channel_id=1, replica_groups=mesh['seq'=8,'wshard'=4] {'seq','wshard'}, use_global_device_ids=true, to_apply=%region_6.0 | all-reduce | flops 1 | bytes 8 | tf_op jit(solution)/shard_map/psum | solution.py:128
  1401.6 26.9 slice.1558
  1428.5 26.9 slice.1390
  1455.4 26.9 slice.1380
  1482.9 27.3 %slice.1388 = f32[2,2048,48]{1,2,0:T(8,128)} slice(f32[2,4096,48]{1,2,0:T(8,128)S(1)} %concatenate.173), slice={[0:2:1], [1:4096:2], [0:48:1]} | slice | bytes 1572864 | tf_op jit(solution)/shard_map/slice | solution.py:153
  1510.2 26.9 slice.1375
  1537.1 26.9 slice.1373
  1624.1 27.8 %slice.1566 = f32[2,2047,48]{1,2,0:T(8,128)} slice(f32[2,4096,48]{1,2,0:T(8,128)} %copy-done.13), slice={[0:2:1], [1:4094:2], [0:48:1]} | slice | bytes 1572096 | tf_op jit(solution)/shard_map/slice | solution.py:153
  1651.8 27.2 %slice.1396 = f32[2,2048,48]{1,2,0:T(8,128)S(1)} slice(f32[2,4096,48]{1,2,0:T(8,128)} %copy-done.13), slice={[0:2:1], [0:4095:2], [0:48:1]} | slice | bytes 1572864 | tf_op jit(solution)/shard_map/slice | solution.py:153
  1679.0 28.0 %slice.1383 = f32[2,2048,48]{1,2,0:T(8,128)} slice(f32[2,4096,48]{1,2,0:T(8,128)} %copy-done.13), slice={[0:2:1], [1:4096:2], [0:48:1]} | slice | bytes 1572864 | tf_op jit(solution)/shard_map/slice | solution.py:153
  1707.7 26.9 slice.1563
  1734.5 26.9 slice.1385
  1761.4 27.3 %slice.1377 = f32[2,2048,48]{1,2,0:T(8,128)} slice(f32[2,4096,48]{1,2,0:T(8,128)S(1)} %get-tuple-element.99), slice={[0:2:1], [1:4096:2], [0:48:1]} | slice | bytes 1572864 | tf_op jit(solution)/shard_map/slice | solution.py:153
  2303.2 15.6 pad.389
  2324.8 26.1 pad.390
  2350.9 29.1 %pad.391 = f32[2,4096,48]{1,2,0:T(8,128)} pad(f32[2,2048,48]{1,2,0:T(8,128)} %add.1147, f32[]{:T(128)} %constant.44.clone.1), padding=0_0_0x1_0_1x0_0_0 | pad | bytes 2359300 | tf_op jit(solution)/shard_map/pad | solution.py:153
  2382.7 17.0 rev.4
  2400.0 27.4 %pad.393 = f32[2,4096,48]{1,2,0:T(8,128)S(1)} pad(f32[2,2048,48]{1,2,0:T(8,128)} %add.1150, f32[]{:T(128)} %constant.44.clone.1), padding=0_0_0x1_0_1x0_0_0 | pad | bytes 2359300 | tf_op jit(solution)/shard_map/pad | solution.py:153
  2427.4 28.0 %pad.392 = f32[2,4096,48]{1,2,0:T(8,128)} pad(f32[2,2048,48]{1,2,0:T(8,128)S(1)} %pad_maximum_fusion.5, f32[]{:T(128)} %constant.44.clone.1), padding=0_0_0x0_1_1x0_0_0 | pad | bytes 2359300 | tf_op jit(solution)/shard_map/pad | solution.py:153
  2458.1 17.1 rev.5
  2507.6 22.7 reduce-scatter.6.cloned.1.call-done
  2562.4 38.2 %all-reduce.105 = (f32[]{:T(128)}, f32[384]{0:T(512)S(1)}, f32[384]{0:T(512)S(1)}, f32[384]{0:T(512)S(1)}) all-reduce(f32[]{:T(128)} %multiply_reduce_fusion.3, f32[384]{0:T(512)S(1)} %fusion.56, f32[384]{0:T(512)S(1)} %fusion.58, f32[384]{0:T(512)S(1)} %get-tuple-element.45), channel_id=1, replica_groups=mesh['seq'=8,'wshard'=4] {'seq','wshard'}, use_global_device_ids=true, to_apply=%region_4.0 | all-reduce | flops 1153 | bytes 9224 | tf_op jit(solution)/shard_map/psum | solution.py:128
  2626.1 74.2 %all-reduce.109 = (f32[128]{0:T(128)}, f32[128]{0:T(128)}, f32[128,768]{1,0:T(8,128)}, f32[192,512]{1,0:T(8,128)}, f32[128]{0:T(128)}, /*index=5*/f32[128,512]{1,0:T(8,128)}, f32[128]{0:T(128)}) all-reduce(f32[128]{0:T(128)S(1)} %dynamic-slice_convert_fusion.3, ...), channel_id=1, replica_groups=mesh['seq'=8,'wshard'=4] {'seq'}, use_global_device_ids=true, to_apply=%region_11.0 | all-reduce | flops 262656 | bytes 1576960 | tf_op jit(solution)/shard_map/psum | solution.py:204
  (879 shorter events, 1390.7 us)
Async XLA Ops:
  7.2 24.6 copy-start
  7.2 14.9 copy-start.78
  13.5 1355.6 %copy-start.120 = (f32[4,1,128]{2,1,0:T(1,128)}, f32[4,1,128]{2,1,0:T(1,128)S(1)}, u32[]{:S(2)}) copy-start(f32[4,1,128]{2,1,0:T(1,128)S(1)} %convert_element_type.159) | copy-start | bytes 6148
  18.9 1350.2 %copy-start.130 = (f32[4,1,128]{2,1,0:T(1,128)}, f32[4,1,128]{2,1,0:T(1,128)S(1)}, u32[]{:S(2)}) copy-start(f32[4,1,128]{2,1,0:T(1,128)S(1)} %convert_element_type.160) | copy-start | bytes 6148
  20.4 1348.8 %copy-start.108 = (f32[2,512]{1,0:T(2,128)}, f32[2,512]{1,0:T(2,128)S(1)}, u32[]{:S(2)}) copy-start(f32[2,512]{1,0:T(2,128)S(1)} %broadcast_multiply_fusion.2) | copy-start | bytes 12292
  22.1 1347.0 %copy-start.114 = (f32[2,512]{1,0:T(2,128)}, f32[2,512]{1,0:T(2,128)S(1)}, u32[]{:S(2)}) copy-start(f32[2,512]{1,0:T(2,128)S(1)} %fusion.51) | copy-start | bytes 12292
  37.3 63.5 %copy-start.116 = (f32[48]{0:T(128)S(1)}, f32[48]{0:T(128)}, u32[]{:S(2)}) copy-start(f32[48]{0:T(128)} %param.25) | copy-start | bytes 580
  37.4 63.8 %all-to-all-start = ((bf16[2,512,2,384]{1,2,0,3:T(2,128)(2,1)}), bf16[2,512,2,384]{1,2,0,3:T(2,128)(2,1)S(1)}, u32[]{:S(2)}, u32[]{:S(2)}) async-start(bf16[2,512,2,384]{1,2,0,3:T(2,128)(2,1)} %copy.114), calls=%async_computation | async-start | bytes 3145728 | tf_op jit(solution)/shard_map/all_to_all | solution.py:96
  43.4 58.3 %copy-start.142 = (f32[48]{0:T(128)}, f32[48]{0:T(128)S(1)}, u32[]{:S(2)}) copy-start(f32[48]{0:T(128)S(1)} %get-tuple-element.68) | copy-start | bytes 580
  43.4 58.3 %copy-start.144 = (f32[48]{0:T(128)}, f32[48]{0:T(128)S(1)}, u32[]{:S(2)}) copy-start(f32[48]{0:T(128)S(1)} %get-tuple-element.69) | copy-start | bytes 580
  43.5 57.4 %copy-start.138 = (f32[48]{0:T(128)}, f32[48]{0:T(128)S(1)}, u32[]{:S(2)}) copy-start(f32[48]{0:T(128)S(1)} %cos.8) | copy-start | bytes 580
  1265.5 56.8 %copy-start.149 = (bf16[128]{0:T(256)(128)(2,1)S(1)}, bf16[128]{0:T(256)(128)(2,1)}, u32[]{:S(2)}) copy-start(bf16[128]{0:T(256)(128)(2,1)} %param.22) | copy-start | bytes 772
  1265.5 62.3 %copy-start.150 = (bf16[128]{0:T(256)(128)(2,1)S(1)}, bf16[128]{0:T(256)(128)(2,1)}, u32[]{:S(2)}) copy-start(bf16[128]{0:T(256)(128)(2,1)} %param.24) | copy-start | bytes 772
  1265.5 68.3 %copy-start.106 = (bf16[128,512]{1,0:T(8,128)(2,1)S(1)}, bf16[128,512]{1,0:T(8,128)(2,1)}, u32[]{:S(2)}) copy-start(bf16[128,512]{1,0:T(8,128)(2,1)} %param.23) | copy-start | bytes 393220
  1265.5 76.2 %copy-start.79 = (bf16[192,512]{1,0:T(8,128)(2,1)S(1)}, bf16[192,512]{1,0:T(8,128)(2,1)}, u32[]{:S(2)}) copy-start(bf16[192,512]{1,0:T(8,128)(2,1)} %param.21) | copy-start | bytes 589828
  1265.5 85.3 %all-to-all-start.1 = ((bf16[8,2,49152]{2,1,0:T(2,128)(2,1)}), bf16[8,2,49152]{2,1,0:T(2,128)(2,1)}, u32[]{:S(2)}, u32[]{:S(2)}) async-start(bf16[8,2,49152]{2,1,0:T(2,128)(2,1)} %reshape.120), calls=%async_computation.1 | async-start | bytes 3145728 | tf_op jit(solution)/shard_map/all_to_all | solution.py:106
  1327.7 41.4 %copy-start.147 = (f32[4,1,128]{2,1,0:T(1,128)}, f32[4,1,128]{2,1,0:T(1,128)S(1)}, u32[]{:S(2)}) copy-start(f32[4,1,128]{2,1,0:T(1,128)S(1)} %convert_element_type.161) | copy-start | bytes 6148
  1341.6 271.1 %copy-start.122 = (f32[2,512]{1,0:T(2,128)}, f32[2,512]{1,0:T(2,128)S(1)}, u32[]{:S(2)}) copy-start(f32[2,512]{1,0:T(2,128)S(1)} %convert_multiply_fusion.12) | copy-start | bytes 12292
  1396.3 220.2 %all-to-all-start.2 = ((bf16[2,512,2,384]{1,2,0,3:T(2,128)(2,1)}), bf16[2,512,2,384]{1,2,0,3:T(2,128)(2,1)}, u32[]{:S(2)}, u32[]{:S(2)}) async-start(bf16[2,512,2,384]{1,2,0,3:T(2,128)(2,1)} %copy.122), calls=%async_computation.2 | async-start | bytes 3145728 | tf_op jit(solution)/shard_map/all_to_all | solution.py:148
  1400.7 1106.8 %reduce-scatter.8.cloned.1.call-start = ((), (), s32[]{:S(2)}) async-start(), calls=%async_computation.9 | async-start | bytes 655360 | tf_op jit(solution)/shard_map/reduce_scatter | solution.py:188
  1482.9 81.1 %copy-start.23 = (f32[2,2047,48]{1,2,0:T(8,128)S(1)}, f32[2,2047,48]{1,2,0:T(8,128)}, u32[]{:S(2)}) copy-start(f32[2,2047,48]{1,2,0:T(8,128)} %slice.1558) | copy-start | bytes 2358148
  1537.1 38.6 %copy-start.22 = (f32[2,2048,48]{1,2,0:T(8,128)S(1)}, f32[2,2048,48]{1,2,0:T(8,128)}, u32[]{:S(2)}) copy-start(f32[2,2048,48]{1,2,0:T(8,128)} %slice.1390) | copy-start | bytes 2359300
  1581.5 27.5 %copy-start.5 = (f32[2,4096,48]{1,2,0:T(8,128)S(1)}, f32[2,4096,48]{1,2,0:T(8,128)}, u32[]{:S(2)}) copy-start(f32[2,4096,48]{1,2,0:T(8,128)} %pad.343) | copy-start | bytes 4718596
  1581.5 27.5 %copy-start.8 = (f32[2,4096,48]{1,2,0:T(8,128)S(1)}, f32[2,4096,48]{1,2,0:T(8,128)}, u32[]{:S(2)}) copy-start(f32[2,4096,48]{1,2,0:T(8,128)} %pad.342) | copy-start | bytes 4718596
  1788.7 15.0 copy-start.26
  1788.7 20.8 copy-start.25
  1920.1 70.0 %copy-start.34 = (f32[2,1024,48]{1,2,0:T(8,128)S(1)}, f32[2,1024,48]{1,2,0:T(8,128)}, u32[]{:S(2)}) copy-start(f32[2,1024,48]{1,2,0:T(8,128)} %slice.1401) | copy-start | bytes 1179652
  1920.1 70.0 %copy-start.35 = (f32[2,1024,48]{1,2,0:T(8,128)S(1)}, f32[2,1024,48]{1,2,0:T(8,128)}, u32[]{:S(2)}) copy-start(f32[2,1024,48]{1,2,0:T(8,128)} %slice.1393) | copy-start | bytes 1179652
  2238.9 22.5 copy-start.37
  2238.9 22.4 copy-start.38
  2382.7 17.0 copy-start.30
  2458.1 17.1 copy-start.10
  2458.1 17.1 copy-start.61
  2458.1 17.1 copy-start.135
  2458.1 17.1 copy-start.137
  2495.5 43.0 %all-to-all-start.3 = ((bf16[8,2,49152]{2,1,0:T(2,128)(2,1)}), bf16[8,2,49152]{2,1,0:T(2,128)(2,1)S(1)}, u32[]{:S(2)}, u32[]{:S(2)}) async-start(bf16[8,2,49152]{2,1,0:T(2,128)(2,1)} %reshape.122), calls=%async_computation.3 | async-start | bytes 3145728 | tf_op jit(solution)/shard_map/all_to_all | solution.py:165
  2501.5 28.8 %copy-start.117 = (f32[48]{0:T(128)S(1)}, f32[48]{0:T(128)}, u32[]{:S(2)}) copy-start(f32[48]{0:T(128)} %param.25) | copy-start | bytes 580
  2501.5 28.8 %copy-start.119 = (f32[48]{0:T(128)S(1)}, f32[48]{0:T(128)}, u32[]{:S(2)}) copy-start(f32[48]{0:T(128)} %param.26) | copy-start | bytes 580
  2501.5 28.8 %copy-start.129 = (f32[48]{0:T(128)S(1)}, f32[48]{0:T(128)}, u32[]{:S(2)}) copy-start(f32[48]{0:T(128)} %copy-done.128) | copy-start | bytes 580
  2501.5 28.8 %copy-start.127 = (f32[48]{0:T(128)S(1)}, f32[48]{0:T(128)}, u32[]{:S(2)}) copy-start(f32[48]{0:T(128)} %param.27) | copy-start | bytes 580
  2501.5 28.8 %copy-start.139 = (f32[48]{0:T(128)S(1)}, f32[48]{0:T(128)}, u32[]{:S(2)}) copy-start(f32[48]{0:T(128)} %copy-done.138) | copy-start | bytes 580
  2501.5 28.8 %copy-start.141 = (f32[48]{0:T(128)S(1)}, f32[48]{0:T(128)}, u32[]{:S(2)}) copy-start(f32[48]{0:T(128)} %copy-done.140) | copy-start | bytes 580
  2501.5 28.8 %copy-start.143 = (f32[48]{0:T(128)S(1)}, f32[48]{0:T(128)}, u32[]{:S(2)}) copy-start(f32[48]{0:T(128)} %copy-done.142) | copy-start | bytes 580
  2501.5 28.8 %copy-start.145 = (f32[48]{0:T(128)S(1)}, f32[48]{0:T(128)}, u32[]{:S(2)}) copy-start(f32[48]{0:T(128)} %copy-done.144) | copy-start | bytes 580
  2501.6 29.0 %copy-start.125 = (f32[48]{0:T(128)S(1)}, f32[48]{0:T(128)}, u32[]{:S(2)}) copy-start(f32[48]{0:T(128)} %copy-done.124) | copy-start | bytes 580
  2501.6 29.0 %copy-start.133 = (f32[48]{0:T(128)S(1)}, f32[48]{0:T(128)}, u32[]{:S(2)}) copy-start(f32[48]{0:T(128)} %copy-done.132) | copy-start | bytes 580
  2501.6 28.7 %reduce-scatter.6.cloned.1.call-start = ((), (), s32[]{:S(2)}) async-start(), calls=%async_computation.8 | async-start | bytes 983040 | tf_op jit(solution)/shard_map/reduce_scatter | solution.py:185
  2505.6 120.5 %reduce-scatter.4.cloned.1.call-start = ((), (), s32[]{:S(2)}) async-start(), calls=%async_computation.7 | async-start | bytes 983040 | tf_op jit(solution)/shard_map/reduce_scatter | solution.py:182
  (111 other events, 606.7 us)
Sparse Core Ops, SparseCore 0:
  1616.6 22.9 reduce-scatter.7
  2505.7 24.5 reduce-scatter.5
  2601.4 24.6 reduce-scatter.3
where the time goes:
time: 2730 us; the launch traced here: 2710 us
  local copies, waits for them, and re-layouts  2180 us (80%)
  blocking collectives  276 us (10%)
  other arithmetic  145 us (5%)
  waiting for transfers between devices  40.1 us (1%)
    slice x138, local copies, waits for them, and re-layouts, per_device(): lax.associative_scan(combine, (step_re, step_im, inject_re, inject_im), a...  775 us
    slice x146, local copies, waits for them, and re-layouts, per_device(): lax.associative_scan(combine, (back_re, back_im, incoming_re, incoming_im...  743 us
    pad x44, local copies, waits for them, and re-layouts, per_device(): lax.associative_scan(combine, (step_re, step_im, inject_re, inject_im), a...  275 us
    pad x44, local copies, waits for them, and re-layouts, per_device(): lax.associative_scan(combine, (back_re, back_im, incoming_re, incoming_im...  224 us
    psum x2, blocking collectives, per_device(): lax.psum((jnp.sum(mask_f * jnp.sum(errors * errors, -1)), jnp.sum(mask_f)...  89.7 us
    psum x1, blocking collectives, per_device(): lax.psum((shares[0], shares[1], shares[2], shares[3], shares[4], shares[5...  74.2 us
    unnamed x313, local copies, waits for them, and re-layouts  68.7 us
    all_gather x1, blocking collectives, per_device(): seg_whole = lax.all_gather(segment_ids, 'seq', axis=1, tiled=True)  57.3 us
  transfers between devices with their start and end apart: 7, of which 3 were waited for; matrix products, arithmetic and copies ran while one was open for 41% of the time, Pallas kernels for 0%

commit v1 on v0

v1 whole, which is shorter than its diff:
```python
import functools

import jax
import jax.numpy as jnp
from jax import lax
from jax.experimental import pallas as pl
from jax.experimental.pallas import tpu as pltpu
from jax.sharding import PartitionSpec as P

CHUNKS = 8
LANES = 128
TILE = 256
MIB = 1024 * 1024
F32 = jnp.float32
BF16 = jnp.bfloat16


def rates_map(real_rate, imag_rate, log_rate):
    time_step = jnp.exp(log_rate)
    grow_re = real_rate * time_step
    turn_im = imag_rate * time_step
    growth = jnp.exp(grow_re)
    abar_re = growth * jnp.cos(turn_im)
    abar_im = growth * jnp.sin(turn_im)
    half_sine = jnp.sin(0.5 * turn_im)
    numer_re = jnp.expm1(grow_re) * jnp.cos(turn_im) - 2.0 * half_sine * half_sine
    divisor = real_rate * real_rate + imag_rate * imag_rate
    scale_re = (numer_re * real_rate + abar_im * imag_rate) / divisor
    scale_im = (abar_im * real_rate - numer_re * imag_rate) / divisor
    return (abar_re, abar_im, scale_re, scale_im)


def cmul(xr, xi, yr, yi):
    return xr * yr - xi * yi, xr * yi + xi * yr


def power2(xr, xi, times):
    for _ in range(times):
        xr, xi = xr * xr - xi * xi, 2.0 * xr * xi
    return xr, xi


def log2(n):
    return n.bit_length() - 1


def wide(v, groups):
    return jnp.concatenate([v] * groups, axis=1)


def fold_rows(v):
    return jnp.sum(v.reshape(-1, 8, v.shape[-1]), axis=0)


def take(ref, at, first, count):
    return jnp.concatenate([ref[first + g, at, :] for g in range(count)], axis=1)


def put(ref, at, first, v):
    for g in range(v.shape[1] // LANES):
        ref[first + g, at, :] = v[:, g * LANES : (g + 1) * LANES]


def one_row(v):
    return jnp.sum(v, axis=0, keepdims=True)


def nt_dot(a, b):
    return lax.dot_general(a, b, (((1,), (1,)), ((), ())), preferred_element_type=F32)


def tn_dot(a, b):
    return lax.dot_general(a, b, (((0,), (0,)), ((), ())), preferred_element_type=F32)


def chunk_scan(ar, ai, br, bi, reverse):
    rows = lax.broadcasted_iota(jnp.int32, ar.shape, 0)
    d = 1
    while d < CHUNKS:
        shift = (CHUNKS - d) if reverse else d
        keep = (rows < CHUNKS - d) if reverse else (rows >= d)
        pr, pi = pltpu.roll(ar, shift, 0), pltpu.roll(ai, shift, 0)
        qr, qi = pltpu.roll(br, shift, 0), pltpu.roll(bi, shift, 0)
        mr, mi = cmul(ar, ai, qr, qi)
        br, bi = jnp.where(keep, br + mr, br), jnp.where(keep, bi + mi, bi)
        mr, mi = cmul(ar, ai, pr, pi)
        ar, ai = jnp.where(keep, mr, ar), jnp.where(keep, mi, ai)
        d *= 2
    return ar, ai, br, bi


def carry_in(recvs, ids, s, own_row, ar, ai, block_len, conj):
    states = ar.shape[1]
    pr, pi = power2(ar, -ai if conj else ai, log2(block_len))
    cr = jnp.zeros((1, states), F32)
    ci = jnp.zeros((1, states), F32)
    own = wide(ids[own_row : own_row + 1, :], states // LANES)
    for ref in reversed(recvs):
        msg = ref[s : s + 1, :]
        same = wide(msg[:, 2 * states :], states // LANES) == own
        cr, ci = cmul(pr, pi, cr, ci)
        cr = cr + jnp.where(same, msg[:, :states], 0.0)
        ci = ci + jnp.where(same, msg[:, states : 2 * states], 0.0)
    return cr, ci


def k1_body(w_ref, x_ref, b0, b1, b2, b3, rates_ref, marks_ref, ids_ref,
            low_ref, proj_ref, s1_ref, msg_ref, vec_ref, w_scr, *, seqs):
    rows, width = x_ref.shape
    states = rates_ref.shape[1]
    shard = b0.shape[0] - 16
    groups = states // LANES
    steps = rows // seqs // CHUNKS
    block_len = rows // seqs
    w = w_ref[0]
    for k, piece in enumerate((b0, b1, b2, b3)):
        at = pl.multiple_of((w ^ k) * shard, shard)
        w_scr[pl.ds(at, shard), :] = piece[:shard, :]
        extra = piece[shard:, :].astype(F32)
        for v in range(4):
            vec_ref[v : v + 1, pl.ds(at, shard)] = extra[0:1, v * shard : (v + 1) * shard]
    vec_ref[4:8, :] = jnp.zeros((4, width), F32)
    gain = vec_ref[0:1, :]
    bias = vec_ref[1:2, :]
    for i in range(rows // TILE):
        at = slice(i * TILE, (i + 1) * TILE)
        x = x_ref[at, :].astype(F32)
        c = x - jnp.mean(x, -1, keepdims=True)
        r = lax.rsqrt(jnp.mean(c * c, -1, keepdims=True) + 1e-05)
        low = (c * r * gain + bias).astype(BF16)
        low_ref[at, :] = low
        p = jnp.dot(low, w_scr[...], preferred_element_type=F32)
        put(proj_ref, at, 0, p.astype(BF16).astype(F32))
    a1r, a1i = rates_ref[0:1, :], rates_ref[1:2, :]
    ar = jnp.broadcast_to(a1r, (CHUNKS, states))
    ai = jnp.broadcast_to(a1i, (CHUNKS, states))

    def step(j, carry):
        out = []
        for s in range(seqs):
            ur, ui, q = carry[s]
            at = pl.ds(s * block_len + j, CHUNKS, stride=steps)
            lk = marks_ref[0, at, :]
            lw = wide(lk, groups)
            nr, ni = cmul(ar, ai, ur, ui)
            out.append((lw * nr + take(proj_ref, at, 0, groups), lw * ni + take(proj_ref, at, groups, groups), q * lk))
        return tuple(out)

    zero = jnp.zeros((CHUNKS, states), F32)
    init = tuple((zero, zero, jnp.ones((CHUNKS, LANES), F32)) for _ in range(seqs))
    ends = lax.fori_loop(0, steps, step, init, unroll=8)
    pr, pi = power2(ar, ai, log2(steps))
    for s in range(seqs):
        ur, ui, q = ends[s]
        qw = wide(q, groups)
        sc = chunk_scan(pr * qw, pi * qw, ur, ui, False)
        for v in range(4):
            s1_ref[s * CHUNKS : (s + 1) * CHUNKS, v * states : (v + 1) * states] = sc[v]
        msg_ref[s : s + 1, :states] = sc[2][CHUNKS - 1 :, :]
        msg_ref[s : s + 1, states : 2 * states] = sc[3][CHUNKS - 1 :, :]
        msg_ref[s : s + 1, 2 * states :] = ids_ref[seqs + s : seqs + s + 1, :]


def k2_body(*refs, seqs, hops):
    (w_ref, scale_ref, x_ref, t_ref, marks_ref, ids_ref, low_ref, proj_ref, s1_ref, rates_ref, vec_ref,
     c0, c1, c2, c3) = refs[:15]
    recvs = refs[15 : 15 + hops]
    (out_ref, state_ref, first_ref, gs_ref, gres_ref, gssm_ref, s2_ref, msg_ref, send_ref, keep_ref, sums_ref,
     wc_scr, wg_scr, act_scr, gate_scr, ssl_scr, sl_scr, gc_scr, gg_scr) = refs[15 + hops :]
    rows, width = x_ref.shape
    states = rates_ref.shape[1]
    groups = states // LANES
    block_len = rows // seqs
    steps = block_len // CHUNKS
    g_shard = width // 4
    c_shard = 2 * states // 4
    w = w_ref[0]
    for k, piece in enumerate((c0, c1, c2, c3)):
        wc_scr[pl.ds(pl.multiple_of((w ^ k) * c_shard, c_shard), c_shard), :] = piece[:c_shard, :]
        wg_scr[pl.ds(pl.multiple_of((w ^ k) * g_shard, g_shard), g_shard), :] = piece[c_shard:, :]
    a1r, a1i = rates_ref[0:1, :], rates_ref[1:2, :]
    ar = jnp.broadcast_to(a1r, (CHUNKS, states))
    ai = jnp.broadcast_to(a1i, (CHUNKS, states))
    zr = jnp.broadcast_to(rates_ref[2:3, :], (CHUNKS, states))
    zi = jnp.broadcast_to(rates_ref[3:4, :], (CHUNKS, states))
    top = lax.broadcasted_iota(jnp.int32, (CHUNKS, states), 0)
    ids = ids_ref[...]
    init = []
    for s in range(seqs):
        cr, ci = carry_in(recvs, ids, s, s, a1r, a1i, block_len, False)
        sc = [s1_ref[s * CHUNKS : (s + 1) * CHUNKS, v * states : (v + 1) * states] for v in range(4)]
        mr, mi = cmul(sc[0], sc[1], cr, ci)
        br = jnp.where(top == 0, cr, pltpu.roll(sc[2] + mr, 1, 0))
        bi = jnp.where(top == 0, ci, pltpu.roll(sc[3] + mi, 1, 0))
        init.append((br, bi))
        fr, fi = cmul(zr, zi, br, bi)
        first_ref[s * CHUNKS : (s + 1) * CHUNKS, :states] = fr
        first_ref[s * CHUNKS : (s + 1) * CHUNKS, states:] = fi

    def step(j, carry):
        out = []
        for s in range(seqs):
            ur, ui = carry[s]
            at = pl.ds(s * block_len + j, CHUNKS, stride=steps)
            lw = wide(marks_ref[0, at, :], groups)
            nr, ni = cmul(ar, ai, ur, ui)
            ur, ui = lw * nr + take(proj_ref, at, 0, groups), lw * ni + take(proj_ref, at, groups, groups)
            sr, si = cmul(zr, zi, ur, ui)
            put(state_ref, at, 0, sr)
            put(state_ref, at, groups, si)
            out.append((ur, ui))
        return tuple(out)

    lax.fori_loop(0, steps, step, tuple(init), unroll=8)

    grad_scale = scale_ref[0, 0]
    skip = vec_ref[2:3, :]
    gbias = vec_ref[3:4, :]
    loss_acc = jnp.zeros((8, width), F32)
    gbias_acc = jnp.zeros((8, width), F32)
    skip_acc = jnp.zeros((8, width), F32)
    for i in range(rows // TILE):
        at = slice(i * TILE, (i + 1) * TILE)
        sl = take(state_ref, at, 0, 2 * groups).astype(BF16)
        sl_scr[at, :] = sl
        low_f = low_ref[at, :].astype(F32)
        so = jnp.dot(sl, wc_scr[...], preferred_element_type=F32) + skip * low_f
        z = jnp.abs(so) * 0.7071067811865476
        e = jnp.exp(-z * z)
        t = 1.0 / (1.0 + 0.3275911 * z)
        poly = t * (0.254829592 + t * (-0.284496736 + t * (1.421413741 + t * (-1.453152027 + t * 1.061405429))))
        tail = 0.5 * poly * e
        phi = jnp.where(so >= 0.0, 1.0 - tail, tail)
        act = (so * phi).astype(BF16)
        act_scr[at, :] = act
        dgelu = phi + so * e * 0.3989422804014327
        act_f = act.astype(F32)
        g = 0.5 * jnp.tanh(0.5 * (jnp.dot(act, wg_scr[...], preferred_element_type=F32) + gbias)) + 0.5
        res = x_ref[at, :].astype(F32) + act_f * g
        out_ref[at, :] = res.astype(BF16)
        err = res - t_ref[at, :].astype(F32)
        em = err * wide(marks_ref[1, at, :], width // LANES)
        loss_acc = loss_acc + fold_rows(em * err)
        gr = grad_scale * em
        gres_ref[at, :] = gr
        gg = gr * act_f * g * (1.0 - g)
        gbias_acc = gbias_acc + fold_rows(gg)
        gl = gg.astype(BF16)
        gate_scr[at, :] = gl
        gssm = dgelu * (gr * g + nt_dot(gl, wg_scr[...]))
        gssm_ref[at, :] = gssm
        skip_acc = skip_acc + fold_rows(gssm * low_f)
        ssl = gssm.astype(BF16)
        ssl_scr[at, :] = ssl
        put(gs_ref, at, 0, nt_dot(ssl, wc_scr[...]).astype(BF16).astype(F32))
    sums_ref[0:1, :] = one_row(gbias_acc)
    sums_ref[1:2, :] = one_row(skip_acc)
    sums_ref[2:3, :] = one_row(loss_acc)
    sums_ref[3:8, :] = jnp.zeros((5, width), F32)

    def back(i, carry):
        j = steps - 1 - i
        out = []
        for s in range(seqs):
            yr, yi, q = carry[s]
            at = pl.ds(s * block_len + j, CHUNKS, stride=steps)
            lk = marks_ref[0, at, :]
            lw = wide(lk, groups)
            nr, ni = cmul(ar, -ai, yr, yi)
            out.append((lw * (nr + take(gs_ref, at, 0, groups)), lw * (ni + take(gs_ref, at, groups, groups)), q * lk))
        return tuple(out)

    zero = jnp.zeros((CHUNKS, states), F32)
    init = tuple((zero, zero, jnp.ones((CHUNKS, LANES), F32)) for _ in range(seqs))
    ends = lax.fori_loop(0, steps, back, init, unroll=8)
    pr, pi = power2(ar, -ai, log2(steps))
    for s in range(seqs):
        yr, yi, q = ends[s]
        qw = wide(q, groups)
        sc = chunk_scan(pr * qw, pi * qw, yr, yi, True)
        for v in range(4):
            s2_ref[s * CHUNKS : (s + 1) * CHUNKS, v * states : (v + 1) * states] = sc[v]
        msg_ref[s : s + 1, :states] = sc[2][:1, :]
        msg_ref[s : s + 1, states : 2 * states] = sc[3][:1, :]
        msg_ref[s : s + 1, 2 * states :] = ids_ref[s : s + 1, :]

    gg_scr[...] = tn_dot(act_scr[...], gate_scr[...])
    gc_scr[...] = tn_dot(sl_scr[...], ssl_scr[...])
    for k, (dst, slot) in enumerate(((keep_ref, 0), (send_ref, 0), (keep_ref, 1), (send_ref, 1))):
        q = w ^ k
        dst[slot, :c_shard, :] = gc_scr[pl.ds(pl.multiple_of(q * c_shard, c_shard), c_shard), :].astype(BF16)
        dst[slot, c_shard:, :] = gg_scr[pl.ds(pl.multiple_of(q * g_shard, g_shard), g_shard), :].astype(BF16)


def split16(v):
    high = v.astype(BF16)
    return high, (v - high.astype(F32)).astype(BF16)


def k3_body(*refs, seqs, hops):
    (w_ref, x_ref, marks_ref, ids_ref, low_ref, proj_ref, state_ref, first_ref, gs_ref, gres_ref, gssm_ref,
     s2_ref, sums_ref, rates_ref, vec_ref, b0, b1, b2, b3) = refs[:19]
    recvs = refs[19 : 19 + hops]
    (ingrad_ref, send_ref, keep_ref, gp_scr, gpl_scr, w_scr, gb_scr, vec_scr) = refs[19 + hops :]
    rows, width = x_ref.shape
    states = rates_ref.shape[1]
    groups = states // LANES
    block_len = rows // seqs
    steps = block_len // CHUNKS
    shard = b0.shape[0] - 16
    w = w_ref[0]
    for k, piece in enumerate((b0, b1, b2, b3)):
        w_scr[pl.ds(pl.multiple_of((w ^ k) * shard, shard), shard), :] = piece[:shard, :]
    a1r, a1i = rates_ref[0:1, :], rates_ref[1:2, :]
    ar = jnp.broadcast_to(a1r, (CHUNKS, states))
    ai = jnp.broadcast_to(a1i, (CHUNKS, states))
    zr = jnp.broadcast_to(rates_ref[2:3, :], (CHUNKS, states))
    zi = jnp.broadcast_to(rates_ref[3:4, :], (CHUNKS, states))
    rowid = lax.broadcasted_iota(jnp.int32, (CHUNKS, states), 0)
    ids = ids_ref[...]
    rate_sums = [jnp.zeros((CHUNKS, states), F32) for _ in range(4)]
    for s in range(seqs):
        cr, ci = carry_in(recvs, ids, s, seqs + s, a1r, a1i, block_len, True)
        sc = [s2_ref[s * CHUNKS : (s + 1) * CHUNKS, v * states : (v + 1) * states] for v in range(4)]
        mr, mi = cmul(sc[0], sc[1], cr, ci)
        yr = jnp.where(rowid == CHUNKS - 1, cr, pltpu.roll(sc[2] + mr, CHUNKS - 1, 0))
        yi = jnp.where(rowid == CHUNKS - 1, ci, pltpu.roll(sc[3] + mi, CHUNKS - 1, 0))

        def one(j, at, prev_r, prev_i, carry):
            yr, yi, gar, gai, gsr, gsi = carry
            lw = wide(marks_ref[0, at, :], groups)
            nr, ni = cmul(ar, -ai, yr, yi)
            dr, di = nr + take(gs_ref, at, 0, groups), ni + take(gs_ref, at, groups, groups)
            yr, yi = lw * dr, lw * di
            pr, pi = take(proj_ref, at, 0, groups), take(proj_ref, at, groups, groups)
            put(gp_scr, at, 0, zr * dr + zi * di)
            put(gp_scr, at, groups, zr * di - zi * dr)
            return (
                yr, yi,
                gar + (prev_r * yr + prev_i * yi), gai + (prev_r * yi - prev_i * yr),
                gsr + (pr * dr + pi * di), gsi + (pr * di - pi * dr),
            )

        def step(i, carry):
            j = steps - 1 - i
            at = pl.ds(s * block_len + j, CHUNKS, stride=steps)
            before = pl.ds(s * block_len + j - 1, CHUNKS, stride=steps)
            return one(j, at, take(state_ref, before, 0, groups), take(state_ref, before, groups, groups), carry)

        carry = lax.fori_loop(0, steps - 1, step, (yr, yi, *rate_sums), unroll=7)
        mine = slice(s * CHUNKS, (s + 1) * CHUNKS)
        at = pl.ds(s * block_len, CHUNKS, stride=steps)
        carry = one(0, at, first_ref[mine, :states], first_ref[mine, states:], carry)
        rate_sums = list(carry[2:])

    skip = vec_ref[2:3, :]
    gain = vec_ref[0:1, :]
    gain_acc = jnp.zeros((8, width), F32)
    bias_acc = jnp.zeros((8, width), F32)
    for i in range(rows // TILE):
        at = slice(i * TILE, (i + 1) * TILE)
        gpl = take(gp_scr, at, 0, 2 * groups).astype(BF16)
        gpl_scr[at, :] = gpl
        gn = nt_dot(gpl, w_scr[...]) + skip * gssm_ref[at, :]
        x = x_ref[at, :].astype(F32)
        c = x - jnp.mean(x, -1, keepdims=True)
        r = lax.rsqrt(jnp.mean(c * c, -1, keepdims=True) + 1e-05)
        n = c * r
        q = gn * gain
        gain_acc = gain_acc + fold_rows(gn * n)
        bias_acc = bias_acc + fold_rows(gn)
        ingrad_ref[at, :] = gres_ref[at, :] + (
            q - jnp.mean(q, -1, keepdims=True) - n * jnp.mean(q * n, -1, keepdims=True)
        ) * r
    gb_scr[...] = tn_dot(low_ref[...], gpl_scr[...])
    sums4 = [one_row(v) for v in rate_sums]
    rate_grads = []
    for k in range(3):
        rate_grads.append(sum(rates_ref[8 + 3 * c + k : 9 + 3 * c + k, :] * sums4[c] for c in range(4)))
    vec_scr[0:1, :] = one_row(gain_acc)
    vec_scr[1:2, :] = one_row(bias_acc)
    vec_scr[2:3, :] = sums_ref[1:2, :]
    vec_scr[3:4, :] = sums_ref[0:1, :]
    loss = jnp.sum(sums_ref[2:3, :], axis=1, keepdims=True)
    extra = 3 * shard // 2
    half = shard // 2
    for k, (dst, slot) in enumerate(((keep_ref, 0), (send_ref, 0), (keep_ref, 1), (send_ref, 1))):
        q = pl.multiple_of((w ^ k) * shard, shard)
        dst[slot, :shard, :] = gb_scr[pl.ds(q, shard), :width].astype(BF16)
        dst[slot, shard:extra, : width // 2] = gb_scr[pl.ds(q, half), width:].astype(BF16)
        dst[slot, shard:extra, width // 2 :] = gb_scr[pl.ds(q + half, half), width:].astype(BF16)
        vec = jnp.concatenate([vec_scr[v : v + 1, pl.ds(q, shard)] for v in range(4)], axis=1)
        lines = [vec] + [jnp.concatenate([g, jnp.zeros((1, width - states), F32)], axis=1) for g in rate_grads]
        lines += [jnp.broadcast_to(loss, (1, width)), jnp.zeros((3, width), F32)]
        high, rest = split16(jnp.concatenate(lines, axis=0))
        dst[slot, extra:, :] = jnp.concatenate([high.astype(F32), rest.astype(F32)], axis=0).astype(BF16)


def whole(n, smem=()):
    return [pl.BlockSpec(memory_space=pltpu.SMEM if i in smem else pltpu.VMEM) for i in range(n)]


def call(body, outs, scratch, smem, *args, flops=1_000_000_000, limit=60):
    return pl.pallas_call(
        body,
        out_shape=[jax.ShapeDtypeStruct(*o) for o in outs],
        in_specs=whole(len(args), smem),
        out_specs=whole(len(outs)),
        scratch_shapes=[pltpu.VMEM(*s) for s in scratch],
        compiler_params=pltpu.CompilerParams(vmem_limit_bytes=limit * MIB),
        cost_estimate=pl.CostEstimate(flops=flops, bytes_accessed=8 * MIB, transcendentals=0),
    )(*args)


def per_device(inputs, teacher, segment_ids, valid_mask, ln_gain, ln_bias, b_weight, c_weight, skip_weight,
               glu_weight, glu_bias, lambda_real, lambda_imag, log_step):
    S, W = lax.axis_size("seq"), lax.axis_size("wshard")
    s_at, w_at = lax.axis_index("seq"), lax.axis_index("wshard")
    seqs, block_len, width = inputs.shape
    rows = seqs * block_len
    length = S * block_len
    own = lambda_real.shape[0]
    states = own * S
    doc_most = {4096: 1024, 32768: 8192}.get(length, length)
    hops = min((doc_most - 2) // block_len + 1, S - 1)

    def swap(v, axis, n, bit):
        return lax.ppermute(v, axis, [(i, i ^ bit) for i in range(n)])

    def gather4(v):
        far = swap(v, "wshard", W, 2)
        near = swap(v, "wshard", W, 1)
        both = swap(far, "wshard", W, 1)
        return (v, near, far, both)

    shard = b_weight.shape[0]
    line = jnp.concatenate([ln_gain, ln_bias, skip_weight, glu_bias, jnp.zeros((b_weight.shape[1] - 4 * shard,), BF16)])
    b_msg = jnp.concatenate([b_weight, jnp.pad(line[None], ((0, 15), (0, 0)))], 0)
    bs = gather4(b_msg)

    rate_parts, rate_back = jax.vjp(rates_map, lambda_real, lambda_imag, log_step)
    one, zero = jnp.ones_like(lambda_real), jnp.zeros_like(lambda_real)
    jac = []
    for c in range(4):
        jac += list(rate_back(tuple(one if i == c else zero for i in range(4))))
    count = jnp.sum(valid_mask).astype(F32)
    count_line = jnp.where(lax.iota(jnp.int32, own) == 0, count, 0.0)
    mine = jnp.stack(list(rate_parts) + [count_line] + [zero] * 3 + jac + [zero] * 4)
    table = lax.dynamic_update_slice(jnp.zeros((mine.shape[0], states), F32), mine, (0, s_at * own))
    bit = 1
    while bit < S:
        table = table + swap(table, "seq", S, bit)
        bit *= 2
    total = jnp.sum(table[4]).reshape(1, 1)
    for bit in (1, 2):
        total = total + swap(total, "wshard", W, bit)
    grad_scale = (length * seqs * W) / total

    cs = gather4(jnp.concatenate([c_weight, glu_weight], 0))

    same = (segment_ids[:, 1:] == segment_ids[:, :-1]).astype(F32)
    link = jnp.concatenate([jnp.ones((seqs, 1), F32), same], 1).reshape(rows, 1)
    mask = valid_mask.astype(F32).reshape(rows, 1)
    marks = jnp.broadcast_to(jnp.stack([link, mask]), (2, rows, LANES))
    ends = jnp.concatenate([segment_ids[:, 0], segment_ids[:, -1]]).astype(F32)
    ids = jnp.broadcast_to(ends[:, None], (2 * seqs, LANES))

    wid = w_at.astype(jnp.int32).reshape(1)
    x = inputs.reshape(rows, width)
    teach = teacher.reshape(rows, width)
    R = seqs * CHUNKS
    slab = (2 * states // LANES, rows, LANES)
    msg_shape = ((seqs, 2 * states + LANES), F32)
    low, proj, s1, fwd, vec = call(
        functools.partial(k1_body, seqs=seqs),
        [((rows, width), BF16), (slab, F32), ((R, 4 * states), F32), msg_shape, ((8, width), F32)],
        [((width, 2 * states), BF16)],
        (0,),
        wid, x, *bs, table, marks, ids,
    )
    fwds = [lax.ppermute(fwd, "seq", [(i, i + k) for i in range(S - k)]) for k in range(1, hops + 1)]
    shard2 = c_weight.shape[0] + glu_weight.shape[0]
    out, state, first, gs, gres, gssm, s2, bwd, send_c, keep_c, sums = call(
        functools.partial(k2_body, seqs=seqs, hops=hops),
        [((rows, width), BF16), (slab, F32), ((R, 2 * states), F32), (slab, F32),
         ((rows, width), F32), ((rows, width), F32), ((R, 4 * states), F32), msg_shape,
         ((2, shard2, width), BF16), ((2, shard2, width), BF16), ((8, width), F32)],
        [((2 * states, width), BF16), ((width, width), BF16), ((rows, width), BF16), ((rows, width), BF16),
         ((rows, width), BF16), ((rows, 2 * states), BF16), ((2 * states, width), F32), ((width, width), F32)],
        (0, 1),
        wid, grad_scale, x, teach, marks, ids, low, proj, s1, table, vec, *cs, *fwds,
    )
    bwds = [lax.ppermute(bwd, "seq", [(i + k, i) for i in range(S - k)]) for k in range(1, hops + 1)]
    extra = 3 * shard // 2
    ingrad, send_b, keep_b = call(
        functools.partial(k3_body, seqs=seqs, hops=hops),
        [((rows, width), F32), ((2, extra + 16, width), BF16), ((2, extra + 16, width), BF16)],
        [(slab, F32), ((rows, 2 * states), BF16), ((width, 2 * states), BF16),
         ((width, 2 * states), F32), ((8, width), F32)],
        (0,),
        wid, x, marks, ids, low, proj, state, first, gs, gres, gssm, s2, sums, table, vec, *bs, *bwds,
    )

    def add16(a, b):
        return (a.astype(F32) + b.astype(F32)).astype(BF16)

    def add_split(a, b):
        v = a[..., :8, :].astype(F32) + b[..., :8, :].astype(F32)
        v = v + (a[..., 8:, :].astype(F32) + b[..., 8:, :].astype(F32))
        high, rest = split16(v)
        return jnp.concatenate([high, rest], -2)

    got = swap(send_c, "wshard", W, 1)
    far = swap(add16(keep_c[1], got[1]), "wshard", W, 2)
    bulk_c = (keep_c[0].astype(F32) + got[0].astype(F32) + far.astype(F32)).astype(BF16)

    def add_b(a, b):
        return jnp.concatenate([add16(a[:extra], b[:extra]), add_split(a[extra:], b[extra:])], 0)

    got = swap(send_b, "wshard", W, 1)
    far = swap(add_b(keep_b[1], got[1]), "wshard", W, 2)
    full_b = add_b(add_b(keep_b[0], got[0]), far)

    bulk = jnp.concatenate([full_b[:extra], bulk_c], 0)
    part = bulk.shape[0] // S
    tails = jnp.broadcast_to(full_b[None, extra:], (S, 16, width))
    parts = jnp.concatenate([bulk.reshape(S, part, width), tails], 1)
    arrived = lax.all_to_all(parts, "seq", 0, 0, tiled=True).astype(F32)
    summed = jnp.sum(arrived[:, :part], 0).astype(BF16)
    tail = jnp.sum(arrived[:, part : part + 8] + arrived[:, part + 8 :], 0)
    spread = lax.all_to_all(jnp.broadcast_to(summed[None], (S, part, width)), "seq", 0, 0, tiled=True)
    bulk = spread.reshape(S * part, width).astype(F32)
    half = shard // 2
    right = bulk[shard:extra]
    gb = jnp.concatenate([bulk[:shard], jnp.concatenate([right[:, : width // 2], right[:, width // 2 :]], 0)], 1)
    gc = bulk[extra : extra + c_weight.shape[0]]
    gg = bulk[extra + c_weight.shape[0] :]
    vecs = tail[0].reshape(4, shard)
    rate_out = lax.dynamic_slice(tail[1:4], (0, s_at * own), (3, own))
    loss = tail[4, 0] / (total[0, 0] * width)
    return (
        out.reshape(inputs.shape), loss, ingrad.reshape(inputs.shape), vecs[0], vecs[1], gb, gc, vecs[2], gg, vecs[3],
        rate_out[0], rate_out[1], rate_out[2],
    )


def solution(mesh):
    placed = (
        P("wshard", "seq", None), P("wshard", "seq", None), P("wshard", "seq"), P("wshard", "seq"),
        P("wshard"), P("wshard"), P("wshard", None), P("wshard", None), P("wshard"), P("wshard", None), P("wshard"),
        P("seq"), P("seq"), P("seq"),
    )
    return jax.shard_map(
        per_device,
        mesh=mesh,
        in_specs=placed,
        out_specs=(
            P("wshard", "seq", None), P(), P("wshard", "seq", None), P("wshard"), P("wshard"), P("wshard", None),
            P("wshard", None), P("wshard"), P("wshard", None), P("wshard"), P("seq"), P("seq"), P("seq"),
        ),
        check_vma=False,
    )
```

time: 2730 us -> 176 us (0.06)
  local copies, waits for them, and re-layouts: 2180 us -> 14.6 us
  blocking collectives: 276 us -> 23 us
  other arithmetic: 145 us -> 13.2 us
  Pallas kernels: 0 us -> 52.9 us
    slice x285 -> x6, local copies, waits for them, and re-layouts: 1520 us -> 2.97 us  [the longest x1 0.91 us: per_device(): ends = jnp.concatenate([segment_ids[:, 0], segment_ids[:, -1]]).astype(F32)]
    pad x88 -> x0, local copies, waits for them, and re-layouts: 499 us -> none  [the longest x44 275 us: per_device(): lax.associative_scan(combine, (step_re, step_im, inject_re, inject_im), a...]
    psum x3 -> x0, blocking collectives: 164 us -> none  [the longest x2 89.7 us: per_device(): lax.psum((jnp.sum(mask_f * jnp.sum(errors * errors, -1)), jnp.sum(mask_f)...]
    all_gather x8 -> x0, blocking collectives: 106 us -> none  [the longest x1 57.3 us: per_device(): seg_whole = lax.all_gather(segment_ids, 'seq', axis=1, tiled=True)]
    add x86 -> x2, other arithmetic: 79.8 us -> 0.62 us  [per_device(): table = table + swap(table, 'seq', S, bit)]
    unnamed x313 -> x33, local copies, waits for them, and re-layouts: 68.7 us -> 5.68 us
    pallas_call x0 -> x3, Pallas kernels: none -> 52.9 us  [call(): pl.pallas_call(body, out_shape=[jax.ShapeDtypeStruct(*o) for o in outs],...]
    rev x2 -> x0, local copies, waits for them, and re-layouts: 34.1 us -> none  [per_device(): lax.associative_scan(combine, (back_re, back_im, incoming_re, incoming_im...]
  transfers between devices with their start and end apart: 7 -> 20, of which waited for: 3 -> 11; matrix products, arithmetic and copies ran while one was open for 41% -> 10% of each run, Pallas kernels for 0% -> 4%
where the time goes in v1:
time: 176 us; the launch traced here: 175 us
  Pallas kernels  52.9 us (30%)
  waiting for transfers between devices  35.4 us (20%)
  starting transfers between devices  30.9 us (18%)
  blocking collectives  23 us (13%)
  local copies, waits for them, and re-layouts  14.6 us (8%)
  other arithmetic  13.2 us (8%)
  between operations  5.41 us (3%)
    pallas_call x3, Pallas kernels, call(): pl.pallas_call(body, out_shape=[jax.ShapeDtypeStruct(*o) for o in outs],...  52.9 us
    all_to_all x1, blocking collectives, per_device(): arrived = lax.all_to_all(parts, 'seq', 0, 0, tiled=True).astype(F32)  23 us
    ppermute x15, waiting for transfers between devices, swap(): return lax.ppermute(v, axis, [(i, i ^ bit) for i in range(n)])  19.8 us
    ppermute x15, starting transfers between devices, swap(): return lax.ppermute(v, axis, [(i, i ^ bit) for i in range(n)])  17.3 us
    all_to_all x1, waiting for transfers between devices, per_device(): lax.all_to_all(jnp.broadcast_to(summed[None], (S, part, width)), 'seq', 0...  11.4 us
    ppermute x2, starting transfers between devices, per_device(): lax.ppermute(fwd, 'seq', [(i, i + k) for i in range(S - k)])  7.34 us
    unnamed x33, local copies, waits for them, and re-layouts  5.68 us
    ppermute x2, waiting for transfers between devices, per_device(): lax.ppermute(bwd, 'seq', [(i + k, i) for i in range(S - k)])  4.22 us
  transfers between devices with their start and end apart: 20, of which 11 were waited for; matrix products, arithmetic and copies ran while one was open for 10% of the time, Pallas kernels for 4%

profile of v1, /device:TPU:0, one launch (start us, length us, event | category | flops | bytes accessed | tf_op | source)
XLA Modules:
  0.0 175.4 jit_solution(16169362658643193326)
XLA Ops:
  0.7 0.8 dynamic-update-slice.3
  1.5 0.8 dynamic-update-slice.4
  2.3 0.8 dynamic-update-slice.5
  3.2 0.8 dynamic-update-slice.6
  4.2 0.9 fusion.4.b0.refs_15_
  5.2 3.0 %collective-permute-start.6 = (bf16[144,768]{1,0:T(8,128)(2,1)S(1)}, bf16[144,768]{1,0:T(8,128)(2,1)S(1)}, u32[]{:S(2)}, u32[]{:S(2)}) collective-permute-start(bf16[144,768]{1,0:T(8,128)(2,1)S(1)} %fusion.4.b0.refs_15_), channel_id=1, source_target_pairs={{0,2},{1,3},{2,0},{3,1},{4,6},{5,7},{6,4},{7,5},{8,10},{9,11},{10,... | collective-permute-start | bytes 663560 | tf_op jit(solution)/shard_map/ppermute | solution.py:428
  8.2 0.9 constant_dynamic-update-slice_fusion.1
  9.1 0.9 constant_dynamic-update-slice_fusion.refs_11_
  10.7 1.4 fusion.26
  12.8 0.8 multiply_bitcast_fusion
  13.5 0.8 multiply_bitcast_fusion.1
  14.3 0.8 fusion.15
  16.2 1.8 %collective-permute-start = (f32[24,384]{1,0:T(8,128)S(1)}, f32[24,384]{1,0:T(8,128)S(1)}, u32[]{:S(2)}, u32[]{:S(2)}) collective-permute-start(f32[24,384]{1,0:T(8,128)S(1)} %dynamic_update_slice.5), channel_id=1, source_target_pairs={{0,4},{4,0},{8,12},{12,8},{16,20},{20,16},{24,28},{28,24},{1,5},{5... | collective-permute-start | bytes 110600 | tf_op jit(solution)/shard_map/ppermute | solution.py:428
  18.0 0.8 slice_compare_fusion
  19.0 1.3 collective-permute-done
  20.7 1.9 %collective-permute-start.1 = (f32[24,384]{1,0:T(8,128)S(1)}, f32[24,384]{1,0:T(8,128)S(1)}, u32[]{:S(2)}, u32[]{:S(2)}) collective-permute-start(f32[24,384]{1,0:T(8,128)S(1)} %add.97), channel_id=1, source_target_pairs={{0,8},{4,12},{8,0},{12,4},{16,24},{20,28},{24,16},{28,20},{1,9},{5... | collective-permute-start | bytes 110600 | tf_op jit(solution)/shard_map/ppermute | solution.py:428
  23.1 0.9 slice_reduce_fusion.3
  24.7 2.9 %collective-permute-start.2 = (f32[24,384]{1,0:T(8,128)S(1)}, f32[24,384]{1,0:T(8,128)S(1)}, u32[]{:S(2)}, u32[]{:S(2)}) collective-permute-start(f32[24,384]{1,0:T(8,128)S(1)} %add.98), channel_id=1, source_target_pairs={{0,16},{4,20},{8,24},{12,28},{16,0},{20,4},{24,8},{28,12},{1,17},{... | collective-permute-start | bytes 110600 | tf_op jit(solution)/shard_map/ppermute | solution.py:428
  27.6 1.9 %collective-permute-done.2 = f32[24,384]{1,0:T(8,128)S(1)} collective-permute-done((f32[24,384]{1,0:T(8,128)S(1)}, f32[24,384]{1,0:T(8,128)S(1)}, u32[]{:S(2)}, u32[]{:S(2)}) %collective-permute-start.2) | collective-permute-done | bytes 36896 | tf_op jit(solution)/shard_map/ppermute | solution.py:428
  30.9 1.3 broadcast_in_dim.50.marks_ref.refs_4_.refs_2_
  32.2 7.8 %shard_map.237 = (bf16[1024,512]{1,0:T(8,128)(2,1)}, f32[6,1024,128]{2,1,0:T(8,128)}, f32[16,1536]{1,0:T(8,128)}, f32[2,896]{1,0:T(2,128)}, f32[8,512]{1,0:T(8,128)}) custom-call(s32[1]{0:T(128)} %bitcast.w_ref.refs_0_, bf16[1024,512]{1,0:T(8,128)(2,1)} %bitcast.89, bf16[144,768]{1,0:T(8,128)(2,1)} %copy-done, bf16[144,768]{1,0:T(8,128)(2,1)} %copy-done.7, ...), custom_call_target="tpu_custom_call" | custom-call | flops 1000000000 | bytes 8388608 | tf_op jit(solution)/shard_map/pallas_call | solution.py:404
  40.1 3.8 %collective-permute-start.12 = (f32[2,896]{1,0:T(2,128)}, f32[2,896]{1,0:T(2,128)S(1)}, u32[]{:S(2)}, u32[]{:S(2)}) collective-permute-start(f32[2,896]{1,0:T(2,128)} %get-tuple-element.36), channel_id=1, source_target_pairs={{0,8},{4,12},{8,16},{12,20},{16,24},{20,28},{1,9},{5,13},{9,17},{1... | collective-permute-start | bytes 21512 | tf_op jit(solution)/shard_map/ppermute | solution.py:481
  43.9 3.6 %collective-permute-start.11 = (f32[2,896]{1,0:T(2,128)}, f32[2,896]{1,0:T(2,128)S(1)}, u32[]{:S(2)}, u32[]{:S(2)}) collective-permute-start(f32[2,896]{1,0:T(2,128)} %get-tuple-element.36), channel_id=1, source_target_pairs={{0,4},{4,8},{8,12},{12,16},{16,20},{20,24},{24,28},{1,5},{5,9},{9,... | collective-permute-start | bytes 21512 | tf_op jit(solution)/shard_map/ppermute | solution.py:481
  47.4 1.3 slice_reduce_fusion.1
  48.8 1.4 collective-permute-done.3
  51.4 2.9 %collective-permute-start.4 = (f32[1,1]{1,0:T(1,128)}, f32[1,1]{1,0:T(1,128)}, u32[]{:S(2)}, u32[]{:S(2)}) collective-permute-start(f32[1,1]{1,0:T(1,128)} %add.100), channel_id=1, source_target_pairs={{0,2},{1,3},{2,0},{3,1},{4,6},{5,7},{6,4},{7,5},{8,10},{9,11},{10,... | collective-permute-start | bytes 20 | tf_op jit(solution)/shard_map/ppermute | solution.py:428
  54.3 0.8 collective-permute-done.4
  56.6 22.4 %shard_map.238 = (bf16[1024,512]{1,0:T(8,128)(2,1)}, f32[6,1024,128]{2,1,0:T(8,128)}, f32[16,768]{1,0:T(8,128)}, f32[6,1024,128]{2,1,0:T(8,128)}, f32[1024,512]{...) custom-call(s32[1]{0:T(128)} %bitcast.w_ref.refs_0_, ...), custom_call_target="tpu_custom_call" | custom-call | flops 1000000000 | bytes 8388608 | tf_op jit(solution)/shard_map/pallas_call | solution.py:404
  79.1 1.3 collective-permute-start.14
  80.4 1.5 collective-permute-start.13
  81.9 2.9 %collective-permute-done.14.refs_20_ = f32[2,896]{1,0:T(2,128)S(1)} collective-permute-done((f32[2,896]{1,0:T(2,128)}, f32[2,896]{1,0:T(2,128)S(1)}, u32[]{:S(2)}, u32[]{:S(2)}) %collective-permute-start.14) | collective-permute-done | bytes 7200 | tf_op jit(solution)/shard_map/ppermute | solution.py:493
  84.8 1.3 collective-permute-done.13.refs_19_
  86.7 22.6 %shard_map.239 = (f32[1024,512]{1,0:T(8,128)}, bf16[2,208,512]{2,1,0:T(8,128)(2,1)}, bf16[2,208,512]{2,1,0:T(8,128)(2,1)}) custom-call(s32[1]{0:T(128)} %bitcast.w_ref.refs_0_, bf16[1024,512]{1,0:T(8,128)(2,1)} %bitcast.91, f32[2,1024,128]{2,1,0:T(8,128)} %broadcast_in_dim.50.marks_ref.refs_4_.refs_2_, f32[4,128]{1,0:T(4,128)} %broadcast_in_dim.51.ids_ref.refs_5_.refs_3_, ...), custom_call_target="tpu_custom_call" | custom-call | flops 1000000000 | bytes 8388608 | tf_op jit(solution)/shard_map/pallas_call | solution.py:404
  109.8 1.5 collective-permute-done.15
  111.3 1.0 fusion.6
  113.0 1.6 collective-permute-start.16
  114.6 5.8 %collective-permute-done.16 = bf16[208,512]{1,0:T(8,128)(2,1)S(1)} collective-permute-done((bf16[208,512]{1,0:T(8,128)(2,1)S(1)}, bf16[208,512]{1,0:T(8,128)(2,1)S(1)}, u32[]{:S(2)}, u32[]{:S(2)}) %collective-permute-start.16) | collective-permute-done | bytes 213024 | tf_op jit(solution)/shard_map/ppermute | solution.py:428
  120.4 0.7 subtract_convert_fusion
  121.2 1.6 collective-permute-start.18
  122.8 1.0 fusion.2
  123.8 6.4 %collective-permute-done.18 = bf16[320,512]{1,0:T(8,128)(2,1)S(1)} collective-permute-done((bf16[320,512]{1,0:T(8,128)(2,1)S(1)}, bf16[320,512]{1,0:T(8,128)(2,1)S(1)}, u32[]{:S(2)}, u32[]{:S(2)}) %collective-permute-start.18) | collective-permute-done | bytes 327712 | tf_op jit(solution)/shard_map/ppermute | solution.py:428
  130.5 23.0 %all_to_all.10 = bf16[8,80,512]{2,1,0:T(8,128)(2,1)S(1)} all-to-all(bf16[8,80,512]{2,1,0:T(8,128)(2,1)S(1)} %pad_maximum_fusion), channel_id=1, replica_groups=mesh['seq'=8,'wshard'=4] {'seq'}, dimensions={0} | all-to-all | bytes 1310720 | tf_op jit(solution)/shard_map/all_to_all | solution.py:528
  153.7 0.9 broadcast_in_dim.55
  154.6 3.5 %all-to-all-start.1 = ((bf16[8,64,512]{2,1,0:T(8,128)(2,1)}), bf16[8,64,512]{2,1,0:T(8,128)(2,1)S(1)}, u32[]{:S(2)}, u32[]{:S(2)}) async-start(bf16[8,64,512]{2,1,0:T(8,128)(2,1)} %broadcast_in_dim.55), calls=%async_computation.1 | async-start | bytes 1048576 | tf_op jit(solution)/shard_map/all_to_all | solution.py:531
  160.4 11.4 %all-to-all-done.1 = bf16[8,64,512]{2,1,0:T(8,128)(2,1)S(1)} async-done(((bf16[8,64,512]{2,1,0:T(8,128)(2,1)}), bf16[8,64,512]{2,1,0:T(8,128)(2,1)S(1)}, u32[]{:S(2)}, u32[]{:S(2)}) %all-to-all-start.1) | async-done | bytes 524320 | tf_op jit(solution)/shard_map/all_to_all | solution.py:531
  172.0 0.7 fusion.25
  172.7 0.8 maximum_maximum_fusion
  173.5 0.8 slice.252
  (86 shorter events, 10.1 us)
Async XLA Ops:
  5.1 27.1 %copy-start = (bf16[144,768]{1,0:T(8,128)(2,1)}, bf16[144,768]{1,0:T(8,128)(2,1)S(1)}, u32[]{:S(2)}) copy-start(bf16[144,768]{1,0:T(8,128)(2,1)S(1)} %fusion.4.b0.refs_15_) | copy-start | bytes 663556
  5.2 17.4 %collective-permute-start.6 = (bf16[144,768]{1,0:T(8,128)(2,1)S(1)}, bf16[144,768]{1,0:T(8,128)(2,1)S(1)}, u32[]{:S(2)}, u32[]{:S(2)}) collective-permute-start(bf16[144,768]{1,0:T(8,128)(2,1)S(1)} %fusion.4.b0.refs_15_), channel_id=1, source_target_pairs={{0,2},{1,3},{2,0},{3,1},{4,6},{5,7},{6,4},{7,5},{8,10},{9,11},{10,... | collective-permute-start | bytes 663560 | tf_op jit(solution)/shard_map/ppermute | solution.py:428
  8.2 22.0 %collective-permute-start.5 = (bf16[144,768]{1,0:T(8,128)(2,1)S(1)}, bf16[144,768]{1,0:T(8,128)(2,1)S(1)}, u32[]{:S(2)}, u32[]{:S(2)}) collective-permute-start(bf16[144,768]{1,0:T(8,128)(2,1)S(1)} %fusion.4.b0.refs_15_), channel_id=1, source_target_pairs={{0,1},{1,0},{2,3},{3,2},{4,5},{5,4},{6,7},{7,6},{8,9},{9,8},{10,11... | collective-permute-start | bytes 663560 | tf_op jit(solution)/shard_map/ppermute | solution.py:428
  10.1 30.0 %copy-start.1 = (bf16[320,512]{1,0:T(8,128)(2,1)}, bf16[320,512]{1,0:T(8,128)(2,1)S(1)}, u32[]{:S(2)}) copy-start(bf16[320,512]{1,0:T(8,128)(2,1)S(1)} %constant_dynamic-update-slice_fusion.refs_11_) | copy-start | bytes 983044
  10.1 12.5 %collective-permute-start.9 = (bf16[320,512]{1,0:T(8,128)(2,1)S(1)}, bf16[320,512]{1,0:T(8,128)(2,1)S(1)}, u32[]{:S(2)}, u32[]{:S(2)}) collective-permute-start(bf16[320,512]{1,0:T(8,128)(2,1)S(1)} %constant_dynamic-update-slice_fusion.refs_11_), channel_id=1, source_target_pairs={{0,2},{1,3},{2,0},{3,1},{4,6},{5,7},{6,4},{7,5},{8,10},{9,11},{10,... | collective-permute-start | bytes 983048 | tf_op jit(solution)/shard_map/ppermute | solution.py:428
  10.2 45.6 %collective-permute-start.8 = (bf16[320,512]{1,0:T(8,128)(2,1)S(1)}, bf16[320,512]{1,0:T(8,128)(2,1)S(1)}, u32[]{:S(2)}, u32[]{:S(2)}) collective-permute-start(bf16[320,512]{1,0:T(8,128)(2,1)S(1)} %constant_dynamic-update-slice_fusion.refs_11_), channel_id=1, source_target_pairs={{0,1},{1,0},{2,3},{3,2},{4,5},{5,4},{6,7},{7,6},{8,9},{9,8},{10,11... | collective-permute-start | bytes 983048 | tf_op jit(solution)/shard_map/ppermute | solution.py:428
  16.2 4.0 %collective-permute-start = (f32[24,384]{1,0:T(8,128)S(1)}, f32[24,384]{1,0:T(8,128)S(1)}, u32[]{:S(2)}, u32[]{:S(2)}) collective-permute-start(f32[24,384]{1,0:T(8,128)S(1)} %dynamic_update_slice.5), channel_id=1, source_target_pairs={{0,4},{4,0},{8,12},{12,8},{16,20},{20,16},{24,28},{28,24},{1,5},{5... | collective-permute-start | bytes 110600 | tf_op jit(solution)/shard_map/ppermute | solution.py:428
  20.7 4.0 %collective-permute-start.1 = (f32[24,384]{1,0:T(8,128)S(1)}, f32[24,384]{1,0:T(8,128)S(1)}, u32[]{:S(2)}, u32[]{:S(2)}) collective-permute-start(f32[24,384]{1,0:T(8,128)S(1)} %add.97), channel_id=1, source_target_pairs={{0,8},{4,12},{8,0},{12,4},{16,24},{20,28},{24,16},{28,20},{1,9},{5... | collective-permute-start | bytes 110600 | tf_op jit(solution)/shard_map/ppermute | solution.py:428
  22.6 9.6 %copy-start.6 = (bf16[144,768]{1,0:T(8,128)(2,1)}, bf16[144,768]{1,0:T(8,128)(2,1)S(1)}, u32[]{:S(2)}) copy-start(bf16[144,768]{1,0:T(8,128)(2,1)S(1)} %collective-permute-done.6.b2.refs_17_) | copy-start | bytes 663556
  22.6 7.6 %collective-permute-start.7 = (bf16[144,768]{1,0:T(8,128)(2,1)S(1)}, bf16[144,768]{1,0:T(8,128)(2,1)S(1)}, u32[]{:S(2)}, u32[]{:S(2)}) collective-permute-start(bf16[144,768]{1,0:T(8,128)(2,1)S(1)} %collective-permute-done.6.b2.refs_17_), channel_id=1, source_target_pairs={{0,1},{1,0},{2,3},{3,2},{4,5},{5,4},{6,7},{7,6},{8,9},{9,8},{10,11... | collective-permute-start | bytes 663560 | tf_op jit(solution)/shard_map/ppermute | solution.py:428
  22.6 17.5 %copy-start.3 = (bf16[320,512]{1,0:T(8,128)(2,1)}, bf16[320,512]{1,0:T(8,128)(2,1)S(1)}, u32[]{:S(2)}) copy-start(bf16[320,512]{1,0:T(8,128)(2,1)S(1)} %collective-permute-done.9.refs_13_) | copy-start | bytes 983044
  22.6 33.2 %collective-permute-start.10 = (bf16[320,512]{1,0:T(8,128)(2,1)S(1)}, bf16[320,512]{1,0:T(8,128)(2,1)S(1)}, u32[]{:S(2)}, u32[]{:S(2)}) collective-permute-start(bf16[320,512]{1,0:T(8,128)(2,1)S(1)} %collective-permute-done.9.refs_13_), channel_id=1, source_target_pairs={{0,1},{1,0},{2,3},{3,2},{4,5},{5,4},{6,7},{7,6},{8,9},{9,8},{10,11... | collective-permute-start | bytes 983048 | tf_op jit(solution)/shard_map/ppermute | solution.py:428
  24.7 4.9 %collective-permute-start.2 = (f32[24,384]{1,0:T(8,128)S(1)}, f32[24,384]{1,0:T(8,128)S(1)}, u32[]{:S(2)}, u32[]{:S(2)}) collective-permute-start(f32[24,384]{1,0:T(8,128)S(1)} %add.98), channel_id=1, source_target_pairs={{0,16},{4,20},{8,24},{12,28},{16,0},{20,4},{24,8},{28,12},{1,17},{... | collective-permute-start | bytes 110600 | tf_op jit(solution)/shard_map/ppermute | solution.py:428
  30.2 2.1 %copy-start.7 = (bf16[144,768]{1,0:T(8,128)(2,1)}, bf16[144,768]{1,0:T(8,128)(2,1)S(1)}, u32[]{:S(2)}) copy-start(bf16[144,768]{1,0:T(8,128)(2,1)S(1)} %collective-permute-done.5.b1.refs_16_) | copy-start | bytes 663556
  30.2 2.1 %copy-start.8 = (bf16[144,768]{1,0:T(8,128)(2,1)}, bf16[144,768]{1,0:T(8,128)(2,1)S(1)}, u32[]{:S(2)}) copy-start(bf16[144,768]{1,0:T(8,128)(2,1)S(1)} %collective-permute-done.7.b3.refs_18_) | copy-start | bytes 663556
  40.1 15.7 %collective-permute-start.12 = (f32[2,896]{1,0:T(2,128)}, f32[2,896]{1,0:T(2,128)S(1)}, u32[]{:S(2)}, u32[]{:S(2)}) collective-permute-start(f32[2,896]{1,0:T(2,128)} %get-tuple-element.36), channel_id=1, source_target_pairs={{0,8},{4,12},{8,16},{12,20},{16,24},{20,28},{1,9},{5,13},{9,17},{1... | collective-permute-start | bytes 21512 | tf_op jit(solution)/shard_map/ppermute | solution.py:481
  43.9 12.0 %collective-permute-start.11 = (f32[2,896]{1,0:T(2,128)}, f32[2,896]{1,0:T(2,128)S(1)}, u32[]{:S(2)}, u32[]{:S(2)}) collective-permute-start(f32[2,896]{1,0:T(2,128)} %get-tuple-element.36), channel_id=1, source_target_pairs={{0,4},{4,8},{8,12},{12,16},{16,20},{20,24},{24,28},{1,5},{5,9},{9,... | collective-permute-start | bytes 21512 | tf_op jit(solution)/shard_map/ppermute | solution.py:481
  48.8 1.4 collective-permute-start.3
  51.4 3.7 %collective-permute-start.4 = (f32[1,1]{1,0:T(1,128)}, f32[1,1]{1,0:T(1,128)}, u32[]{:S(2)}, u32[]{:S(2)}) collective-permute-start(f32[1,1]{1,0:T(1,128)} %add.100), channel_id=1, source_target_pairs={{0,2},{1,3},{2,0},{3,1},{4,6},{5,7},{6,4},{7,5},{8,10},{9,11},{10,... | collective-permute-start | bytes 20 | tf_op jit(solution)/shard_map/ppermute | solution.py:428
  55.8 0.7 copy-start.4
  55.8 0.7 copy-start.9
  55.8 0.7 copy-start.10
  55.9 0.8 copy-start.5
  79.1 5.7 %collective-permute-start.14 = (f32[2,896]{1,0:T(2,128)}, f32[2,896]{1,0:T(2,128)S(1)}, u32[]{:S(2)}, u32[]{:S(2)}) collective-permute-start(f32[2,896]{1,0:T(2,128)} %get-tuple-element.45), channel_id=1, source_target_pairs={{8,0},{12,4},{16,8},{20,12},{24,16},{28,20},{9,1},{13,5},{17,9},{2... | collective-permute-start | bytes 21512 | tf_op jit(solution)/shard_map/ppermute | solution.py:493
  80.4 5.7 %collective-permute-start.13 = (f32[2,896]{1,0:T(2,128)}, f32[2,896]{1,0:T(2,128)S(1)}, u32[]{:S(2)}, u32[]{:S(2)}) collective-permute-start(f32[2,896]{1,0:T(2,128)} %get-tuple-element.45), channel_id=1, source_target_pairs={{4,0},{8,4},{12,8},{16,12},{20,16},{24,20},{28,24},{5,1},{9,5},{13... | collective-permute-start | bytes 21512 | tf_op jit(solution)/shard_map/ppermute | solution.py:493
  84.8 1.3 copy-start.11
  86.1 0.6 copy-start.12
  86.7 22.6 %copy-start.13 = (bf16[2,320,512]{2,1,0:T(8,128)(2,1)S(1)}, bf16[2,320,512]{2,1,0:T(8,128)(2,1)}, u32[]{:S(2)}) copy-start(bf16[2,320,512]{2,1,0:T(8,128)(2,1)} %get-tuple-element.49) | copy-start | bytes 1966084
  86.7 34.4 %copy-start.2 = (bf16[2,320,512]{2,1,0:T(8,128)(2,1)S(1)}, bf16[2,320,512]{2,1,0:T(8,128)(2,1)}, u32[]{:S(2)}) copy-start(bf16[2,320,512]{2,1,0:T(8,128)(2,1)} %get-tuple-element.48) | copy-start | bytes 1966084
  109.3 2.0 %collective-permute-start.15 = (bf16[2,208,512]{2,1,0:T(8,128)(2,1)}, bf16[2,208,512]{2,1,0:T(8,128)(2,1)S(1)}, u32[]{:S(2)}, u32[]{:S(2)}) collective-permute-start(bf16[2,208,512]{2,1,0:T(8,128)(2,1)} %get-tuple-element.47), channel_id=1, source_target_pairs={{0,1},{1,0},{2,3},{3,2},{4,5},{5,4},{6,7},{7,6},{8,9},{9,8},{10,11... | collective-permute-start | bytes 1277960 | tf_op jit(solution)/shard_map/ppermute | solution.py:428
  109.3 11.8 %collective-permute-start.17 = (bf16[2,320,512]{2,1,0:T(8,128)(2,1)S(1)}, bf16[2,320,512]{2,1,0:T(8,128)(2,1)S(1)}, u32[]{:S(2)}, u32[]{:S(2)}) collective-permute-start(bf16[2,320,512]{2,1,0:T(8,128)(2,1)S(1)} %copy-done.13), channel_id=1, source_target_pairs={{0,1},{1,0},{2,3},{3,2},{4,5},{5,4},{6,7},{7,6},{8,9},{9,8},{10,11... | collective-permute-start | bytes 1966088 | tf_op jit(solution)/shard_map/ppermute | solution.py:428
  113.0 7.4 %collective-permute-start.16 = (bf16[208,512]{1,0:T(8,128)(2,1)S(1)}, bf16[208,512]{1,0:T(8,128)(2,1)S(1)}, u32[]{:S(2)}, u32[]{:S(2)}) collective-permute-start(bf16[208,512]{1,0:T(8,128)(2,1)S(1)} %pad_maximum_fusion.2), channel_id=1, source_target_pairs={{0,2},{1,3},{2,0},{3,1},{4,6},{5,7},{6,4},{7,5},{8,10},{9,11},{10,... | collective-permute-start | bytes 638984 | tf_op jit(solution)/shard_map/ppermute | solution.py:428
  121.2 9.0 %collective-permute-start.18 = (bf16[320,512]{1,0:T(8,128)(2,1)S(1)}, bf16[320,512]{1,0:T(8,128)(2,1)S(1)}, u32[]{:S(2)}, u32[]{:S(2)}) collective-permute-start(bf16[320,512]{1,0:T(8,128)(2,1)S(1)} %fusion.3), channel_id=1, source_target_pairs={{0,2},{1,3},{2,0},{3,1},{4,6},{5,7},{6,4},{7,5},{8,10},{9,11},{10,... | collective-permute-start | bytes 983048 | tf_op jit(solution)/shard_map/ppermute | solution.py:428
  154.6 17.2 %all-to-all-start.1 = ((bf16[8,64,512]{2,1,0:T(8,128)(2,1)}), bf16[8,64,512]{2,1,0:T(8,128)(2,1)S(1)}, u32[]{:S(2)}, u32[]{:S(2)}) async-start(bf16[8,64,512]{2,1,0:T(8,128)(2,1)} %broadcast_in_dim.55), calls=%async_computation.1 | async-start | bytes 1048576 | tf_op jit(solution)/shard_map/all_to_all | solution.py:531

commit v2 on v1

v2 whole, which is shorter than its diff:
```python
import functools

import jax
import jax.numpy as jnp
from jax import lax
from jax.experimental import pallas as pl
from jax.experimental.pallas import tpu as pltpu
from jax.sharding import Mesh
from jax.sharding import PartitionSpec as P

CHUNKS = 8
LANES = 128
TILE = 256
PAD = 8
MIB = 1024 * 1024
F32 = jnp.float32
BF16 = jnp.bfloat16


def small_expm1(x):
    return x * (1.0 + x / 2 * (1.0 + x / 3 * (1.0 + x / 4 * (1.0 + x / 5 * (1.0 + x / 6)))))


def rates_map(real_rate, imag_rate, log_rate):
    time_step = jnp.exp(log_rate)
    grow_re = real_rate * time_step
    turn_im = imag_rate * time_step
    growth = jnp.exp(grow_re)
    abar_re = growth * jnp.cos(turn_im)
    abar_im = growth * jnp.sin(turn_im)
    half_sine = jnp.sin(0.5 * turn_im)
    numer_re = small_expm1(grow_re) * jnp.cos(turn_im) - 2.0 * half_sine * half_sine
    divisor = real_rate * real_rate + imag_rate * imag_rate
    scale_re = (numer_re * real_rate + abar_im * imag_rate) / divisor
    scale_im = (abar_im * real_rate - numer_re * imag_rate) / divisor
    return (abar_re, abar_im, scale_re, scale_im)


def cmul(xr, xi, yr, yi):
    return xr * yr - xi * yi, xr * yi + xi * yr


def power2(xr, xi, times):
    for _ in range(times):
        xr, xi = xr * xr - xi * xi, 2.0 * xr * xi
    return xr, xi


def log2(n):
    return n.bit_length() - 1


def power(xr, xi, n):
    out = None
    while n:
        if n & 1:
            out = (xr, xi) if out is None else cmul(*out, xr, xi)
        n >>= 1
        if n:
            xr, xi = power2(xr, xi, 1)
    return out


def chunk_powers(ar, ai, steps):
    first = lax.broadcasted_iota(jnp.int32, ar.shape, 0) == 0
    sr, si = power(ar, ai, steps - PAD)
    pr, pi = power(ar, ai, steps)
    return jnp.where(first, sr, pr), jnp.where(first, si, pi)


def padded(i, block_len):
    start = i * TILE + PAD * (2 + i * TILE // block_len)
    return slice(start, start + TILE)


def run(count, body, carry, unroll):
    def block(k, c):
        for u in range(unroll):
            c = body(k * unroll + u, c)
        return c

    whole_blocks = count // unroll
    carry = lax.fori_loop(0, whole_blocks, block, carry)
    for i in range(whole_blocks * unroll, count):
        carry = body(i, carry)
    return carry


def wide(v, groups):
    return jnp.concatenate([v] * groups, axis=1)


def fold_rows(v):
    return jnp.sum(v.reshape(-1, 8, v.shape[-1]), axis=0)


def take(ref, at, first, count):
    return jnp.concatenate([ref[first + g, at, :] for g in range(count)], axis=1)


def put(ref, at, first, v):
    for g in range(v.shape[1] // LANES):
        ref[first + g, at, :] = v[:, g * LANES : (g + 1) * LANES]


def clear_pads(ref, seqs, pitch):
    for g in range(ref.shape[0]):
        ref[g, :PAD, :] = jnp.zeros((PAD, LANES), F32)
        for s in range(seqs):
            ref[g, PAD + s * pitch : 2 * PAD + s * pitch, :] = jnp.zeros((PAD, LANES), F32)


def one_row(v):
    return jnp.sum(v, axis=0, keepdims=True)


def nt_dot(a, b):
    return lax.dot_general(a, b, (((1,), (1,)), ((), ())), preferred_element_type=F32)


def tn_dot(a, b):
    return lax.dot_general(a, b, (((0,), (0,)), ((), ())), preferred_element_type=F32)


def chunk_scan(ar, ai, br, bi, reverse):
    rows = lax.broadcasted_iota(jnp.int32, ar.shape, 0)
    d = 1
    while d < CHUNKS:
        shift = (CHUNKS - d) if reverse else d
        keep = (rows < CHUNKS - d) if reverse else (rows >= d)
        pr, pi = pltpu.roll(ar, shift, 0), pltpu.roll(ai, shift, 0)
        qr, qi = pltpu.roll(br, shift, 0), pltpu.roll(bi, shift, 0)
        mr, mi = cmul(ar, ai, qr, qi)
        br, bi = jnp.where(keep, br + mr, br), jnp.where(keep, bi + mi, bi)
        mr, mi = cmul(ar, ai, pr, pi)
        ar, ai = jnp.where(keep, mr, ar), jnp.where(keep, mi, ai)
        d *= 2
    return ar, ai, br, bi


def carry_in(recvs, ids, s, own_row, ar, ai, block_len, conj):
    states = ar.shape[1]
    pr, pi = power2(ar, -ai if conj else ai, log2(block_len))
    cr = jnp.zeros((1, states), F32)
    ci = jnp.zeros((1, states), F32)
    own = wide(ids[own_row : own_row + 1, :], states // LANES)
    for ref in reversed(recvs):
        msg = ref[s : s + 1, :]
        same = wide(msg[:, 2 * states :], states // LANES) == own
        cr, ci = cmul(pr, pi, cr, ci)
        cr = cr + jnp.where(same, msg[:, :states], 0.0)
        ci = ci + jnp.where(same, msg[:, states : 2 * states], 0.0)
    return cr, ci


def fetch(pairs, sems):
    copies = [pltpu.make_async_copy(src, dst, sems.at[k]) for k, (src, dst) in enumerate(pairs)]
    for c in copies:
        c.start()
    for c in copies:
        c.wait()


def k0_body(at_ref, b_ref, g_ref, n_ref, s_ref, q_ref, lr_ref, li_ref, ls_ref, msg_ref, table_ref,
            b_scr, v_scr, l_scr, scr, sems):
    shard, cols = b_scr.shape
    own = lr_ref.shape[1]
    fetch(
        [(b_ref, b_scr)]
        + [(r, v_scr.at[k]) for k, r in enumerate((g_ref, n_ref, s_ref, q_ref))]
        + [(r, l_scr.at[k]) for k, r in enumerate((lr_ref, li_ref, ls_ref))],
        sems,
    )
    msg_ref[:shard, :] = b_scr[...]
    line = jnp.concatenate([v_scr[k] for k in range(4)] + [jnp.zeros((1, cols - 4 * shard), BF16)], axis=1)
    msg_ref[shard:, :] = jnp.broadcast_to(line, (16, cols))
    scr[...] = jnp.zeros_like(scr)
    for k in range(3):
        scr[k : k + 1, :own] = l_scr[k]
    table_ref[...] = pltpu.roll(scr[...], at_ref[0] * own, 1)


def k0b_body(c_ref, g_ref, seg_hbm, mask_hbm, msg_ref, link_ref, valid_ref, ids_ref, seg_ref, mask_ref, c_scr, g_scr, sems):
    c_shard = c_ref.shape[0]
    seqs, block_len = seg_ref.shape
    fetch([(c_ref, c_scr), (g_ref, g_scr), (seg_hbm, seg_ref), (mask_hbm, mask_ref)], sems)
    msg_ref[:c_shard, :] = c_scr[...]
    msg_ref[c_shard:, :] = g_scr[...]
    seg = seg_ref[...].astype(F32)
    link_ref[:PAD, :] = jnp.ones((PAD, LANES), F32)
    lane = lax.broadcasted_iota(jnp.int32, (1, block_len), 1)
    for s in range(seqs):
        row = seg[s : s + 1, :]
        link = jnp.where((row == pltpu.roll(row, 1, 1)) | (lane == 0), 1.0, 0.0)
        mask = mask_ref[s : s + 1, :].astype(F32)
        start = PAD + s * (block_len + PAD)
        link_ref[start : start + PAD, :] = jnp.ones((PAD, LANES), F32)
        for src, dst, start in ((link, link_ref, start + PAD), (mask, valid_ref, s * block_len)):
            for k in range(block_len // LANES):
                piece = jnp.broadcast_to(src[:, k * LANES : (k + 1) * LANES], (LANES, LANES))
                at = start + k * LANES
                dst[at : at + LANES, :] = jnp.transpose(piece)
        ids_ref[s : s + 1, :] = jnp.broadcast_to(row[:, :1], (1, LANES))
        ids_ref[seqs + s : seqs + s + 1, :] = jnp.broadcast_to(row[:, block_len - 1 :], (1, LANES))


def k1a_body(w_ref, x_ref, b0, b1, b2, b3, low_ref, proj_ref, vec_ref, full_ref, *, seqs):
    rows, width = x_ref.shape
    shard = b0.shape[0] - 16
    block_len = rows // seqs
    pitch = block_len + PAD
    w = w_ref[1]
    for k, piece in enumerate((b0, b1, b2, b3)):
        at = pl.multiple_of((w ^ k) * shard, shard)
        full_ref[pl.ds(at, shard), :] = piece[:shard, :]
        extra = piece[shard:, :].astype(F32)
        for v in range(4):
            vec_ref[v : v + 1, pl.ds(at, shard)] = extra[0:1, v * shard : (v + 1) * shard]
    vec_ref[4:8, :] = jnp.zeros((4, width), F32)
    gain = vec_ref[0:1, :]
    bias = vec_ref[1:2, :]
    for i in range(rows // TILE):
        at = slice(i * TILE, (i + 1) * TILE)
        low = (centre(x_ref[at, :])[0] * gain + bias).astype(BF16)
        low_ref[at, :] = low
        p = jnp.dot(low, full_ref[...], preferred_element_type=F32)
        put(proj_ref, padded(i, block_len), 0, p.astype(BF16).astype(F32))
    clear_pads(proj_ref, seqs, pitch)


def k1b_body(proj_ref, table_ref, link_ref, ids_ref, s1_ref, msg_ref, rates_ref, *, seqs):
    states = table_ref.shape[1]
    groups = states // LANES
    pitch = (proj_ref.shape[1] - PAD) // seqs
    block_len = pitch - PAD
    steps = block_len // CHUNKS + 1
    lam = [table_ref[v : v + 1, :] for v in range(3)]
    parts, back = jax.vjp(rates_map, *lam)
    one, zero = jnp.ones_like(lam[0]), jnp.zeros_like(lam[0])
    for v in range(4):
        rates_ref[v : v + 1, :] = parts[v]
        for k, jac in enumerate(back(tuple(one if i == v else zero for i in range(4)))):
            rates_ref[8 + 3 * v + k : 9 + 3 * v + k, :] = jac
    rates_ref[4:8, :] = jnp.zeros((4, states), F32)
    rates_ref[20:24, :] = jnp.zeros((4, states), F32)
    ar = jnp.broadcast_to(parts[0], (CHUNKS, states))
    ai = jnp.broadcast_to(parts[1], (CHUNKS, states))

    def step(j, carry):
        out = []
        for s in range(seqs):
            ur, ui, q = carry[s]
            at = pl.ds(PAD + s * pitch + j, CHUNKS, stride=steps)
            lk = link_ref[at, :]
            lw = wide(lk, groups)
            nr, ni = cmul(ar, ai, ur, ui)
            out.append((lw * nr + take(proj_ref, at, 0, groups), lw * ni + take(proj_ref, at, groups, groups), q * lk))
        return tuple(out)

    zero = jnp.zeros((CHUNKS, states), F32)
    init = tuple((zero, zero, jnp.ones((CHUNKS, LANES), F32)) for _ in range(seqs))
    ends = run(steps, step, init, 13)
    pr, pi = chunk_powers(ar, ai, steps)
    for s in range(seqs):
        ur, ui, q = ends[s]
        qw = wide(q, groups)
        sc = chunk_scan(pr * qw, pi * qw, ur, ui, False)
        for v in range(4):
            s1_ref[s * CHUNKS : (s + 1) * CHUNKS, v * states : (v + 1) * states] = sc[v]
        msg_ref[s : s + 1, :states] = sc[2][CHUNKS - 1 :, :]
        msg_ref[s : s + 1, states : 2 * states] = sc[3][CHUNKS - 1 :, :]
        msg_ref[s : s + 1, 2 * states :] = ids_ref[seqs + s : seqs + s + 1, :]


def k2_body(*refs, seqs, hops):
    (w_ref, x_ref, t_ref, link_ref, valid_ref, ids_ref, low_ref, proj_ref, s1_ref, rates_ref, vec_ref,
     c0, c1, c2, c3) = refs[:15]
    recvs = refs[15 : 15 + hops]
    (out_ref, state_ref, gs_ref, gres_ref, gssm_ref, s2_ref, msg_ref, send_ref, keep_ref,
     wc_scr, wg_scr, act_scr, gate_scr, ssl_scr, sl_scr, gc_scr, gg_scr, sum_scr) = refs[15 + hops :]
    rows, width = x_ref.shape
    states = rates_ref.shape[1]
    groups = states // LANES
    block_len = rows // seqs
    steps = block_len // CHUNKS + 1
    pitch = block_len + PAD
    g_shard = width // 4
    c_shard = 2 * states // 4
    w = w_ref[1]
    for k, piece in enumerate((c0, c1, c2, c3)):
        wc_scr[pl.ds(pl.multiple_of((w ^ k) * c_shard, c_shard), c_shard), :] = piece[:c_shard, :]
        wg_scr[pl.ds(pl.multiple_of((w ^ k) * g_shard, g_shard), g_shard), :] = piece[c_shard:, :]
    a1r, a1i = rates_ref[0:1, :], rates_ref[1:2, :]
    ar = jnp.broadcast_to(a1r, (CHUNKS, states))
    ai = jnp.broadcast_to(a1i, (CHUNKS, states))
    zr = jnp.broadcast_to(rates_ref[2:3, :], (CHUNKS, states))
    zi = jnp.broadcast_to(rates_ref[3:4, :], (CHUNKS, states))
    top = lax.broadcasted_iota(jnp.int32, (CHUNKS, states), 0)
    ids = ids_ref[...]
    init, carries = [], []
    for s in range(seqs):
        cr, ci = carry_in(recvs, ids, s, s, a1r, a1i, block_len, False)
        sc = [s1_ref[s * CHUNKS : (s + 1) * CHUNKS, v * states : (v + 1) * states] for v in range(4)]
        mr, mi = cmul(sc[0], sc[1], cr, ci)
        init.append((pltpu.roll(sc[2] + mr, 1, 0), pltpu.roll(sc[3] + mi, 1, 0)))
        carries.append((cr, ci))

    def step(j, carry):
        out = []
        for s in range(seqs):
            ur, ui = carry[s]
            at = pl.ds(PAD + s * pitch + j, CHUNKS, stride=steps)
            lw = wide(link_ref[at, :], groups)
            nr, ni = cmul(ar, ai, ur, ui)
            ur, ui = lw * nr + take(proj_ref, at, 0, groups), lw * ni + take(proj_ref, at, groups, groups)
            sr, si = cmul(zr, zi, ur, ui)
            put(state_ref, at, 0, sr)
            put(state_ref, at, groups, si)
            out.append((ur, ui))
        return tuple(out)

    for g in range(2 * groups):
        state_ref[g, :PAD, :] = jnp.zeros((PAD, LANES), F32)
    entry = list(run(PAD, step, tuple(init), PAD))
    for s in range(seqs):
        ur, ui = (jnp.where(top == 0, c, u) for c, u in zip(carries[s], entry[s]))
        sr, si = cmul(zr, zi, ur, ui)
        at = pl.ds(PAD + s * pitch + PAD - 1, CHUNKS, stride=steps)
        put(state_ref, at, 0, sr)
        put(state_ref, at, groups, si)
        entry[s] = (ur, ui)
    run(steps - PAD, lambda i, c: step(i + PAD, c), tuple(entry), 8)

    skip = vec_ref[2:3, :]
    gbias = vec_ref[3:4, :]
    loss_acc = jnp.zeros((8, width), F32)
    gbias_acc = jnp.zeros((8, width), F32)
    skip_acc = jnp.zeros((8, width), F32)
    for i in range(rows // TILE):
        at = slice(i * TILE, (i + 1) * TILE)
        pad_at = padded(i, block_len)
        sl = take(state_ref, pad_at, 0, 2 * groups).astype(BF16)
        sl_scr[at, :] = sl
        low_f = low_ref[at, :].astype(F32)
        so = jnp.dot(sl, wc_scr[...], preferred_element_type=F32) + skip * low_f
        z = jnp.abs(so) * 0.7071067811865476
        e = jnp.exp(-z * z)
        t = 1.0 / (1.0 + 0.3275911 * z)
        poly = t * (0.254829592 + t * (-0.284496736 + t * (1.421413741 + t * (-1.453152027 + t * 1.061405429))))
        tail = 0.5 * poly * e
        phi = jnp.where(so >= 0.0, 1.0 - tail, tail)
        act = (so * phi).astype(BF16)
        act_scr[at, :] = act
        dgelu = phi + so * e * 0.3989422804014327
        act_f = act.astype(F32)
        g = 0.5 * jnp.tanh(0.5 * (jnp.dot(act, wg_scr[...], preferred_element_type=F32) + gbias)) + 0.5
        res = x_ref[at, :].astype(F32) + act_f * g
        out_ref[at, :] = res.astype(BF16)
        err = res - t_ref[at, :].astype(F32)
        em = err * wide(valid_ref[at, :], width // LANES)
        loss_acc = loss_acc + fold_rows(em * err)
        gr = em
        gres_ref[at, :] = gr
        gg = gr * act_f * g * (1.0 - g)
        gbias_acc = gbias_acc + fold_rows(gg)
        gl = gg.astype(BF16)
        gate_scr[at, :] = gl
        gssm = dgelu * (gr * g + nt_dot(gl, wg_scr[...]))
        gssm_ref[at, :] = gssm
        skip_acc = skip_acc + fold_rows(gssm * low_f)
        ssl = gssm.astype(BF16)
        ssl_scr[at, :] = ssl
        put(gs_ref, pad_at, 0, nt_dot(ssl, wc_scr[...]).astype(BF16).astype(F32))
    clear_pads(gs_ref, seqs, pitch)
    sum_scr[0:1, :] = one_row(skip_acc)
    sum_scr[1:2, :] = one_row(gbias_acc)
    loss = jnp.sum(one_row(loss_acc), axis=1, keepdims=True)
    count = one_row(fold_rows(valid_ref[...]))

    def back(i, carry):
        j = steps - 1 - i
        out = []
        for s in range(seqs):
            yr, yi, q = carry[s]
            at = pl.ds(PAD + s * pitch + j, CHUNKS, stride=steps)
            lk = link_ref[at, :]
            lw = wide(lk, groups)
            nr, ni = cmul(ar, -ai, yr, yi)
            out.append((lw * (nr + take(gs_ref, at, 0, groups)), lw * (ni + take(gs_ref, at, groups, groups)), q * lk))
        return tuple(out)

    zero = jnp.zeros((CHUNKS, states), F32)
    init = tuple((zero, zero, jnp.ones((CHUNKS, LANES), F32)) for _ in range(seqs))
    firsts = run(steps - PAD, back, init, 8)
    ends = run(PAD, lambda i, c: back(i + steps - PAD, c), firsts, PAD)
    pr, pi = chunk_powers(ar, -ai, steps)
    for s in range(seqs):
        yr, yi, q = (jnp.where(top[:, : v.shape[1]] == 0, u, v) for u, v in zip(firsts[s], ends[s]))
        qw = wide(q, groups)
        sc = chunk_scan(pr * qw, pi * qw, yr, yi, True)
        for v in range(4):
            s2_ref[s * CHUNKS : (s + 1) * CHUNKS, v * states : (v + 1) * states] = sc[v]
        msg_ref[s : s + 1, :states] = sc[2][:1, :]
        msg_ref[s : s + 1, states : 2 * states] = sc[3][:1, :]
        msg_ref[s : s + 1, 2 * states :] = ids_ref[s : s + 1, :]

    gg_scr[...] = tn_dot(act_scr[...], gate_scr[...])
    gc_scr[...] = tn_dot(sl_scr[...], ssl_scr[...])
    for k, dst in enumerate((keep_ref, send_ref, keep_ref, send_ref)):
        q = w ^ k
        slot = q // 2
        dst[slot, :c_shard, :] = gc_scr[pl.ds(pl.multiple_of(q * c_shard, c_shard), c_shard), :].astype(BF16)
        lanes = pl.multiple_of(q * g_shard, g_shard)
        dst[slot, c_shard : c_shard + g_shard, :] = gg_scr[pl.ds(lanes, g_shard), :].astype(BF16)
        line = jnp.concatenate(
            [sum_scr[v : v + 1, pl.ds(lanes, g_shard)] for v in range(2)]
            + [jnp.broadcast_to(loss, (1, LANES)), count], axis=1)
        dst[slot, c_shard + g_shard :, :] = split_rows([line])


def split16(v):
    high = v.astype(BF16)
    return high, (v - high.astype(F32)).astype(BF16)


def split_rows(lines):
    width = lines[0].shape[1]
    v = jnp.concatenate(lines + [jnp.zeros((8 - len(lines), width), F32)], axis=0)
    high, rest = split16(v)
    return jnp.concatenate([high.astype(F32), rest.astype(F32)], axis=0).astype(BF16)


def k3_body(*refs, seqs, hops):
    (w_ref, x_ref, link_ref, ids_ref, low_ref, proj_ref, state_ref, gs_ref, gssm_ref,
     s2_ref, rates_ref, vec_ref, w_full) = refs[:13]
    recvs = refs[13 : 13 + hops]
    (gn_ref, send_ref, keep_ref, gp_scr, gpl_scr, gb_scr, vec_scr) = refs[13 + hops :]
    rows, width = x_ref.shape
    states = rates_ref.shape[1]
    groups = states // LANES
    block_len = rows // seqs
    steps = block_len // CHUNKS + 1
    pitch = block_len + PAD
    shard = width // 4
    w = w_ref[1]
    a1r, a1i = rates_ref[0:1, :], rates_ref[1:2, :]
    ar = jnp.broadcast_to(a1r, (CHUNKS, states))
    ai = jnp.broadcast_to(a1i, (CHUNKS, states))
    zr = jnp.broadcast_to(rates_ref[2:3, :], (CHUNKS, states))
    zi = jnp.broadcast_to(rates_ref[3:4, :], (CHUNKS, states))
    rowid = lax.broadcasted_iota(jnp.int32, (CHUNKS, states), 0)
    ids = ids_ref[...]
    rate_sums = [jnp.zeros((CHUNKS, states), F32) for _ in range(4)]
    for s in range(seqs):
        cr, ci = carry_in(recvs, ids, s, seqs + s, a1r, a1i, block_len, True)
        sc = [s2_ref[s * CHUNKS : (s + 1) * CHUNKS, v * states : (v + 1) * states] for v in range(4)]
        mr, mi = cmul(sc[0], sc[1], cr, ci)
        yr = jnp.where(rowid == CHUNKS - 1, cr, pltpu.roll(sc[2] + mr, CHUNKS - 1, 0))
        yi = jnp.where(rowid == CHUNKS - 1, ci, pltpu.roll(sc[3] + mi, CHUNKS - 1, 0))

        def step(i, carry):
            yr, yi, gar, gai, gsr, gsi = carry
            j = steps - 1 - i
            at = pl.ds(PAD + s * pitch + j, CHUNKS, stride=steps)
            before = pl.ds(PAD + s * pitch + j - 1, CHUNKS, stride=steps)
            lw = wide(link_ref[at, :], groups)
            nr, ni = cmul(ar, -ai, yr, yi)
            dr, di = nr + take(gs_ref, at, 0, groups), ni + take(gs_ref, at, groups, groups)
            yr, yi = lw * dr, lw * di
            pr, pi = take(proj_ref, at, 0, groups), take(proj_ref, at, groups, groups)
            ur, ui = take(state_ref, before, 0, groups), take(state_ref, before, groups, groups)
            put(gp_scr, at, 0, zr * dr + zi * di)
            put(gp_scr, at, groups, zr * di - zi * dr)
            return (
                yr, yi,
                gar + (ur * yr + ui * yi), gai + (ur * yi - ui * yr),
                gsr + (pr * dr + pi * di), gsi + (pr * di - pi * dr),
            )

        carry = run(steps - PAD, step, (yr, yi, *rate_sums), 8)
        yr, yi = (jnp.where(rowid == 0, 0.0, v) for v in carry[:2])
        carry = run(PAD, lambda i, c: step(i + steps - PAD, c), (yr, yi, *carry[2:]), PAD)
        rate_sums = list(carry[2:])

    skip = vec_ref[2:3, :]
    gain_acc = jnp.zeros((8, width), F32)
    bias_acc = jnp.zeros((8, width), F32)
    for i in range(rows // TILE):
        at = slice(i * TILE, (i + 1) * TILE)
        gpl = take(gp_scr, padded(i, block_len), 0, 2 * groups).astype(BF16)
        gpl_scr[at, :] = gpl
        gn = nt_dot(gpl, w_full[...]) + skip * gssm_ref[at, :]
        gn_ref[at, :] = gn
        n, _ = centre(x_ref[at, :])
        gain_acc = gain_acc + fold_rows(gn * n)
        bias_acc = bias_acc + fold_rows(gn)
    gb_scr[...] = tn_dot(low_ref[...], gpl_scr[...])
    sums4 = [one_row(v) for v in rate_sums]
    rate_grads = []
    for k in range(3):
        rate_grads.append(sum(rates_ref[8 + 3 * c + k : 9 + 3 * c + k, :] * sums4[c] for c in range(4)))
    vec_scr[0:1, :] = one_row(gain_acc)
    vec_scr[1:2, :] = one_row(bias_acc)
    extra = 3 * shard // 2
    half = shard // 2
    for k, dst in enumerate((keep_ref, send_ref, keep_ref, send_ref)):
        slot = (w ^ k) // 2
        q = pl.multiple_of((w ^ k) * shard, shard)
        dst[slot, :shard, :] = gb_scr[pl.ds(q, shard), :width].astype(BF16)
        dst[slot, shard:extra, : width // 2] = gb_scr[pl.ds(q, half), width:].astype(BF16)
        dst[slot, shard:extra, width // 2 :] = gb_scr[pl.ds(q + half, half), width:].astype(BF16)
        line = jnp.concatenate(
            [vec_scr[v : v + 1, pl.ds(q, shard)] for v in range(2)] + [jnp.zeros((1, width - 2 * shard), F32)], axis=1)
        lines = [line] + [jnp.concatenate([g, jnp.zeros((1, width - states), F32)], axis=1) for g in rate_grads]
        dst[slot, extra:, :] = split_rows(lines)


def centre(values):
    x = values.astype(F32)
    c = x - jnp.mean(x, -1, keepdims=True)
    r = lax.rsqrt(jnp.mean(c * c, -1, keepdims=True) + 1e-05)
    return c * r, r


def k4_body(scale_ref, x_ref, gn_ref, gres_ref, vec_ref, out_ref):
    rows = x_ref.shape[0]
    scale = scale_ref[0, 0]
    gain = vec_ref[0:1, :]
    for i in range(rows // TILE):
        at = slice(i * TILE, (i + 1) * TILE)
        n, r = centre(x_ref[at, :])
        q = gn_ref[at, :] * gain
        back = (q - jnp.mean(q, -1, keepdims=True) - n * jnp.mean(q * n, -1, keepdims=True)) * r
        out_ref[at, :] = scale * (gres_ref[at, :] + back)


def pack_body(w_ref, keep_ref, got_ref, mine_ref, send_ref, tail_ref):
    bulk = mine_ref.shape[0]
    y = w_ref[1] // 2

    def both(slot, rows):
        return keep_ref[slot, rows, :].astype(F32) + got_ref[slot, rows, :].astype(F32)

    mine_ref[...] = both(y, slice(0, bulk)).astype(BF16)
    send_ref[...] = both(1 - y, slice(0, bulk)).astype(BF16)
    for slot in range(2):
        v = both(slot, slice(bulk, bulk + 16))
        tail_ref[slot] = v[:4] + v[8:12]


def unpack_body(scale_ref, back_ref, gb_ref, gc_ref, gg_ref, b_scr, c_scr):
    scale = scale_ref[0, 0]
    pieces = back_ref.shape[0]
    b_rows, c_rows = b_scr.shape[0] // pieces, c_scr.shape[0] // pieces
    for s in range(pieces):
        v = back_ref[s].astype(F32) * scale
        b_scr[s * b_rows : (s + 1) * b_rows, :] = v[:b_rows, :]
        c_scr[s * c_rows : (s + 1) * c_rows, :] = v[b_rows:, :]
    shard, cols = gb_ref.shape
    width = b_scr.shape[1]
    half = shard // 2
    gb_ref[:, :width] = b_scr[:shard, :]
    gb_ref[:half, width:] = b_scr[shard:, : cols - width]
    gb_ref[half:, width:] = b_scr[shard:, cols - width :]
    gc_ref[...] = c_scr[: gc_ref.shape[0], :]
    gg_ref[...] = c_scr[gc_ref.shape[0] :, :]


def whole(n, smem=(), far=()):
    return [pl.BlockSpec(memory_space=pltpu.SMEM if i in smem else pltpu.HBM if i in far else pltpu.VMEM) for i in range(n)]


def call(body, outs, scratch, smem, *args, us=1, limit=30, far=(), copies=0):
    return pl.pallas_call(
        body,
        out_shape=[jax.ShapeDtypeStruct(*o) for o in outs],
        in_specs=whole(len(args), smem, far),
        out_specs=whole(len(outs)),
        scratch_shapes=[pltpu.VMEM(*s) for s in scratch] + [pltpu.SemaphoreType.DMA((copies,))] * (copies > 0),
        compiler_params=pltpu.CompilerParams(vmem_limit_bytes=limit * MIB),
        cost_estimate=pl.CostEstimate(flops=us * 1_000_000_000, bytes_accessed=MIB, transcendentals=0),
    )(*args)


def per_device(inputs, teacher, segment_ids, valid_mask, ln_gain, ln_bias, b_weight, c_weight, skip_weight,
               glu_weight, glu_bias, lambda_real, lambda_imag, log_step):
    S = lax.axis_size("seq")
    s_at = lax.axis_index("seq")
    w_at = 2 * lax.axis_index("wy") + lax.axis_index("wc")
    seqs, block_len, width = inputs.shape
    rows = seqs * block_len
    padded_rows = PAD + seqs * (block_len + PAD)
    length = S * block_len
    own = lambda_real.shape[0]
    states = own * S
    doc_most = {4096: 1024, 32768: 8192}.get(length, length)
    hops = min((doc_most - 2) // block_len + 1, S - 1)
    shard, c_shard, g_shard = b_weight.shape[0], c_weight.shape[0], glu_weight.shape[0]

    def swap(v, axis, bit=1, n=2):
        return lax.ppermute(v, axis, [(i, i ^ bit) for i in range(n)])

    def after(v, *others):
        return lax.optimization_barrier((v, *others))[0]

    idx = jnp.stack([s_at, w_at]).astype(jnp.int32)
    b_msg, table = call(
        k0_body,
        [((shard + 16, b_weight.shape[1]), BF16), ((8, states), F32)],
        [(b_weight.shape, BF16), ((4, 1, shard), BF16), ((3, 1, own), F32), ((8, states), F32)],
        (0,),
        idx, b_weight, *(v[None] for v in (ln_gain, ln_bias, skip_weight, glu_bias, lambda_real, lambda_imag, log_step)),
        far=range(1, 9), copies=8, limit=60,
    )
    b_far = swap(b_msg, "wy")
    b_near = swap(b_msg, "wc")
    c_msg, link, valid, ids = call(
        k0b_body,
        [((c_shard + g_shard, width), BF16), ((padded_rows, LANES), F32), ((rows, LANES), F32),
         ((2 * seqs, LANES), F32)],
        [((seqs, block_len), jnp.int32), ((seqs, block_len), jnp.int32), (c_weight.shape, BF16), (glu_weight.shape, BF16)],
        (),
        c_weight, glu_weight, segment_ids, valid_mask, far=range(4), copies=4, us=2, limit=8,
    )
    c_far = swap(c_msg, "wy")
    table, bit = after(table, c_msg), 1
    while bit < S:
        radix = 4 if 4 * bit <= S else 2
        table = sum([swap(table, "seq", k * bit, S) for k in range(1, radix)], table)
        bit *= radix
    bs = (b_msg, b_near, b_far, swap(b_far, "wc"))

    x = inputs.reshape(rows, width)
    teach = teacher.reshape(rows, width)
    R = seqs * CHUNKS
    slab = (2 * states // LANES, padded_rows, LANES)
    msg_shape = ((seqs, 2 * states + LANES), F32)
    low, proj, vec, w_full = call(
        functools.partial(k1a_body, seqs=seqs),
        [((rows, width), BF16), (slab, F32), ((8, width), F32), ((width, 2 * states), BF16)],
        [],
        (0,),
        idx, x, *bs, us=2, limit=8,
    )
    s1, fwd, rates = call(
        functools.partial(k1b_body, seqs=seqs),
        [((R, 4 * states), F32), msg_shape, ((24, states), F32)],
        [],
        (),
        proj, table, link, ids, us=2, limit=8,
    )
    cs = (c_msg, swap(c_msg, "wc"), c_far, swap(c_far, "wc"))
    fwds = [lax.ppermute(fwd, "seq", [(i, i + k) for i in range(S - k)]) for k in range(1, hops + 1)]
    c_bulk = c_shard + g_shard
    out, state, gs, gres, gssm, s2, bwd, send_c, keep_c = call(
        functools.partial(k2_body, seqs=seqs, hops=hops),
        [((rows, width), BF16), (slab, F32), (slab, F32),
         ((rows, width), F32), ((rows, width), F32), ((R, 4 * states), F32), msg_shape,
         ((2, c_bulk + 16, width), BF16), ((2, c_bulk + 16, width), BF16)],
        [((2 * states, width), BF16), ((width, width), BF16), ((rows, width), BF16), ((rows, width), BF16),
         ((rows, width), BF16), ((rows, 2 * states), BF16), ((2 * states, width), F32), ((width, width), F32),
         ((8, width), F32)],
        (0,),
        idx, x, teach, link, valid, ids, low, proj, s1, rates, vec, *cs, *fwds, us=10, limit=18,
    )
    bwds = [lax.ppermute(bwd, "seq", [(i + k, i) for i in range(S - k)]) for k in range(1, hops + 1)]
    got_c = swap(after(send_c, *bwds), "wc")
    mine_c, half_c, tail_c = call(
        pack_body,
        [((c_bulk, width), BF16), ((c_bulk, width), BF16), ((2, 4, width), F32)],
        [],
        (0,),
        idx, keep_c, got_c, limit=4,
    )
    half_c, bwds = lax.optimization_barrier((half_c, bwds))
    far_c = swap(half_c, "wy")
    b_bulk = 3 * shard // 2
    gn, send_b, keep_b = call(
        functools.partial(k3_body, seqs=seqs, hops=hops),
        [((rows, width), F32), ((2, b_bulk + 16, width), BF16), ((2, b_bulk + 16, width), BF16)],
        [(slab, F32), ((rows, 2 * states), BF16), ((width, 2 * states), F32), ((8, width), F32)],
        (0,),
        idx, x, link, ids, low, proj, state, gs, gssm, s2, rates, vec, w_full, *bwds, us=8, limit=14,
    )
    mine_c = (mine_c.astype(F32) + far_c.astype(F32)).astype(BF16).reshape(S, c_bulk // S, width)
    got_b = swap(after(send_b, mine_c), "wc")
    tail_b, part_b = add_tail(keep_b, got_b, b_bulk)
    tails = jnp.concatenate([tail_c, tail_b], 1)
    high, rest = split16(tails)
    tails = jnp.broadcast_to(jnp.concatenate([high, rest], 1)[None], (S, 2, 16, width))
    parts = jnp.concatenate([part_b.reshape(2, S, b_bulk // S, width).transpose(1, 0, 2, 3), tails], 2)
    arrived = lax.all_to_all(parts.reshape(2 * S, -1, width), ("seq", "wy"), 0, 0, tiled=True)

    bit = 1
    while bit < S:
        v = mine_c.reshape(-1, 2, c_bulk // S, width)
        me = (s_at // bit) % 2
        got = swap(pick(v, 1 - me, 1), "seq", bit, S)
        mine_c = (pick(v, me, 1).astype(F32) + got.astype(F32)).astype(BF16)
        bit *= 2
    total_b = jnp.sum(arrived.astype(F32), 0)
    sum_b = total_b[: b_bulk // S].astype(BF16)
    tail = total_b[b_bulk // S :]
    tail = tail[:8] + tail[8:]
    c_line = tail[0].reshape(4, LANES)
    total = c_line[3, 0]
    scale = length * seqs * lax.axis_size(("wy", "wc")) / total
    both = jnp.concatenate([sum_b, mine_c.reshape(-1, width)], 0)
    sent = jnp.broadcast_to(both[None], (S, *both.shape))
    back = lax.all_to_all(sent, "seq", 0, 0, tiled=True)
    (ingrad,) = call(
        k4_body, [((rows, width), F32)], [], (0,), scale.reshape(1, 1), x, gn, gres, vec, us=3, limit=8,
    )
    gb, gc, gg = call(
        unpack_body,
        [((shard, 2 * states), F32), ((c_shard, width), F32), ((g_shard, width), F32)],
        [((b_bulk, width), F32), ((c_bulk, width), F32)],
        (0,),
        scale.reshape(1, 1), back, limit=8,
    )
    tail_b = tail[4:]
    tail_c = c_line
    line = tail_b[0] * scale
    rate_out = lax.dynamic_slice(tail_b[1:4] * scale, (0, s_at * own), (3, own))
    loss = tail_c[2, 0] / (total * width)
    return (
        out.reshape(inputs.shape), loss, ingrad.reshape(inputs.shape), line[:shard], line[shard : 2 * shard], gb,
        gc, tail_c[0] * scale, gg, tail_c[1] * scale,
        rate_out[0], rate_out[1], rate_out[2],
    )


def add_tail(keep, got, bulk):
    v = keep.astype(F32) + got.astype(F32)
    return v[:, bulk : bulk + 4] + v[:, bulk + 8 : bulk + 12], v[:, :bulk].astype(BF16)


def pick(v, at, axis=0):
    return lax.dynamic_index_in_dim(v, at, axis, keepdims=False)


def solution(mesh):
    sizes = mesh.devices.shape
    fine = Mesh(mesh.devices.reshape(sizes[0], 2, sizes[1] // 2), ("seq", "wy", "wc"))
    w = ("wy", "wc")
    tokens = P(w, "seq", None)
    return jax.shard_map(
        per_device,
        mesh=fine,
        in_specs=(
            tokens, tokens, P(w, "seq"), P(w, "seq"), P(w), P(w), P(w, None), P(w, None), P(w), P(w, None), P(w),
            P("seq"), P("seq"), P("seq"),
        ),
        out_specs=(
            tokens, P(), tokens, P(w), P(w), P(w, None), P(w, None), P(w), P(w, None), P(w),
            P("seq"), P("seq"), P("seq"),
        ),
        check_vma=False,
    )
```

time: 176 us -> 115 us (0.65)
  Pallas kernels: 52.9 us -> 26.4 us
  blocking collectives: 23 us -> 0 us
  other arithmetic: 13.2 us -> 3.5 us
  local copies, waits for them, and re-layouts: 14.6 us -> 6.6 us
  starting transfers between devices: 30.9 us -> 36.3 us
  waiting for transfers between devices: 35.4 us -> 37.2 us
    pallas_call x3 -> x9, Pallas kernels: 52.9 us -> 26.4 us  [call(): pl.pallas_call(body, out_shape=[jax.ShapeDtypeStruct(*o) for o in outs],...]
    all_to_all x1 -> x0, blocking collectives: 23 us -> none  [per_device(): arrived = lax.all_to_all(parts, 'seq', 0, 0, tiled=True).astype(F32)]
    all_to_all x1 -> x2, starting transfers between devices: 3.49 us -> 11.2 us  [the longest x1 6.07 us: per_device(): lax.all_to_all(parts.reshape(2 * S, -1, width), ('seq', 'wy'), 0, 0, tile...]
    all_to_all x1 -> x2, waiting for transfers between devices: 11.4 us -> 3.95 us  [the longest x1 3.94 us: per_device(): back = lax.all_to_all(sent, 'seq', 0, 0, tiled=True)]
    ppermute x15 -> x16, waiting for transfers between devices: 19.8 us -> 25.3 us  [swap(): return lax.ppermute(v, axis, [(i, i ^ bit) for i in range(n)])]
    convert_element_type x8 -> x4, other arithmetic: 3.93 us -> 1.13 us  [the longest x1 1.05 us: per_device(): (mine_c.astype(F32) + far_c.astype(F32)).astype(BF16)]
    another operation x5 -> x1, other arithmetic: 3.05 us -> 0.59 us  [per_device(): idx = jnp.stack([s_at, w_at]).astype(jnp.int32)]
    slice x6 -> x5, local copies, waits for them, and re-layouts: 2.97 us -> 0.58 us  [the longest x1 0.52 us: per_device(): total = c_line[3, 0]]
  transfers between devices with their start and end apart: 20 -> 22, of which waited for: 11 -> 14; matrix products, arithmetic and copies ran while one was open for 10% -> 2% of each run, Pallas kernels for 4% -> 10%
where the time goes in v2:
time: 115 us; the launch traced here: 114 us
  waiting for transfers between devices  37.2 us (32%)
  starting transfers between devices  36.3 us (32%)
  Pallas kernels  26.4 us (23%)
  local copies, waits for them, and re-layouts  6.6 us (6%)
  between operations  4.18 us (4%)
  other arithmetic  3.5 us (3%)
    pallas_call x9, Pallas kernels, call(): pl.pallas_call(body, out_shape=[jax.ShapeDtypeStruct(*o) for o in outs],...  26.4 us
    ppermute x16, waiting for transfers between devices, swap(): return lax.ppermute(v, axis, [(i, i ^ bit) for i in range(n)])  25.3 us
    ppermute x16, starting transfers between devices, swap(): return lax.ppermute(v, axis, [(i, i ^ bit) for i in range(n)])  16.4 us
    ppermute x2, waiting for transfers between devices, per_device(): lax.ppermute(bwd, 'seq', [(i + k, i) for i in range(S - k)])  6.59 us
    all_to_all x1, starting transfers between devices, per_device(): lax.all_to_all(parts.reshape(2 * S, -1, width), ('seq', 'wy'), 0, 0, tile...  6.07 us
    ppermute x2, starting transfers between devices, per_device(): lax.ppermute(fwd, 'seq', [(i, i + k) for i in range(S - k)])  5.95 us
    all_to_all x1, starting transfers between devices, per_device(): back = lax.all_to_all(sent, 'seq', 0, 0, tiled=True)  5.17 us
    unnamed x26, local copies, waits for them, and re-layouts  4.55 us
  transfers between devices with their start and end apart: 22, of which 14 were waited for; matrix products, arithmetic and copies ran while one was open for 2% of the time, Pallas kernels for 10%

profile of v2, /device:TPU:0, one launch (start us, length us, event | category | flops | bytes accessed | tf_op | source)
XLA Modules:
  0.0 114.1 jit_solution(8848286863330762811)
XLA Ops:
  0.7 0.6 pad_add_fusion.at_ref.w_ref.refs_0_
  1.3 2.4 %shard_map.238 = (bf16[144,768]{1,0:T(8,128)(2,1)}, f32[8,384]{1,0:T(8,128)}) custom-call(s32[2]{0:T(128)} %pad_add_fusion.at_ref.w_ref.refs_0_, bf16[128,768]{1,0:T(8,128)(2,1)} %b_ref.1, bf16[1,128]{1,0:T(2,128)(2,1)} %bitcast.63, bf16[1,128]{1,0:T(2,128)(2,1)} %bitcast.64, bf16[1,128]{1,0:T(2,128)(2,1)} %bitcast.65, bf16[1,128]{1,0:T(2,128)(2,1)} %bitcast.66, ...), custom_call_target="tpu_custom_call" | custom-call | flops 1000000000 | bytes 1048576 | tf_op jit(solution)/shard_map/pallas_call | solution.py:574
  3.7 3.0 %collective-permute-start.1 = (bf16[144,768]{1,0:T(8,128)(2,1)}, bf16[144,768]{1,0:T(8,128)(2,1)S(1)}, u32[]{:S(2)}, u32[]{:S(2)}) collective-permute-start(bf16[144,768]{1,0:T(8,128)(2,1)} %get-tuple-element.52.b0), channel_id=1, source_target_pairs={{0,2},{2,0},{1,3},{3,1},{4,6},{6,4},{5,7},{7,5},{8,10},{10,8},{9,1... | collective-permute-start | bytes 663560 | tf_op jit(solution)/shard_map/ppermute | solution.py:601
  6.8 0.9 shard_map.237
  7.8 2.0 %collective-permute-start.3 = (f32[8,384]{1,0:T(8,128)S(1)}, f32[8,384]{1,0:T(8,128)S(1)}, u32[]{:S(2)}, u32[]{:S(2)}) collective-permute-start(f32[8,384]{1,0:T(8,128)S(1)} %copy-done.12), channel_id=1, source_target_pairs={{0,4},{4,0},{8,12},{12,8},{16,20},{20,16},{24,28},{28,24},{1,5},{5... | collective-permute-start | bytes 36872 | tf_op jit(solution)/shard_map/ppermute | solution.py:601
  9.7 1.6 %collective-permute-start.4 = (f32[8,384]{1,0:T(8,128)S(1)}, f32[8,384]{1,0:T(8,128)S(1)}, u32[]{:S(2)}, u32[]{:S(2)}) collective-permute-start(f32[8,384]{1,0:T(8,128)S(1)} %copy-done.12), channel_id=1, source_target_pairs={{0,8},{4,12},{8,0},{12,4},{16,24},{20,28},{24,16},{28,20},{1,9},{5... | collective-permute-start | bytes 36872 | tf_op jit(solution)/shard_map/ppermute | solution.py:601
  11.3 0.2 collective-permute-done.3
  11.5 1.7 %collective-permute-done.1.b2 = bf16[144,768]{1,0:T(8,128)(2,1)S(1)} collective-permute-done((bf16[144,768]{1,0:T(8,128)(2,1)}, bf16[144,768]{1,0:T(8,128)(2,1)S(1)}, u32[]{:S(2)}, u32[]{:S(2)}) %collective-permute-start.1) | collective-permute-done | bytes 221216 | tf_op jit(solution)/shard_map/ppermute | solution.py:601
  13.2 0.2 collective-permute-done.4
  13.4 2.5 %collective-permute-done.5 = f32[8,384]{1,0:T(8,128)S(1)} collective-permute-done((f32[8,384]{1,0:T(8,128)S(1)}, f32[8,384]{1,0:T(8,128)S(1)}, u32[]{:S(2)}, u32[]{:S(2)}) %collective-permute-start.5) | collective-permute-done | bytes 12320 | tf_op jit(solution)/shard_map/ppermute | solution.py:601
  15.9 2.6 %collective-permute-start.6 = (f32[8,384]{1,0:T(8,128)S(1)}, f32[8,384]{1,0:T(8,128)S(1)}, u32[]{:S(2)}, u32[]{:S(2)}) collective-permute-start(f32[8,384]{1,0:T(8,128)S(1)} %add_add_fusion), channel_id=1, source_target_pairs={{0,16},{4,20},{8,24},{12,28},{16,0},{20,4},{24,8},{28,12},{1,17},{... | collective-permute-start | bytes 36872 | tf_op jit(solution)/shard_map/ppermute | solution.py:601
  18.5 2.0 %collective-permute-done.6 = f32[8,384]{1,0:T(8,128)S(1)} collective-permute-done((f32[8,384]{1,0:T(8,128)S(1)}, f32[8,384]{1,0:T(8,128)S(1)}, u32[]{:S(2)}, u32[]{:S(2)}) %collective-permute-start.6) | collective-permute-done | bytes 12320 | tf_op jit(solution)/shard_map/ppermute | solution.py:601
  20.6 2.0 %shard_map.239 = (bf16[1024,512]{1,0:T(8,128)(2,1)S(1)}, f32[6,1048,128]{2,1,0:T(8,128)S(1)}, f32[8,512]{1,0:T(8,128)S(1)}, bf16[512,768]{1,0:T(8,128)(2,1)S(1)}) custom-call(s32[2]{0:T(128)S(1)} %copy-done.7, bf16[1024,512]{1,0:T(8,128)(2,1)S(1)} %bitcast.52, bf16[144,768]{1,0:T(8,128)(2,1)S(1)} %copy-done.2, bf16[144,768]{1,0:T(8,128)(2,1)S(1)} %collective-permute-done.b1, ...), custom_call_target="tpu_custom_call" | custom-call | flops 2000000000 | bytes 1048576 | tf_op jit(solution)/shard_map/pallas_call | solution.py:574
  22.6 0.7 shard_map.240
  23.3 2.5 %collective-permute-start.10 = (f32[2,896]{1,0:T(2,128)S(1)}, f32[2,896]{1,0:T(2,128)S(1)}, u32[]{:S(2)}, u32[]{:S(2)}) collective-permute-start(f32[2,896]{1,0:T(2,128)S(1)} %get-tuple-element.61), channel_id=1, source_target_pairs={{0,4},{4,8},{8,12},{12,16},{16,20},{20,24},{24,28},{1,5},{5,9},{9,... | collective-permute-start | bytes 21512 | tf_op jit(solution)/shard_map/ppermute | solution.py:653
  25.8 3.5 %collective-permute-start.11 = (f32[2,896]{1,0:T(2,128)S(1)}, f32[2,896]{1,0:T(2,128)S(1)}, u32[]{:S(2)}, u32[]{:S(2)}) collective-permute-start(f32[2,896]{1,0:T(2,128)S(1)} %get-tuple-element.61), channel_id=1, source_target_pairs={{0,8},{4,12},{8,16},{12,20},{16,24},{20,28},{1,9},{5,13},{9,17},{1... | collective-permute-start | bytes 21512 | tf_op jit(solution)/shard_map/ppermute | solution.py:653
  29.3 1.3 %collective-permute-done.11.refs_16_ = f32[2,896]{1,0:T(2,128)S(1)} collective-permute-done((f32[2,896]{1,0:T(2,128)S(1)}, f32[2,896]{1,0:T(2,128)S(1)}, u32[]{:S(2)}, u32[]{:S(2)}) %collective-permute-start.11) | collective-permute-done | bytes 7200 | tf_op jit(solution)/shard_map/ppermute | solution.py:653
  30.6 10.8 %shard_map.241 = (bf16[1024,512]{1,0:T(8,128)(2,1)}, f32[6,1048,128]{2,1,0:T(8,128)S(1)}, f32[6,1048,128]{2,1,0:T(8,128)S(1)}, f32[1024,512]{1,0:T(8,128)S(1)}, ...) custom-call(s32[2]{0:T(128)S(1)} %copy-done.7, ...), custom_call_target="tpu_custom_call" | custom-call | flops 10000000000 | bytes 1048576 | tf_op jit(solution)/shard_map/pallas_call | solution.py:574
  41.4 1.3 %collective-permute-start.12 = (f32[2,896]{1,0:T(2,128)S(1)}, f32[2,896]{1,0:T(2,128)S(1)}, u32[]{:S(2)}, u32[]{:S(2)}) collective-permute-start(f32[2,896]{1,0:T(2,128)S(1)} %get-tuple-element.70), channel_id=1, source_target_pairs={{4,0},{8,4},{12,8},{16,12},{20,16},{24,20},{28,24},{5,1},{9,5},{13... | collective-permute-start | bytes 21512 | tf_op jit(solution)/shard_map/ppermute | solution.py:666
  42.7 1.5 %collective-permute-start.13 = (f32[2,896]{1,0:T(2,128)S(1)}, f32[2,896]{1,0:T(2,128)S(1)}, u32[]{:S(2)}, u32[]{:S(2)}) collective-permute-start(f32[2,896]{1,0:T(2,128)S(1)} %get-tuple-element.70), channel_id=1, source_target_pairs={{8,0},{12,4},{16,8},{20,12},{24,16},{28,20},{9,1},{13,5},{17,9},{2... | collective-permute-start | bytes 21512 | tf_op jit(solution)/shard_map/ppermute | solution.py:666
  44.2 3.2 %collective-permute-done.12.refs_13_ = f32[2,896]{1,0:T(2,128)S(1)} collective-permute-done((f32[2,896]{1,0:T(2,128)S(1)}, f32[2,896]{1,0:T(2,128)S(1)}, u32[]{:S(2)}, u32[]{:S(2)}) %collective-permute-start.12) | collective-permute-done | bytes 7200 | tf_op jit(solution)/shard_map/ppermute | solution.py:666
  47.4 3.4 %collective-permute-done.13.refs_14_ = f32[2,896]{1,0:T(2,128)S(1)} collective-permute-done((f32[2,896]{1,0:T(2,128)S(1)}, f32[2,896]{1,0:T(2,128)S(1)}, u32[]{:S(2)}, u32[]{:S(2)}) %collective-permute-start.13) | collective-permute-done | bytes 7200 | tf_op jit(solution)/shard_map/ppermute | solution.py:666
  50.8 2.1 %collective-permute-done.14.got_ref = bf16[2,336,512]{2,1,0:T(8,128)(2,1)S(1)} collective-permute-done((bf16[2,336,512]{2,1,0:T(8,128)(2,1)S(1)}, bf16[2,336,512]{2,1,0:T(8,128)(2,1)S(1)}, u32[]{:S(2)}, u32[]{:S(2)}) %collective-permute-start.14) | collective-permute-done | bytes 688160 | tf_op jit(solution)/shard_map/ppermute | solution.py:601
  52.9 0.7 shard_map.242
  53.6 1.6 %collective-permute-start.16 = (bf16[320,512]{1,0:T(8,128)(2,1)S(1)}, bf16[320,512]{1,0:T(8,128)(2,1)}, u32[]{:S(2)}, u32[]{:S(2)}) collective-permute-start(bf16[320,512]{1,0:T(8,128)(2,1)S(1)} %get-tuple-element.81), channel_id=1, source_target_pairs={{0,2},{2,0},{1,3},{3,1},{4,6},{6,4},{5,7},{7,5},{8,10},{10,8},{9,1... | collective-permute-start | bytes 983048 | tf_op jit(solution)/shard_map/ppermute | solution.py:601
  55.2 5.2 %shard_map.243 = (f32[1024,512]{1,0:T(8,128)S(1)}, bf16[2,208,512]{2,1,0:T(8,128)(2,1)S(1)}, bf16[2,208,512]{2,1,0:T(8,128)(2,1)S(1)}) custom-call(s32[2]{0:T(128)S(1)} %copy-done.7, bf16[1024,512]{1,0:T(8,128)(2,1)S(1)} %bitcast.54, f32[1048,128]{1,0:T(8,128)S(1)} %get-tuple-element.49.link_ref.refs_3_.refs_2_, ...), custom_call_target="tpu_custom_call" | custom-call | flops 8000000000 | bytes 1048576 | tf_op jit(solution)/shard_map/pallas_call | solution.py:574
  60.5 1.3 %copy-done.10 = f32[1024,512]{1,0:T(8,128)} copy-done((f32[1024,512]{1,0:T(8,128)}, f32[1024,512]{1,0:T(8,128)S(1)}, u32[]{:S(2)}) %copy-start.10) | copy-done | bytes 2097176
  61.8 1.8 %collective-permute-done.16 = bf16[320,512]{1,0:T(8,128)(2,1)} collective-permute-done((bf16[320,512]{1,0:T(8,128)(2,1)S(1)}, bf16[320,512]{1,0:T(8,128)(2,1)}, u32[]{:S(2)}, u32[]{:S(2)}) %collective-permute-start.16) | collective-permute-done | bytes 327712 | tf_op jit(solution)/shard_map/ppermute | solution.py:601
  63.6 1.1 add_convert_fusion
  64.6 0.1 convert_add_fusion
  65.0 0.9 pad_maximum_fusion
  65.8 6.1 %all-to-all-start = ((bf16[16,40,512]{2,1,0:T(8,128)(2,1)}), bf16[16,40,512]{2,1,0:T(8,128)(2,1)S(1)}, u32[]{:S(2)}, u32[]{:S(2)}) async-start(bf16[16,40,512]{2,1,0:T(8,128)(2,1)} %bitcast.14), calls=%async_computation | async-start | bytes 1310720 | tf_op jit(solution)/shard_map/all_to_all | solution.py:692
  72.0 2.0 %collective-permute-start.17 = (bf16[4,40,512]{2,1,0:T(8,128)(2,1)S(1)}, bf16[4,40,512]{2,1,0:T(8,128)(2,1)S(1)}, u32[]{:S(2)}, u32[]{:S(2)}) collective-permute-start(bf16[4,40,512]{2,1,0:T(8,128)(2,1)S(1)} %dynamic-slice_bitcast_fusion), channel_id=1, source_target_pairs={{0,4},{4,0},{8,12},{12,8},{16,20},{20,16},{24,28},{28,24},{1,5},{5... | collective-permute-start | bytes 491528 | tf_op jit(solution)/shard_map/ppermute | solution.py:601
  73.9 8.1 %collective-permute-done.17 = bf16[4,40,512]{2,1,0:T(8,128)(2,1)S(1)} collective-permute-done((bf16[4,40,512]{2,1,0:T(8,128)(2,1)S(1)}, bf16[4,40,512]{2,1,0:T(8,128)(2,1)S(1)}, u32[]{:S(2)}, u32[]{:S(2)}) %collective-permute-start.17) | collective-permute-done | bytes 163872 | tf_op jit(solution)/shard_map/ppermute | solution.py:601
  82.1 1.3 %collective-permute-start.18 = (bf16[2,40,512]{2,1,0:T(8,128)(2,1)S(1)}, bf16[2,40,512]{2,1,0:T(8,128)(2,1)S(1)}, u32[]{:S(2)}, u32[]{:S(2)}) collective-permute-start(bf16[2,40,512]{2,1,0:T(8,128)(2,1)S(1)} %dynamic-slice_bitcast_fusion.1), channel_id=1, source_target_pairs={{0,8},{4,12},{8,0},{12,4},{16,24},{20,28},{24,16},{28,20},{1,9},{5... | collective-permute-start | bytes 245768 | tf_op jit(solution)/shard_map/ppermute | solution.py:601
  83.3 3.8 %collective-permute-done.18 = bf16[2,40,512]{2,1,0:T(8,128)(2,1)S(1)} collective-permute-done((bf16[2,40,512]{2,1,0:T(8,128)(2,1)S(1)}, bf16[2,40,512]{2,1,0:T(8,128)(2,1)S(1)}, u32[]{:S(2)}, u32[]{:S(2)}) %collective-permute-start.18) | collective-permute-done | bytes 81952 | tf_op jit(solution)/shard_map/ppermute | solution.py:601
  87.1 2.3 %collective-permute-start.19 = (bf16[1,40,512]{2,1,0:T(8,128)(2,1)S(1)}, bf16[1,40,512]{2,1,0:T(8,128)(2,1)S(1)}, u32[]{:S(2)}, u32[]{:S(2)}) collective-permute-start(bf16[1,40,512]{2,1,0:T(8,128)(2,1)S(1)} %constant_dynamic-slice_fusion), channel_id=1, source_target_pairs={{0,16},{4,20},{8,24},{12,28},{16,0},{20,4},{24,8},{28,12},{1,17},{... | collective-permute-start | bytes 122888 | tf_op jit(solution)/shard_map/ppermute | solution.py:601
  89.4 3.0 %collective-permute-done.19 = bf16[1,40,512]{2,1,0:T(8,128)(2,1)S(1)} collective-permute-done((bf16[1,40,512]{2,1,0:T(8,128)(2,1)S(1)}, bf16[1,40,512]{2,1,0:T(8,128)(2,1)S(1)}, u32[]{:S(2)}, u32[]{:S(2)}) %collective-permute-start.19) | collective-permute-done | bytes 40992 | tf_op jit(solution)/shard_map/ppermute | solution.py:601
  92.6 0.5 fusion.6
  93.1 0.8 broadcast_in_dim.41
  93.9 5.2 %all-to-all-start.1 = ((bf16[8,64,512]{2,1,0:T(8,128)(2,1)}), bf16[8,64,512]{2,1,0:T(8,128)(2,1)S(1)}, u32[]{:S(2)}, u32[]{:S(2)}) async-start(bf16[8,64,512]{2,1,0:T(8,128)(2,1)} %broadcast_in_dim.41), calls=%async_computation.1 | async-start | bytes 1048576 | tf_op jit(solution)/shard_map/all_to_all | solution.py:710
  101.2 0.5 slice_bitcast_fusion.2
  101.7 0.5 fusion.4
  102.2 1.6 %copy-done.9 = f32[1024,512]{1,0:T(8,128)S(1)} copy-done((f32[1024,512]{1,0:T(8,128)S(1)}, f32[1024,512]{1,0:T(8,128)}, u32[]{:S(2)}) %copy-start.9) | copy-done | bytes 2097176
  103.8 1.6 %copy-done.11 = f32[1024,512]{1,0:T(8,128)S(1)} copy-done((f32[1024,512]{1,0:T(8,128)S(1)}, f32[1024,512]{1,0:T(8,128)}, u32[]{:S(2)}) %copy-start.11) | copy-done | bytes 2097176
  105.4 2.7 %shard_map.244 = f32[1024,512]{1,0:T(8,128)} custom-call(f32[1,1]{1,0:T(1,128)} %div.30.scale_ref, bf16[1024,512]{1,0:T(8,128)(2,1)S(1)} %bitcast.55, f32[1024,512]{1,0:T(8,128)S(1)} %copy-done.11, f32[1024,512]{1,0:T(8,128)S(1)} %copy-done.9, f32[8,512]{1,0:T(8,128)S(1)} %get-tuple-element.60.refs_10_.refs_11_.vec_ref), custom_call_target="tpu_custom_call" | custom-call | flops 3000000000 | bytes 1048576 | tf_op jit(solution)/shard_map/pallas_call | solution.py:574
  108.1 3.9 %all-to-all-done.1.back_ref = bf16[8,64,512]{2,1,0:T(8,128)(2,1)S(1)} async-done(((bf16[8,64,512]{2,1,0:T(8,128)(2,1)}), bf16[8,64,512]{2,1,0:T(8,128)(2,1)S(1)}, u32[]{:S(2)}, u32[]{:S(2)}) %all-to-all-start.1) | async-done | bytes 524320 | tf_op jit(solution)/shard_map/all_to_all | solution.py:710
  112.0 1.0 shard_map.245
  (62 shorter events, 0.7 us)
Async XLA Ops:
  0.6 6.1 %copy-start.5 = (s32[2,512]{1,0:T(2,128)S(1)}, s32[2,512]{1,0:T(2,128)}, u32[]{:S(2)}) copy-start(s32[2,512]{1,0:T(2,128)} %seg_hbm.1) | copy-start | bytes 12292
  0.7 6.1 %copy-start.6 = (s32[2,512]{1,0:T(2,128)S(1)}, s32[2,512]{1,0:T(2,128)}, u32[]{:S(2)}) copy-start(s32[2,512]{1,0:T(2,128)} %mask_hbm.1) | copy-start | bytes 12292
  0.7 6.1 %copy-start.3 = (bf16[192,512]{1,0:T(8,128)(2,1)S(1)}, bf16[192,512]{1,0:T(8,128)(2,1)}, u32[]{:S(2)}) copy-start(bf16[192,512]{1,0:T(8,128)(2,1)} %c_ref.1) | copy-start | bytes 589828
  0.7 6.1 %copy-start.4 = (bf16[128,512]{1,0:T(8,128)(2,1)S(1)}, bf16[128,512]{1,0:T(8,128)(2,1)}, u32[]{:S(2)}) copy-start(bf16[128,512]{1,0:T(8,128)(2,1)} %g_ref.1) | copy-start | bytes 393220
  3.7 4.1 %copy-start.12 = (f32[8,384]{1,0:T(8,128)S(1)}, f32[8,384]{1,0:T(8,128)}, u32[]{:S(2)}) copy-start(f32[8,384]{1,0:T(8,128)} %get-tuple-element.57) | copy-start | bytes 36868
  3.7 7.9 %copy-start.2 = (bf16[144,768]{1,0:T(8,128)(2,1)S(1)}, bf16[144,768]{1,0:T(8,128)(2,1)}, u32[]{:S(2)}) copy-start(bf16[144,768]{1,0:T(8,128)(2,1)} %get-tuple-element.52.b0) | copy-start | bytes 663556
  3.7 16.9 %copy-start.1 = (bf16[2,512,512]{2,1,0:T(8,128)(2,1)S(1)}, bf16[2,512,512]{2,1,0:T(8,128)(2,1)}, u32[]{:S(2)}) copy-start(bf16[2,512,512]{2,1,0:T(8,128)(2,1)} %param.14) | copy-start | bytes 3145732
  3.7 16.9 %copy-start.7 = (s32[2]{0:T(128)S(1)}, s32[2]{0:T(128)}, u32[]{:S(2)}) copy-start(s32[2]{0:T(128)} %pad_add_fusion.at_ref.w_ref.refs_0_) | copy-start | bytes 28
  3.7 9.5 %collective-permute-start.1 = (bf16[144,768]{1,0:T(8,128)(2,1)}, bf16[144,768]{1,0:T(8,128)(2,1)S(1)}, u32[]{:S(2)}, u32[]{:S(2)}) collective-permute-start(bf16[144,768]{1,0:T(8,128)(2,1)} %get-tuple-element.52.b0), channel_id=1, source_target_pairs={{0,2},{2,0},{1,3},{3,1},{4,6},{6,4},{5,7},{7,5},{8,10},{10,8},{9,1... | collective-permute-start | bytes 663560 | tf_op jit(solution)/shard_map/ppermute | solution.py:601
  7.7 12.9 %collective-permute-start.8 = (bf16[320,512]{1,0:T(8,128)(2,1)S(1)}, bf16[320,512]{1,0:T(8,128)(2,1)S(1)}, u32[]{:S(2)}, u32[]{:S(2)}) collective-permute-start(bf16[320,512]{1,0:T(8,128)(2,1)S(1)} %get-tuple-element.56.refs_11_), channel_id=1, source_target_pairs={{0,2},{2,0},{1,3},{3,1},{4,6},{6,4},{5,7},{7,5},{8,10},{10,8},{9,1... | collective-permute-start | bytes 983048 | tf_op jit(solution)/shard_map/ppermute | solution.py:601
  7.8 3.7 %collective-permute-start.3 = (f32[8,384]{1,0:T(8,128)S(1)}, f32[8,384]{1,0:T(8,128)S(1)}, u32[]{:S(2)}, u32[]{:S(2)}) collective-permute-start(f32[8,384]{1,0:T(8,128)S(1)} %copy-done.12), channel_id=1, source_target_pairs={{0,4},{4,0},{8,12},{12,8},{16,20},{20,16},{24,28},{28,24},{1,5},{5... | collective-permute-start | bytes 36872 | tf_op jit(solution)/shard_map/ppermute | solution.py:601
  9.7 3.7 %collective-permute-start.4 = (f32[8,384]{1,0:T(8,128)S(1)}, f32[8,384]{1,0:T(8,128)S(1)}, u32[]{:S(2)}, u32[]{:S(2)}) collective-permute-start(f32[8,384]{1,0:T(8,128)S(1)} %copy-done.12), channel_id=1, source_target_pairs={{0,8},{4,12},{8,0},{12,4},{16,24},{20,28},{24,16},{28,20},{1,9},{5... | collective-permute-start | bytes 36872 | tf_op jit(solution)/shard_map/ppermute | solution.py:601
  11.3 4.6 %collective-permute-start.5 = (f32[8,384]{1,0:T(8,128)S(1)}, f32[8,384]{1,0:T(8,128)S(1)}, u32[]{:S(2)}, u32[]{:S(2)}) collective-permute-start(f32[8,384]{1,0:T(8,128)S(1)} %copy-done.12), channel_id=1, source_target_pairs={{0,12},{4,8},{8,4},{12,0},{16,28},{20,24},{24,20},{28,16},{1,13},{... | collective-permute-start | bytes 36872 | tf_op jit(solution)/shard_map/ppermute | solution.py:601
  11.5 9.0 %collective-permute-start = (bf16[144,768]{1,0:T(8,128)(2,1)S(1)}, bf16[144,768]{1,0:T(8,128)(2,1)S(1)}, u32[]{:S(2)}, u32[]{:S(2)}) collective-permute-start(bf16[144,768]{1,0:T(8,128)(2,1)S(1)} %copy-done.2), channel_id=1, source_target_pairs={{0,1},{1,0},{2,3},{3,2},{4,5},{5,4},{6,7},{7,6},{8,9},{9,8},{10,11... | collective-permute-start | bytes 663560 | tf_op jit(solution)/shard_map/ppermute | solution.py:601
  13.2 7.4 %collective-permute-start.2 = (bf16[144,768]{1,0:T(8,128)(2,1)S(1)}, bf16[144,768]{1,0:T(8,128)(2,1)S(1)}, u32[]{:S(2)}, u32[]{:S(2)}) collective-permute-start(bf16[144,768]{1,0:T(8,128)(2,1)S(1)} %collective-permute-done.1.b2), channel_id=1, source_target_pairs={{0,1},{1,0},{2,3},{3,2},{4,5},{5,4},{6,7},{7,6},{8,9},{9,8},{10,11... | collective-permute-start | bytes 663560 | tf_op jit(solution)/shard_map/ppermute | solution.py:601
  15.9 4.6 %collective-permute-start.6 = (f32[8,384]{1,0:T(8,128)S(1)}, f32[8,384]{1,0:T(8,128)S(1)}, u32[]{:S(2)}, u32[]{:S(2)}) collective-permute-start(f32[8,384]{1,0:T(8,128)S(1)} %add_add_fusion), channel_id=1, source_target_pairs={{0,16},{4,20},{8,24},{12,28},{16,0},{20,4},{24,8},{28,12},{1,17},{... | collective-permute-start | bytes 36872 | tf_op jit(solution)/shard_map/ppermute | solution.py:601
  18.5 10.8 %collective-permute-start.7 = (bf16[320,512]{1,0:T(8,128)(2,1)S(1)}, bf16[320,512]{1,0:T(8,128)(2,1)S(1)}, u32[]{:S(2)}, u32[]{:S(2)}) collective-permute-start(bf16[320,512]{1,0:T(8,128)(2,1)S(1)} %get-tuple-element.56.refs_11_), channel_id=1, source_target_pairs={{0,1},{1,0},{2,3},{3,2},{4,5},{5,4},{6,7},{7,6},{8,9},{9,8},{10,11... | collective-permute-start | bytes 983048 | tf_op jit(solution)/shard_map/ppermute | solution.py:601
  20.5 10.1 %collective-permute-start.9 = (bf16[320,512]{1,0:T(8,128)(2,1)S(1)}, bf16[320,512]{1,0:T(8,128)(2,1)S(1)}, u32[]{:S(2)}, u32[]{:S(2)}) collective-permute-start(bf16[320,512]{1,0:T(8,128)(2,1)S(1)} %collective-permute-done.8.refs_13_), channel_id=1, source_target_pairs={{0,1},{1,0},{2,3},{3,2},{4,5},{5,4},{6,7},{7,6},{8,9},{9,8},{10,11... | collective-permute-start | bytes 983048 | tf_op jit(solution)/shard_map/ppermute | solution.py:601
  22.6 8.1 %copy-start = (bf16[2,512,512]{2,1,0:T(8,128)(2,1)S(1)}, bf16[2,512,512]{2,1,0:T(8,128)(2,1)}, u32[]{:S(2)}) copy-start(bf16[2,512,512]{2,1,0:T(8,128)(2,1)} %param.15) | copy-start | bytes 3145732
  23.3 6.0 %collective-permute-start.10 = (f32[2,896]{1,0:T(2,128)S(1)}, f32[2,896]{1,0:T(2,128)S(1)}, u32[]{:S(2)}, u32[]{:S(2)}) collective-permute-start(f32[2,896]{1,0:T(2,128)S(1)} %get-tuple-element.61), channel_id=1, source_target_pairs={{0,4},{4,8},{8,12},{12,16},{16,20},{20,24},{24,28},{1,5},{5,9},{9,... | collective-permute-start | bytes 21512 | tf_op jit(solution)/shard_map/ppermute | solution.py:653
  25.8 4.8 %collective-permute-start.11 = (f32[2,896]{1,0:T(2,128)S(1)}, f32[2,896]{1,0:T(2,128)S(1)}, u32[]{:S(2)}, u32[]{:S(2)}) collective-permute-start(f32[2,896]{1,0:T(2,128)S(1)} %get-tuple-element.61), channel_id=1, source_target_pairs={{0,8},{4,12},{8,16},{12,20},{16,24},{20,28},{1,9},{5,13},{9,17},{1... | collective-permute-start | bytes 21512 | tf_op jit(solution)/shard_map/ppermute | solution.py:653
  41.4 19.0 %copy-start.8 = (f32[1024,512]{1,0:T(8,128)}, f32[1024,512]{1,0:T(8,128)S(1)}, u32[]{:S(2)}) copy-start(f32[1024,512]{1,0:T(8,128)S(1)} %get-tuple-element.79.gres_ref) | copy-start | bytes 6291460
  41.4 6.0 %collective-permute-start.12 = (f32[2,896]{1,0:T(2,128)S(1)}, f32[2,896]{1,0:T(2,128)S(1)}, u32[]{:S(2)}, u32[]{:S(2)}) collective-permute-start(f32[2,896]{1,0:T(2,128)S(1)} %get-tuple-element.70), channel_id=1, source_target_pairs={{4,0},{8,4},{12,8},{16,12},{20,16},{24,20},{28,24},{5,1},{9,5},{13... | collective-permute-start | bytes 21512 | tf_op jit(solution)/shard_map/ppermute | solution.py:666
  42.7 8.1 %collective-permute-start.13 = (f32[2,896]{1,0:T(2,128)S(1)}, f32[2,896]{1,0:T(2,128)S(1)}, u32[]{:S(2)}, u32[]{:S(2)}) collective-permute-start(f32[2,896]{1,0:T(2,128)S(1)} %get-tuple-element.70), channel_id=1, source_target_pairs={{8,0},{12,4},{16,8},{20,12},{24,16},{28,20},{9,1},{13,5},{17,9},{2... | collective-permute-start | bytes 21512 | tf_op jit(solution)/shard_map/ppermute | solution.py:666
  50.8 2.1 %collective-permute-start.14 = (bf16[2,336,512]{2,1,0:T(8,128)(2,1)S(1)}, bf16[2,336,512]{2,1,0:T(8,128)(2,1)S(1)}, u32[]{:S(2)}, u32[]{:S(2)}) collective-permute-start(bf16[2,336,512]{2,1,0:T(8,128)(2,1)S(1)} %get-tuple-element.71), channel_id=1, source_target_pairs={{0,1},{1,0},{2,3},{3,2},{4,5},{5,4},{6,7},{7,6},{8,9},{9,8},{10,11... | collective-permute-start | bytes 2064392 | tf_op jit(solution)/shard_map/ppermute | solution.py:601
  53.6 9.9 %collective-permute-start.16 = (bf16[320,512]{1,0:T(8,128)(2,1)S(1)}, bf16[320,512]{1,0:T(8,128)(2,1)}, u32[]{:S(2)}, u32[]{:S(2)}) collective-permute-start(bf16[320,512]{1,0:T(8,128)(2,1)S(1)} %get-tuple-element.81), channel_id=1, source_target_pairs={{0,2},{2,0},{1,3},{3,1},{4,6},{6,4},{5,7},{7,5},{8,10},{10,8},{9,1... | collective-permute-start | bytes 983048 | tf_op jit(solution)/shard_map/ppermute | solution.py:601
  60.5 1.3 %copy-start.10 = (f32[1024,512]{1,0:T(8,128)}, f32[1024,512]{1,0:T(8,128)S(1)}, u32[]{:S(2)}) copy-start(f32[1024,512]{1,0:T(8,128)S(1)} %get-tuple-element.78.gn_ref) | copy-start | bytes 6291460
  61.8 2.8 %collective-permute-start.15 = (bf16[2,208,512]{2,1,0:T(8,128)(2,1)S(1)}, bf16[2,208,512]{2,1,0:T(8,128)(2,1)S(1)}, u32[]{:S(2)}, u32[]{:S(2)}) collective-permute-start(bf16[2,208,512]{2,1,0:T(8,128)(2,1)S(1)} %get-tuple-element.76), channel_id=1, source_target_pairs={{0,1},{1,0},{2,3},{3,2},{4,5},{5,4},{6,7},{7,6},{8,9},{9,8},{10,11... | collective-permute-start | bytes 1277960 | tf_op jit(solution)/shard_map/ppermute | solution.py:601
  65.8 26.6 %all-to-all-start = ((bf16[16,40,512]{2,1,0:T(8,128)(2,1)}), bf16[16,40,512]{2,1,0:T(8,128)(2,1)S(1)}, u32[]{:S(2)}, u32[]{:S(2)}) async-start(bf16[16,40,512]{2,1,0:T(8,128)(2,1)} %bitcast.14), calls=%async_computation | async-start | bytes 1310720 | tf_op jit(solution)/shard_map/all_to_all | solution.py:692
  72.0 10.0 %collective-permute-start.17 = (bf16[4,40,512]{2,1,0:T(8,128)(2,1)S(1)}, bf16[4,40,512]{2,1,0:T(8,128)(2,1)S(1)}, u32[]{:S(2)}, u32[]{:S(2)}) collective-permute-start(bf16[4,40,512]{2,1,0:T(8,128)(2,1)S(1)} %dynamic-slice_bitcast_fusion), channel_id=1, source_target_pairs={{0,4},{4,0},{8,12},{12,8},{16,20},{20,16},{24,28},{28,24},{1,5},{5... | collective-permute-start | bytes 491528 | tf_op jit(solution)/shard_map/ppermute | solution.py:601
  82.1 5.0 %collective-permute-start.18 = (bf16[2,40,512]{2,1,0:T(8,128)(2,1)S(1)}, bf16[2,40,512]{2,1,0:T(8,128)(2,1)S(1)}, u32[]{:S(2)}, u32[]{:S(2)}) collective-permute-start(bf16[2,40,512]{2,1,0:T(8,128)(2,1)S(1)} %dynamic-slice_bitcast_fusion.1), channel_id=1, source_target_pairs={{0,8},{4,12},{8,0},{12,4},{16,24},{20,28},{24,16},{28,20},{1,9},{5... | collective-permute-start | bytes 245768 | tf_op jit(solution)/shard_map/ppermute | solution.py:601
  87.1 5.3 %collective-permute-start.19 = (bf16[1,40,512]{2,1,0:T(8,128)(2,1)S(1)}, bf16[1,40,512]{2,1,0:T(8,128)(2,1)S(1)}, u32[]{:S(2)}, u32[]{:S(2)}) collective-permute-start(bf16[1,40,512]{2,1,0:T(8,128)(2,1)S(1)} %constant_dynamic-slice_fusion), channel_id=1, source_target_pairs={{0,16},{4,20},{8,24},{12,28},{16,0},{20,4},{24,8},{28,12},{1,17},{... | collective-permute-start | bytes 122888 | tf_op jit(solution)/shard_map/ppermute | solution.py:601
  93.9 18.1 %all-to-all-start.1 = ((bf16[8,64,512]{2,1,0:T(8,128)(2,1)}), bf16[8,64,512]{2,1,0:T(8,128)(2,1)S(1)}, u32[]{:S(2)}, u32[]{:S(2)}) async-start(bf16[8,64,512]{2,1,0:T(8,128)(2,1)} %broadcast_in_dim.41), calls=%async_computation.1 | async-start | bytes 1048576 | tf_op jit(solution)/shard_map/all_to_all | solution.py:710
  102.2 1.6 %copy-start.9 = (f32[1024,512]{1,0:T(8,128)S(1)}, f32[1024,512]{1,0:T(8,128)}, u32[]{:S(2)}) copy-start(f32[1024,512]{1,0:T(8,128)} %copy-done.8) | copy-start | bytes 6291460
  103.8 1.6 %copy-start.11 = (f32[1024,512]{1,0:T(8,128)S(1)}, f32[1024,512]{1,0:T(8,128)}, u32[]{:S(2)}) copy-start(f32[1024,512]{1,0:T(8,128)} %copy-done.10) | copy-start | bytes 6291460

commit v3 on v2

--- a/solution.py
+++ b/solution.py
@@ -138,15 +138,15 @@
     return ar, ai, br, bi
 
 
-def carry_in(recvs, ids, s, own_row, ar, ai, block_len, conj):
+def carry_in(recvs, ids, s, own_row, ar, ai, block_len, conj, blocks):
     states = ar.shape[1]
     pr, pi = power2(ar, -ai if conj else ai, log2(block_len))
     cr = jnp.zeros((1, states), F32)
     ci = jnp.zeros((1, states), F32)
     own = wide(ids[own_row : own_row + 1, :], states // LANES)
-    for ref in reversed(recvs):
-        msg = ref[s : s + 1, :]
-        same = wide(msg[:, 2 * states :], states // LANES) == own
+    for k in range(len(recvs), 0, -1):
+        msg = recvs[k - 1][s : s + 1, :]
+        same = (wide(msg[:, 2 * states :], states // LANES) == own) & (blocks >= k)
         cr, ci = cmul(pr, pi, cr, ci)
         cr = cr + jnp.where(same, msg[:, :states], 0.0)
         ci = ci + jnp.where(same, msg[:, states : 2 * states], 0.0)
@@ -180,12 +180,15 @@
     table_ref[...] = pltpu.roll(scr[...], at_ref[0] * own, 1)
 
 
-def k0b_body(c_ref, g_ref, seg_hbm, mask_hbm, msg_ref, link_ref, valid_ref, ids_ref, seg_ref, mask_ref, c_scr, g_scr, sems):
+def k0b_body(c_ref, g_ref, msg_ref, c_scr, g_scr, sems):
     c_shard = c_ref.shape[0]
-    seqs, block_len = seg_ref.shape
-    fetch([(c_ref, c_scr), (g_ref, g_scr), (seg_hbm, seg_ref), (mask_hbm, mask_ref)], sems)
+    fetch([(c_ref, c_scr), (g_ref, g_scr)], sems)
     msg_ref[:c_shard, :] = c_scr[...]
     msg_ref[c_shard:, :] = g_scr[...]
+
+
+def lay_marks(seg_ref, mask_ref, link_ref, valid_ref, ids_ref):
+    seqs, block_len = seg_ref.shape
     seg = seg_ref[...].astype(F32)
     link_ref[:PAD, :] = jnp.ones((PAD, LANES), F32)
     lane = lax.broadcasted_iota(jnp.int32, (1, block_len), 1)
@@ -204,7 +207,8 @@
         ids_ref[seqs + s : seqs + s + 1, :] = jnp.broadcast_to(row[:, block_len - 1 :], (1, LANES))
 
 
-def k1a_body(w_ref, x_ref, b0, b1, b2, b3, low_ref, proj_ref, vec_ref, full_ref, *, seqs):
+def k1_body(w_ref, x_ref, b0, b1, b2, b3, table_ref, seg_ref, mask_ref,
+            low_ref, proj_ref, vec_ref, full_ref, s1_ref, msg_ref, rates_ref, link_ref, valid_ref, ids_ref, *, seqs):
     rows, width = x_ref.shape
     shard = b0.shape[0] - 16
     block_len = rows // seqs
@@ -226,13 +230,9 @@
         p = jnp.dot(low, full_ref[...], preferred_element_type=F32)
         put(proj_ref, padded(i, block_len), 0, p.astype(BF16).astype(F32))
     clear_pads(proj_ref, seqs, pitch)
-
-
-def k1b_body(proj_ref, table_ref, link_ref, ids_ref, s1_ref, msg_ref, rates_ref, *, seqs):
+    lay_marks(seg_ref, mask_ref, link_ref, valid_ref, ids_ref)
     states = table_ref.shape[1]
     groups = states // LANES
-    pitch = (proj_ref.shape[1] - PAD) // seqs
-    block_len = pitch - PAD
     steps = block_len // CHUNKS + 1
     lam = [table_ref[v : v + 1, :] for v in range(3)]
     parts, back = jax.vjp(rates_map, *lam)
@@ -299,7 +299,7 @@
     ids = ids_ref[...]
     init, carries = [], []
     for s in range(seqs):
-        cr, ci = carry_in(recvs, ids, s, s, a1r, a1i, block_len, False)
+        cr, ci = carry_in(recvs, ids, s, s, a1r, a1i, block_len, False, w_ref[0])
         sc = [s1_ref[s * CHUNKS : (s + 1) * CHUNKS, v * states : (v + 1) * states] for v in range(4)]
         mr, mi = cmul(sc[0], sc[1], cr, ci)
         init.append((pltpu.roll(sc[2] + mr, 1, 0), pltpu.roll(sc[3] + mi, 1, 0)))
@@ -360,7 +360,7 @@
         em = err * wide(valid_ref[at, :], width // LANES)
         loss_acc = loss_acc + fold_rows(em * err)
         gr = em
-        gres_ref[at, :] = gr
+        gres_ref[at, :] = gr.astype(BF16)
         gg = gr * act_f * g * (1.0 - g)
         gbias_acc = gbias_acc + fold_rows(gg)
         gl = gg.astype(BF16)
@@ -415,7 +415,7 @@
         line = jnp.concatenate(
             [sum_scr[v : v + 1, pl.ds(lanes, g_shard)] for v in range(2)]
             + [jnp.broadcast_to(loss, (1, LANES)), count], axis=1)
-        dst[slot, c_shard + g_shard :, :] = split_rows([line])
+        dst[slot, c_shard + g_shard :, :] = split_rows([jnp.zeros((3, width), F32), line])
 
 
 def split16(v):
@@ -425,12 +425,13 @@
 
 def split_rows(lines):
     width = lines[0].shape[1]
-    v = jnp.concatenate(lines + [jnp.zeros((8 - len(lines), width), F32)], axis=0)
+    rows = sum(v.shape[0] for v in lines)
+    v = jnp.concatenate(lines + [jnp.zeros((8 - rows, width), F32)] * (rows < 8), axis=0)
     high, rest = split16(v)
     return jnp.concatenate([high.astype(F32), rest.astype(F32)], axis=0).astype(BF16)
 
 
-def k3_body(*refs, seqs, hops):
+def k3_body(*refs, seqs, hops, blocks):
     (w_ref, x_ref, link_ref, ids_ref, low_ref, proj_ref, state_ref, gs_ref, gssm_ref,
      s2_ref, rates_ref, vec_ref, w_full) = refs[:13]
     recvs = refs[13 : 13 + hops]
@@ -452,7 +453,7 @@
     ids = ids_ref[...]
     rate_sums = [jnp.zeros((CHUNKS, states), F32) for _ in range(4)]
     for s in range(seqs):
-        cr, ci = carry_in(recvs, ids, s, seqs + s, a1r, a1i, block_len, True)
+        cr, ci = carry_in(recvs, ids, s, seqs + s, a1r, a1i, block_len, True, blocks - 1 - w_ref[0])
         sc = [s2_ref[s * CHUNKS : (s + 1) * CHUNKS, v * states : (v + 1) * states] for v in range(4)]
         mr, mi = cmul(sc[0], sc[1], cr, ci)
         yr = jnp.where(rowid == CHUNKS - 1, cr, pltpu.roll(sc[2] + mr, CHUNKS - 1, 0))
@@ -490,7 +491,7 @@
         gpl = take(gp_scr, padded(i, block_len), 0, 2 * groups).astype(BF16)
         gpl_scr[at, :] = gpl
         gn = nt_dot(gpl, w_full[...]) + skip * gssm_ref[at, :]
-        gn_ref[at, :] = gn
+        gn_ref[at, :] = gn.astype(BF16)
         n, _ = centre(x_ref[at, :])
         gain_acc = gain_acc + fold_rows(gn * n)
         bias_acc = bias_acc + fold_rows(gn)
@@ -509,10 +510,8 @@
         dst[slot, :shard, :] = gb_scr[pl.ds(q, shard), :width].astype(BF16)
         dst[slot, shard:extra, : width // 2] = gb_scr[pl.ds(q, half), width:].astype(BF16)
         dst[slot, shard:extra, width // 2 :] = gb_scr[pl.ds(q + half, half), width:].astype(BF16)
-        line = jnp.concatenate(
-            [vec_scr[v : v + 1, pl.ds(q, shard)] for v in range(2)] + [jnp.zeros((1, width - 2 * shard), F32)], axis=1)
-        lines = [line] + [jnp.concatenate([g, jnp.zeros((1, width - states), F32)], axis=1) for g in rate_grads]
-        dst[slot, extra:, :] = split_rows(lines)
+        mine = [vec_scr[v : v + 1, pl.ds(q, shard)] for v in range(2)] + [jnp.zeros((1, shard), F32)]
+        dst[slot, extra:, :] = split_rows([jnp.concatenate(p, axis=1) for p in zip(rate_grads, mine)])
 
 
 def centre(values):
@@ -522,40 +521,93 @@
     return c * r, r
 
 
-def k4_body(scale_ref, x_ref, gn_ref, gres_ref, vec_ref, out_ref):
-    rows = x_ref.shape[0]
-    scale = scale_ref[0, 0]
+def sum_body(c0, c1, c2, c3, sum_ref):
+    sum_ref[...] = total((c0, c1, c2, c3), slice(0, sum_ref.shape[0]))
+
+
+def quarter_body(w_ref, keep_ref, got_ref, *outs):
+    half = outs[0].shape[0] - 16
+    x, y = w_ref[0] % 2, w_ref[1] // 2
+    for out, slot, side in zip(outs, (y, 1 - y, y, 1 - y), (x, x, 1 - x, 1 - x)):
+        def both(rows):
+            return keep_ref[slot, rows, :].astype(F32) + got_ref[slot, rows, :].astype(F32)
+
+        out[:half, :] = both(pl.ds(pl.multiple_of(side * half, half), half)).astype(BF16)
+        v = both(slice(2 * half, 2 * half + 16))
+        out[half:, :] = split_rows([v[:8] + v[8:]])
+
+
+def total(refs, rows):
+    return sum([r[rows, :].astype(F32) for r in refs[1:]], refs[0][rows, :].astype(F32))
+
+
+def deal_body(w_ref, *refs):
+    n = len(refs) - 6
+    bs, c_sum, outs, b_scr = refs[:4], refs[4], refs[5 : 5 + n], refs[5 + n]
+    b_half, c_half = b_scr.shape[0], c_sum.shape[0] - 16
+    b_part, c_part = b_half // n, c_half // n
+    b_scr[...] = total(bs, slice(0, b_half))
+    tail = total(bs, slice(b_half, b_half + 16)) + c_sum[c_half:, :]
+    ends = split_rows([tail[:8] + tail[8:]]).astype(F32)
+    for k, out in enumerate(outs):
+        at = (w_ref[0] // 2) ^ k
+        rows = [
+            b_scr[pl.ds(pl.multiple_of(at * b_part, 8), b_part), :],
+            c_sum[pl.ds(pl.multiple_of(at * c_part, 8), c_part), :],
+            ends[:4], ends[8:12],
+        ]
+        out[...] = jnp.concatenate(rows, axis=0).astype(BF16)
+
+
+def close_body(*refs):
+    parts, (piece_ref, tail_ref) = refs[:-2], refs[-2:]
+    bulk = piece_ref.shape[0]
+    v = total(parts, slice(0, bulk + 8))
+    piece_ref[...] = v[:bulk].astype(BF16)
+    tail_ref[...] = jnp.concatenate([v[bulk : bulk + 4] + v[bulk + 4 :], jnp.zeros((4, v.shape[1]), F32)], axis=0)
+
+
+def scale_of(tail, tokens):
+    return tokens / tail[3:4, 3 * LANES : 3 * LANES + 1]
+
+
+def finish_body(w_ref, tail_ref, x_ref, gn_ref, gres_ref, vec_ref,
+                out_ref, loss_ref, gain_ref, bias_ref, skip_ref, gate_ref, real_ref, imag_ref, step_ref, *, tokens):
+    rows, width = x_ref.shape
+    states = width - gain_ref.shape[1]
+    own = real_ref.shape[1]
+    tail = tail_ref[...]
+    scale = scale_of(tail, tokens)
     gain = vec_ref[0:1, :]
     for i in range(rows // TILE):
         at = slice(i * TILE, (i + 1) * TILE)
         n, r = centre(x_ref[at, :])
-        q = gn_ref[at, :] * gain
+        q = gn_ref[at, :].astype(F32) * gain
         back = (q - jnp.mean(q, -1, keepdims=True) - n * jnp.mean(q * n, -1, keepdims=True)) * r
-        out_ref[at, :] = scale * (gres_ref[at, :] + back)
-
-
-def pack_body(w_ref, keep_ref, got_ref, mine_ref, send_ref, tail_ref):
-    bulk = mine_ref.shape[0]
-    y = w_ref[1] // 2
-
-    def both(slot, rows):
-        return keep_ref[slot, rows, :].astype(F32) + got_ref[slot, rows, :].astype(F32)
-
-    mine_ref[...] = both(y, slice(0, bulk)).astype(BF16)
-    send_ref[...] = both(1 - y, slice(0, bulk)).astype(BF16)
-    for slot in range(2):
-        v = both(slot, slice(bulk, bulk + 16))
-        tail_ref[slot] = v[:4] + v[8:12]
-
-
-def unpack_body(scale_ref, back_ref, gb_ref, gc_ref, gg_ref, b_scr, c_scr):
-    scale = scale_ref[0, 0]
-    pieces = back_ref.shape[0]
-    b_rows, c_rows = b_scr.shape[0] // pieces, c_scr.shape[0] // pieces
-    for s in range(pieces):
-        v = back_ref[s].astype(F32) * scale
-        b_scr[s * b_rows : (s + 1) * b_rows, :] = v[:b_rows, :]
-        c_scr[s * c_rows : (s + 1) * c_rows, :] = v[b_rows:, :]
+        out_ref[at, :] = scale * (gres_ref[at, :].astype(F32) + back)
+    scaled = tail * scale
+    gain_ref[...] = scaled[0:1, states:]
+    bias_ref[...] = scaled[1:2, states:]
+    skip_ref[...] = scaled[3:4, :LANES]
+    gate_ref[...] = scaled[3:4, LANES : 2 * LANES]
+    loss_ref[...] = tail[3:4, 2 * LANES : 2 * LANES + 1] * scale * (1.0 / (tokens * width))
+    rates = pltpu.roll(scaled[:, :states], states - w_ref[0] * own, 1)
+    for k, ref in enumerate((real_ref, imag_ref, step_ref)):
+        ref[...] = rates[k : k + 1, :own]
+
+
+def unpack_body(w_ref, tail_ref, *refs, tokens):
+    pieces, (gb_ref, gc_ref, gg_ref, b_scr, c_scr) = refs[:-5], refs[-5:]
+    scale = scale_of(tail_ref[...], tokens)
+    S = len(pieces)
+    b_rows, c_rows = b_scr.shape[0] // S, c_scr.shape[0] // S
+    for k, piece in enumerate(pieces):
+        s = w_ref[0] ^ k
+        v = piece[...].astype(F32) * scale
+        b_at = s % 2 * (b_scr.shape[0] // 2) + s // 2 * b_rows
+        c_at = s % 2 * (c_scr.shape[0] // 2) + s // 2 * c_rows
+        b_scr[pl.ds(pl.multiple_of(b_at, 8), b_rows), :] = v[:b_rows, :]
+        c_scr[pl.ds(pl.multiple_of(c_at, 8), c_rows), :] = v[b_rows:, :]
     shard, cols = gb_ref.shape
     width = b_scr.shape[1]
     half = shard // 2
@@ -614,16 +666,15 @@
     )
     b_far = swap(b_msg, "wy")
     b_near = swap(b_msg, "wc")
-    c_msg, link, valid, ids = call(
+    (c_msg,) = call(
         k0b_body,
-        [((c_shard + g_shard, width), BF16), ((padded_rows, LANES), F32), ((rows, LANES), F32),
-         ((2 * seqs, LANES), F32)],
-        [((seqs, block_len), jnp.int32), ((seqs, block_len), jnp.int32), (c_weight.shape, BF16), (glu_weight.shape, BF16)],
+        [((c_shard + g_shard, width), BF16)],
+        [(c_weight.shape, BF16), (glu_weight.shape, BF16)],
         (),
-        c_weight, glu_weight, segment_ids, valid_mask, far=range(4), copies=4, us=2, limit=8,
+        c_weight, glu_weight, far=range(2), copies=2, limit=4,
     )
     c_far = swap(c_msg, "wy")
-    table, bit = after(table, c_msg), 1
+    bit = 1
     while bit < S:
         radix = 4 if 4 * bit <= S else 2
         table = sum([swap(table, "seq", k * bit, S) for k in range(1, radix)], table)
@@ -635,27 +686,22 @@
     R = seqs * CHUNKS
     slab = (2 * states // LANES, padded_rows, LANES)
     msg_shape = ((seqs, 2 * states + LANES), F32)
-    low, proj, vec, w_full = call(
-        functools.partial(k1a_body, seqs=seqs),
-        [((rows, width), BF16), (slab, F32), ((8, width), F32), ((width, 2 * states), BF16)],
+    low, proj, vec, w_full, s1, fwd, rates, link, valid, ids = call(
+        functools.partial(k1_body, seqs=seqs),
+        [((rows, width), BF16), (slab, F32), ((8, width), F32), ((width, 2 * states), BF16),
+         ((R, 4 * states), F32), msg_shape, ((24, states), F32),
+         ((padded_rows, LANES), F32), ((rows, LANES), F32), ((2 * seqs, LANES), F32)],
         [],
         (0,),
-        idx, x, *bs, us=2, limit=8,
-    )
-    s1, fwd, rates = call(
-        functools.partial(k1b_body, seqs=seqs),
-        [((R, 4 * states), F32), msg_shape, ((24, states), F32)],
-        [],
-        (),
-        proj, table, link, ids, us=2, limit=8,
+        idx, x, *bs, table, segment_ids, valid_mask, us=4, limit=8,
     )
     cs = (c_msg, swap(c_msg, "wc"), c_far, swap(c_far, "wc"))
-    fwds = [lax.ppermute(fwd, "seq", [(i, i + k) for i in range(S - k)]) for k in range(1, hops + 1)]
+    fwds = [lax.ppermute(fwd, "seq", [(i, (i + k) % S) for i in range(S)]) for k in range(1, hops + 1)]
     c_bulk = c_shard + g_shard
     out, state, gs, gres, gssm, s2, bwd, send_c, keep_c = call(
         functools.partial(k2_body, seqs=seqs, hops=hops),
         [((rows, width), BF16), (slab, F32), (slab, F32),
-         ((rows, width), F32), ((rows, width), F32), ((R, 4 * states), F32), msg_shape,
+         ((rows, width), BF16), ((rows, width), F32), ((R, 4 * states), F32), msg_shape,
          ((2, c_bulk + 16, width), BF16), ((2, c_bulk + 16, width), BF16)],
         [((2 * states, width), BF16), ((width, width), BF16), ((rows, width), BF16), ((rows, width), BF16),
          ((rows, width), BF16), ((rows, 2 * states), BF16), ((2 * states, width), F32), ((width, width), F32),
@@ -663,80 +709,88 @@
         (0,),
         idx, x, teach, link, valid, ids, low, proj, s1, rates, vec, *cs, *fwds, us=10, limit=18,
     )
-    bwds = [lax.ppermute(bwd, "seq", [(i + k, i) for i in range(S - k)]) for k in range(1, hops + 1)]
-    got_c = swap(after(send_c, *bwds), "wc")
-    mine_c, half_c, tail_c = call(
-        pack_body,
-        [((c_bulk, width), BF16), ((c_bulk, width), BF16), ((2, 4, width), F32)],
-        [],
-        (0,),
-        idx, keep_c, got_c, limit=4,
-    )
-    half_c, bwds = lax.optimization_barrier((half_c, bwds))
-    far_c = swap(half_c, "wy")
+    bwds = [lax.ppermute(bwd, "seq", [((i + k) % S, i) for i in range(S)]) for k in range(1, hops + 1)]
+    def cross(v, flip_x, flip_y):
+        return lax.ppermute(
+            v, ("seq", "wy"), [(2 * a + b, 2 * (a ^ flip_x) + (b ^ flip_y)) for a in range(S) for b in range(2)])
+
+    def quarters(keep, got):
+        shape = ((keep.shape[1] - 16) // 2 + 16, width)
+        return call(quarter_body, [(shape, BF16)] * 4, [], (0,), idx, keep, got, limit=4)
+
+    def exchange(q):
+        return (q[0], cross(q[1], 0, 1), cross(q[2], 1, 0), cross(q[3], 1, 1))
+
+    q_c = quarters(keep_c, swap(send_c, "wc"))
+    q_c, bwds = lax.optimization_barrier((q_c, bwds))
+    part_c = exchange(q_c)
     b_bulk = 3 * shard // 2
+    b_part, c_part = b_bulk // S, c_bulk // S
     gn, send_b, keep_b = call(
-        functools.partial(k3_body, seqs=seqs, hops=hops),
-        [((rows, width), F32), ((2, b_bulk + 16, width), BF16), ((2, b_bulk + 16, width), BF16)],
+        functools.partial(k3_body, seqs=seqs, hops=hops, blocks=S),
+        [((rows, width), BF16), ((2, b_bulk + 16, width), BF16), ((2, b_bulk + 16, width), BF16)],
         [(slab, F32), ((rows, 2 * states), BF16), ((width, 2 * states), F32), ((8, width), F32)],
         (0,),
         idx, x, link, ids, low, proj, state, gs, gssm, s2, rates, vec, w_full, *bwds, us=8, limit=14,
     )
-    mine_c = (mine_c.astype(F32) + far_c.astype(F32)).astype(BF16).reshape(S, c_bulk // S, width)
-    got_b = swap(after(send_b, mine_c), "wc")
-    tail_b, part_b = add_tail(keep_b, got_b, b_bulk)
-    tails = jnp.concatenate([tail_c, tail_b], 1)
-    high, rest = split16(tails)
-    tails = jnp.broadcast_to(jnp.concatenate([high, rest], 1)[None], (S, 2, 16, width))
-    parts = jnp.concatenate([part_b.reshape(2, S, b_bulk // S, width).transpose(1, 0, 2, 3), tails], 2)
-    arrived = lax.all_to_all(parts.reshape(2 * S, -1, width), ("seq", "wy"), 0, 0, tiled=True)
-
-    bit = 1
-    while bit < S:
-        v = mine_c.reshape(-1, 2, c_bulk // S, width)
-        me = (s_at // bit) % 2
-        got = swap(pick(v, 1 - me, 1), "seq", bit, S)
-        mine_c = (pick(v, me, 1).astype(F32) + got.astype(F32)).astype(BF16)
-        bit *= 2
-    total_b = jnp.sum(arrived.astype(F32), 0)
-    sum_b = total_b[: b_bulk // S].astype(BF16)
-    tail = total_b[b_bulk // S :]
-    tail = tail[:8] + tail[8:]
-    c_line = tail[0].reshape(4, LANES)
-    total = c_line[3, 0]
-    scale = length * seqs * lax.axis_size(("wy", "wc")) / total
-    both = jnp.concatenate([sum_b, mine_c.reshape(-1, width)], 0)
-    sent = jnp.broadcast_to(both[None], (S, *both.shape))
-    back = lax.all_to_all(sent, "seq", 0, 0, tiled=True)
-    (ingrad,) = call(
-        k4_body, [((rows, width), F32)], [], (0,), scale.reshape(1, 1), x, gn, gres, vec, us=3, limit=8,
+    (c_sum,) = call(sum_body, [((c_bulk // 2 + 16, width), F32)], [], (), *part_c, limit=4)
+    send_b, c_sum = lax.optimization_barrier((send_b, c_sum))
+    part_b = exchange(quarters(keep_b, swap(send_b, "wc")))
+    tokens = float(length * seqs * lax.axis_size(("wy", "wc")))
+    deal = S // 2
+    if b_part % 8 == 0 and c_part % 8 == 0:
+        dealt = call(
+            deal_body, [((b_part + c_part + 8, width), BF16)] * deal,
+            [((b_bulk // 2, width), F32)], (0,), idx, *part_b, c_sum, limit=4,
+        )
+        parts = [dealt[0]] + [swap(dealt[k], "seq", 2 * k, S) for k in range(1, deal)]
+        piece, tail = call(
+            close_body, [((b_part + c_part, width), BF16), ((8, width), F32)], [], (), *parts, limit=4,
+        )
+        pieces = {0: piece}
+        for k in range(1, deal):
+            pieces[2 * k] = swap(piece, "seq", 2 * k, S)
+        for k in range(deal):
+            pieces[2 * k + 1] = swap(pieces[2 * k], "seq", 1, S)
+        pieces = [pieces[k] for k in range(S)]
+    else:
+        piece, tail, pieces = sum_by_all_to_all(part_b, c_sum, S, s_at)
+    ingrad, loss, *lines = call(
+        functools.partial(finish_body, tokens=tokens),
+        [((rows, width), F32), ((1, 1), F32)] + [((1, shard), F32)] * 4 + [((1, own), F32)] * 3,
+        [], (0,), idx, tail, x, gn, gres, vec, us=3, limit=8,
     )
     gb, gc, gg = call(
-        unpack_body,
+        functools.partial(unpack_body, tokens=tokens),
         [((shard, 2 * states), F32), ((c_shard, width), F32), ((g_shard, width), F32)],
         [((b_bulk, width), F32), ((c_bulk, width), F32)],
         (0,),
-        scale.reshape(1, 1), back, limit=8,
-    )
-    tail_b = tail[4:]
-    tail_c = c_line
-    line = tail_b[0] * scale
-    rate_out = lax.dynamic_slice(tail_b[1:4] * scale, (0, s_at * own), (3, own))
-    loss = tail_c[2, 0] / (total * width)
+        idx, tail, *pieces, limit=8,
+    )
+    gain, bias, skip, gate, real, imag, step = (v[0] for v in lines)
     return (
-        out.reshape(inputs.shape), loss, ingrad.reshape(inputs.shape), line[:shard], line[shard : 2 * shard], gb,
-        gc, tail_c[0] * scale, gg, tail_c[1] * scale,
-        rate_out[0], rate_out[1], rate_out[2],
-    )
-
-
-def add_tail(keep, got, bulk):
-    v = keep.astype(F32) + got.astype(F32)
-    return v[:, bulk : bulk + 4] + v[:, bulk + 8 : bulk + 12], v[:, :bulk].astype(BF16)
-
-
-def pick(v, at, axis=0):
-    return lax.dynamic_index_in_dim(v, at, axis, keepdims=False)
+        out.reshape(inputs.shape), loss[0, 0], ingrad.reshape(inputs.shape), gain, bias, gb, gc, skip, gg, gate,
+        real, imag, step,
+    )
+
+
+def sum_by_all_to_all(part_b, v_c, S, s_at):
+    v_b = sum([p.astype(F32) for p in part_b[1:]], part_b[0].astype(F32))
+    width = v_b.shape[1]
+    tail = v_b[-16:-8] + v_b[-8:] + v_c[-16:-8] + v_c[-8:]
+    high = lax.reduce_precision(tail, 8, 7)
+    ends = jnp.concatenate([high, tail - high], 0).astype(BF16)
+    both = jnp.concatenate([v[:-16].astype(BF16).reshape(S // 2, -1, width) for v in (v_b, v_c)], 1)
+    bulk = both.shape[1]
+    both = jnp.concatenate([both, jnp.broadcast_to(ends[None], (S // 2, 16, width))], 1)
+    empty = jnp.zeros_like(both)
+    mine = (lax.iota(jnp.int32, S) % 2 == s_at % 2)[:, None, None]
+    sent = jnp.where(mine, jnp.stack([both, both], 1).reshape(S, bulk + 16, width), jnp.stack([empty, empty], 1).reshape(S, bulk + 16, width))
+    v = jnp.sum(lax.all_to_all(sent, "seq", 0, 0, tiled=True).astype(F32), 0)
+    piece, tail = v[:bulk].astype(BF16), v[bulk : bulk + 8] + v[bulk + 8 :]
+    back = lax.all_to_all(jnp.broadcast_to(piece[None], (S, bulk, width)), "seq", 0, 0, tiled=True)
+    order = lax.iota(jnp.int32, S) ^ s_at
+    return piece, tail, [lax.dynamic_index_in_dim(back, order[k], 0, keepdims=False) for k in range(S)]
 
 
 def solution(mesh):

time: 115 us -> 93.7 us (0.81)
  waiting for transfers between devices: 37.2 us -> 27.1 us
  local copies, waits for them, and re-layouts: 6.6 us -> 0.04 us
  between operations: 4.18 us -> 0.85 us
  other arithmetic: 3.5 us -> 0.6 us
  Pallas kernels: 26.4 us -> 28.8 us
    ppermute x16 -> x22, waiting for transfers between devices: 25.3 us -> 13.8 us  [swap(): return lax.ppermute(v, axis, [(i, i ^ bit) for i in range(n)])]
    all_to_all x2 -> x0, starting transfers between devices: 11.2 us -> none  [the longest x1 6.07 us: per_device(): lax.all_to_all(parts.reshape(2 * S, -1, width), ('seq', 'wy'), 0, 0, tile...]
    ppermute x16 -> x22, starting transfers between devices: 16.4 us -> 23.5 us  [swap(): return lax.ppermute(v, axis, [(i, i ^ bit) for i in range(n)])]
    ppermute x4 -> x10, waiting for transfers between devices: 7.91 us -> 13.3 us  [the longest x6 7.49 us: cross(): lax.ppermute(v, ('seq', 'wy'), [(2 * a + b, 2 * (a ^ flip_x) + (b ^ flip_...]
    unnamed x26 -> x18, local copies, waits for them, and re-layouts: 4.55 us -> 0.04 us
    ppermute x4 -> x10, starting transfers between devices: 8.7 us -> 12.7 us  [the longest x6 7.04 us: cross(): lax.ppermute(v, ('seq', 'wy'), [(2 * a + b, 2 * (a ^ flip_x) + (b ^ flip_...]
    all_to_all x2 -> x0, waiting for transfers between devices: 3.95 us -> none  [the longest x1 3.94 us: per_device(): back = lax.all_to_all(sent, 'seq', 0, 0, tiled=True)]
    pallas_call x9 -> x12, Pallas kernels: 26.4 us -> 28.8 us  [call(): pl.pallas_call(body, out_shape=[jax.ShapeDtypeStruct(*o) for o in outs],...]
  transfers between devices with their start and end apart: 22 -> 32, of which waited for: 14 -> 21; matrix products, arithmetic and copies ran while one was open for 2% -> 0% of each run, Pallas kernels for 10% -> 13%
where the time goes in v3:
time: 93.7 us; the launch traced here: 93.5 us
  starting transfers between devices  36.1 us (39%)
  Pallas kernels  28.8 us (31%)
  waiting for transfers between devices  27.1 us (29%)
    pallas_call x12, Pallas kernels, call(): pl.pallas_call(body, out_shape=[jax.ShapeDtypeStruct(*o) for o in outs],...  28.8 us
    ppermute x22, starting transfers between devices, swap(): return lax.ppermute(v, axis, [(i, i ^ bit) for i in range(n)])  23.5 us
    ppermute x22, waiting for transfers between devices, swap(): return lax.ppermute(v, axis, [(i, i ^ bit) for i in range(n)])  13.8 us
    ppermute x6, waiting for transfers between devices, cross(): lax.ppermute(v, ('seq', 'wy'), [(2 * a + b, 2 * (a ^ flip_x) + (b ^ flip_...  7.49 us
    ppermute x6, starting transfers between devices, cross(): lax.ppermute(v, ('seq', 'wy'), [(2 * a + b, 2 * (a ^ flip_x) + (b ^ flip_...  7.04 us
    ppermute x2, waiting for transfers between devices, per_device(): lax.ppermute(fwd, 'seq', [(i, (i + k) % S) for i in range(S)])  4.84 us
    ppermute x2, starting transfers between devices, per_device(): lax.ppermute(fwd, 'seq', [(i, (i + k) % S) for i in range(S)])  3.34 us
    ppermute x2, starting transfers between devices, per_device(): lax.ppermute(bwd, 'seq', [((i + k) % S, i) for i in range(S)])  2.28 us
  transfers between devices with their start and end apart: 32, of which 21 were waited for; matrix products, arithmetic and copies ran while one was open for 0% of the time, Pallas kernels for 13%

profile of v3, /device:TPU:0, one launch (start us, length us, event | category | flops | bytes accessed | tf_op | source)
XLA Modules:
  0.0 93.5 jit_solution(9347277567533183422)
XLA Ops:
  0.7 0.6 pad_add_fusion.at_ref.w_ref.refs_0_
  1.3 2.5 %shard_map.237 = (bf16[144,768]{1,0:T(8,128)(2,1)}, f32[8,384]{1,0:T(8,128)}) custom-call(s32[2]{0:T(128)} %pad_add_fusion.at_ref.w_ref.refs_0_, bf16[128,768]{1,0:T(8,128)(2,1)} %b_ref.1, bf16[1,128]{1,0:T(2,128)(2,1)} %bitcast.26, bf16[1,128]{1,0:T(2,128)(2,1)} %bitcast.27, bf16[1,128]{1,0:T(2,128)(2,1)} %bitcast.28, bf16[1,128]{1,0:T(2,128)(2,1)} %bitcast.29, ...), custom_call_target="tpu_custom_call" | custom-call | flops 1000000000 | bytes 1048576 | tf_op jit(solution)/shard_map/pallas_call | solution.py:626
  3.8 3.0 %collective-permute-start.1 = (bf16[144,768]{1,0:T(8,128)(2,1)}, bf16[144,768]{1,0:T(8,128)(2,1)S(1)}, u32[]{:S(2)}, u32[]{:S(2)}) collective-permute-start(bf16[144,768]{1,0:T(8,128)(2,1)} %get-tuple-element.71.b0), channel_id=1, source_target_pairs={{0,2},{2,0},{1,3},{3,1},{4,6},{6,4},{5,7},{7,5},{8,10},{10,8},{9,1... | collective-permute-start | bytes 663560 | tf_op jit(solution)/shard_map/ppermute | solution.py:653
  6.9 0.4 shard_map.239.refs_11_
  7.4 3.0 %collective-permute-start.5 = (f32[8,384]{1,0:T(8,128)S(1)}, f32[8,384]{1,0:T(8,128)S(1)}, u32[]{:S(2)}, u32[]{:S(2)}) collective-permute-start(f32[8,384]{1,0:T(8,128)S(1)} %copy-done.8), channel_id=1, source_target_pairs={{0,12},{4,8},{8,4},{12,0},{16,28},{20,24},{24,20},{28,16},{1,13},{... | collective-permute-start | bytes 36872 | tf_op jit(solution)/shard_map/ppermute | solution.py:653
  10.4 0.4 collective-permute-start.4
  11.0 1.2 %collective-permute-done.5 = f32[8,384]{1,0:T(8,128)S(1)} collective-permute-done((f32[8,384]{1,0:T(8,128)S(1)}, f32[8,384]{1,0:T(8,128)S(1)}, u32[]{:S(2)}, u32[]{:S(2)}) %collective-permute-start.5) | collective-permute-done | bytes 12320 | tf_op jit(solution)/shard_map/ppermute | solution.py:653
  12.2 1.1 %collective-permute-done.1.b2 = bf16[144,768]{1,0:T(8,128)(2,1)S(1)} collective-permute-done((bf16[144,768]{1,0:T(8,128)(2,1)}, bf16[144,768]{1,0:T(8,128)(2,1)S(1)}, u32[]{:S(2)}, u32[]{:S(2)}) %collective-permute-start.1) | collective-permute-done | bytes 221216 | tf_op jit(solution)/shard_map/ppermute | solution.py:653
  13.3 0.8 collective-permute-done.4
  14.1 0.4 collective-permute-done.3
  14.5 2.6 %collective-permute-start.6 = (f32[8,384]{1,0:T(8,128)S(1)}, f32[8,384]{1,0:T(8,128)S(1)}, u32[]{:S(2)}, u32[]{:S(2)}) collective-permute-start(f32[8,384]{1,0:T(8,128)S(1)} %add_add_fusion), channel_id=1, source_target_pairs={{0,16},{4,20},{8,24},{12,28},{16,0},{20,4},{24,8},{28,12},{1,17},{... | collective-permute-start | bytes 36872 | tf_op jit(solution)/shard_map/ppermute | solution.py:653
  17.1 2.1 %collective-permute-done.6 = f32[8,384]{1,0:T(8,128)S(1)} collective-permute-done((f32[8,384]{1,0:T(8,128)S(1)}, f32[8,384]{1,0:T(8,128)S(1)}, u32[]{:S(2)}, u32[]{:S(2)}) %collective-permute-start.6) | collective-permute-done | bytes 12320 | tf_op jit(solution)/shard_map/ppermute | solution.py:653
  19.6 2.7 %shard_map.238 = (bf16[1024,512]{1,0:T(8,128)(2,1)S(1)}, f32[6,1048,128]{2,1,0:T(8,128)S(1)}, f32[8,512]{1,0:T(8,128)S(1)}, bf16[512,768]{1,0:T(8,128)(2,1)S(1)}...) custom-call(s32[2]{0:T(128)S(1)} %copy-done.7, ...), custom_call_target="tpu_custom_call" | custom-call | flops 4000000000 | bytes 1048576 | tf_op jit(solution)/shard_map/pallas_call | solution.py:626
  22.3 1.8 %collective-permute-start.11 = (f32[2,896]{1,0:T(2,128)S(1)}, f32[2,896]{1,0:T(2,128)S(1)}, u32[]{:S(2)}, u32[]{:S(2)}) collective-permute-start(f32[2,896]{1,0:T(2,128)S(1)} %get-tuple-element.81), channel_id=1, source_target_pairs={{0,8},{4,12},{8,16},{12,20},{16,24},{20,28},{24,0},{28,4},{1,9},{5... | collective-permute-start | bytes 21512 | tf_op jit(solution)/shard_map/ppermute | solution.py:699
  24.1 1.5 %collective-permute-start.10 = (f32[2,896]{1,0:T(2,128)S(1)}, f32[2,896]{1,0:T(2,128)S(1)}, u32[]{:S(2)}, u32[]{:S(2)}) collective-permute-start(f32[2,896]{1,0:T(2,128)S(1)} %get-tuple-element.81), channel_id=1, source_target_pairs={{0,4},{4,8},{8,12},{12,16},{16,20},{20,24},{24,28},{28,0},{1,5},{5... | collective-permute-start | bytes 21512 | tf_op jit(solution)/shard_map/ppermute | solution.py:699
  25.6 2.2 %collective-permute-done.11.refs_16_ = f32[2,896]{1,0:T(2,128)S(1)} collective-permute-done((f32[2,896]{1,0:T(2,128)S(1)}, f32[2,896]{1,0:T(2,128)S(1)}, u32[]{:S(2)}, u32[]{:S(2)}) %collective-permute-start.11) | collective-permute-done | bytes 7200 | tf_op jit(solution)/shard_map/ppermute | solution.py:699
  27.8 2.7 %collective-permute-done.10.refs_15_ = f32[2,896]{1,0:T(2,128)S(1)} collective-permute-done((f32[2,896]{1,0:T(2,128)S(1)}, f32[2,896]{1,0:T(2,128)S(1)}, u32[]{:S(2)}, u32[]{:S(2)}) %collective-permute-start.10) | collective-permute-done | bytes 7200 | tf_op jit(solution)/shard_map/ppermute | solution.py:699
  30.5 10.8 %shard_map.240 = (bf16[1024,512]{1,0:T(8,128)(2,1)}, f32[6,1048,128]{2,1,0:T(8,128)S(1)}, f32[6,1048,128]{2,1,0:T(8,128)S(1)}, bf16[1024,512]{1,0:T(8,128)(2,1)S...) custom-call(s32[2]{0:T(128)S(1)} %copy-done.7, ...), custom_call_target="tpu_custom_call" | custom-call | flops 10000000000 | bytes 1048576 | tf_op jit(solution)/shard_map/pallas_call | solution.py:626
  41.7 1.9 %collective-permute-start.13 = (f32[2,896]{1,0:T(2,128)S(1)}, f32[2,896]{1,0:T(2,128)S(1)}, u32[]{:S(2)}, u32[]{:S(2)}) collective-permute-start(f32[2,896]{1,0:T(2,128)S(1)} %get-tuple-element.94), channel_id=1, source_target_pairs={{4,0},{8,4},{12,8},{16,12},{20,16},{24,20},{28,24},{0,28},{5,1},{9... | collective-permute-start | bytes 21512 | tf_op jit(solution)/shard_map/ppermute | solution.py:712
  43.6 0.7 shard_map.241
  44.3 0.6 collective-permute-done.14.refs_14_
  45.3 1.7 %collective-permute-start.15 = (bf16[176,512]{1,0:T(8,128)(2,1)S(1)}, bf16[176,512]{1,0:T(8,128)(2,1)S(1)}, u32[]{:S(2)}, u32[]{:S(2)}) collective-permute-start(bf16[176,512]{1,0:T(8,128)(2,1)S(1)} %get-tuple-element.100), channel_id=1, source_target_pairs={{0,2},{2,0},{4,6},{6,4},{8,10},{10,8},{12,14},{14,12},{16,18},{18,... | collective-permute-start | bytes 540680 | tf_op jit(solution)/shard_map/ppermute | solution.py:714
  46.9 1.5 %collective-permute-start.16 = (bf16[176,512]{1,0:T(8,128)(2,1)S(1)}, bf16[176,512]{1,0:T(8,128)(2,1)S(1)}, u32[]{:S(2)}, u32[]{:S(2)}) collective-permute-start(bf16[176,512]{1,0:T(8,128)(2,1)S(1)} %get-tuple-element.101), channel_id=1, source_target_pairs={{0,4},{2,6},{4,0},{6,2},{8,12},{10,14},{12,8},{14,10},{16,20},{18,... | collective-permute-start | bytes 540680 | tf_op jit(solution)/shard_map/ppermute | solution.py:714
  48.8 5.2 %shard_map.242 = (bf16[1024,512]{1,0:T(8,128)(2,1)S(1)}, bf16[2,208,512]{2,1,0:T(8,128)(2,1)S(1)}, bf16[2,208,512]{2,1,0:T(8,128)(2,1)S(1)}) custom-call(s32[2]{0:T(128)S(1)} %copy-done.7, bf16[1024,512]{1,0:T(8,128)(2,1)S(1)} %bitcast.24, f32[1048,128]{1,0:T(8,128)S(1)} %get-tuple-element.73.refs_3_.refs_2_, ...), custom_call_target="tpu_custom_call" | custom-call | flops 8000000000 | bytes 1048576 | tf_op jit(solution)/shard_map/pallas_call | solution.py:626
  54.1 2.0 %collective-permute-done.17.c3 = bf16[176,512]{1,0:T(8,128)(2,1)S(1)} collective-permute-done((bf16[176,512]{1,0:T(8,128)(2,1)S(1)}, bf16[176,512]{1,0:T(8,128)(2,1)S(1)}, u32[]{:S(2)}, u32[]{:S(2)}) %collective-permute-start.17) | collective-permute-done | bytes 180256 | tf_op jit(solution)/shard_map/ppermute | solution.py:714
  56.3 1.8 %collective-permute-done.18.got_ref = bf16[2,208,512]{2,1,0:T(8,128)(2,1)S(1)} collective-permute-done((bf16[2,208,512]{2,1,0:T(8,128)(2,1)S(1)}, bf16[2,208,512]{2,1,0:T(8,128)(2,1)S(1)}, u32[]{:S(2)}, u32[]{:S(2)}) %collective-permute-start.18) | collective-permute-done | bytes 426016 | tf_op jit(solution)/shard_map/ppermute | solution.py:653
  58.0 0.7 shard_map.244
  58.7 1.5 %collective-permute-start.19 = (bf16[112,512]{1,0:T(8,128)(2,1)S(1)}, bf16[112,512]{1,0:T(8,128)(2,1)S(1)}, u32[]{:S(2)}, u32[]{:S(2)}) collective-permute-start(bf16[112,512]{1,0:T(8,128)(2,1)S(1)} %get-tuple-element.105), channel_id=1, source_target_pairs={{0,2},{2,0},{4,6},{6,4},{8,10},{10,8},{12,14},{14,12},{16,18},{18,... | collective-permute-start | bytes 344072 | tf_op jit(solution)/shard_map/ppermute | solution.py:714
  60.2 1.5 %collective-permute-start.20 = (bf16[112,512]{1,0:T(8,128)(2,1)S(1)}, bf16[112,512]{1,0:T(8,128)(2,1)S(1)}, u32[]{:S(2)}, u32[]{:S(2)}) collective-permute-start(bf16[112,512]{1,0:T(8,128)(2,1)S(1)} %get-tuple-element.106), channel_id=1, source_target_pairs={{0,4},{2,6},{4,0},{6,2},{8,12},{10,14},{12,8},{14,10},{16,20},{18,... | collective-permute-start | bytes 344072 | tf_op jit(solution)/shard_map/ppermute | solution.py:714
  61.7 0.6 collective-permute-start.21
  62.3 1.7 %collective-permute-done.19.refs_1_ = bf16[112,512]{1,0:T(8,128)(2,1)S(1)} collective-permute-done((bf16[112,512]{1,0:T(8,128)(2,1)S(1)}, bf16[112,512]{1,0:T(8,128)(2,1)S(1)}, u32[]{:S(2)}, u32[]{:S(2)}) %collective-permute-start.19) | collective-permute-done | bytes 114720 | tf_op jit(solution)/shard_map/ppermute | solution.py:714
  64.0 2.3 %collective-permute-done.20.refs_2_ = bf16[112,512]{1,0:T(8,128)(2,1)S(1)} collective-permute-done((bf16[112,512]{1,0:T(8,128)(2,1)S(1)}, bf16[112,512]{1,0:T(8,128)(2,1)S(1)}, u32[]{:S(2)}, u32[]{:S(2)}) %collective-permute-start.20) | collective-permute-done | bytes 114720 | tf_op jit(solution)/shard_map/ppermute | solution.py:714
  66.2 1.4 %collective-permute-done.21.refs_3_ = bf16[112,512]{1,0:T(8,128)(2,1)S(1)} collective-permute-done((bf16[112,512]{1,0:T(8,128)(2,1)S(1)}, bf16[112,512]{1,0:T(8,128)(2,1)S(1)}, u32[]{:S(2)}, u32[]{:S(2)}) %collective-permute-start.21) | collective-permute-done | bytes 114720 | tf_op jit(solution)/shard_map/ppermute | solution.py:714
  67.6 0.6 shard_map.245
  68.3 1.5 %collective-permute-start.22 = (bf16[72,512]{1,0:T(8,128)(2,1)S(1)}, bf16[72,512]{1,0:T(8,128)(2,1)S(1)}, u32[]{:S(2)}, u32[]{:S(2)}) collective-permute-start(bf16[72,512]{1,0:T(8,128)(2,1)S(1)} %get-tuple-element.110), channel_id=1, source_target_pairs={{0,8},{4,12},{8,0},{12,4},{16,24},{20,28},{24,16},{28,20},{1,9},{5... | collective-permute-start | bytes 221192 | tf_op jit(solution)/shard_map/ppermute | solution.py:653
  69.8 2.5 %collective-permute-start.23 = (bf16[72,512]{1,0:T(8,128)(2,1)S(1)}, bf16[72,512]{1,0:T(8,128)(2,1)S(1)}, u32[]{:S(2)}, u32[]{:S(2)}) collective-permute-start(bf16[72,512]{1,0:T(8,128)(2,1)S(1)} %get-tuple-element.111), channel_id=1, source_target_pairs={{0,16},{4,20},{8,24},{12,28},{16,0},{20,4},{24,8},{28,12},{1,17},{... | collective-permute-start | bytes 221192 | tf_op jit(solution)/shard_map/ppermute | solution.py:653
  72.2 0.5 collective-permute-start.24
  72.9 3.8 %collective-permute-done.23.refs_2_ = bf16[72,512]{1,0:T(8,128)(2,1)S(1)} collective-permute-done((bf16[72,512]{1,0:T(8,128)(2,1)S(1)}, bf16[72,512]{1,0:T(8,128)(2,1)S(1)}, u32[]{:S(2)}, u32[]{:S(2)}) %collective-permute-start.23) | collective-permute-done | bytes 73760 | tf_op jit(solution)/shard_map/ppermute | solution.py:653
  76.7 1.7 %collective-permute-done.24.refs_3_ = bf16[72,512]{1,0:T(8,128)(2,1)S(1)} collective-permute-done((bf16[72,512]{1,0:T(8,128)(2,1)S(1)}, bf16[72,512]{1,0:T(8,128)(2,1)S(1)}, u32[]{:S(2)}, u32[]{:S(2)}) %collective-permute-start.24) | collective-permute-done | bytes 73760 | tf_op jit(solution)/shard_map/ppermute | solution.py:653
  78.4 1.0 %collective-permute-start.30 = (bf16[64,512]{1,0:T(8,128)(2,1)S(1)}, bf16[64,512]{1,0:T(8,128)(2,1)S(1)}, u32[]{:S(2)}, u32[]{:S(2)}) collective-permute-start(bf16[64,512]{1,0:T(8,128)(2,1)S(1)} %get-tuple-element.120.refs_0_), channel_id=1, source_target_pairs={{0,24},{4,28},{8,16},{12,20},{16,8},{20,12},{24,0},{28,4},{1,25},{... | collective-permute-start | bytes 196616 | tf_op jit(solution)/shard_map/ppermute | solution.py:653
  79.5 0.4 collective-permute-start.28
  79.8 3.0 %collective-permute-start.26 = (bf16[64,512]{1,0:T(8,128)(2,1)S(1)}, bf16[64,512]{1,0:T(8,128)(2,1)S(1)}, u32[]{:S(2)}, u32[]{:S(2)}) collective-permute-start(bf16[64,512]{1,0:T(8,128)(2,1)S(1)} %get-tuple-element.120.refs_0_), channel_id=1, source_target_pairs={{0,8},{4,12},{8,0},{12,4},{16,24},{20,28},{24,16},{28,20},{1,9},{5... | collective-permute-start | bytes 196616 | tf_op jit(solution)/shard_map/ppermute | solution.py:653
  82.9 1.6 %collective-permute-start.25 = (bf16[64,512]{1,0:T(8,128)(2,1)S(1)}, bf16[64,512]{1,0:T(8,128)(2,1)S(1)}, u32[]{:S(2)}, u32[]{:S(2)}) collective-permute-start(bf16[64,512]{1,0:T(8,128)(2,1)S(1)} %get-tuple-element.120.refs_0_), channel_id=1, source_target_pairs={{0,4},{4,0},{8,12},{12,8},{16,20},{20,16},{24,28},{28,24},{1,5},{5... | collective-permute-start | bytes 196616 | tf_op jit(solution)/shard_map/ppermute | solution.py:653
  84.6 1.6 %collective-permute-start.31 = (bf16[64,512]{1,0:T(8,128)(2,1)S(1)}, bf16[64,512]{1,0:T(8,128)(2,1)S(1)}, u32[]{:S(2)}, u32[]{:S(2)}) collective-permute-start(bf16[64,512]{1,0:T(8,128)(2,1)S(1)} %collective-permute-done.30.refs_6_), channel_id=1, source_target_pairs={{0,4},{4,0},{8,12},{12,8},{16,20},{20,16},{24,28},{28,24},{1,5},{5... | collective-permute-start | bytes 196616 | tf_op jit(solution)/shard_map/ppermute | solution.py:653
  86.2 1.4 %collective-permute-start.29 = (bf16[64,512]{1,0:T(8,128)(2,1)S(1)}, bf16[64,512]{1,0:T(8,128)(2,1)S(1)}, u32[]{:S(2)}, u32[]{:S(2)}) collective-permute-start(bf16[64,512]{1,0:T(8,128)(2,1)S(1)} %collective-permute-done.28.refs_4_), channel_id=1, source_target_pairs={{0,4},{4,0},{8,12},{12,8},{16,20},{20,16},{24,28},{28,24},{1,5},{5... | collective-permute-start | bytes 196616 | tf_op jit(solution)/shard_map/ppermute | solution.py:653
  87.6 0.7 collective-permute-start.27
  88.2 3.3 %shard_map.247 = (f32[1024,512]{1,0:T(8,128)}, f32[1,1]{1,0:T(1,128)}, f32[1,128]{1,0:T(1,128)}, f32[1,128]{1,0:T(1,128)}, f32[1,128]{1,0:T(1,128)}, /*index=5*/...) custom-call(s32[2]{0:T(128)S(1)} %copy-done.7, f32[8,512]{1,0:T(8,128)S(1)} %get-tuple-element.113.tail_ref, ...), custom_call_target="tpu_custom_call" | custom-call | flops 3000000000 | bytes 1048576 | tf_op jit(solution)/shard_map/pallas_call | solution.py:626
  91.8 1.6 %shard_map.248 = (f32[128,768]{1,0:T(8,128)}, f32[192,512]{1,0:T(8,128)}, f32[128,512]{1,0:T(8,128)}) custom-call(s32[2]{0:T(128)S(1)} %copy-done.7, f32[8,512]{1,0:T(8,128)S(1)} %get-tuple-element.113.tail_ref, bf16[64,512]{1,0:T(8,128)(2,1)S(1)} %get-tuple-element.120.refs_0_, bf16[64,512]{1,0:T(8,128)(2,1)S(1)} %collective-permute-done.25.refs_1_, ...), custom_call_target="tpu_custom_call" | custom-call | flops 1000000000 | bytes 1048576 | tf_op jit(solution)/shard_map/pallas_call | solution.py:626
  (49 shorter events, 2.6 us)
Async XLA Ops:
  0.6 6.2 %copy-start.4 = (bf16[128,512]{1,0:T(8,128)(2,1)S(1)}, bf16[128,512]{1,0:T(8,128)(2,1)}, u32[]{:S(2)}) copy-start(bf16[128,512]{1,0:T(8,128)(2,1)} %g_ref.1) | copy-start | bytes 393220
  0.7 6.2 %copy-start.3 = (bf16[192,512]{1,0:T(8,128)(2,1)S(1)}, bf16[192,512]{1,0:T(8,128)(2,1)}, u32[]{:S(2)}) copy-start(bf16[192,512]{1,0:T(8,128)(2,1)} %c_ref.1) | copy-start | bytes 589828
  1.3 18.3 %copy-start.1 = (bf16[2,512,512]{2,1,0:T(8,128)(2,1)S(1)}, bf16[2,512,512]{2,1,0:T(8,128)(2,1)}, u32[]{:S(2)}) copy-start(bf16[2,512,512]{2,1,0:T(8,128)(2,1)} %param.14) | copy-start | bytes 3145732
  1.3 18.3 %copy-start.5 = (s32[2,512]{1,0:T(2,128)S(1)}, s32[2,512]{1,0:T(2,128)}, u32[]{:S(2)}) copy-start(s32[2,512]{1,0:T(2,128)} %seg_ref.1) | copy-start | bytes 12292
  1.3 18.3 %copy-start.6 = (s32[2,512]{1,0:T(2,128)S(1)}, s32[2,512]{1,0:T(2,128)}, u32[]{:S(2)}) copy-start(s32[2,512]{1,0:T(2,128)} %mask_ref.1) | copy-start | bytes 12292
  1.3 18.3 %copy-start.7 = (s32[2]{0:T(128)S(1)}, s32[2]{0:T(128)}, u32[]{:S(2)}) copy-start(s32[2]{0:T(128)} %pad_add_fusion.at_ref.w_ref.refs_0_) | copy-start | bytes 28
  3.8 3.6 %copy-start.8 = (f32[8,384]{1,0:T(8,128)S(1)}, f32[8,384]{1,0:T(8,128)}, u32[]{:S(2)}) copy-start(f32[8,384]{1,0:T(8,128)} %get-tuple-element.72) | copy-start | bytes 36868
  3.8 8.4 %copy-start.2 = (bf16[144,768]{1,0:T(8,128)(2,1)S(1)}, bf16[144,768]{1,0:T(8,128)(2,1)}, u32[]{:S(2)}) copy-start(bf16[144,768]{1,0:T(8,128)(2,1)} %get-tuple-element.71.b0) | copy-start | bytes 663556
  3.8 9.5 %collective-permute-start.1 = (bf16[144,768]{1,0:T(8,128)(2,1)}, bf16[144,768]{1,0:T(8,128)(2,1)S(1)}, u32[]{:S(2)}, u32[]{:S(2)}) collective-permute-start(bf16[144,768]{1,0:T(8,128)(2,1)} %get-tuple-element.71.b0), channel_id=1, source_target_pairs={{0,2},{2,0},{1,3},{3,1},{4,6},{6,4},{5,7},{7,5},{8,10},{10,8},{9,1... | collective-permute-start | bytes 663560 | tf_op jit(solution)/shard_map/ppermute | solution.py:653
  7.3 12.2 %collective-permute-start.8 = (bf16[320,512]{1,0:T(8,128)(2,1)S(1)}, bf16[320,512]{1,0:T(8,128)(2,1)S(1)}, u32[]{:S(2)}, u32[]{:S(2)}) collective-permute-start(bf16[320,512]{1,0:T(8,128)(2,1)S(1)} %shard_map.239.refs_11_), channel_id=1, source_target_pairs={{0,2},{2,0},{1,3},{3,1},{4,6},{6,4},{5,7},{7,5},{8,10},{10,8},{9,1... | collective-permute-start | bytes 983048 | tf_op jit(solution)/shard_map/ppermute | solution.py:653
  7.4 4.7 %collective-permute-start.5 = (f32[8,384]{1,0:T(8,128)S(1)}, f32[8,384]{1,0:T(8,128)S(1)}, u32[]{:S(2)}, u32[]{:S(2)}) collective-permute-start(f32[8,384]{1,0:T(8,128)S(1)} %copy-done.8), channel_id=1, source_target_pairs={{0,12},{4,8},{8,4},{12,0},{16,28},{20,24},{24,20},{28,16},{1,13},{... | collective-permute-start | bytes 36872 | tf_op jit(solution)/shard_map/ppermute | solution.py:653
  10.4 3.7 %collective-permute-start.4 = (f32[8,384]{1,0:T(8,128)S(1)}, f32[8,384]{1,0:T(8,128)S(1)}, u32[]{:S(2)}, u32[]{:S(2)}) collective-permute-start(f32[8,384]{1,0:T(8,128)S(1)} %copy-done.8), channel_id=1, source_target_pairs={{0,8},{4,12},{8,0},{12,4},{16,24},{20,28},{24,16},{28,20},{1,9},{5... | collective-permute-start | bytes 36872 | tf_op jit(solution)/shard_map/ppermute | solution.py:653
  10.8 3.7 %collective-permute-start.3 = (f32[8,384]{1,0:T(8,128)S(1)}, f32[8,384]{1,0:T(8,128)S(1)}, u32[]{:S(2)}, u32[]{:S(2)}) collective-permute-start(f32[8,384]{1,0:T(8,128)S(1)} %copy-done.8), channel_id=1, source_target_pairs={{0,4},{4,0},{8,12},{12,8},{16,20},{20,16},{24,28},{28,24},{1,5},{5... | collective-permute-start | bytes 36872 | tf_op jit(solution)/shard_map/ppermute | solution.py:653
  12.2 7.3 %collective-permute-start = (bf16[144,768]{1,0:T(8,128)(2,1)S(1)}, bf16[144,768]{1,0:T(8,128)(2,1)S(1)}, u32[]{:S(2)}, u32[]{:S(2)}) collective-permute-start(bf16[144,768]{1,0:T(8,128)(2,1)S(1)} %copy-done.2), channel_id=1, source_target_pairs={{0,1},{1,0},{2,3},{3,2},{4,5},{5,4},{6,7},{7,6},{8,9},{9,8},{10,11... | collective-permute-start | bytes 663560 | tf_op jit(solution)/shard_map/ppermute | solution.py:653
  13.3 6.2 %collective-permute-start.2 = (bf16[144,768]{1,0:T(8,128)(2,1)S(1)}, bf16[144,768]{1,0:T(8,128)(2,1)S(1)}, u32[]{:S(2)}, u32[]{:S(2)}) collective-permute-start(bf16[144,768]{1,0:T(8,128)(2,1)S(1)} %collective-permute-done.1.b2), channel_id=1, source_target_pairs={{0,1},{1,0},{2,3},{3,2},{4,5},{5,4},{6,7},{7,6},{8,9},{9,8},{10,11... | collective-permute-start | bytes 663560 | tf_op jit(solution)/shard_map/ppermute | solution.py:653
  14.5 4.7 %collective-permute-start.6 = (f32[8,384]{1,0:T(8,128)S(1)}, f32[8,384]{1,0:T(8,128)S(1)}, u32[]{:S(2)}, u32[]{:S(2)}) collective-permute-start(f32[8,384]{1,0:T(8,128)S(1)} %add_add_fusion), channel_id=1, source_target_pairs={{0,16},{4,20},{8,24},{12,28},{16,0},{20,4},{24,8},{28,12},{1,17},{... | collective-permute-start | bytes 36872 | tf_op jit(solution)/shard_map/ppermute | solution.py:653
  17.1 8.5 %collective-permute-start.7 = (bf16[320,512]{1,0:T(8,128)(2,1)S(1)}, bf16[320,512]{1,0:T(8,128)(2,1)S(1)}, u32[]{:S(2)}, u32[]{:S(2)}) collective-permute-start(bf16[320,512]{1,0:T(8,128)(2,1)S(1)} %shard_map.239.refs_11_), channel_id=1, source_target_pairs={{0,1},{1,0},{2,3},{3,2},{4,5},{5,4},{6,7},{7,6},{8,9},{9,8},{10,11... | collective-permute-start | bytes 983048 | tf_op jit(solution)/shard_map/ppermute | solution.py:653
  19.5 11.0 %collective-permute-start.9 = (bf16[320,512]{1,0:T(8,128)(2,1)S(1)}, bf16[320,512]{1,0:T(8,128)(2,1)S(1)}, u32[]{:S(2)}, u32[]{:S(2)}) collective-permute-start(bf16[320,512]{1,0:T(8,128)(2,1)S(1)} %collective-permute-done.8.refs_13_), channel_id=1, source_target_pairs={{0,1},{1,0},{2,3},{3,2},{4,5},{5,4},{6,7},{7,6},{8,9},{9,8},{10,11... | collective-permute-start | bytes 983048 | tf_op jit(solution)/shard_map/ppermute | solution.py:653
  19.6 10.9 %copy-start = (bf16[2,512,512]{2,1,0:T(8,128)(2,1)S(1)}, bf16[2,512,512]{2,1,0:T(8,128)(2,1)}, u32[]{:S(2)}) copy-start(bf16[2,512,512]{2,1,0:T(8,128)(2,1)} %param.15) | copy-start | bytes 3145732
  22.3 5.5 %collective-permute-start.11 = (f32[2,896]{1,0:T(2,128)S(1)}, f32[2,896]{1,0:T(2,128)S(1)}, u32[]{:S(2)}, u32[]{:S(2)}) collective-permute-start(f32[2,896]{1,0:T(2,128)S(1)} %get-tuple-element.81), channel_id=1, source_target_pairs={{0,8},{4,12},{8,16},{12,20},{16,24},{20,28},{24,0},{28,4},{1,9},{5... | collective-permute-start | bytes 21512 | tf_op jit(solution)/shard_map/ppermute | solution.py:699
  24.1 6.3 %collective-permute-start.10 = (f32[2,896]{1,0:T(2,128)S(1)}, f32[2,896]{1,0:T(2,128)S(1)}, u32[]{:S(2)}, u32[]{:S(2)}) collective-permute-start(f32[2,896]{1,0:T(2,128)S(1)} %get-tuple-element.81), channel_id=1, source_target_pairs={{0,4},{4,8},{8,12},{12,16},{16,20},{20,24},{24,28},{28,0},{1,5},{5... | collective-permute-start | bytes 21512 | tf_op jit(solution)/shard_map/ppermute | solution.py:699
  41.3 2.3 %collective-permute-start.12 = (bf16[2,336,512]{2,1,0:T(8,128)(2,1)S(1)}, bf16[2,336,512]{2,1,0:T(8,128)(2,1)S(1)}, u32[]{:S(2)}, u32[]{:S(2)}) collective-permute-start(bf16[2,336,512]{2,1,0:T(8,128)(2,1)S(1)} %get-tuple-element.89), channel_id=1, source_target_pairs={{0,1},{1,0},{2,3},{3,2},{4,5},{5,4},{6,7},{7,6},{8,9},{9,8},{10,11... | collective-permute-start | bytes 2064392 | tf_op jit(solution)/shard_map/ppermute | solution.py:653
  41.3 3.6 %collective-permute-start.14 = (f32[2,896]{1,0:T(2,128)S(1)}, f32[2,896]{1,0:T(2,128)S(1)}, u32[]{:S(2)}, u32[]{:S(2)}) collective-permute-start(f32[2,896]{1,0:T(2,128)S(1)} %get-tuple-element.94), channel_id=1, source_target_pairs={{8,0},{12,4},{16,8},{20,12},{24,16},{28,20},{0,24},{4,28},{9,1},{1... | collective-permute-start | bytes 21512 | tf_op jit(solution)/shard_map/ppermute | solution.py:712
  41.7 3.6 %collective-permute-start.13 = (f32[2,896]{1,0:T(2,128)S(1)}, f32[2,896]{1,0:T(2,128)S(1)}, u32[]{:S(2)}, u32[]{:S(2)}) collective-permute-start(f32[2,896]{1,0:T(2,128)S(1)} %get-tuple-element.94), channel_id=1, source_target_pairs={{4,0},{8,4},{12,8},{16,12},{20,16},{24,20},{28,24},{0,28},{5,1},{9... | collective-permute-start | bytes 21512 | tf_op jit(solution)/shard_map/ppermute | solution.py:712
  45.3 8.7 %collective-permute-start.15 = (bf16[176,512]{1,0:T(8,128)(2,1)S(1)}, bf16[176,512]{1,0:T(8,128)(2,1)S(1)}, u32[]{:S(2)}, u32[]{:S(2)}) collective-permute-start(bf16[176,512]{1,0:T(8,128)(2,1)S(1)} %get-tuple-element.100), channel_id=1, source_target_pairs={{0,2},{2,0},{4,6},{6,4},{8,10},{10,8},{12,14},{14,12},{16,18},{18,... | collective-permute-start | bytes 540680 | tf_op jit(solution)/shard_map/ppermute | solution.py:714
  46.9 7.2 %collective-permute-start.16 = (bf16[176,512]{1,0:T(8,128)(2,1)S(1)}, bf16[176,512]{1,0:T(8,128)(2,1)S(1)}, u32[]{:S(2)}, u32[]{:S(2)}) collective-permute-start(bf16[176,512]{1,0:T(8,128)(2,1)S(1)} %get-tuple-element.101), channel_id=1, source_target_pairs={{0,4},{2,6},{4,0},{6,2},{8,12},{10,14},{12,8},{14,10},{16,20},{18,... | collective-permute-start | bytes 540680 | tf_op jit(solution)/shard_map/ppermute | solution.py:714
  48.4 7.7 %collective-permute-start.17 = (bf16[176,512]{1,0:T(8,128)(2,1)S(1)}, bf16[176,512]{1,0:T(8,128)(2,1)S(1)}, u32[]{:S(2)}, u32[]{:S(2)}) collective-permute-start(bf16[176,512]{1,0:T(8,128)(2,1)S(1)} %get-tuple-element.102), channel_id=1, source_target_pairs={{0,6},{2,4},{4,2},{6,0},{8,14},{10,12},{12,10},{14,8},{16,22},{18,... | collective-permute-start | bytes 540680 | tf_op jit(solution)/shard_map/ppermute | solution.py:714
  56.2 1.8 %collective-permute-start.18 = (bf16[2,208,512]{2,1,0:T(8,128)(2,1)S(1)}, bf16[2,208,512]{2,1,0:T(8,128)(2,1)S(1)}, u32[]{:S(2)}, u32[]{:S(2)}) collective-permute-start(bf16[2,208,512]{2,1,0:T(8,128)(2,1)S(1)} %get-tuple-element.103), channel_id=1, source_target_pairs={{0,1},{1,0},{2,3},{3,2},{4,5},{5,4},{6,7},{7,6},{8,9},{9,8},{10,11... | collective-permute-start | bytes 1277960 | tf_op jit(solution)/shard_map/ppermute | solution.py:653
  58.7 5.3 %collective-permute-start.19 = (bf16[112,512]{1,0:T(8,128)(2,1)S(1)}, bf16[112,512]{1,0:T(8,128)(2,1)S(1)}, u32[]{:S(2)}, u32[]{:S(2)}) collective-permute-start(bf16[112,512]{1,0:T(8,128)(2,1)S(1)} %get-tuple-element.105), channel_id=1, source_target_pairs={{0,2},{2,0},{4,6},{6,4},{8,10},{10,8},{12,14},{14,12},{16,18},{18,... | collective-permute-start | bytes 344072 | tf_op jit(solution)/shard_map/ppermute | solution.py:714
  60.2 6.0 %collective-permute-start.20 = (bf16[112,512]{1,0:T(8,128)(2,1)S(1)}, bf16[112,512]{1,0:T(8,128)(2,1)S(1)}, u32[]{:S(2)}, u32[]{:S(2)}) collective-permute-start(bf16[112,512]{1,0:T(8,128)(2,1)S(1)} %get-tuple-element.106), channel_id=1, source_target_pairs={{0,4},{2,6},{4,0},{6,2},{8,12},{10,14},{12,8},{14,10},{16,20},{18,... | collective-permute-start | bytes 344072 | tf_op jit(solution)/shard_map/ppermute | solution.py:714
  61.7 5.9 %collective-permute-start.21 = (bf16[112,512]{1,0:T(8,128)(2,1)S(1)}, bf16[112,512]{1,0:T(8,128)(2,1)S(1)}, u32[]{:S(2)}, u32[]{:S(2)}) collective-permute-start(bf16[112,512]{1,0:T(8,128)(2,1)S(1)} %get-tuple-element.107), channel_id=1, source_target_pairs={{0,6},{2,4},{4,2},{6,0},{8,14},{10,12},{12,10},{14,8},{16,22},{18,... | collective-permute-start | bytes 344072 | tf_op jit(solution)/shard_map/ppermute | solution.py:714
  68.3 4.6 %collective-permute-start.22 = (bf16[72,512]{1,0:T(8,128)(2,1)S(1)}, bf16[72,512]{1,0:T(8,128)(2,1)S(1)}, u32[]{:S(2)}, u32[]{:S(2)}) collective-permute-start(bf16[72,512]{1,0:T(8,128)(2,1)S(1)} %get-tuple-element.110), channel_id=1, source_target_pairs={{0,8},{4,12},{8,0},{12,4},{16,24},{20,28},{24,16},{28,20},{1,9},{5... | collective-permute-start | bytes 221192 | tf_op jit(solution)/shard_map/ppermute | solution.py:653
  69.8 6.9 %collective-permute-start.23 = (bf16[72,512]{1,0:T(8,128)(2,1)S(1)}, bf16[72,512]{1,0:T(8,128)(2,1)S(1)}, u32[]{:S(2)}, u32[]{:S(2)}) collective-permute-start(bf16[72,512]{1,0:T(8,128)(2,1)S(1)} %get-tuple-element.111), channel_id=1, source_target_pairs={{0,16},{4,20},{8,24},{12,28},{16,0},{20,4},{24,8},{28,12},{1,17},{... | collective-permute-start | bytes 221192 | tf_op jit(solution)/shard_map/ppermute | solution.py:653
  72.2 6.2 %collective-permute-start.24 = (bf16[72,512]{1,0:T(8,128)(2,1)S(1)}, bf16[72,512]{1,0:T(8,128)(2,1)S(1)}, u32[]{:S(2)}, u32[]{:S(2)}) collective-permute-start(bf16[72,512]{1,0:T(8,128)(2,1)S(1)} %get-tuple-element.112), channel_id=1, source_target_pairs={{0,24},{4,28},{8,16},{12,20},{16,8},{20,12},{24,0},{28,4},{1,25},{... | collective-permute-start | bytes 221192 | tf_op jit(solution)/shard_map/ppermute | solution.py:653
  78.4 6.2 %collective-permute-start.30 = (bf16[64,512]{1,0:T(8,128)(2,1)S(1)}, bf16[64,512]{1,0:T(8,128)(2,1)S(1)}, u32[]{:S(2)}, u32[]{:S(2)}) collective-permute-start(bf16[64,512]{1,0:T(8,128)(2,1)S(1)} %get-tuple-element.120.refs_0_), channel_id=1, source_target_pairs={{0,24},{4,28},{8,16},{12,20},{16,8},{20,12},{24,0},{28,4},{1,25},{... | collective-permute-start | bytes 196616 | tf_op jit(solution)/shard_map/ppermute | solution.py:653
  79.5 6.7 %collective-permute-start.28 = (bf16[64,512]{1,0:T(8,128)(2,1)S(1)}, bf16[64,512]{1,0:T(8,128)(2,1)S(1)}, u32[]{:S(2)}, u32[]{:S(2)}) collective-permute-start(bf16[64,512]{1,0:T(8,128)(2,1)S(1)} %get-tuple-element.120.refs_0_), channel_id=1, source_target_pairs={{0,16},{4,20},{8,24},{12,28},{16,0},{20,4},{24,8},{28,12},{1,17},{... | collective-permute-start | bytes 196616 | tf_op jit(solution)/shard_map/ppermute | solution.py:653
  79.8 7.7 %collective-permute-start.26 = (bf16[64,512]{1,0:T(8,128)(2,1)S(1)}, bf16[64,512]{1,0:T(8,128)(2,1)S(1)}, u32[]{:S(2)}, u32[]{:S(2)}) collective-permute-start(bf16[64,512]{1,0:T(8,128)(2,1)S(1)} %get-tuple-element.120.refs_0_), channel_id=1, source_target_pairs={{0,8},{4,12},{8,0},{12,4},{16,24},{20,28},{24,16},{28,20},{1,9},{5... | collective-permute-start | bytes 196616 | tf_op jit(solution)/shard_map/ppermute | solution.py:653
  82.9 8.7 %collective-permute-start.25 = (bf16[64,512]{1,0:T(8,128)(2,1)S(1)}, bf16[64,512]{1,0:T(8,128)(2,1)S(1)}, u32[]{:S(2)}, u32[]{:S(2)}) collective-permute-start(bf16[64,512]{1,0:T(8,128)(2,1)S(1)} %get-tuple-element.120.refs_0_), channel_id=1, source_target_pairs={{0,4},{4,0},{8,12},{12,8},{16,20},{20,16},{24,28},{28,24},{1,5},{5... | collective-permute-start | bytes 196616 | tf_op jit(solution)/shard_map/ppermute | solution.py:653
  84.6 6.9 %collective-permute-start.31 = (bf16[64,512]{1,0:T(8,128)(2,1)S(1)}, bf16[64,512]{1,0:T(8,128)(2,1)S(1)}, u32[]{:S(2)}, u32[]{:S(2)}) collective-permute-start(bf16[64,512]{1,0:T(8,128)(2,1)S(1)} %collective-permute-done.30.refs_6_), channel_id=1, source_target_pairs={{0,4},{4,0},{8,12},{12,8},{16,20},{20,16},{24,28},{28,24},{1,5},{5... | collective-permute-start | bytes 196616 | tf_op jit(solution)/shard_map/ppermute | solution.py:653
  86.2 5.4 %collective-permute-start.29 = (bf16[64,512]{1,0:T(8,128)(2,1)S(1)}, bf16[64,512]{1,0:T(8,128)(2,1)S(1)}, u32[]{:S(2)}, u32[]{:S(2)}) collective-permute-start(bf16[64,512]{1,0:T(8,128)(2,1)S(1)} %collective-permute-done.28.refs_4_), channel_id=1, source_target_pairs={{0,4},{4,0},{8,12},{12,8},{16,20},{20,16},{24,28},{28,24},{1,5},{5... | collective-permute-start | bytes 196616 | tf_op jit(solution)/shard_map/ppermute | solution.py:653
  87.6 4.3 %collective-permute-start.27 = (bf16[64,512]{1,0:T(8,128)(2,1)S(1)}, bf16[64,512]{1,0:T(8,128)(2,1)S(1)}, u32[]{:S(2)}, u32[]{:S(2)}) collective-permute-start(bf16[64,512]{1,0:T(8,128)(2,1)S(1)} %collective-permute-done.26.refs_2_), channel_id=1, source_target_pairs={{0,4},{4,0},{8,12},{12,8},{16,20},{20,16},{24,28},{28,24},{1,5},{5... | collective-permute-start | bytes 196616 | tf_op jit(solution)/shard_map/ppermute | solution.py:653

commit v4 on v3

--- a/solution.py
+++ b/solution.py
@@ -10,7 +10,7 @@
 
 CHUNKS = 8
 LANES = 128
-TILE = 256
+TILE = 512
 PAD = 8
 MIB = 1024 * 1024
 F32 = jnp.float32
@@ -73,6 +73,10 @@
     return slice(start, start + TILE)
 
 
+def add_to(ref, i, v):
+    ref[...] = v if i == 0 else ref[...] + v
+
+
 def run(count, body, carry, unroll):
     def block(k, c):
         for u in range(unroll):
@@ -108,6 +112,10 @@
         ref[g, :PAD, :] = jnp.zeros((PAD, LANES), F32)
         for s in range(seqs):
             ref[g, PAD + s * pitch : 2 * PAD + s * pitch, :] = jnp.zeros((PAD, LANES), F32)
+
+
+def own_w():
+    return 2 * lax.axis_index("wy") + lax.axis_index("wc")
 
 
 def one_row(v):
@@ -161,7 +169,7 @@
         c.wait()
 
 
-def k0_body(at_ref, b_ref, g_ref, n_ref, s_ref, q_ref, lr_ref, li_ref, ls_ref, msg_ref, table_ref,
+def k0_body(b_ref, g_ref, n_ref, s_ref, q_ref, lr_ref, li_ref, ls_ref, msg_ref, table_ref,
             b_scr, v_scr, l_scr, scr, sems):
     shard, cols = b_scr.shape
     own = lr_ref.shape[1]
@@ -177,7 +185,7 @@
     scr[...] = jnp.zeros_like(scr)
     for k in range(3):
         scr[k : k + 1, :own] = l_scr[k]
-    table_ref[...] = pltpu.roll(scr[...], at_ref[0] * own, 1)
+    table_ref[...] = pltpu.roll(scr[...], lax.axis_index("seq") * own, 1)
 
 
 def k0b_body(c_ref, g_ref, msg_ref, c_scr, g_scr, sems):
@@ -207,13 +215,13 @@
         ids_ref[seqs + s : seqs + s + 1, :] = jnp.broadcast_to(row[:, block_len - 1 :], (1, LANES))
 
 
-def k1_body(w_ref, x_ref, b0, b1, b2, b3, table_ref, seg_ref, mask_ref,
+def k1_body(x_ref, b0, b1, b2, b3, table_ref, seg_ref, mask_ref,
             low_ref, proj_ref, vec_ref, full_ref, s1_ref, msg_ref, rates_ref, link_ref, valid_ref, ids_ref, *, seqs):
     rows, width = x_ref.shape
     shard = b0.shape[0] - 16
     block_len = rows // seqs
     pitch = block_len + PAD
-    w = w_ref[1]
+    w = own_w()
     for k, piece in enumerate((b0, b1, b2, b3)):
         at = pl.multiple_of((w ^ k) * shard, shard)
         full_ref[pl.ds(at, shard), :] = piece[:shard, :]
@@ -273,11 +281,11 @@
 
 
 def k2_body(*refs, seqs, hops):
-    (w_ref, x_ref, t_ref, link_ref, valid_ref, ids_ref, low_ref, proj_ref, s1_ref, rates_ref, vec_ref,
-     c0, c1, c2, c3) = refs[:15]
-    recvs = refs[15 : 15 + hops]
+    (x_ref, t_ref, link_ref, valid_ref, ids_ref, low_ref, proj_ref, s1_ref, rates_ref, vec_ref,
+     c0, c1, c2, c3) = refs[:14]
+    recvs = refs[14 : 14 + hops]
     (out_ref, state_ref, gs_ref, gres_ref, gssm_ref, s2_ref, msg_ref, send_ref, keep_ref,
-     wc_scr, wg_scr, act_scr, gate_scr, ssl_scr, sl_scr, gc_scr, gg_scr, sum_scr) = refs[15 + hops :]
+     wc_scr, wg_scr, gc_scr, gg_scr, sum_scr) = refs[14 + hops :]
     rows, width = x_ref.shape
     states = rates_ref.shape[1]
     groups = states // LANES
@@ -286,7 +294,7 @@
     pitch = block_len + PAD
     g_shard = width // 4
     c_shard = 2 * states // 4
-    w = w_ref[1]
+    w = own_w()
     for k, piece in enumerate((c0, c1, c2, c3)):
         wc_scr[pl.ds(pl.multiple_of((w ^ k) * c_shard, c_shard), c_shard), :] = piece[:c_shard, :]
         wg_scr[pl.ds(pl.multiple_of((w ^ k) * g_shard, g_shard), g_shard), :] = piece[c_shard:, :]
@@ -299,7 +307,7 @@
     ids = ids_ref[...]
     init, carries = [], []
     for s in range(seqs):
-        cr, ci = carry_in(recvs, ids, s, s, a1r, a1i, block_len, False, w_ref[0])
+        cr, ci = carry_in(recvs, ids, s, s, a1r, a1i, block_len, False, lax.axis_index("seq"))
         sc = [s1_ref[s * CHUNKS : (s + 1) * CHUNKS, v * states : (v + 1) * states] for v in range(4)]
         mr, mi = cmul(sc[0], sc[1], cr, ci)
         init.append((pltpu.roll(sc[2] + mr, 1, 0), pltpu.roll(sc[3] + mi, 1, 0)))
@@ -332,7 +340,7 @@
     run(steps - PAD, lambda i, c: step(i + PAD, c), tuple(entry), 8)
 
     skip = vec_ref[2:3, :]
-    gbias = vec_ref[3:4, :]
+    gbias = 0.5 * vec_ref[3:4, :]
     loss_acc = jnp.zeros((8, width), F32)
     gbias_acc = jnp.zeros((8, width), F32)
     skip_acc = jnp.zeros((8, width), F32)
@@ -340,37 +348,31 @@
         at = slice(i * TILE, (i + 1) * TILE)
         pad_at = padded(i, block_len)
         sl = take(state_ref, pad_at, 0, 2 * groups).astype(BF16)
-        sl_scr[at, :] = sl
-        low_f = low_ref[at, :].astype(F32)
-        so = jnp.dot(sl, wc_scr[...], preferred_element_type=F32) + skip * low_f
-        z = jnp.abs(so) * 0.7071067811865476
-        e = jnp.exp(-z * z)
-        t = 1.0 / (1.0 + 0.3275911 * z)
-        poly = t * (0.254829592 + t * (-0.284496736 + t * (1.421413741 + t * (-1.453152027 + t * 1.061405429))))
-        tail = 0.5 * poly * e
+        so = jnp.dot(sl, wc_scr[...], preferred_element_type=F32) + skip * low_ref[at, :].astype(F32)
+        e = jnp.exp2(so * so * -0.7213475204444817)
+        t = 1.0 / (1.0 + 0.23164189 * jnp.abs(so))
+        tail = e * t * (0.127414796 + t * (-0.142248368 + t * (0.7107068705 + t * (-0.7265760135 + t * 0.5307027145))))
         phi = jnp.where(so >= 0.0, 1.0 - tail, tail)
         act = (so * phi).astype(BF16)
-        act_scr[at, :] = act
         dgelu = phi + so * e * 0.3989422804014327
-        act_f = act.astype(F32)
-        g = 0.5 * jnp.tanh(0.5 * (jnp.dot(act, wg_scr[...], preferred_element_type=F32) + gbias)) + 0.5
-        res = x_ref[at, :].astype(F32) + act_f * g
+        g = 0.5 * jnp.tanh(0.5 * jnp.dot(act, wg_scr[...], preferred_element_type=F32) + gbias) + 0.5
+        gated = act.astype(F32) * g
+        res = x_ref[at, :].astype(F32) + gated
         out_ref[at, :] = res.astype(BF16)
         err = res - t_ref[at, :].astype(F32)
-        em = err * wide(valid_ref[at, :], width // LANES)
-        loss_acc = loss_acc + fold_rows(em * err)
-        gr = em
+        gr = err * wide(valid_ref[at, :], width // LANES)
+        loss_acc = loss_acc + fold_rows(gr * err)
         gres_ref[at, :] = gr.astype(BF16)
-        gg = gr * act_f * g * (1.0 - g)
+        gg = gr * gated * (1.0 - g)
         gbias_acc = gbias_acc + fold_rows(gg)
         gl = gg.astype(BF16)
-        gate_scr[at, :] = gl
+        add_to(gg_scr, i, tn_dot(act, gl))
         gssm = dgelu * (gr * g + nt_dot(gl, wg_scr[...]))
         gssm_ref[at, :] = gssm
-        skip_acc = skip_acc + fold_rows(gssm * low_f)
+        skip_acc = skip_acc + fold_rows(gssm * low_ref[at, :].astype(F32))
         ssl = gssm.astype(BF16)
-        ssl_scr[at, :] = ssl
         put(gs_ref, pad_at, 0, nt_dot(ssl, wc_scr[...]).astype(BF16).astype(F32))
+        add_to(gc_scr, i, tn_dot(sl, ssl))
     clear_pads(gs_ref, seqs, pitch)
     sum_scr[0:1, :] = one_row(skip_acc)
     sum_scr[1:2, :] = one_row(gbias_acc)
@@ -404,8 +406,6 @@
         msg_ref[s : s + 1, states : 2 * states] = sc[3][:1, :]
         msg_ref[s : s + 1, 2 * states :] = ids_ref[s : s + 1, :]
 
-    gg_scr[...] = tn_dot(act_scr[...], gate_scr[...])
-    gc_scr[...] = tn_dot(sl_scr[...], ssl_scr[...])
     for k, dst in enumerate((keep_ref, send_ref, keep_ref, send_ref)):
         q = w ^ k
         slot = q // 2
@@ -432,10 +432,10 @@
 
 
 def k3_body(*refs, seqs, hops, blocks):
-    (w_ref, x_ref, link_ref, ids_ref, low_ref, proj_ref, state_ref, gs_ref, gssm_ref,
-     s2_ref, rates_ref, vec_ref, w_full) = refs[:13]
-    recvs = refs[13 : 13 + hops]
-    (gn_ref, send_ref, keep_ref, gp_scr, gpl_scr, gb_scr, vec_scr) = refs[13 + hops :]
+    (x_ref, link_ref, ids_ref, low_ref, proj_ref, state_ref, gs_ref, gssm_ref,
+     s2_ref, rates_ref, vec_ref, w_full) = refs[:12]
+    recvs = refs[12 : 12 + hops]
+    (gn_ref, send_ref, keep_ref, gp_scr, gpl_scr, gb_scr, vec_scr) = refs[12 + hops :]
     rows, width = x_ref.shape
     states = rates_ref.shape[1]
     groups = states // LANES
@@ -443,7 +443,7 @@
     steps = block_len // CHUNKS + 1
     pitch = block_len + PAD
     shard = width // 4
-    w = w_ref[1]
+    w = own_w()
     a1r, a1i = rates_ref[0:1, :], rates_ref[1:2, :]
     ar = jnp.broadcast_to(a1r, (CHUNKS, states))
     ai = jnp.broadcast_to(a1i, (CHUNKS, states))
@@ -453,7 +453,7 @@
     ids = ids_ref[...]
     rate_sums = [jnp.zeros((CHUNKS, states), F32) for _ in range(4)]
     for s in range(seqs):
-        cr, ci = carry_in(recvs, ids, s, seqs + s, a1r, a1i, block_len, True, blocks - 1 - w_ref[0])
+        cr, ci = carry_in(recvs, ids, s, seqs + s, a1r, a1i, block_len, True, blocks - 1 - lax.axis_index("seq"))
         sc = [s2_ref[s * CHUNKS : (s + 1) * CHUNKS, v * states : (v + 1) * states] for v in range(4)]
         mr, mi = cmul(sc[0], sc[1], cr, ci)
         yr = jnp.where(rowid == CHUNKS - 1, cr, pltpu.roll(sc[2] + mr, CHUNKS - 1, 0))
@@ -525,9 +525,9 @@
     sum_ref[...] = total((c0, c1, c2, c3), slice(0, sum_ref.shape[0]))
 
 
-def quarter_body(w_ref, keep_ref, got_ref, *outs):
+def quarter_body(keep_ref, got_ref, *outs):
     half = outs[0].shape[0] - 16
-    x, y = w_ref[0] % 2, w_ref[1] // 2
+    x, y = lax.axis_index("seq") % 2, lax.axis_index("wy")
     for out, slot, side in zip(outs, (y, 1 - y, y, 1 - y), (x, x, 1 - x, 1 - x)):
         def both(rows):
             return keep_ref[slot, rows, :].astype(F32) + got_ref[slot, rows, :].astype(F32)
@@ -541,7 +541,7 @@
     return sum([r[rows, :].astype(F32) for r in refs[1:]], refs[0][rows, :].astype(F32))
 
 
-def deal_body(w_ref, *refs):
+def deal_body(*refs):
     n = len(refs) - 6
     bs, c_sum, outs, b_scr = refs[:4], refs[4], refs[5 : 5 + n], refs[5 + n]
     b_half, c_half = b_scr.shape[0], c_sum.shape[0] - 16
@@ -550,7 +550,7 @@
     tail = total(bs, slice(b_half, b_half + 16)) + c_sum[c_half:, :]
     ends = split_rows([tail[:8] + tail[8:]]).astype(F32)
     for k, out in enumerate(outs):
-        at = (w_ref[0] // 2) ^ k
+        at = (lax.axis_index("seq") // 2) ^ k
         rows = [
             b_scr[pl.ds(pl.multiple_of(at * b_part, 8), b_part), :],
             c_sum[pl.ds(pl.multiple_of(at * c_part, 8), c_part), :],
@@ -571,38 +571,42 @@
     return tokens / tail[3:4, 3 * LANES : 3 * LANES + 1]
 
 
-def finish_body(w_ref, tail_ref, x_ref, gn_ref, gres_ref, vec_ref,
+def norm_body(x_ref, gn_ref, gres_ref, vec_ref, ig_ref):
+    gain = vec_ref[0:1, :]
+    for i in range(x_ref.shape[0] // TILE):
+        at = slice(i * TILE, (i + 1) * TILE)
+        n, r = centre(x_ref[at, :])
+        q = gn_ref[at, :].astype(F32) * gain
+        back = (q - jnp.mean(q, -1, keepdims=True) - n * jnp.mean(q * n, -1, keepdims=True)) * r
+        ig_ref[at, :] = (gres_ref[at, :].astype(F32) + back).astype(BF16)
+
+
+def finish_body(tail_ref, ig_ref,
                 out_ref, loss_ref, gain_ref, bias_ref, skip_ref, gate_ref, real_ref, imag_ref, step_ref, *, tokens):
-    rows, width = x_ref.shape
+    width = ig_ref.shape[1]
     states = width - gain_ref.shape[1]
     own = real_ref.shape[1]
     tail = tail_ref[...]
     scale = scale_of(tail, tokens)
-    gain = vec_ref[0:1, :]
-    for i in range(rows // TILE):
-        at = slice(i * TILE, (i + 1) * TILE)
-        n, r = centre(x_ref[at, :])
-        q = gn_ref[at, :].astype(F32) * gain
-        back = (q - jnp.mean(q, -1, keepdims=True) - n * jnp.mean(q * n, -1, keepdims=True)) * r
-        out_ref[at, :] = scale * (gres_ref[at, :].astype(F32) + back)
+    out_ref[...] = scale * ig_ref[...].astype(F32)
     scaled = tail * scale
     gain_ref[...] = scaled[0:1, states:]
     bias_ref[...] = scaled[1:2, states:]
     skip_ref[...] = scaled[3:4, :LANES]
     gate_ref[...] = scaled[3:4, LANES : 2 * LANES]
     loss_ref[...] = tail[3:4, 2 * LANES : 2 * LANES + 1] * scale * (1.0 / (tokens * width))
-    rates = pltpu.roll(scaled[:, :states], states - w_ref[0] * own, 1)
+    rates = pltpu.roll(scaled[:, :states], states - lax.axis_index("seq") * own, 1)
     for k, ref in enumerate((real_ref, imag_ref, step_ref)):
         ref[...] = rates[k : k + 1, :own]
 
 
-def unpack_body(w_ref, tail_ref, *refs, tokens):
+def unpack_body(tail_ref, *refs, tokens):
     pieces, (gb_ref, gc_ref, gg_ref, b_scr, c_scr) = refs[:-5], refs[-5:]
     scale = scale_of(tail_ref[...], tokens)
     S = len(pieces)
     b_rows, c_rows = b_scr.shape[0] // S, c_scr.shape[0] // S
     for k, piece in enumerate(pieces):
-        s = w_ref[0] ^ k
+        s = lax.axis_index("seq") ^ k
         v = piece[...].astype(F32) * scale
         b_at = s % 2 * (b_scr.shape[0] // 2) + s // 2 * b_rows
         c_at = s % 2 * (c_scr.shape[0] // 2) + s // 2 * c_rows
@@ -618,15 +622,15 @@
     gg_ref[...] = c_scr[gc_ref.shape[0] :, :]
 
 
-def whole(n, smem=(), far=()):
-    return [pl.BlockSpec(memory_space=pltpu.SMEM if i in smem else pltpu.HBM if i in far else pltpu.VMEM) for i in range(n)]
-
-
-def call(body, outs, scratch, smem, *args, us=1, limit=30, far=(), copies=0):
+def whole(n, far=()):
+    return [pl.BlockSpec(memory_space=pltpu.HBM if i in far else pltpu.VMEM) for i in range(n)]
+
+
+def call(body, outs, scratch, *args, us=1, limit=30, far=(), copies=0):
     return pl.pallas_call(
         body,
         out_shape=[jax.ShapeDtypeStruct(*o) for o in outs],
-        in_specs=whole(len(args), smem, far),
+        in_specs=whole(len(args), far),
         out_specs=whole(len(outs)),
         scratch_shapes=[pltpu.VMEM(*s) for s in scratch] + [pltpu.SemaphoreType.DMA((copies,))] * (copies > 0),
         compiler_params=pltpu.CompilerParams(vmem_limit_bytes=limit * MIB),
@@ -638,7 +642,6 @@
                glu_weight, glu_bias, lambda_real, lambda_imag, log_step):
     S = lax.axis_size("seq")
     s_at = lax.axis_index("seq")
-    w_at = 2 * lax.axis_index("wy") + lax.axis_index("wc")
     seqs, block_len, width = inputs.shape
     rows = seqs * block_len
     padded_rows = PAD + seqs * (block_len + PAD)
@@ -655,14 +658,12 @@
     def after(v, *others):
         return lax.optimization_barrier((v, *others))[0]
 
-    idx = jnp.stack([s_at, w_at]).astype(jnp.int32)
     b_msg, table = call(
         k0_body,
         [((shard + 16, b_weight.shape[1]), BF16), ((8, states), F32)],
         [(b_weight.shape, BF16), ((4, 1, shard), BF16), ((3, 1, own), F32), ((8, states), F32)],
-        (0,),
-        idx, b_weight, *(v[None] for v in (ln_gain, ln_bias, skip_weight, glu_bias, lambda_real, lambda_imag, log_step)),
-        far=range(1, 9), copies=8, limit=60,
+        b_weight, *(v[None] for v in (ln_gain, ln_bias, skip_weight, glu_bias, lambda_real, lambda_imag, log_step)),
+        far=range(8), copies=8, limit=60,
     )
     b_far = swap(b_msg, "wy")
     b_near = swap(b_msg, "wc")
@@ -670,10 +671,9 @@
         k0b_body,
         [((c_shard + g_shard, width), BF16)],
         [(c_weight.shape, BF16), (glu_weight.shape, BF16)],
-        (),
         c_weight, glu_weight, far=range(2), copies=2, limit=4,
     )
-    c_far = swap(c_msg, "wy")
+    c_far = swap(after(c_msg, b_far), "wy")
     bit = 1
     while bit < S:
         radix = 4 if 4 * bit <= S else 2
@@ -692,10 +692,9 @@
          ((R, 4 * states), F32), msg_shape, ((24, states), F32),
          ((padded_rows, LANES), F32), ((rows, LANES), F32), ((2 * seqs, LANES), F32)],
         [],
-        (0,),
-        idx, x, *bs, table, segment_ids, valid_mask, us=4, limit=8,
-    )
-    cs = (c_msg, swap(c_msg, "wc"), c_far, swap(c_far, "wc"))
+        x, *bs, table, segment_ids, valid_mask, us=2, limit=8,
+    )
+    cs = (c_msg, swap(c_msg, "wc"), c_far, swap(after(c_far, fwd), "wc"))
     fwds = [lax.ppermute(fwd, "seq", [(i, (i + k) % S) for i in range(S)]) for k in range(1, hops + 1)]
     c_bulk = c_shard + g_shard
     out, state, gs, gres, gssm, s2, bwd, send_c, keep_c = call(
@@ -703,11 +702,9 @@
         [((rows, width), BF16), (slab, F32), (slab, F32),
          ((rows, width), BF16), ((rows, width), F32), ((R, 4 * states), F32), msg_shape,
          ((2, c_bulk + 16, width), BF16), ((2, c_bulk + 16, width), BF16)],
-        [((2 * states, width), BF16), ((width, width), BF16), ((rows, width), BF16), ((rows, width), BF16),
-         ((rows, width), BF16), ((rows, 2 * states), BF16), ((2 * states, width), F32), ((width, width), F32),
+        [((2 * states, width), BF16), ((width, width), BF16), ((2 * states, width), F32), ((width, width), F32),
          ((8, width), F32)],
-        (0,),
-        idx, x, teach, link, valid, ids, low, proj, s1, rates, vec, *cs, *fwds, us=10, limit=18,
+        x, teach, link, valid, ids, low, proj, s1, rates, vec, *cs, *fwds, us=10, limit=18,
     )
     bwds = [lax.ppermute(bwd, "seq", [((i + k) % S, i) for i in range(S)]) for k in range(1, hops + 1)]
     def cross(v, flip_x, flip_y):
@@ -716,13 +713,13 @@
 
     def quarters(keep, got):
         shape = ((keep.shape[1] - 16) // 2 + 16, width)
-        return call(quarter_body, [(shape, BF16)] * 4, [], (0,), idx, keep, got, limit=4)
+        return call(quarter_body, [(shape, BF16)] * 4, [], keep, got, limit=4)
 
     def exchange(q):
         return (q[0], cross(q[1], 0, 1), cross(q[2], 1, 0), cross(q[3], 1, 1))
 
     q_c = quarters(keep_c, swap(send_c, "wc"))
-    q_c, bwds = lax.optimization_barrier((q_c, bwds))
+    bwds = lax.optimization_barrier((bwds, q_c))[0]
     part_c = exchange(q_c)
     b_bulk = 3 * shard // 2
     b_part, c_part = b_bulk // S, c_bulk // S
@@ -730,22 +727,23 @@
         functools.partial(k3_body, seqs=seqs, hops=hops, blocks=S),
         [((rows, width), BF16), ((2, b_bulk + 16, width), BF16), ((2, b_bulk + 16, width), BF16)],
         [(slab, F32), ((rows, 2 * states), BF16), ((width, 2 * states), F32), ((8, width), F32)],
-        (0,),
-        idx, x, link, ids, low, proj, state, gs, gssm, s2, rates, vec, w_full, *bwds, us=8, limit=14,
-    )
-    (c_sum,) = call(sum_body, [((c_bulk // 2 + 16, width), F32)], [], (), *part_c, limit=4)
+        x, link, ids, low, proj, state, gs, gssm, s2, rates, vec, w_full, *bwds, us=8, limit=14,
+    )
+    (c_sum,) = call(sum_body, [((c_bulk // 2 + 16, width), F32)], [], *part_c, limit=4)
     send_b, c_sum = lax.optimization_barrier((send_b, c_sum))
     part_b = exchange(quarters(keep_b, swap(send_b, "wc")))
+    (ig,) = call(norm_body, [((rows, width), BF16)], [], x, gn, gres, vec, us=3, limit=8)
+    part_b, ig = lax.optimization_barrier((part_b, ig))
     tokens = float(length * seqs * lax.axis_size(("wy", "wc")))
     deal = S // 2
     if b_part % 8 == 0 and c_part % 8 == 0:
         dealt = call(
             deal_body, [((b_part + c_part + 8, width), BF16)] * deal,
-            [((b_bulk // 2, width), F32)], (0,), idx, *part_b, c_sum, limit=4,
+            [((b_bulk // 2, width), F32)], *part_b, c_sum, limit=4,
         )
         parts = [dealt[0]] + [swap(dealt[k], "seq", 2 * k, S) for k in range(1, deal)]
         piece, tail = call(
-            close_body, [((b_part + c_part, width), BF16), ((8, width), F32)], [], (), *parts, limit=4,
+            close_body, [((b_part + c_part, width), BF16), ((8, width), F32)], [], *parts, limit=4,
         )
         pieces = {0: piece}
         for k in range(1, deal):
@@ -758,14 +756,13 @@
     ingrad, loss, *lines = call(
         functools.partial(finish_body, tokens=tokens),
         [((rows, width), F32), ((1, 1), F32)] + [((1, shard), F32)] * 4 + [((1, own), F32)] * 3,
-        [], (0,), idx, tail, x, gn, gres, vec, us=3, limit=8,
+        [], tail, ig, limit=8,
     )
     gb, gc, gg = call(
         functools.partial(unpack_body, tokens=tokens),
         [((shard, 2 * states), F32), ((c_shard, width), F32), ((g_shard, width), F32)],
         [((b_bulk, width), F32), ((c_bulk, width), F32)],
-        (0,),
-        idx, tail, *pieces, limit=8,
+        tail, *pieces, limit=8,
     )
     gain, bias, skip, gate, real, imag, step = (v[0] for v in lines)
     return (

time: 93.7 us -> 85.5 us (0.912)
  Pallas kernels: 28.8 us -> 23.5 us
  waiting for transfers between devices: 27.1 us -> 24 us
    pallas_call x12 -> x13, Pallas kernels: 28.8 us -> 23.5 us  [call(): pl.pallas_call(body, out_shape=[jax.ShapeDtypeStruct(*o) for o in outs],...]
    ppermute x22, waiting for transfers between devices: 13.8 us -> 11.8 us  [swap(): return lax.ppermute(v, axis, [(i, i ^ bit) for i in range(n)])]
    ppermute x22, starting transfers between devices: 23.5 us -> 24.5 us  [swap(): return lax.ppermute(v, axis, [(i, i ^ bit) for i in range(n)])]
    ppermute x2, waiting for transfers between devices: 0.95 us -> 0.01 us  [per_device(): lax.ppermute(bwd, 'seq', [((i + k) % S, i) for i in range(S)])]
  transfers between devices with their start and end apart: 32 -> 32, of which waited for: 21 -> 16; matrix products, arithmetic and copies ran while one was open for 0% -> 0% of each run, Pallas kernels for 13% -> 12%
where the time goes in v4:
time: 85.5 us; the launch traced here: 85.3 us
  starting transfers between devices  36.9 us (43%)
  waiting for transfers between devices  24 us (28%)
  Pallas kernels  23.5 us (27%)
  between operations  0.89 us (1%)
    ppermute x22, starting transfers between devices, swap(): return lax.ppermute(v, axis, [(i, i ^ bit) for i in range(n)])  24.5 us
    pallas_call x13, Pallas kernels, call(): pl.pallas_call(body, out_shape=[jax.ShapeDtypeStruct(*o) for o in outs],...  23.5 us
    ppermute x22, waiting for transfers between devices, swap(): return lax.ppermute(v, axis, [(i, i ^ bit) for i in range(n)])  11.8 us
    ppermute x6, waiting for transfers between devices, cross(): lax.ppermute(v, ('seq', 'wy'), [(2 * a + b, 2 * (a ^ flip_x) + (b ^ flip_...  7.32 us
    ppermute x6, starting transfers between devices, cross(): lax.ppermute(v, ('seq', 'wy'), [(2 * a + b, 2 * (a ^ flip_x) + (b ^ flip_...  7.11 us
    ppermute x2, waiting for transfers between devices, per_device(): lax.ppermute(fwd, 'seq', [(i, (i + k) % S) for i in range(S)])  4.84 us
    ppermute x2, starting transfers between devices, per_device(): lax.ppermute(fwd, 'seq', [(i, (i + k) % S) for i in range(S)])  3.01 us
    ppermute x2, starting transfers between devices, per_device(): lax.ppermute(bwd, 'seq', [((i + k) % S, i) for i in range(S)])  2.31 us
  transfers between devices with their start and end apart: 32, of which 16 were waited for; matrix products, arithmetic and copies ran while one was open for 0% of the time, Pallas kernels for 12%

profile of v4, /device:TPU:0, one launch (start us, length us, event | category | flops | bytes accessed | tf_op | source)
XLA Modules:
  0.0 85.3 jit_solution(10533301972927186617)
XLA Ops:
  0.7 1.8 %shard_map.237 = (bf16[144,768]{1,0:T(8,128)(2,1)}, f32[8,384]{1,0:T(8,128)}) custom-call(bf16[128,768]{1,0:T(8,128)(2,1)} %b_ref.1, bf16[1,128]{1,0:T(2,128)(2,1)} %bitcast.24, bf16[1,128]{1,0:T(2,128)(2,1)} %bitcast.25, bf16[1,128]{1,0:T(2,128)(2,1)} %bitcast.26, bf16[1,128]{1,0:T(2,128)(2,1)} %bitcast.27, f32[1,48]{1,0:T(1,128)} %bitcast.28, ...), custom_call_target="tpu_custom_call" | custom-call | flops 1000000000 | bytes 1048576 | tf_op jit(solution)/shard_map/pallas_call | solution.py:630
  2.6 3.0 %collective-permute-start.1 = (bf16[144,768]{1,0:T(8,128)(2,1)}, bf16[144,768]{1,0:T(8,128)(2,1)S(1)}, u32[]{:S(2)}, u32[]{:S(2)}) collective-permute-start(bf16[144,768]{1,0:T(8,128)(2,1)} %get-tuple-element.74.b0), channel_id=1, source_target_pairs={{0,2},{2,0},{1,3},{3,1},{4,6},{6,4},{5,7},{7,5},{8,10},{10,8},{9,1... | collective-permute-start | bytes 663560 | tf_op jit(solution)/shard_map/ppermute | solution.py:656
  5.6 2.5 %collective-permute-start.5 = (f32[8,384]{1,0:T(8,128)}, f32[8,384]{1,0:T(8,128)S(1)}, u32[]{:S(2)}, u32[]{:S(2)}) collective-permute-start(f32[8,384]{1,0:T(8,128)} %get-tuple-element.75), channel_id=1, source_target_pairs={{0,12},{4,8},{8,4},{12,0},{16,28},{20,24},{24,20},{28,16},{1,13},{... | collective-permute-start | bytes 36872 | tf_op jit(solution)/shard_map/ppermute | solution.py:656
  8.1 0.4 collective-permute-start.4
  8.5 0.5 collective-permute-start.3
  9.1 0.5 shard_map.239.refs_10_
  9.6 1.7 %collective-permute-done.1.b2 = bf16[144,768]{1,0:T(8,128)(2,1)S(1)} collective-permute-done((bf16[144,768]{1,0:T(8,128)(2,1)}, bf16[144,768]{1,0:T(8,128)(2,1)S(1)}, u32[]{:S(2)}, u32[]{:S(2)}) %collective-permute-start.1) | collective-permute-done | bytes 221216 | tf_op jit(solution)/shard_map/ppermute | solution.py:656
  11.2 1.7 %collective-permute-start.8 = (bf16[320,512]{1,0:T(8,128)(2,1)S(1)}, bf16[320,512]{1,0:T(8,128)(2,1)S(1)}, u32[]{:S(2)}, u32[]{:S(2)}) collective-permute-start(bf16[320,512]{1,0:T(8,128)(2,1)S(1)} %shard_map.239.refs_10_), channel_id=1, source_target_pairs={{0,2},{2,0},{1,3},{3,1},{4,6},{6,4},{5,7},{7,5},{8,10},{10,8},{9,1... | collective-permute-start | bytes 983048 | tf_op jit(solution)/shard_map/ppermute | solution.py:656
  13.0 2.7 %collective-permute-start.6 = (f32[8,384]{1,0:T(8,128)S(1)}, f32[8,384]{1,0:T(8,128)S(1)}, u32[]{:S(2)}, u32[]{:S(2)}) collective-permute-start(f32[8,384]{1,0:T(8,128)S(1)} %add_add_fusion), channel_id=1, source_target_pairs={{0,16},{4,20},{8,24},{12,28},{16,0},{20,4},{24,8},{28,12},{1,17},{... | collective-permute-start | bytes 36872 | tf_op jit(solution)/shard_map/ppermute | solution.py:656
  15.9 1.8 %collective-permute-done.6 = f32[8,384]{1,0:T(8,128)S(1)} collective-permute-done((f32[8,384]{1,0:T(8,128)S(1)}, f32[8,384]{1,0:T(8,128)S(1)}, u32[]{:S(2)}, u32[]{:S(2)}) %collective-permute-start.6) | collective-permute-done | bytes 12320 | tf_op jit(solution)/shard_map/ppermute | solution.py:656
  17.7 2.2 %shard_map.238 = (bf16[1024,512]{1,0:T(8,128)(2,1)S(1)}, f32[6,1048,128]{2,1,0:T(8,128)S(1)}, f32[8,512]{1,0:T(8,128)S(1)}, bf16[512,768]{1,0:T(8,128)(2,1)S(1)}...) custom-call(bf16[1024,512]{1,0:T(8,128)(2,1)S(1)} %bitcast.20, ...), custom_call_target="tpu_custom_call" | custom-call | flops 2000000000 | bytes 1048576 | tf_op jit(solution)/shard_map/pallas_call | solution.py:630
  20.1 1.5 %collective-permute-start.11 = (f32[2,896]{1,0:T(2,128)S(1)}, f32[2,896]{1,0:T(2,128)S(1)}, u32[]{:S(2)}, u32[]{:S(2)}) collective-permute-start(f32[2,896]{1,0:T(2,128)S(1)} %get-tuple-element.85), channel_id=1, source_target_pairs={{0,8},{4,12},{8,16},{12,20},{16,24},{20,28},{24,0},{28,4},{1,9},{5... | collective-permute-start | bytes 21512 | tf_op jit(solution)/shard_map/ppermute | solution.py:698
  21.6 1.5 %collective-permute-start.10 = (f32[2,896]{1,0:T(2,128)S(1)}, f32[2,896]{1,0:T(2,128)S(1)}, u32[]{:S(2)}, u32[]{:S(2)}) collective-permute-start(f32[2,896]{1,0:T(2,128)S(1)} %get-tuple-element.85), channel_id=1, source_target_pairs={{0,4},{4,8},{8,12},{12,16},{16,20},{20,24},{24,28},{28,0},{1,5},{5... | collective-permute-start | bytes 21512 | tf_op jit(solution)/shard_map/ppermute | solution.py:698
  23.1 2.4 %collective-permute-done.11.refs_15_ = f32[2,896]{1,0:T(2,128)S(1)} collective-permute-done((f32[2,896]{1,0:T(2,128)S(1)}, f32[2,896]{1,0:T(2,128)S(1)}, u32[]{:S(2)}, u32[]{:S(2)}) %collective-permute-start.11) | collective-permute-done | bytes 7200 | tf_op jit(solution)/shard_map/ppermute | solution.py:698
  25.6 2.4 %collective-permute-done.10.refs_14_ = f32[2,896]{1,0:T(2,128)S(1)} collective-permute-done((f32[2,896]{1,0:T(2,128)S(1)}, f32[2,896]{1,0:T(2,128)S(1)}, u32[]{:S(2)}, u32[]{:S(2)}) %collective-permute-start.10) | collective-permute-done | bytes 7200 | tf_op jit(solution)/shard_map/ppermute | solution.py:698
  28.0 9.8 %shard_map.240 = (bf16[1024,512]{1,0:T(8,128)(2,1)}, f32[6,1048,128]{2,1,0:T(8,128)S(1)}, f32[6,1048,128]{2,1,0:T(8,128)S(1)}, bf16[1024,512]{1,0:T(8,128)(2,1)S...) custom-call(bf16[1024,512]{1,0:T(8,128)(2,1)S(1)} %bitcast.21, ...), custom_call_target="tpu_custom_call" | custom-call | flops 10000000000 | bytes 1048576 | tf_op jit(solution)/shard_map/pallas_call | solution.py:630
  37.8 0.5 collective-permute-start.13
  38.3 1.8 %collective-permute-start.12 = (f32[2,896]{1,0:T(2,128)S(1)}, f32[2,896]{1,0:T(2,128)S(1)}, u32[]{:S(2)}, u32[]{:S(2)}) collective-permute-start(f32[2,896]{1,0:T(2,128)S(1)} %get-tuple-element.93), channel_id=1, source_target_pairs={{4,0},{8,4},{12,8},{16,12},{20,16},{24,20},{28,24},{0,28},{5,1},{9... | collective-permute-start | bytes 21512 | tf_op jit(solution)/shard_map/ppermute | solution.py:709
  40.3 1.5 %collective-permute-start.15 = (bf16[176,512]{1,0:T(8,128)(2,1)S(1)}, bf16[176,512]{1,0:T(8,128)(2,1)S(1)}, u32[]{:S(2)}, u32[]{:S(2)}) collective-permute-start(bf16[176,512]{1,0:T(8,128)(2,1)S(1)} %get-tuple-element.97), channel_id=1, source_target_pairs={{0,2},{2,0},{4,6},{6,4},{8,10},{10,8},{12,14},{14,12},{16,18},{18,... | collective-permute-start | bytes 540680 | tf_op jit(solution)/shard_map/ppermute | solution.py:711
  42.0 1.8 %collective-permute-start.17 = (bf16[176,512]{1,0:T(8,128)(2,1)S(1)}, bf16[176,512]{1,0:T(8,128)(2,1)S(1)}, u32[]{:S(2)}, u32[]{:S(2)}) collective-permute-start(bf16[176,512]{1,0:T(8,128)(2,1)S(1)} %get-tuple-element.99), channel_id=1, source_target_pairs={{0,6},{2,4},{4,2},{6,0},{8,14},{10,12},{12,10},{14,8},{16,22},{18,... | collective-permute-start | bytes 540680 | tf_op jit(solution)/shard_map/ppermute | solution.py:711
  43.9 4.5 %shard_map.242 = (bf16[1024,512]{1,0:T(8,128)(2,1)S(1)}, bf16[2,208,512]{2,1,0:T(8,128)(2,1)S(1)}, bf16[2,208,512]{2,1,0:T(8,128)(2,1)S(1)}) custom-call(bf16[1024,512]{1,0:T(8,128)(2,1)S(1)} %bitcast.22, f32[1048,128]{1,0:T(8,128)S(1)} %get-tuple-element.76.refs_2_.refs_1_, f32[4,128]{1,0:T(4,128)S(1)} %get-tuple-element.78.refs_4_.refs_2_, ...), custom_call_target="tpu_custom_call" | custom-call | flops 8000000000 | bytes 1048576 | tf_op jit(solution)/shard_map/pallas_call | solution.py:630
  48.4 0.9 %collective-permute-done.16.c2 = bf16[176,512]{1,0:T(8,128)(2,1)S(1)} collective-permute-done((bf16[176,512]{1,0:T(8,128)(2,1)S(1)}, bf16[176,512]{1,0:T(8,128)(2,1)S(1)}, u32[]{:S(2)}, u32[]{:S(2)}) %collective-permute-start.16) | collective-permute-done | bytes 180256 | tf_op jit(solution)/shard_map/ppermute | solution.py:711
  49.3 2.6 %collective-permute-done.17.c3 = bf16[176,512]{1,0:T(8,128)(2,1)S(1)} collective-permute-done((bf16[176,512]{1,0:T(8,128)(2,1)S(1)}, bf16[176,512]{1,0:T(8,128)(2,1)S(1)}, u32[]{:S(2)}, u32[]{:S(2)}) %collective-permute-start.17) | collective-permute-done | bytes 180256 | tf_op jit(solution)/shard_map/ppermute | solution.py:711
  52.0 1.8 %collective-permute-done.18.got_ref = bf16[2,208,512]{2,1,0:T(8,128)(2,1)S(1)} collective-permute-done((bf16[2,208,512]{2,1,0:T(8,128)(2,1)S(1)}, bf16[2,208,512]{2,1,0:T(8,128)(2,1)S(1)}, u32[]{:S(2)}, u32[]{:S(2)}) %collective-permute-start.18) | collective-permute-done | bytes 426016 | tf_op jit(solution)/shard_map/ppermute | solution.py:656
  53.9 1.5 %collective-permute-start.19 = (bf16[112,512]{1,0:T(8,128)(2,1)S(1)}, bf16[112,512]{1,0:T(8,128)(2,1)S(1)}, u32[]{:S(2)}, u32[]{:S(2)}) collective-permute-start(bf16[112,512]{1,0:T(8,128)(2,1)S(1)} %get-tuple-element.106), channel_id=1, source_target_pairs={{0,2},{2,0},{4,6},{6,4},{8,10},{10,8},{12,14},{14,12},{16,18},{18,... | collective-permute-start | bytes 344072 | tf_op jit(solution)/shard_map/ppermute | solution.py:711
  55.5 0.3 collective-permute-start.20
  55.7 1.7 %collective-permute-start.21 = (bf16[112,512]{1,0:T(8,128)(2,1)S(1)}, bf16[112,512]{1,0:T(8,128)(2,1)S(1)}, u32[]{:S(2)}, u32[]{:S(2)}) collective-permute-start(bf16[112,512]{1,0:T(8,128)(2,1)S(1)} %get-tuple-element.108), channel_id=1, source_target_pairs={{0,6},{2,4},{4,2},{6,0},{8,14},{10,12},{12,10},{14,8},{16,22},{18,... | collective-permute-start | bytes 344072 | tf_op jit(solution)/shard_map/ppermute | solution.py:711
  57.5 1.4 %shard_map.245.ig_ref = bf16[1024,512]{1,0:T(8,128)(2,1)S(1)} custom-call(bf16[1024,512]{1,0:T(8,128)(2,1)S(1)} %bitcast.23, bf16[1024,512]{1,0:T(8,128)(2,1)S(1)} %get-tuple-element.109.gn_ref, bf16[1024,512]{1,0:T(8,128)(2,1)S(1)} %get-tuple-element.110.gres_ref, f32[8,512]{1,0:T(8,128)S(1)} %get-tuple-element.83.refs_9_.refs_10_.vec_ref), custom_call_target="tpu_custom_call" | custom-call | flops 3000000000 | bytes 1048576 | tf_op jit(solution)/shard_map/pallas_call | solution.py:630
  58.9 0.3 collective-permute-done.19.refs_1_
  59.2 2.3 %collective-permute-done.20.refs_2_ = bf16[112,512]{1,0:T(8,128)(2,1)S(1)} collective-permute-done((bf16[112,512]{1,0:T(8,128)(2,1)S(1)}, bf16[112,512]{1,0:T(8,128)(2,1)S(1)}, u32[]{:S(2)}, u32[]{:S(2)}) %collective-permute-start.20) | collective-permute-done | bytes 114720 | tf_op jit(solution)/shard_map/ppermute | solution.py:711
  61.5 1.3 %collective-permute-done.21.refs_3_ = bf16[112,512]{1,0:T(8,128)(2,1)S(1)} collective-permute-done((bf16[112,512]{1,0:T(8,128)(2,1)S(1)}, bf16[112,512]{1,0:T(8,128)(2,1)S(1)}, u32[]{:S(2)}, u32[]{:S(2)}) %collective-permute-start.21) | collective-permute-done | bytes 114720 | tf_op jit(solution)/shard_map/ppermute | solution.py:711
  62.9 0.3 collective-permute-start.22
  63.2 0.8 collective-permute-start.23
  64.0 3.3 %collective-permute-start.24 = (bf16[72,512]{1,0:T(8,128)(2,1)S(1)}, bf16[72,512]{1,0:T(8,128)(2,1)S(1)}, u32[]{:S(2)}, u32[]{:S(2)}) collective-permute-start(bf16[72,512]{1,0:T(8,128)(2,1)S(1)} %get-tuple-element.119), channel_id=1, source_target_pairs={{0,24},{4,28},{8,16},{12,20},{16,8},{20,12},{24,0},{28,4},{1,25},{... | collective-permute-start | bytes 221192 | tf_op jit(solution)/shard_map/ppermute | solution.py:656
  67.4 3.7 %collective-permute-done.23.refs_2_ = bf16[72,512]{1,0:T(8,128)(2,1)S(1)} collective-permute-done((bf16[72,512]{1,0:T(8,128)(2,1)S(1)}, bf16[72,512]{1,0:T(8,128)(2,1)S(1)}, u32[]{:S(2)}, u32[]{:S(2)}) %collective-permute-start.23) | collective-permute-done | bytes 73760 | tf_op jit(solution)/shard_map/ppermute | solution.py:656
  71.1 2.6 %collective-permute-start.30 = (bf16[64,512]{1,0:T(8,128)(2,1)S(1)}, bf16[64,512]{1,0:T(8,128)(2,1)S(1)}, u32[]{:S(2)}, u32[]{:S(2)}) collective-permute-start(bf16[64,512]{1,0:T(8,128)(2,1)S(1)} %get-tuple-element.126.refs_0_), channel_id=1, source_target_pairs={{0,24},{4,28},{8,16},{12,20},{16,8},{20,12},{24,0},{28,4},{1,25},{... | collective-permute-start | bytes 196616 | tf_op jit(solution)/shard_map/ppermute | solution.py:656
  73.7 0.5 collective-permute-start.28
  74.3 1.3 %collective-permute-start.26 = (bf16[64,512]{1,0:T(8,128)(2,1)S(1)}, bf16[64,512]{1,0:T(8,128)(2,1)S(1)}, u32[]{:S(2)}, u32[]{:S(2)}) collective-permute-start(bf16[64,512]{1,0:T(8,128)(2,1)S(1)} %get-tuple-element.126.refs_0_), channel_id=1, source_target_pairs={{0,8},{4,12},{8,0},{12,4},{16,24},{20,28},{24,16},{28,20},{1,9},{5... | collective-permute-start | bytes 196616 | tf_op jit(solution)/shard_map/ppermute | solution.py:656
  75.6 1.2 %collective-permute-start.25 = (bf16[64,512]{1,0:T(8,128)(2,1)S(1)}, bf16[64,512]{1,0:T(8,128)(2,1)S(1)}, u32[]{:S(2)}, u32[]{:S(2)}) collective-permute-start(bf16[64,512]{1,0:T(8,128)(2,1)S(1)} %get-tuple-element.126.refs_0_), channel_id=1, source_target_pairs={{0,4},{4,0},{8,12},{12,8},{16,20},{20,16},{24,28},{28,24},{1,5},{5... | collective-permute-start | bytes 196616 | tf_op jit(solution)/shard_map/ppermute | solution.py:656
  76.7 0.5 collective-permute-done.30.refs_6_
  77.2 1.2 %collective-permute-start.31 = (bf16[64,512]{1,0:T(8,128)(2,1)S(1)}, bf16[64,512]{1,0:T(8,128)(2,1)S(1)}, u32[]{:S(2)}, u32[]{:S(2)}) collective-permute-start(bf16[64,512]{1,0:T(8,128)(2,1)S(1)} %collective-permute-done.30.refs_6_), channel_id=1, source_target_pairs={{0,4},{4,0},{8,12},{12,8},{16,20},{20,16},{24,28},{28,24},{1,5},{5... | collective-permute-start | bytes 196616 | tf_op jit(solution)/shard_map/ppermute | solution.py:656
  78.4 0.6 collective-permute-done.28.refs_4_
  79.0 0.9 %collective-permute-start.29 = (bf16[64,512]{1,0:T(8,128)(2,1)S(1)}, bf16[64,512]{1,0:T(8,128)(2,1)S(1)}, u32[]{:S(2)}, u32[]{:S(2)}) collective-permute-start(bf16[64,512]{1,0:T(8,128)(2,1)S(1)} %collective-permute-done.28.refs_4_), channel_id=1, source_target_pairs={{0,4},{4,0},{8,12},{12,8},{16,20},{20,16},{24,28},{28,24},{1,5},{5... | collective-permute-start | bytes 196616 | tf_op jit(solution)/shard_map/ppermute | solution.py:656
  79.9 1.1 %collective-permute-start.27 = (bf16[64,512]{1,0:T(8,128)(2,1)S(1)}, bf16[64,512]{1,0:T(8,128)(2,1)S(1)}, u32[]{:S(2)}, u32[]{:S(2)}) collective-permute-start(bf16[64,512]{1,0:T(8,128)(2,1)S(1)} %collective-permute-done.26.refs_2_), channel_id=1, source_target_pairs={{0,4},{4,0},{8,12},{12,8},{16,20},{20,16},{24,28},{28,24},{1,5},{5... | collective-permute-start | bytes 196616 | tf_op jit(solution)/shard_map/ppermute | solution.py:656
  81.0 1.5 %shard_map.248 = (f32[1024,512]{1,0:T(8,128)}, f32[1,1]{1,0:T(1,128)}, f32[1,128]{1,0:T(1,128)}, f32[1,128]{1,0:T(1,128)}, f32[1,128]{1,0:T(1,128)}, /*index=5*/...) custom-call(f32[8,512]{1,0:T(8,128)S(1)} %get-tuple-element.120.tail_ref, ...), custom_call_target="tpu_custom_call" | custom-call | flops 1000000000 | bytes 1048576 | tf_op jit(solution)/shard_map/pallas_call | solution.py:630
  82.6 0.7 collective-permute-done.29.refs_5_
  83.3 0.9 %collective-permute-done.27.refs_3_ = bf16[64,512]{1,0:T(8,128)(2,1)S(1)} collective-permute-done((bf16[64,512]{1,0:T(8,128)(2,1)S(1)}, bf16[64,512]{1,0:T(8,128)(2,1)S(1)}, u32[]{:S(2)}, u32[]{:S(2)}) %collective-permute-start.27) | collective-permute-done | bytes 65568 | tf_op jit(solution)/shard_map/ppermute | solution.py:656
  84.2 1.1 %shard_map.249 = (f32[128,768]{1,0:T(8,128)}, f32[192,512]{1,0:T(8,128)}, f32[128,512]{1,0:T(8,128)}) custom-call(f32[8,512]{1,0:T(8,128)S(1)} %get-tuple-element.120.tail_ref, bf16[64,512]{1,0:T(8,128)(2,1)S(1)} %get-tuple-element.126.refs_0_, bf16[64,512]{1,0:T(8,128)(2,1)S(1)} %collective-permute-done.25.refs_1_, ...), custom_call_target="tpu_custom_call" | custom-call | flops 1000000000 | bytes 1048576 | tf_op jit(solution)/shard_map/pallas_call | solution.py:630
  (47 shorter events, 1.3 us)
Async XLA Ops:
  0.6 8.4 %copy-start.4 = (bf16[128,512]{1,0:T(8,128)(2,1)S(1)}, bf16[128,512]{1,0:T(8,128)(2,1)}, u32[]{:S(2)}) copy-start(bf16[128,512]{1,0:T(8,128)(2,1)} %g_ref.1) | copy-start | bytes 393220
  0.7 8.4 %copy-start.3 = (bf16[192,512]{1,0:T(8,128)(2,1)S(1)}, bf16[192,512]{1,0:T(8,128)(2,1)}, u32[]{:S(2)}) copy-start(bf16[192,512]{1,0:T(8,128)(2,1)} %c_ref.1) | copy-start | bytes 589828
  0.7 17.0 %copy-start.1 = (bf16[2,512,512]{2,1,0:T(8,128)(2,1)S(1)}, bf16[2,512,512]{2,1,0:T(8,128)(2,1)}, u32[]{:S(2)}) copy-start(bf16[2,512,512]{2,1,0:T(8,128)(2,1)} %param.14) | copy-start | bytes 3145732
  0.7 17.0 %copy-start.5 = (s32[2,512]{1,0:T(2,128)S(1)}, s32[2,512]{1,0:T(2,128)}, u32[]{:S(2)}) copy-start(s32[2,512]{1,0:T(2,128)} %seg_ref.1) | copy-start | bytes 12292
  0.7 17.0 %copy-start.6 = (s32[2,512]{1,0:T(2,128)S(1)}, s32[2,512]{1,0:T(2,128)}, u32[]{:S(2)}) copy-start(s32[2,512]{1,0:T(2,128)} %mask_ref.1) | copy-start | bytes 12292
  2.5 10.5 %copy-start.7 = (f32[8,384]{1,0:T(8,128)S(1)}, f32[8,384]{1,0:T(8,128)}, u32[]{:S(2)}) copy-start(f32[8,384]{1,0:T(8,128)} %get-tuple-element.75) | copy-start | bytes 36868
  2.5 15.2 %copy-start.2 = (bf16[144,768]{1,0:T(8,128)(2,1)S(1)}, bf16[144,768]{1,0:T(8,128)(2,1)}, u32[]{:S(2)}) copy-start(bf16[144,768]{1,0:T(8,128)(2,1)} %get-tuple-element.74.b0) | copy-start | bytes 663556
  2.6 8.7 %collective-permute-start.1 = (bf16[144,768]{1,0:T(8,128)(2,1)}, bf16[144,768]{1,0:T(8,128)(2,1)S(1)}, u32[]{:S(2)}, u32[]{:S(2)}) collective-permute-start(bf16[144,768]{1,0:T(8,128)(2,1)} %get-tuple-element.74.b0), channel_id=1, source_target_pairs={{0,2},{2,0},{1,3},{3,1},{4,6},{6,4},{5,7},{7,5},{8,10},{10,8},{9,1... | collective-permute-start | bytes 663560 | tf_op jit(solution)/shard_map/ppermute | solution.py:656
  5.6 7.4 %collective-permute-start.5 = (f32[8,384]{1,0:T(8,128)}, f32[8,384]{1,0:T(8,128)S(1)}, u32[]{:S(2)}, u32[]{:S(2)}) collective-permute-start(f32[8,384]{1,0:T(8,128)} %get-tuple-element.75), channel_id=1, source_target_pairs={{0,12},{4,8},{8,4},{12,0},{16,28},{20,24},{24,20},{28,16},{1,13},{... | collective-permute-start | bytes 36872 | tf_op jit(solution)/shard_map/ppermute | solution.py:656
  8.1 4.9 %collective-permute-start.4 = (f32[8,384]{1,0:T(8,128)}, f32[8,384]{1,0:T(8,128)S(1)}, u32[]{:S(2)}, u32[]{:S(2)}) collective-permute-start(f32[8,384]{1,0:T(8,128)} %get-tuple-element.75), channel_id=1, source_target_pairs={{0,8},{4,12},{8,0},{12,4},{16,24},{20,28},{24,16},{28,20},{1,9},{5... | collective-permute-start | bytes 36872 | tf_op jit(solution)/shard_map/ppermute | solution.py:656
  8.5 4.4 %collective-permute-start.3 = (f32[8,384]{1,0:T(8,128)}, f32[8,384]{1,0:T(8,128)S(1)}, u32[]{:S(2)}, u32[]{:S(2)}) collective-permute-start(f32[8,384]{1,0:T(8,128)} %get-tuple-element.75), channel_id=1, source_target_pairs={{0,4},{4,0},{8,12},{12,8},{16,20},{20,16},{24,28},{28,24},{1,5},{5... | collective-permute-start | bytes 36872 | tf_op jit(solution)/shard_map/ppermute | solution.py:656
  9.1 8.6 %collective-permute-start = (bf16[144,768]{1,0:T(8,128)(2,1)}, bf16[144,768]{1,0:T(8,128)(2,1)S(1)}, u32[]{:S(2)}, u32[]{:S(2)}) collective-permute-start(bf16[144,768]{1,0:T(8,128)(2,1)} %get-tuple-element.74.b0), channel_id=1, source_target_pairs={{0,1},{1,0},{2,3},{3,2},{4,5},{5,4},{6,7},{7,6},{8,9},{9,8},{10,11... | collective-permute-start | bytes 663560 | tf_op jit(solution)/shard_map/ppermute | solution.py:656
  11.2 8.9 %collective-permute-start.8 = (bf16[320,512]{1,0:T(8,128)(2,1)S(1)}, bf16[320,512]{1,0:T(8,128)(2,1)S(1)}, u32[]{:S(2)}, u32[]{:S(2)}) collective-permute-start(bf16[320,512]{1,0:T(8,128)(2,1)S(1)} %shard_map.239.refs_10_), channel_id=1, source_target_pairs={{0,2},{2,0},{1,3},{3,1},{4,6},{6,4},{5,7},{7,5},{8,10},{10,8},{9,1... | collective-permute-start | bytes 983048 | tf_op jit(solution)/shard_map/ppermute | solution.py:656
  13.0 4.7 %collective-permute-start.2 = (bf16[144,768]{1,0:T(8,128)(2,1)S(1)}, bf16[144,768]{1,0:T(8,128)(2,1)S(1)}, u32[]{:S(2)}, u32[]{:S(2)}) collective-permute-start(bf16[144,768]{1,0:T(8,128)(2,1)S(1)} %collective-permute-done.1.b2), channel_id=1, source_target_pairs={{0,1},{1,0},{2,3},{3,2},{4,5},{5,4},{6,7},{7,6},{8,9},{9,8},{10,11... | collective-permute-start | bytes 663560 | tf_op jit(solution)/shard_map/ppermute | solution.py:656
  13.0 4.7 %collective-permute-start.6 = (f32[8,384]{1,0:T(8,128)S(1)}, f32[8,384]{1,0:T(8,128)S(1)}, u32[]{:S(2)}, u32[]{:S(2)}) collective-permute-start(f32[8,384]{1,0:T(8,128)S(1)} %add_add_fusion), channel_id=1, source_target_pairs={{0,16},{4,20},{8,24},{12,28},{16,0},{20,4},{24,8},{28,12},{1,17},{... | collective-permute-start | bytes 36872 | tf_op jit(solution)/shard_map/ppermute | solution.py:656
  15.7 7.5 %collective-permute-start.7 = (bf16[320,512]{1,0:T(8,128)(2,1)S(1)}, bf16[320,512]{1,0:T(8,128)(2,1)S(1)}, u32[]{:S(2)}, u32[]{:S(2)}) collective-permute-start(bf16[320,512]{1,0:T(8,128)(2,1)S(1)} %shard_map.239.refs_10_), channel_id=1, source_target_pairs={{0,1},{1,0},{2,3},{3,2},{4,5},{5,4},{6,7},{7,6},{8,9},{9,8},{10,11... | collective-permute-start | bytes 983048 | tf_op jit(solution)/shard_map/ppermute | solution.py:656
  17.7 10.3 %copy-start = (bf16[2,512,512]{2,1,0:T(8,128)(2,1)S(1)}, bf16[2,512,512]{2,1,0:T(8,128)(2,1)}, u32[]{:S(2)}) copy-start(bf16[2,512,512]{2,1,0:T(8,128)(2,1)} %param.15) | copy-start | bytes 3145732
  20.1 7.9 %collective-permute-start.9 = (bf16[320,512]{1,0:T(8,128)(2,1)S(1)}, bf16[320,512]{1,0:T(8,128)(2,1)S(1)}, u32[]{:S(2)}, u32[]{:S(2)}) collective-permute-start(bf16[320,512]{1,0:T(8,128)(2,1)S(1)} %collective-permute-done.8.refs_12_), channel_id=1, source_target_pairs={{0,1},{1,0},{2,3},{3,2},{4,5},{5,4},{6,7},{7,6},{8,9},{9,8},{10,11... | collective-permute-start | bytes 983048 | tf_op jit(solution)/shard_map/ppermute | solution.py:656
  20.1 5.4 %collective-permute-start.11 = (f32[2,896]{1,0:T(2,128)S(1)}, f32[2,896]{1,0:T(2,128)S(1)}, u32[]{:S(2)}, u32[]{:S(2)}) collective-permute-start(f32[2,896]{1,0:T(2,128)S(1)} %get-tuple-element.85), channel_id=1, source_target_pairs={{0,8},{4,12},{8,16},{12,20},{16,24},{20,28},{24,0},{28,4},{1,9},{5... | collective-permute-start | bytes 21512 | tf_op jit(solution)/shard_map/ppermute | solution.py:698
  21.6 6.3 %collective-permute-start.10 = (f32[2,896]{1,0:T(2,128)S(1)}, f32[2,896]{1,0:T(2,128)S(1)}, u32[]{:S(2)}, u32[]{:S(2)}) collective-permute-start(f32[2,896]{1,0:T(2,128)S(1)} %get-tuple-element.85), channel_id=1, source_target_pairs={{0,4},{4,8},{8,12},{12,16},{16,20},{20,24},{24,28},{28,0},{1,5},{5... | collective-permute-start | bytes 21512 | tf_op jit(solution)/shard_map/ppermute | solution.py:698
  37.8 2.3 %collective-permute-start.14 = (bf16[2,336,512]{2,1,0:T(8,128)(2,1)S(1)}, bf16[2,336,512]{2,1,0:T(8,128)(2,1)S(1)}, u32[]{:S(2)}, u32[]{:S(2)}) collective-permute-start(bf16[2,336,512]{2,1,0:T(8,128)(2,1)S(1)} %get-tuple-element.95), channel_id=1, source_target_pairs={{0,1},{1,0},{2,3},{3,2},{4,5},{5,4},{6,7},{7,6},{8,9},{9,8},{10,11... | collective-permute-start | bytes 2064392 | tf_op jit(solution)/shard_map/ppermute | solution.py:656
  37.8 6.1 %collective-permute-start.13 = (f32[2,896]{1,0:T(2,128)S(1)}, f32[2,896]{1,0:T(2,128)S(1)}, u32[]{:S(2)}, u32[]{:S(2)}) collective-permute-start(f32[2,896]{1,0:T(2,128)S(1)} %get-tuple-element.93), channel_id=1, source_target_pairs={{8,0},{12,4},{16,8},{20,12},{24,16},{28,20},{0,24},{4,28},{9,1},{1... | collective-permute-start | bytes 21512 | tf_op jit(solution)/shard_map/ppermute | solution.py:709
  38.3 5.6 %collective-permute-start.12 = (f32[2,896]{1,0:T(2,128)S(1)}, f32[2,896]{1,0:T(2,128)S(1)}, u32[]{:S(2)}, u32[]{:S(2)}) collective-permute-start(f32[2,896]{1,0:T(2,128)S(1)} %get-tuple-element.93), channel_id=1, source_target_pairs={{4,0},{8,4},{12,8},{16,12},{20,16},{24,20},{28,24},{0,28},{5,1},{9... | collective-permute-start | bytes 21512 | tf_op jit(solution)/shard_map/ppermute | solution.py:709
  40.3 8.1 %collective-permute-start.15 = (bf16[176,512]{1,0:T(8,128)(2,1)S(1)}, bf16[176,512]{1,0:T(8,128)(2,1)S(1)}, u32[]{:S(2)}, u32[]{:S(2)}) collective-permute-start(bf16[176,512]{1,0:T(8,128)(2,1)S(1)} %get-tuple-element.97), channel_id=1, source_target_pairs={{0,2},{2,0},{4,6},{6,4},{8,10},{10,8},{12,14},{14,12},{16,18},{18,... | collective-permute-start | bytes 540680 | tf_op jit(solution)/shard_map/ppermute | solution.py:711
  41.8 7.5 %collective-permute-start.16 = (bf16[176,512]{1,0:T(8,128)(2,1)S(1)}, bf16[176,512]{1,0:T(8,128)(2,1)S(1)}, u32[]{:S(2)}, u32[]{:S(2)}) collective-permute-start(bf16[176,512]{1,0:T(8,128)(2,1)S(1)} %get-tuple-element.98), channel_id=1, source_target_pairs={{0,4},{2,6},{4,0},{6,2},{8,12},{10,14},{12,8},{14,10},{16,20},{18,... | collective-permute-start | bytes 540680 | tf_op jit(solution)/shard_map/ppermute | solution.py:711
  42.0 9.8 %collective-permute-start.17 = (bf16[176,512]{1,0:T(8,128)(2,1)S(1)}, bf16[176,512]{1,0:T(8,128)(2,1)S(1)}, u32[]{:S(2)}, u32[]{:S(2)}) collective-permute-start(bf16[176,512]{1,0:T(8,128)(2,1)S(1)} %get-tuple-element.99), channel_id=1, source_target_pairs={{0,6},{2,4},{4,2},{6,0},{8,14},{10,12},{12,10},{14,8},{16,22},{18,... | collective-permute-start | bytes 540680 | tf_op jit(solution)/shard_map/ppermute | solution.py:711
  51.9 1.8 %collective-permute-start.18 = (bf16[2,208,512]{2,1,0:T(8,128)(2,1)S(1)}, bf16[2,208,512]{2,1,0:T(8,128)(2,1)S(1)}, u32[]{:S(2)}, u32[]{:S(2)}) collective-permute-start(bf16[2,208,512]{2,1,0:T(8,128)(2,1)S(1)} %get-tuple-element.104), channel_id=1, source_target_pairs={{0,1},{1,0},{2,3},{3,2},{4,5},{5,4},{6,7},{7,6},{8,9},{9,8},{10,11... | collective-permute-start | bytes 1277960 | tf_op jit(solution)/shard_map/ppermute | solution.py:656
  53.9 5.3 %collective-permute-start.19 = (bf16[112,512]{1,0:T(8,128)(2,1)S(1)}, bf16[112,512]{1,0:T(8,128)(2,1)S(1)}, u32[]{:S(2)}, u32[]{:S(2)}) collective-permute-start(bf16[112,512]{1,0:T(8,128)(2,1)S(1)} %get-tuple-element.106), channel_id=1, source_target_pairs={{0,2},{2,0},{4,6},{6,4},{8,10},{10,8},{12,14},{14,12},{16,18},{18,... | collective-permute-start | bytes 344072 | tf_op jit(solution)/shard_map/ppermute | solution.py:711
  55.5 6.0 %collective-permute-start.20 = (bf16[112,512]{1,0:T(8,128)(2,1)S(1)}, bf16[112,512]{1,0:T(8,128)(2,1)S(1)}, u32[]{:S(2)}, u32[]{:S(2)}) collective-permute-start(bf16[112,512]{1,0:T(8,128)(2,1)S(1)} %get-tuple-element.107), channel_id=1, source_target_pairs={{0,4},{2,6},{4,0},{6,2},{8,12},{10,14},{12,8},{14,10},{16,20},{18,... | collective-permute-start | bytes 344072 | tf_op jit(solution)/shard_map/ppermute | solution.py:711
  55.7 7.1 %collective-permute-start.21 = (bf16[112,512]{1,0:T(8,128)(2,1)S(1)}, bf16[112,512]{1,0:T(8,128)(2,1)S(1)}, u32[]{:S(2)}, u32[]{:S(2)}) collective-permute-start(bf16[112,512]{1,0:T(8,128)(2,1)S(1)} %get-tuple-element.108), channel_id=1, source_target_pairs={{0,6},{2,4},{4,2},{6,0},{8,14},{10,12},{12,10},{14,8},{16,22},{18,... | collective-permute-start | bytes 344072 | tf_op jit(solution)/shard_map/ppermute | solution.py:711
  62.9 4.5 %collective-permute-start.22 = (bf16[72,512]{1,0:T(8,128)(2,1)S(1)}, bf16[72,512]{1,0:T(8,128)(2,1)S(1)}, u32[]{:S(2)}, u32[]{:S(2)}) collective-permute-start(bf16[72,512]{1,0:T(8,128)(2,1)S(1)} %get-tuple-element.117), channel_id=1, source_target_pairs={{0,8},{4,12},{8,0},{12,4},{16,24},{20,28},{24,16},{28,20},{1,9},{5... | collective-permute-start | bytes 221192 | tf_op jit(solution)/shard_map/ppermute | solution.py:656
  63.2 7.8 %collective-permute-start.23 = (bf16[72,512]{1,0:T(8,128)(2,1)S(1)}, bf16[72,512]{1,0:T(8,128)(2,1)S(1)}, u32[]{:S(2)}, u32[]{:S(2)}) collective-permute-start(bf16[72,512]{1,0:T(8,128)(2,1)S(1)} %get-tuple-element.118), channel_id=1, source_target_pairs={{0,16},{4,20},{8,24},{12,28},{16,0},{20,4},{24,8},{28,12},{1,17},{... | collective-permute-start | bytes 221192 | tf_op jit(solution)/shard_map/ppermute | solution.py:656
  64.0 7.0 %collective-permute-start.24 = (bf16[72,512]{1,0:T(8,128)(2,1)S(1)}, bf16[72,512]{1,0:T(8,128)(2,1)S(1)}, u32[]{:S(2)}, u32[]{:S(2)}) collective-permute-start(bf16[72,512]{1,0:T(8,128)(2,1)S(1)} %get-tuple-element.119), channel_id=1, source_target_pairs={{0,24},{4,28},{8,16},{12,20},{16,8},{20,12},{24,0},{28,4},{1,25},{... | collective-permute-start | bytes 221192 | tf_op jit(solution)/shard_map/ppermute | solution.py:656
  71.1 6.1 %collective-permute-start.30 = (bf16[64,512]{1,0:T(8,128)(2,1)S(1)}, bf16[64,512]{1,0:T(8,128)(2,1)S(1)}, u32[]{:S(2)}, u32[]{:S(2)}) collective-permute-start(bf16[64,512]{1,0:T(8,128)(2,1)S(1)} %get-tuple-element.126.refs_0_), channel_id=1, source_target_pairs={{0,24},{4,28},{8,16},{12,20},{16,8},{20,12},{24,0},{28,4},{1,25},{... | collective-permute-start | bytes 196616 | tf_op jit(solution)/shard_map/ppermute | solution.py:656
  73.7 5.3 %collective-permute-start.28 = (bf16[64,512]{1,0:T(8,128)(2,1)S(1)}, bf16[64,512]{1,0:T(8,128)(2,1)S(1)}, u32[]{:S(2)}, u32[]{:S(2)}) collective-permute-start(bf16[64,512]{1,0:T(8,128)(2,1)S(1)} %get-tuple-element.126.refs_0_), channel_id=1, source_target_pairs={{0,16},{4,20},{8,24},{12,28},{16,0},{20,4},{24,8},{28,12},{1,17},{... | collective-permute-start | bytes 196616 | tf_op jit(solution)/shard_map/ppermute | solution.py:656
  74.3 5.6 %collective-permute-start.26 = (bf16[64,512]{1,0:T(8,128)(2,1)S(1)}, bf16[64,512]{1,0:T(8,128)(2,1)S(1)}, u32[]{:S(2)}, u32[]{:S(2)}) collective-permute-start(bf16[64,512]{1,0:T(8,128)(2,1)S(1)} %get-tuple-element.126.refs_0_), channel_id=1, source_target_pairs={{0,8},{4,12},{8,0},{12,4},{16,24},{20,28},{24,16},{28,20},{1,9},{5... | collective-permute-start | bytes 196616 | tf_op jit(solution)/shard_map/ppermute | solution.py:656
  75.6 7.0 %collective-permute-start.25 = (bf16[64,512]{1,0:T(8,128)(2,1)S(1)}, bf16[64,512]{1,0:T(8,128)(2,1)S(1)}, u32[]{:S(2)}, u32[]{:S(2)}) collective-permute-start(bf16[64,512]{1,0:T(8,128)(2,1)S(1)} %get-tuple-element.126.refs_0_), channel_id=1, source_target_pairs={{0,4},{4,0},{8,12},{12,8},{16,20},{20,16},{24,28},{28,24},{1,5},{5... | collective-permute-start | bytes 196616 | tf_op jit(solution)/shard_map/ppermute | solution.py:656
  77.2 5.3 %collective-permute-start.31 = (bf16[64,512]{1,0:T(8,128)(2,1)S(1)}, bf16[64,512]{1,0:T(8,128)(2,1)S(1)}, u32[]{:S(2)}, u32[]{:S(2)}) collective-permute-start(bf16[64,512]{1,0:T(8,128)(2,1)S(1)} %collective-permute-done.30.refs_6_), channel_id=1, source_target_pairs={{0,4},{4,0},{8,12},{12,8},{16,20},{20,16},{24,28},{28,24},{1,5},{5... | collective-permute-start | bytes 196616 | tf_op jit(solution)/shard_map/ppermute | solution.py:656
  79.0 4.3 %collective-permute-start.29 = (bf16[64,512]{1,0:T(8,128)(2,1)S(1)}, bf16[64,512]{1,0:T(8,128)(2,1)S(1)}, u32[]{:S(2)}, u32[]{:S(2)}) collective-permute-start(bf16[64,512]{1,0:T(8,128)(2,1)S(1)} %collective-permute-done.28.refs_4_), channel_id=1, source_target_pairs={{0,4},{4,0},{8,12},{12,8},{16,20},{20,16},{24,28},{28,24},{1,5},{5... | collective-permute-start | bytes 196616 | tf_op jit(solution)/shard_map/ppermute | solution.py:656
  79.9 4.3 %collective-permute-start.27 = (bf16[64,512]{1,0:T(8,128)(2,1)S(1)}, bf16[64,512]{1,0:T(8,128)(2,1)S(1)}, u32[]{:S(2)}, u32[]{:S(2)}) collective-permute-start(bf16[64,512]{1,0:T(8,128)(2,1)S(1)} %collective-permute-done.26.refs_2_), channel_id=1, source_target_pairs={{0,4},{4,0},{8,12},{12,8},{16,20},{20,16},{24,28},{28,24},{1,5},{5... | collective-permute-start | bytes 196616 | tf_op jit(solution)/shard_map/ppermute | solution.py:656

commit v5 on v4

--- a/solution.py
+++ b/solution.py
@@ -216,7 +216,7 @@
 
 
 def k1_body(x_ref, b0, b1, b2, b3, table_ref, seg_ref, mask_ref,
-            low_ref, proj_ref, vec_ref, full_ref, s1_ref, msg_ref, rates_ref, link_ref, valid_ref, ids_ref, *, seqs):
+            low_ref, n_ref, proj_ref, vec_ref, full_ref, s1_ref, msg_ref, rates_ref, link_ref, valid_ref, ids_ref, *, seqs):
     rows, width = x_ref.shape
     shard = b0.shape[0] - 16
     block_len = rows // seqs
@@ -233,7 +233,9 @@
     bias = vec_ref[1:2, :]
     for i in range(rows // TILE):
         at = slice(i * TILE, (i + 1) * TILE)
-        low = (centre(x_ref[at, :])[0] * gain + bias).astype(BF16)
+        n = centre(x_ref[at, :])[0]
+        n_ref[at, :] = n.astype(BF16)
+        low = (n * gain + bias).astype(BF16)
         low_ref[at, :] = low
         p = jnp.dot(low, full_ref[...], preferred_element_type=F32)
         put(proj_ref, padded(i, block_len), 0, p.astype(BF16).astype(F32))
@@ -284,8 +286,8 @@
     (x_ref, t_ref, link_ref, valid_ref, ids_ref, low_ref, proj_ref, s1_ref, rates_ref, vec_ref,
      c0, c1, c2, c3) = refs[:14]
     recvs = refs[14 : 14 + hops]
-    (out_ref, state_ref, gs_ref, gres_ref, gssm_ref, s2_ref, msg_ref, send_ref, keep_ref,
-     wc_scr, wg_scr, gc_scr, gg_scr, sum_scr) = refs[14 + hops :]
+    (out_hbm, state_ref, gs_ref, gres_ref, gssm_ref, s2_ref, msg_ref, send_ref, keep_ref,
+     wc_scr, wg_scr, gc_scr, gg_scr, sum_scr, out_ref, sems) = refs[14 + hops :]
     rows, width = x_ref.shape
     states = rates_ref.shape[1]
     groups = states // LANES
@@ -341,6 +343,7 @@
 
     skip = vec_ref[2:3, :]
     gbias = 0.5 * vec_ref[3:4, :]
+    leaving = []
     loss_acc = jnp.zeros((8, width), F32)
     gbias_acc = jnp.zeros((8, width), F32)
     skip_acc = jnp.zeros((8, width), F32)
@@ -359,6 +362,8 @@
         gated = act.astype(F32) * g
         res = x_ref[at, :].astype(F32) + gated
         out_ref[at, :] = res.astype(BF16)
+        leaving.append(pltpu.make_async_copy(out_ref.at[at, :], out_hbm.at[at, :], sems.at[i]))
+        leaving[-1].start()
         err = res - t_ref[at, :].astype(F32)
         gr = err * wide(valid_ref[at, :], width // LANES)
         loss_acc = loss_acc + fold_rows(gr * err)
@@ -416,6 +421,8 @@
             [sum_scr[v : v + 1, pl.ds(lanes, g_shard)] for v in range(2)]
             + [jnp.broadcast_to(loss, (1, LANES)), count], axis=1)
         dst[slot, c_shard + g_shard :, :] = split_rows([jnp.zeros((3, width), F32), line])
+    for copy in leaving:
+        copy.wait()
 
 
 def split16(v):
@@ -432,11 +439,11 @@
 
 
 def k3_body(*refs, seqs, hops, blocks):
-    (x_ref, link_ref, ids_ref, low_ref, proj_ref, state_ref, gs_ref, gssm_ref,
+    (n_ref, link_ref, ids_ref, low_ref, proj_ref, state_ref, gs_ref, gssm_ref,
      s2_ref, rates_ref, vec_ref, w_full) = refs[:12]
     recvs = refs[12 : 12 + hops]
     (gn_ref, send_ref, keep_ref, gp_scr, gpl_scr, gb_scr, vec_scr) = refs[12 + hops :]
-    rows, width = x_ref.shape
+    rows, width = n_ref.shape
     states = rates_ref.shape[1]
     groups = states // LANES
     block_len = rows // seqs
@@ -492,8 +499,7 @@
         gpl_scr[at, :] = gpl
         gn = nt_dot(gpl, w_full[...]) + skip * gssm_ref[at, :]
         gn_ref[at, :] = gn.astype(BF16)
-        n, _ = centre(x_ref[at, :])
-        gain_acc = gain_acc + fold_rows(gn * n)
+        gain_acc = gain_acc + fold_rows(gn * n_ref[at, :].astype(F32))
         bias_acc = bias_acc + fold_rows(gn)
     gb_scr[...] = tn_dot(low_ref[...], gpl_scr[...])
     sums4 = [one_row(v) for v in rate_sums]
@@ -626,12 +632,12 @@
     return [pl.BlockSpec(memory_space=pltpu.HBM if i in far else pltpu.VMEM) for i in range(n)]
 
 
-def call(body, outs, scratch, *args, us=1, limit=30, far=(), copies=0):
+def call(body, outs, scratch, *args, us=1, limit=30, far=(), far_outs=(), copies=0):
     return pl.pallas_call(
         body,
         out_shape=[jax.ShapeDtypeStruct(*o) for o in outs],
         in_specs=whole(len(args), far),
-        out_specs=whole(len(outs)),
+        out_specs=whole(len(outs), far_outs),
         scratch_shapes=[pltpu.VMEM(*s) for s in scratch] + [pltpu.SemaphoreType.DMA((copies,))] * (copies > 0),
         compiler_params=pltpu.CompilerParams(vmem_limit_bytes=limit * MIB),
         cost_estimate=pl.CostEstimate(flops=us * 1_000_000_000, bytes_accessed=MIB, transcendentals=0),
@@ -686,9 +692,9 @@
     R = seqs * CHUNKS
     slab = (2 * states // LANES, padded_rows, LANES)
     msg_shape = ((seqs, 2 * states + LANES), F32)
-    low, proj, vec, w_full, s1, fwd, rates, link, valid, ids = call(
+    low, norm, proj, vec, w_full, s1, fwd, rates, link, valid, ids = call(
         functools.partial(k1_body, seqs=seqs),
-        [((rows, width), BF16), (slab, F32), ((8, width), F32), ((width, 2 * states), BF16),
+        [((rows, width), BF16), ((rows, width), BF16), (slab, F32), ((8, width), F32), ((width, 2 * states), BF16),
          ((R, 4 * states), F32), msg_shape, ((24, states), F32),
          ((padded_rows, LANES), F32), ((rows, LANES), F32), ((2 * seqs, LANES), F32)],
         [],
@@ -703,8 +709,8 @@
          ((rows, width), BF16), ((rows, width), F32), ((R, 4 * states), F32), msg_shape,
          ((2, c_bulk + 16, width), BF16), ((2, c_bulk + 16, width), BF16)],
         [((2 * states, width), BF16), ((width, width), BF16), ((2 * states, width), F32), ((width, width), F32),
-         ((8, width), F32)],
-        x, teach, link, valid, ids, low, proj, s1, rates, vec, *cs, *fwds, us=10, limit=18,
+         ((8, width), F32), ((rows, width), BF16)],
+        x, teach, link, valid, ids, low, proj, s1, rates, vec, *cs, *fwds, us=10, limit=20, far_outs=(0,), copies=rows // TILE,
     )
     bwds = [lax.ppermute(bwd, "seq", [((i + k) % S, i) for i in range(S)]) for k in range(1, hops + 1)]
     def cross(v, flip_x, flip_y):
@@ -727,11 +733,11 @@
         functools.partial(k3_body, seqs=seqs, hops=hops, blocks=S),
         [((rows, width), BF16), ((2, b_bulk + 16, width), BF16), ((2, b_bulk + 16, width), BF16)],
         [(slab, F32), ((rows, 2 * states), BF16), ((width, 2 * states), F32), ((8, width), F32)],
-        x, link, ids, low, proj, state, gs, gssm, s2, rates, vec, w_full, *bwds, us=8, limit=14,
+        norm, link, ids, low, proj, state, gs, gssm, s2, rates, vec, w_full, *bwds, us=8, limit=14,
     )
     (c_sum,) = call(sum_body, [((c_bulk // 2 + 16, width), F32)], [], *part_c, limit=4)
-    send_b, c_sum = lax.optimization_barrier((send_b, c_sum))
-    part_b = exchange(quarters(keep_b, swap(send_b, "wc")))
+    got_b = swap(after(send_b, part_c[3]), "wc")
+    part_b = exchange(quarters(keep_b, got_b))
     (ig,) = call(norm_body, [((rows, width), BF16)], [], x, gn, gres, vec, us=3, limit=8)
     part_b, ig = lax.optimization_barrier((part_b, ig))
     tokens = float(length * seqs * lax.axis_size(("wy", "wc")))

time: 85.5 us -> 83.7 us (0.979)
  Pallas kernels: 23.5 us -> 22 us
    ppermute x22, waiting for transfers between devices: 11.8 us -> 10.1 us  [swap(): return lax.ppermute(v, axis, [(i, i ^ bit) for i in range(n)])]
    pallas_call x13, Pallas kernels: 23.5 us -> 22 us  [call(): pl.pallas_call(body, out_shape=[jax.ShapeDtypeStruct(*o) for o in outs],...]
    ppermute x22, starting transfers between devices: 24.5 us -> 25.6 us  [swap(): return lax.ppermute(v, axis, [(i, i ^ bit) for i in range(n)])]
  transfers between devices with their start and end apart: 32 -> 32, of which waited for: 16 -> 18; matrix products, arithmetic and copies ran while one was open for 0% -> 0% of each run, Pallas kernels for 12% -> 12%
where the time goes in v5:
time: 83.7 us; the launch traced here: 83.5 us
  starting transfers between devices  37.3 us (45%)
  waiting for transfers between devices  23.3 us (28%)
  Pallas kernels  22 us (26%)
  between operations  0.89 us (1%)
    ppermute x22, starting transfers between devices, swap(): return lax.ppermute(v, axis, [(i, i ^ bit) for i in range(n)])  25.6 us
    pallas_call x13, Pallas kernels, call(): pl.pallas_call(body, out_shape=[jax.ShapeDtypeStruct(*o) for o in outs],...  22 us
    ppermute x22, waiting for transfers between devices, swap(): return lax.ppermute(v, axis, [(i, i ^ bit) for i in range(n)])  10.1 us
    ppermute x6, waiting for transfers between devices, cross(): lax.ppermute(v, ('seq', 'wy'), [(2 * a + b, 2 * (a ^ flip_x) + (b ^ flip_...  7.78 us
    ppermute x6, starting transfers between devices, cross(): lax.ppermute(v, ('seq', 'wy'), [(2 * a + b, 2 * (a ^ flip_x) + (b ^ flip_...  6.31 us
    ppermute x2, waiting for transfers between devices, per_device(): lax.ppermute(fwd, 'seq', [(i, (i + k) % S) for i in range(S)])  4.84 us
    ppermute x2, starting transfers between devices, per_device(): lax.ppermute(fwd, 'seq', [(i, (i + k) % S) for i in range(S)])  3.03 us
    ppermute x2, starting transfers between devices, per_device(): lax.ppermute(bwd, 'seq', [((i + k) % S, i) for i in range(S)])  2.35 us
  transfers between devices with their start and end apart: 32, of which 18 were waited for; matrix products, arithmetic and copies ran while one was open for 0% of the time, Pallas kernels for 12%

profile of v5, /device:TPU:0, one launch (start us, length us, event | category | flops | bytes accessed | tf_op | source)
XLA Modules:
  0.0 83.5 jit_solution(18093242641874808208)
XLA Ops:
  0.7 1.8 %shard_map.237 = (bf16[144,768]{1,0:T(8,128)(2,1)}, f32[8,384]{1,0:T(8,128)}) custom-call(bf16[128,768]{1,0:T(8,128)(2,1)} %b_ref.1, bf16[1,128]{1,0:T(2,128)(2,1)} %bitcast.23, bf16[1,128]{1,0:T(2,128)(2,1)} %bitcast.24, bf16[1,128]{1,0:T(2,128)(2,1)} %bitcast.25, bf16[1,128]{1,0:T(2,128)(2,1)} %bitcast.26, f32[1,48]{1,0:T(1,128)} %bitcast.27, ...), custom_call_target="tpu_custom_call" | custom-call | flops 1000000000 | bytes 1048576 | tf_op jit(solution)/shard_map/pallas_call | solution.py:636
  2.6 3.0 %collective-permute-start.1 = (bf16[144,768]{1,0:T(8,128)(2,1)}, bf16[144,768]{1,0:T(8,128)(2,1)S(1)}, u32[]{:S(2)}, u32[]{:S(2)}) collective-permute-start(bf16[144,768]{1,0:T(8,128)(2,1)} %get-tuple-element.74.b0), channel_id=1, source_target_pairs={{0,2},{2,0},{1,3},{3,1},{4,6},{6,4},{5,7},{7,5},{8,10},{10,8},{9,1... | collective-permute-start | bytes 663560 | tf_op jit(solution)/shard_map/ppermute | solution.py:662
  5.6 2.5 %collective-permute-start.5 = (f32[8,384]{1,0:T(8,128)}, f32[8,384]{1,0:T(8,128)S(1)}, u32[]{:S(2)}, u32[]{:S(2)}) collective-permute-start(f32[8,384]{1,0:T(8,128)} %get-tuple-element.75), channel_id=1, source_target_pairs={{0,12},{4,8},{8,4},{12,0},{16,28},{20,24},{24,20},{28,16},{1,13},{... | collective-permute-start | bytes 36872 | tf_op jit(solution)/shard_map/ppermute | solution.py:662
  8.1 0.4 collective-permute-start.4
  8.5 0.5 collective-permute-start.3
  9.1 0.5 shard_map.239.refs_10_
  9.6 1.7 %collective-permute-done.1.b2 = bf16[144,768]{1,0:T(8,128)(2,1)S(1)} collective-permute-done((bf16[144,768]{1,0:T(8,128)(2,1)}, bf16[144,768]{1,0:T(8,128)(2,1)S(1)}, u32[]{:S(2)}, u32[]{:S(2)}) %collective-permute-start.1) | collective-permute-done | bytes 221216 | tf_op jit(solution)/shard_map/ppermute | solution.py:662
  11.2 1.7 %collective-permute-start.8 = (bf16[320,512]{1,0:T(8,128)(2,1)S(1)}, bf16[320,512]{1,0:T(8,128)(2,1)S(1)}, u32[]{:S(2)}, u32[]{:S(2)}) collective-permute-start(bf16[320,512]{1,0:T(8,128)(2,1)S(1)} %shard_map.239.refs_10_), channel_id=1, source_target_pairs={{0,2},{2,0},{1,3},{3,1},{4,6},{6,4},{5,7},{7,5},{8,10},{10,8},{9,1... | collective-permute-start | bytes 983048 | tf_op jit(solution)/shard_map/ppermute | solution.py:662
  13.0 2.7 %collective-permute-start.6 = (f32[8,384]{1,0:T(8,128)S(1)}, f32[8,384]{1,0:T(8,128)S(1)}, u32[]{:S(2)}, u32[]{:S(2)}) collective-permute-start(f32[8,384]{1,0:T(8,128)S(1)} %add_add_fusion), channel_id=1, source_target_pairs={{0,16},{4,20},{8,24},{12,28},{16,0},{20,4},{24,8},{28,12},{1,17},{... | collective-permute-start | bytes 36872 | tf_op jit(solution)/shard_map/ppermute | solution.py:662
  15.7 0.2 collective-permute-start.7
  15.9 1.8 %collective-permute-done.6 = f32[8,384]{1,0:T(8,128)S(1)} collective-permute-done((f32[8,384]{1,0:T(8,128)S(1)}, f32[8,384]{1,0:T(8,128)S(1)}, u32[]{:S(2)}, u32[]{:S(2)}) %collective-permute-start.6) | collective-permute-done | bytes 12320 | tf_op jit(solution)/shard_map/ppermute | solution.py:662
  17.7 2.2 %shard_map.238 = (bf16[1024,512]{1,0:T(8,128)(2,1)S(1)}, bf16[1024,512]{1,0:T(8,128)(2,1)S(1)}, f32[6,1048,128]{2,1,0:T(8,128)S(1)}, f32[8,512]{1,0:T(8,128)S(1)...) custom-call(bf16[1024,512]{1,0:T(8,128)(2,1)S(1)} %bitcast.20, ...), custom_call_target="tpu_custom_call" | custom-call | flops 2000000000 | bytes 1048576 | tf_op jit(solution)/shard_map/pallas_call | solution.py:636
  20.1 1.5 %collective-permute-start.11 = (f32[2,896]{1,0:T(2,128)S(1)}, f32[2,896]{1,0:T(2,128)S(1)}, u32[]{:S(2)}, u32[]{:S(2)}) collective-permute-start(f32[2,896]{1,0:T(2,128)S(1)} %get-tuple-element.85), channel_id=1, source_target_pairs={{0,8},{4,12},{8,16},{12,20},{16,24},{20,28},{24,0},{28,4},{1,9},{5... | collective-permute-start | bytes 21512 | tf_op jit(solution)/shard_map/ppermute | solution.py:704
  21.7 1.5 %collective-permute-start.10 = (f32[2,896]{1,0:T(2,128)S(1)}, f32[2,896]{1,0:T(2,128)S(1)}, u32[]{:S(2)}, u32[]{:S(2)}) collective-permute-start(f32[2,896]{1,0:T(2,128)S(1)} %get-tuple-element.85), channel_id=1, source_target_pairs={{0,4},{4,8},{8,12},{12,16},{16,20},{20,24},{24,28},{28,0},{1,5},{5... | collective-permute-start | bytes 21512 | tf_op jit(solution)/shard_map/ppermute | solution.py:704
  23.2 2.4 %collective-permute-done.11.refs_15_ = f32[2,896]{1,0:T(2,128)S(1)} collective-permute-done((f32[2,896]{1,0:T(2,128)S(1)}, f32[2,896]{1,0:T(2,128)S(1)}, u32[]{:S(2)}, u32[]{:S(2)}) %collective-permute-start.11) | collective-permute-done | bytes 7200 | tf_op jit(solution)/shard_map/ppermute | solution.py:704
  25.6 2.4 %collective-permute-done.10.refs_14_ = f32[2,896]{1,0:T(2,128)S(1)} collective-permute-done((f32[2,896]{1,0:T(2,128)S(1)}, f32[2,896]{1,0:T(2,128)S(1)}, u32[]{:S(2)}, u32[]{:S(2)}) %collective-permute-start.10) | collective-permute-done | bytes 7200 | tf_op jit(solution)/shard_map/ppermute | solution.py:704
  28.0 8.9 %shard_map.240 = (bf16[1024,512]{1,0:T(8,128)(2,1)}, f32[6,1048,128]{2,1,0:T(8,128)S(1)}, f32[6,1048,128]{2,1,0:T(8,128)S(1)}, bf16[1024,512]{1,0:T(8,128)(2,1)S...) custom-call(bf16[1024,512]{1,0:T(8,128)(2,1)S(1)} %bitcast.21, ...), custom_call_target="tpu_custom_call" | custom-call | flops 10000000000 | bytes 1048576 | tf_op jit(solution)/shard_map/pallas_call | solution.py:636
  37.0 0.5 collective-permute-start.13
  37.6 1.8 %collective-permute-start.12 = (f32[2,896]{1,0:T(2,128)S(1)}, f32[2,896]{1,0:T(2,128)S(1)}, u32[]{:S(2)}, u32[]{:S(2)}) collective-permute-start(f32[2,896]{1,0:T(2,128)S(1)} %get-tuple-element.94), channel_id=1, source_target_pairs={{4,0},{8,4},{12,8},{16,12},{20,16},{24,20},{28,24},{0,28},{5,1},{9... | collective-permute-start | bytes 21512 | tf_op jit(solution)/shard_map/ppermute | solution.py:715
  39.6 1.1 %collective-permute-start.15 = (bf16[176,512]{1,0:T(8,128)(2,1)S(1)}, bf16[176,512]{1,0:T(8,128)(2,1)S(1)}, u32[]{:S(2)}, u32[]{:S(2)}) collective-permute-start(bf16[176,512]{1,0:T(8,128)(2,1)S(1)} %get-tuple-element.100), channel_id=1, source_target_pairs={{0,6},{2,4},{4,2},{6,0},{8,14},{10,12},{12,10},{14,8},{16,22},{18,... | collective-permute-start | bytes 540680 | tf_op jit(solution)/shard_map/ppermute | solution.py:717
  40.7 0.5 collective-permute-done.12.refs_12_
  41.2 4.0 %shard_map.242 = (bf16[1024,512]{1,0:T(8,128)(2,1)S(1)}, bf16[2,208,512]{2,1,0:T(8,128)(2,1)S(1)}, bf16[2,208,512]{2,1,0:T(8,128)(2,1)S(1)}) custom-call(bf16[1024,512]{1,0:T(8,128)(2,1)S(1)} %get-tuple-element.88.refs_0_, f32[1048,128]{1,0:T(8,128)S(1)} %get-tuple-element.76.refs_2_.refs_1_, f32[4,128]{1,0:T(4,128)S(1)} %get-tuple-element.78.refs_4_.refs_2_, ...), custom_call_target="tpu_custom_call" | custom-call | flops 8000000000 | bytes 1048576 | tf_op jit(solution)/shard_map/pallas_call | solution.py:636
  45.2 1.7 %collective-permute-done.15.c3 = bf16[176,512]{1,0:T(8,128)(2,1)S(1)} collective-permute-done((bf16[176,512]{1,0:T(8,128)(2,1)S(1)}, bf16[176,512]{1,0:T(8,128)(2,1)S(1)}, u32[]{:S(2)}, u32[]{:S(2)}) %collective-permute-start.15) | collective-permute-done | bytes 180256 | tf_op jit(solution)/shard_map/ppermute | solution.py:717
  46.9 1.5 %collective-permute-start.20 = (bf16[176,512]{1,0:T(8,128)(2,1)S(1)}, bf16[176,512]{1,0:T(8,128)(2,1)S(1)}, u32[]{:S(2)}, u32[]{:S(2)}) collective-permute-start(bf16[176,512]{1,0:T(8,128)(2,1)S(1)} %get-tuple-element.98), channel_id=1, source_target_pairs={{0,2},{2,0},{4,6},{6,4},{8,10},{10,8},{12,14},{14,12},{16,18},{18,... | collective-permute-start | bytes 540680 | tf_op jit(solution)/shard_map/ppermute | solution.py:717
  48.8 1.5 %collective-permute-start.17 = (bf16[112,512]{1,0:T(8,128)(2,1)S(1)}, bf16[112,512]{1,0:T(8,128)(2,1)S(1)}, u32[]{:S(2)}, u32[]{:S(2)}) collective-permute-start(bf16[112,512]{1,0:T(8,128)(2,1)S(1)} %get-tuple-element.107), channel_id=1, source_target_pairs={{0,2},{2,0},{4,6},{6,4},{8,10},{10,8},{12,14},{14,12},{16,18},{18,... | collective-permute-start | bytes 344072 | tf_op jit(solution)/shard_map/ppermute | solution.py:717
  50.3 0.8 collective-permute-start.18
  51.2 1.2 %collective-permute-start.19 = (bf16[112,512]{1,0:T(8,128)(2,1)S(1)}, bf16[112,512]{1,0:T(8,128)(2,1)S(1)}, u32[]{:S(2)}, u32[]{:S(2)}) collective-permute-start(bf16[112,512]{1,0:T(8,128)(2,1)S(1)} %get-tuple-element.109), channel_id=1, source_target_pairs={{0,6},{2,4},{4,2},{6,0},{8,14},{10,12},{12,10},{14,8},{16,22},{18,... | collective-permute-start | bytes 344072 | tf_op jit(solution)/shard_map/ppermute | solution.py:717
  52.4 1.4 %shard_map.244.ig_ref = bf16[1024,512]{1,0:T(8,128)(2,1)S(1)} custom-call(bf16[1024,512]{1,0:T(8,128)(2,1)S(1)} %bitcast.22, bf16[1024,512]{1,0:T(8,128)(2,1)S(1)} %get-tuple-element.110.gn_ref, bf16[1024,512]{1,0:T(8,128)(2,1)S(1)} %get-tuple-element.111.gres_ref, f32[8,512]{1,0:T(8,128)S(1)} %get-tuple-element.83.refs_9_.refs_10_.vec_ref), custom_call_target="tpu_custom_call" | custom-call | flops 3000000000 | bytes 1048576 | tf_op jit(solution)/shard_map/pallas_call | solution.py:636
  53.8 0.5 collective-permute-done.20.c1
  54.3 1.5 %collective-permute-done.21.c2 = bf16[176,512]{1,0:T(8,128)(2,1)S(1)} collective-permute-done((bf16[176,512]{1,0:T(8,128)(2,1)S(1)}, bf16[176,512]{1,0:T(8,128)(2,1)S(1)}, u32[]{:S(2)}, u32[]{:S(2)}) %collective-permute-start.21) | collective-permute-done | bytes 180256 | tf_op jit(solution)/shard_map/ppermute | solution.py:717
  55.9 0.5 collective-permute-done.17.refs_1_
  56.3 1.9 %collective-permute-done.18.refs_2_ = bf16[112,512]{1,0:T(8,128)(2,1)S(1)} collective-permute-done((bf16[112,512]{1,0:T(8,128)(2,1)S(1)}, bf16[112,512]{1,0:T(8,128)(2,1)S(1)}, u32[]{:S(2)}, u32[]{:S(2)}) %collective-permute-start.18) | collective-permute-done | bytes 114720 | tf_op jit(solution)/shard_map/ppermute | solution.py:717
  58.2 1.8 %collective-permute-done.19.refs_3_ = bf16[112,512]{1,0:T(8,128)(2,1)S(1)} collective-permute-done((bf16[112,512]{1,0:T(8,128)(2,1)S(1)}, bf16[112,512]{1,0:T(8,128)(2,1)S(1)}, u32[]{:S(2)}, u32[]{:S(2)}) %collective-permute-start.19) | collective-permute-done | bytes 114720 | tf_op jit(solution)/shard_map/ppermute | solution.py:717
  60.1 0.3 collective-permute-start.22
  60.4 2.1 %collective-permute-start.23 = (bf16[72,512]{1,0:T(8,128)(2,1)S(1)}, bf16[72,512]{1,0:T(8,128)(2,1)S(1)}, u32[]{:S(2)}, u32[]{:S(2)}) collective-permute-start(bf16[72,512]{1,0:T(8,128)(2,1)S(1)} %get-tuple-element.118), channel_id=1, source_target_pairs={{0,16},{4,20},{8,24},{12,28},{16,0},{20,4},{24,8},{28,12},{1,17},{... | collective-permute-start | bytes 221192 | tf_op jit(solution)/shard_map/ppermute | solution.py:662
  62.5 2.0 %collective-permute-start.24 = (bf16[72,512]{1,0:T(8,128)(2,1)S(1)}, bf16[72,512]{1,0:T(8,128)(2,1)S(1)}, u32[]{:S(2)}, u32[]{:S(2)}) collective-permute-start(bf16[72,512]{1,0:T(8,128)(2,1)S(1)} %get-tuple-element.119), channel_id=1, source_target_pairs={{0,24},{4,28},{8,16},{12,20},{16,8},{20,12},{24,0},{28,4},{1,25},{... | collective-permute-start | bytes 221192 | tf_op jit(solution)/shard_map/ppermute | solution.py:662
  64.7 4.1 %collective-permute-done.23.refs_2_ = bf16[72,512]{1,0:T(8,128)(2,1)S(1)} collective-permute-done((bf16[72,512]{1,0:T(8,128)(2,1)S(1)}, bf16[72,512]{1,0:T(8,128)(2,1)S(1)}, u32[]{:S(2)}, u32[]{:S(2)}) %collective-permute-start.23) | collective-permute-done | bytes 73760 | tf_op jit(solution)/shard_map/ppermute | solution.py:662
  68.8 2.1 %collective-permute-start.30 = (bf16[64,512]{1,0:T(8,128)(2,1)S(1)}, bf16[64,512]{1,0:T(8,128)(2,1)S(1)}, u32[]{:S(2)}, u32[]{:S(2)}) collective-permute-start(bf16[64,512]{1,0:T(8,128)(2,1)S(1)} %get-tuple-element.126.refs_0_), channel_id=1, source_target_pairs={{0,24},{4,28},{8,16},{12,20},{16,8},{20,12},{24,0},{28,4},{1,25},{... | collective-permute-start | bytes 196616 | tf_op jit(solution)/shard_map/ppermute | solution.py:662
  70.9 1.5 %collective-permute-start.28 = (bf16[64,512]{1,0:T(8,128)(2,1)S(1)}, bf16[64,512]{1,0:T(8,128)(2,1)S(1)}, u32[]{:S(2)}, u32[]{:S(2)}) collective-permute-start(bf16[64,512]{1,0:T(8,128)(2,1)S(1)} %get-tuple-element.126.refs_0_), channel_id=1, source_target_pairs={{0,16},{4,20},{8,24},{12,28},{16,0},{20,4},{24,8},{28,12},{1,17},{... | collective-permute-start | bytes 196616 | tf_op jit(solution)/shard_map/ppermute | solution.py:662
  72.4 0.9 %collective-permute-start.26 = (bf16[64,512]{1,0:T(8,128)(2,1)S(1)}, bf16[64,512]{1,0:T(8,128)(2,1)S(1)}, u32[]{:S(2)}, u32[]{:S(2)}) collective-permute-start(bf16[64,512]{1,0:T(8,128)(2,1)S(1)} %get-tuple-element.126.refs_0_), channel_id=1, source_target_pairs={{0,8},{4,12},{8,0},{12,4},{16,24},{20,28},{24,16},{28,20},{1,9},{5... | collective-permute-start | bytes 196616 | tf_op jit(solution)/shard_map/ppermute | solution.py:662
  73.3 1.8 %collective-permute-start.25 = (bf16[64,512]{1,0:T(8,128)(2,1)S(1)}, bf16[64,512]{1,0:T(8,128)(2,1)S(1)}, u32[]{:S(2)}, u32[]{:S(2)}) collective-permute-start(bf16[64,512]{1,0:T(8,128)(2,1)S(1)} %get-tuple-element.126.refs_0_), channel_id=1, source_target_pairs={{0,4},{4,0},{8,12},{12,8},{16,20},{20,16},{24,28},{28,24},{1,5},{5... | collective-permute-start | bytes 196616 | tf_op jit(solution)/shard_map/ppermute | solution.py:662
  75.1 1.7 %collective-permute-start.31 = (bf16[64,512]{1,0:T(8,128)(2,1)S(1)}, bf16[64,512]{1,0:T(8,128)(2,1)S(1)}, u32[]{:S(2)}, u32[]{:S(2)}) collective-permute-start(bf16[64,512]{1,0:T(8,128)(2,1)S(1)} %collective-permute-done.30.refs_6_), channel_id=1, source_target_pairs={{0,4},{4,0},{8,12},{12,8},{16,20},{20,16},{24,28},{28,24},{1,5},{5... | collective-permute-start | bytes 196616 | tf_op jit(solution)/shard_map/ppermute | solution.py:662
  76.8 1.3 %collective-permute-start.29 = (bf16[64,512]{1,0:T(8,128)(2,1)S(1)}, bf16[64,512]{1,0:T(8,128)(2,1)S(1)}, u32[]{:S(2)}, u32[]{:S(2)}) collective-permute-start(bf16[64,512]{1,0:T(8,128)(2,1)S(1)} %collective-permute-done.28.refs_4_), channel_id=1, source_target_pairs={{0,4},{4,0},{8,12},{12,8},{16,20},{20,16},{24,28},{28,24},{1,5},{5... | collective-permute-start | bytes 196616 | tf_op jit(solution)/shard_map/ppermute | solution.py:662
  78.1 0.7 collective-permute-start.27
  78.9 1.5 %shard_map.248 = (f32[1024,512]{1,0:T(8,128)}, f32[1,1]{1,0:T(1,128)}, f32[1,128]{1,0:T(1,128)}, f32[1,128]{1,0:T(1,128)}, f32[1,128]{1,0:T(1,128)}, /*index=5*/...) custom-call(f32[8,512]{1,0:T(8,128)S(1)} %get-tuple-element.120.tail_ref, ...), custom_call_target="tpu_custom_call" | custom-call | flops 1000000000 | bytes 1048576 | tf_op jit(solution)/shard_map/pallas_call | solution.py:636
  80.4 0.7 collective-permute-done.29.refs_5_
  81.1 1.3 %collective-permute-done.27.refs_3_ = bf16[64,512]{1,0:T(8,128)(2,1)S(1)} collective-permute-done((bf16[64,512]{1,0:T(8,128)(2,1)S(1)}, bf16[64,512]{1,0:T(8,128)(2,1)S(1)}, u32[]{:S(2)}, u32[]{:S(2)}) %collective-permute-start.27) | collective-permute-done | bytes 65568 | tf_op jit(solution)/shard_map/ppermute | solution.py:662
  82.4 1.1 %shard_map.249 = (f32[128,768]{1,0:T(8,128)}, f32[192,512]{1,0:T(8,128)}, f32[128,512]{1,0:T(8,128)}) custom-call(f32[8,512]{1,0:T(8,128)S(1)} %get-tuple-element.120.tail_ref, bf16[64,512]{1,0:T(8,128)(2,1)S(1)} %get-tuple-element.126.refs_0_, bf16[64,512]{1,0:T(8,128)(2,1)S(1)} %collective-permute-done.25.refs_1_, ...), custom_call_target="tpu_custom_call" | custom-call | flops 1000000000 | bytes 1048576 | tf_op jit(solution)/shard_map/pallas_call | solution.py:636
  (47 shorter events, 1.5 us)
Async XLA Ops:
  0.6 8.4 %copy-start.4 = (bf16[128,512]{1,0:T(8,128)(2,1)S(1)}, bf16[128,512]{1,0:T(8,128)(2,1)}, u32[]{:S(2)}) copy-start(bf16[128,512]{1,0:T(8,128)(2,1)} %g_ref.1) | copy-start | bytes 393220
  0.7 8.4 %copy-start.3 = (bf16[192,512]{1,0:T(8,128)(2,1)S(1)}, bf16[192,512]{1,0:T(8,128)(2,1)}, u32[]{:S(2)}) copy-start(bf16[192,512]{1,0:T(8,128)(2,1)} %c_ref.1) | copy-start | bytes 589828
  0.7 17.0 %copy-start.1 = (bf16[2,512,512]{2,1,0:T(8,128)(2,1)S(1)}, bf16[2,512,512]{2,1,0:T(8,128)(2,1)}, u32[]{:S(2)}) copy-start(bf16[2,512,512]{2,1,0:T(8,128)(2,1)} %param.14) | copy-start | bytes 3145732
  0.7 17.0 %copy-start.5 = (s32[2,512]{1,0:T(2,128)S(1)}, s32[2,512]{1,0:T(2,128)}, u32[]{:S(2)}) copy-start(s32[2,512]{1,0:T(2,128)} %seg_ref.1) | copy-start | bytes 12292
  0.7 17.0 %copy-start.6 = (s32[2,512]{1,0:T(2,128)S(1)}, s32[2,512]{1,0:T(2,128)}, u32[]{:S(2)}) copy-start(s32[2,512]{1,0:T(2,128)} %mask_ref.1) | copy-start | bytes 12292
  2.5 10.5 %copy-start.7 = (f32[8,384]{1,0:T(8,128)S(1)}, f32[8,384]{1,0:T(8,128)}, u32[]{:S(2)}) copy-start(f32[8,384]{1,0:T(8,128)} %get-tuple-element.75) | copy-start | bytes 36868
  2.5 15.2 %copy-start.2 = (bf16[144,768]{1,0:T(8,128)(2,1)S(1)}, bf16[144,768]{1,0:T(8,128)(2,1)}, u32[]{:S(2)}) copy-start(bf16[144,768]{1,0:T(8,128)(2,1)} %get-tuple-element.74.b0) | copy-start | bytes 663556
  2.6 8.7 %collective-permute-start.1 = (bf16[144,768]{1,0:T(8,128)(2,1)}, bf16[144,768]{1,0:T(8,128)(2,1)S(1)}, u32[]{:S(2)}, u32[]{:S(2)}) collective-permute-start(bf16[144,768]{1,0:T(8,128)(2,1)} %get-tuple-element.74.b0), channel_id=1, source_target_pairs={{0,2},{2,0},{1,3},{3,1},{4,6},{6,4},{5,7},{7,5},{8,10},{10,8},{9,1... | collective-permute-start | bytes 663560 | tf_op jit(solution)/shard_map/ppermute | solution.py:662
  5.6 7.4 %collective-permute-start.5 = (f32[8,384]{1,0:T(8,128)}, f32[8,384]{1,0:T(8,128)S(1)}, u32[]{:S(2)}, u32[]{:S(2)}) collective-permute-start(f32[8,384]{1,0:T(8,128)} %get-tuple-element.75), channel_id=1, source_target_pairs={{0,12},{4,8},{8,4},{12,0},{16,28},{20,24},{24,20},{28,16},{1,13},{... | collective-permute-start | bytes 36872 | tf_op jit(solution)/shard_map/ppermute | solution.py:662
  8.1 4.9 %collective-permute-start.4 = (f32[8,384]{1,0:T(8,128)}, f32[8,384]{1,0:T(8,128)S(1)}, u32[]{:S(2)}, u32[]{:S(2)}) collective-permute-start(f32[8,384]{1,0:T(8,128)} %get-tuple-element.75), channel_id=1, source_target_pairs={{0,8},{4,12},{8,0},{12,4},{16,24},{20,28},{24,16},{28,20},{1,9},{5... | collective-permute-start | bytes 36872 | tf_op jit(solution)/shard_map/ppermute | solution.py:662
  8.5 4.4 %collective-permute-start.3 = (f32[8,384]{1,0:T(8,128)}, f32[8,384]{1,0:T(8,128)S(1)}, u32[]{:S(2)}, u32[]{:S(2)}) collective-permute-start(f32[8,384]{1,0:T(8,128)} %get-tuple-element.75), channel_id=1, source_target_pairs={{0,4},{4,0},{8,12},{12,8},{16,20},{20,16},{24,28},{28,24},{1,5},{5... | collective-permute-start | bytes 36872 | tf_op jit(solution)/shard_map/ppermute | solution.py:662
  9.1 8.6 %collective-permute-start = (bf16[144,768]{1,0:T(8,128)(2,1)}, bf16[144,768]{1,0:T(8,128)(2,1)S(1)}, u32[]{:S(2)}, u32[]{:S(2)}) collective-permute-start(bf16[144,768]{1,0:T(8,128)(2,1)} %get-tuple-element.74.b0), channel_id=1, source_target_pairs={{0,1},{1,0},{2,3},{3,2},{4,5},{5,4},{6,7},{7,6},{8,9},{9,8},{10,11... | collective-permute-start | bytes 663560 | tf_op jit(solution)/shard_map/ppermute | solution.py:662
  11.2 8.9 %collective-permute-start.8 = (bf16[320,512]{1,0:T(8,128)(2,1)S(1)}, bf16[320,512]{1,0:T(8,128)(2,1)S(1)}, u32[]{:S(2)}, u32[]{:S(2)}) collective-permute-start(bf16[320,512]{1,0:T(8,128)(2,1)S(1)} %shard_map.239.refs_10_), channel_id=1, source_target_pairs={{0,2},{2,0},{1,3},{3,1},{4,6},{6,4},{5,7},{7,5},{8,10},{10,8},{9,1... | collective-permute-start | bytes 983048 | tf_op jit(solution)/shard_map/ppermute | solution.py:662
  13.0 4.7 %collective-permute-start.2 = (bf16[144,768]{1,0:T(8,128)(2,1)S(1)}, bf16[144,768]{1,0:T(8,128)(2,1)S(1)}, u32[]{:S(2)}, u32[]{:S(2)}) collective-permute-start(bf16[144,768]{1,0:T(8,128)(2,1)S(1)} %collective-permute-done.1.b2), channel_id=1, source_target_pairs={{0,1},{1,0},{2,3},{3,2},{4,5},{5,4},{6,7},{7,6},{8,9},{9,8},{10,11... | collective-permute-start | bytes 663560 | tf_op jit(solution)/shard_map/ppermute | solution.py:662
  13.0 4.7 %collective-permute-start.6 = (f32[8,384]{1,0:T(8,128)S(1)}, f32[8,384]{1,0:T(8,128)S(1)}, u32[]{:S(2)}, u32[]{:S(2)}) collective-permute-start(f32[8,384]{1,0:T(8,128)S(1)} %add_add_fusion), channel_id=1, source_target_pairs={{0,16},{4,20},{8,24},{12,28},{16,0},{20,4},{24,8},{28,12},{1,17},{... | collective-permute-start | bytes 36872 | tf_op jit(solution)/shard_map/ppermute | solution.py:662
  15.7 7.5 %collective-permute-start.7 = (bf16[320,512]{1,0:T(8,128)(2,1)S(1)}, bf16[320,512]{1,0:T(8,128)(2,1)S(1)}, u32[]{:S(2)}, u32[]{:S(2)}) collective-permute-start(bf16[320,512]{1,0:T(8,128)(2,1)S(1)} %shard_map.239.refs_10_), channel_id=1, source_target_pairs={{0,1},{1,0},{2,3},{3,2},{4,5},{5,4},{6,7},{7,6},{8,9},{9,8},{10,11... | collective-permute-start | bytes 983048 | tf_op jit(solution)/shard_map/ppermute | solution.py:662
  17.7 10.3 %copy-start = (bf16[2,512,512]{2,1,0:T(8,128)(2,1)S(1)}, bf16[2,512,512]{2,1,0:T(8,128)(2,1)}, u32[]{:S(2)}) copy-start(bf16[2,512,512]{2,1,0:T(8,128)(2,1)} %param.15) | copy-start | bytes 3145732
  20.1 7.9 %collective-permute-start.9 = (bf16[320,512]{1,0:T(8,128)(2,1)S(1)}, bf16[320,512]{1,0:T(8,128)(2,1)S(1)}, u32[]{:S(2)}, u32[]{:S(2)}) collective-permute-start(bf16[320,512]{1,0:T(8,128)(2,1)S(1)} %collective-permute-done.8.refs_12_), channel_id=1, source_target_pairs={{0,1},{1,0},{2,3},{3,2},{4,5},{5,4},{6,7},{7,6},{8,9},{9,8},{10,11... | collective-permute-start | bytes 983048 | tf_op jit(solution)/shard_map/ppermute | solution.py:662
  20.1 5.4 %collective-permute-start.11 = (f32[2,896]{1,0:T(2,128)S(1)}, f32[2,896]{1,0:T(2,128)S(1)}, u32[]{:S(2)}, u32[]{:S(2)}) collective-permute-start(f32[2,896]{1,0:T(2,128)S(1)} %get-tuple-element.85), channel_id=1, source_target_pairs={{0,8},{4,12},{8,16},{12,20},{16,24},{20,28},{24,0},{28,4},{1,9},{5... | collective-permute-start | bytes 21512 | tf_op jit(solution)/shard_map/ppermute | solution.py:704
  21.7 6.3 %collective-permute-start.10 = (f32[2,896]{1,0:T(2,128)S(1)}, f32[2,896]{1,0:T(2,128)S(1)}, u32[]{:S(2)}, u32[]{:S(2)}) collective-permute-start(f32[2,896]{1,0:T(2,128)S(1)} %get-tuple-element.85), channel_id=1, source_target_pairs={{0,4},{4,8},{8,12},{12,16},{16,20},{20,24},{24,28},{28,0},{1,5},{5... | collective-permute-start | bytes 21512 | tf_op jit(solution)/shard_map/ppermute | solution.py:704
  37.0 2.4 %collective-permute-start.14 = (bf16[2,336,512]{2,1,0:T(8,128)(2,1)S(1)}, bf16[2,336,512]{2,1,0:T(8,128)(2,1)S(1)}, u32[]{:S(2)}, u32[]{:S(2)}) collective-permute-start(bf16[2,336,512]{2,1,0:T(8,128)(2,1)S(1)} %get-tuple-element.96), channel_id=1, source_target_pairs={{0,1},{1,0},{2,3},{3,2},{4,5},{5,4},{6,7},{7,6},{8,9},{9,8},{10,11... | collective-permute-start | bytes 2064392 | tf_op jit(solution)/shard_map/ppermute | solution.py:662
  37.0 3.7 %collective-permute-start.13 = (f32[2,896]{1,0:T(2,128)S(1)}, f32[2,896]{1,0:T(2,128)S(1)}, u32[]{:S(2)}, u32[]{:S(2)}) collective-permute-start(f32[2,896]{1,0:T(2,128)S(1)} %get-tuple-element.94), channel_id=1, source_target_pairs={{8,0},{12,4},{16,8},{20,12},{24,16},{28,20},{0,24},{4,28},{9,1},{1... | collective-permute-start | bytes 21512 | tf_op jit(solution)/shard_map/ppermute | solution.py:715
  37.6 3.6 %collective-permute-start.12 = (f32[2,896]{1,0:T(2,128)S(1)}, f32[2,896]{1,0:T(2,128)S(1)}, u32[]{:S(2)}, u32[]{:S(2)}) collective-permute-start(f32[2,896]{1,0:T(2,128)S(1)} %get-tuple-element.94), channel_id=1, source_target_pairs={{4,0},{8,4},{12,8},{16,12},{20,16},{24,20},{28,24},{0,28},{5,1},{9... | collective-permute-start | bytes 21512 | tf_op jit(solution)/shard_map/ppermute | solution.py:715
  39.6 7.3 %collective-permute-start.15 = (bf16[176,512]{1,0:T(8,128)(2,1)S(1)}, bf16[176,512]{1,0:T(8,128)(2,1)S(1)}, u32[]{:S(2)}, u32[]{:S(2)}) collective-permute-start(bf16[176,512]{1,0:T(8,128)(2,1)S(1)} %get-tuple-element.100), channel_id=1, source_target_pairs={{0,6},{2,4},{4,2},{6,0},{8,14},{10,12},{12,10},{14,8},{16,22},{18,... | collective-permute-start | bytes 540680 | tf_op jit(solution)/shard_map/ppermute | solution.py:717
  46.9 1.8 %collective-permute-start.16 = (bf16[2,208,512]{2,1,0:T(8,128)(2,1)S(1)}, bf16[2,208,512]{2,1,0:T(8,128)(2,1)S(1)}, u32[]{:S(2)}, u32[]{:S(2)}) collective-permute-start(bf16[2,208,512]{2,1,0:T(8,128)(2,1)S(1)} %get-tuple-element.105), channel_id=1, source_target_pairs={{0,1},{1,0},{2,3},{3,2},{4,5},{5,4},{6,7},{7,6},{8,9},{9,8},{10,11... | collective-permute-start | bytes 1277960 | tf_op jit(solution)/shard_map/ppermute | solution.py:662
  46.9 7.3 %collective-permute-start.20 = (bf16[176,512]{1,0:T(8,128)(2,1)S(1)}, bf16[176,512]{1,0:T(8,128)(2,1)S(1)}, u32[]{:S(2)}, u32[]{:S(2)}) collective-permute-start(bf16[176,512]{1,0:T(8,128)(2,1)S(1)} %get-tuple-element.98), channel_id=1, source_target_pairs={{0,2},{2,0},{4,6},{6,4},{8,10},{10,8},{12,14},{14,12},{16,18},{18,... | collective-permute-start | bytes 540680 | tf_op jit(solution)/shard_map/ppermute | solution.py:717
  48.4 7.4 %collective-permute-start.21 = (bf16[176,512]{1,0:T(8,128)(2,1)S(1)}, bf16[176,512]{1,0:T(8,128)(2,1)S(1)}, u32[]{:S(2)}, u32[]{:S(2)}) collective-permute-start(bf16[176,512]{1,0:T(8,128)(2,1)S(1)} %get-tuple-element.99), channel_id=1, source_target_pairs={{0,4},{2,6},{4,0},{6,2},{8,12},{10,14},{12,8},{14,10},{16,20},{18,... | collective-permute-start | bytes 540680 | tf_op jit(solution)/shard_map/ppermute | solution.py:717
  48.8 7.5 %collective-permute-start.17 = (bf16[112,512]{1,0:T(8,128)(2,1)S(1)}, bf16[112,512]{1,0:T(8,128)(2,1)S(1)}, u32[]{:S(2)}, u32[]{:S(2)}) collective-permute-start(bf16[112,512]{1,0:T(8,128)(2,1)S(1)} %get-tuple-element.107), channel_id=1, source_target_pairs={{0,2},{2,0},{4,6},{6,4},{8,10},{10,8},{12,14},{14,12},{16,18},{18,... | collective-permute-start | bytes 344072 | tf_op jit(solution)/shard_map/ppermute | solution.py:717
  50.3 7.9 %collective-permute-start.18 = (bf16[112,512]{1,0:T(8,128)(2,1)S(1)}, bf16[112,512]{1,0:T(8,128)(2,1)S(1)}, u32[]{:S(2)}, u32[]{:S(2)}) collective-permute-start(bf16[112,512]{1,0:T(8,128)(2,1)S(1)} %get-tuple-element.108), channel_id=1, source_target_pairs={{0,4},{2,6},{4,0},{6,2},{8,12},{10,14},{12,8},{14,10},{16,20},{18,... | collective-permute-start | bytes 344072 | tf_op jit(solution)/shard_map/ppermute | solution.py:717
  51.2 8.8 %collective-permute-start.19 = (bf16[112,512]{1,0:T(8,128)(2,1)S(1)}, bf16[112,512]{1,0:T(8,128)(2,1)S(1)}, u32[]{:S(2)}, u32[]{:S(2)}) collective-permute-start(bf16[112,512]{1,0:T(8,128)(2,1)S(1)} %get-tuple-element.109), channel_id=1, source_target_pairs={{0,6},{2,4},{4,2},{6,0},{8,14},{10,12},{12,10},{14,8},{16,22},{18,... | collective-permute-start | bytes 344072 | tf_op jit(solution)/shard_map/ppermute | solution.py:717
  60.1 4.6 %collective-permute-start.22 = (bf16[72,512]{1,0:T(8,128)(2,1)S(1)}, bf16[72,512]{1,0:T(8,128)(2,1)S(1)}, u32[]{:S(2)}, u32[]{:S(2)}) collective-permute-start(bf16[72,512]{1,0:T(8,128)(2,1)S(1)} %get-tuple-element.117), channel_id=1, source_target_pairs={{0,8},{4,12},{8,0},{12,4},{16,24},{20,28},{24,16},{28,20},{1,9},{5... | collective-permute-start | bytes 221192 | tf_op jit(solution)/shard_map/ppermute | solution.py:662
  60.4 8.4 %collective-permute-start.23 = (bf16[72,512]{1,0:T(8,128)(2,1)S(1)}, bf16[72,512]{1,0:T(8,128)(2,1)S(1)}, u32[]{:S(2)}, u32[]{:S(2)}) collective-permute-start(bf16[72,512]{1,0:T(8,128)(2,1)S(1)} %get-tuple-element.118), channel_id=1, source_target_pairs={{0,16},{4,20},{8,24},{12,28},{16,0},{20,4},{24,8},{28,12},{1,17},{... | collective-permute-start | bytes 221192 | tf_op jit(solution)/shard_map/ppermute | solution.py:662
  62.5 6.2 %collective-permute-start.24 = (bf16[72,512]{1,0:T(8,128)(2,1)S(1)}, bf16[72,512]{1,0:T(8,128)(2,1)S(1)}, u32[]{:S(2)}, u32[]{:S(2)}) collective-permute-start(bf16[72,512]{1,0:T(8,128)(2,1)S(1)} %get-tuple-element.119), channel_id=1, source_target_pairs={{0,24},{4,28},{8,16},{12,20},{16,8},{20,12},{24,0},{28,4},{1,25},{... | collective-permute-start | bytes 221192 | tf_op jit(solution)/shard_map/ppermute | solution.py:662
  68.8 6.2 %collective-permute-start.30 = (bf16[64,512]{1,0:T(8,128)(2,1)S(1)}, bf16[64,512]{1,0:T(8,128)(2,1)S(1)}, u32[]{:S(2)}, u32[]{:S(2)}) collective-permute-start(bf16[64,512]{1,0:T(8,128)(2,1)S(1)} %get-tuple-element.126.refs_0_), channel_id=1, source_target_pairs={{0,24},{4,28},{8,16},{12,20},{16,8},{20,12},{24,0},{28,4},{1,25},{... | collective-permute-start | bytes 196616 | tf_op jit(solution)/shard_map/ppermute | solution.py:662
  70.9 5.9 %collective-permute-start.28 = (bf16[64,512]{1,0:T(8,128)(2,1)S(1)}, bf16[64,512]{1,0:T(8,128)(2,1)S(1)}, u32[]{:S(2)}, u32[]{:S(2)}) collective-permute-start(bf16[64,512]{1,0:T(8,128)(2,1)S(1)} %get-tuple-element.126.refs_0_), channel_id=1, source_target_pairs={{0,16},{4,20},{8,24},{12,28},{16,0},{20,4},{24,8},{28,12},{1,17},{... | collective-permute-start | bytes 196616 | tf_op jit(solution)/shard_map/ppermute | solution.py:662
  72.4 5.7 %collective-permute-start.26 = (bf16[64,512]{1,0:T(8,128)(2,1)S(1)}, bf16[64,512]{1,0:T(8,128)(2,1)S(1)}, u32[]{:S(2)}, u32[]{:S(2)}) collective-permute-start(bf16[64,512]{1,0:T(8,128)(2,1)S(1)} %get-tuple-element.126.refs_0_), channel_id=1, source_target_pairs={{0,8},{4,12},{8,0},{12,4},{16,24},{20,28},{24,16},{28,20},{1,9},{5... | collective-permute-start | bytes 196616 | tf_op jit(solution)/shard_map/ppermute | solution.py:662
  73.3 7.1 %collective-permute-start.25 = (bf16[64,512]{1,0:T(8,128)(2,1)S(1)}, bf16[64,512]{1,0:T(8,128)(2,1)S(1)}, u32[]{:S(2)}, u32[]{:S(2)}) collective-permute-start(bf16[64,512]{1,0:T(8,128)(2,1)S(1)} %get-tuple-element.126.refs_0_), channel_id=1, source_target_pairs={{0,4},{4,0},{8,12},{12,8},{16,20},{20,16},{24,28},{28,24},{1,5},{5... | collective-permute-start | bytes 196616 | tf_op jit(solution)/shard_map/ppermute | solution.py:662
  75.1 5.3 %collective-permute-start.31 = (bf16[64,512]{1,0:T(8,128)(2,1)S(1)}, bf16[64,512]{1,0:T(8,128)(2,1)S(1)}, u32[]{:S(2)}, u32[]{:S(2)}) collective-permute-start(bf16[64,512]{1,0:T(8,128)(2,1)S(1)} %collective-permute-done.30.refs_6_), channel_id=1, source_target_pairs={{0,4},{4,0},{8,12},{12,8},{16,20},{20,16},{24,28},{28,24},{1,5},{5... | collective-permute-start | bytes 196616 | tf_op jit(solution)/shard_map/ppermute | solution.py:662
  76.8 4.3 %collective-permute-start.29 = (bf16[64,512]{1,0:T(8,128)(2,1)S(1)}, bf16[64,512]{1,0:T(8,128)(2,1)S(1)}, u32[]{:S(2)}, u32[]{:S(2)}) collective-permute-start(bf16[64,512]{1,0:T(8,128)(2,1)S(1)} %collective-permute-done.28.refs_4_), channel_id=1, source_target_pairs={{0,4},{4,0},{8,12},{12,8},{16,20},{20,16},{24,28},{28,24},{1,5},{5... | collective-permute-start | bytes 196616 | tf_op jit(solution)/shard_map/ppermute | solution.py:662
  78.1 4.3 %collective-permute-start.27 = (bf16[64,512]{1,0:T(8,128)(2,1)S(1)}, bf16[64,512]{1,0:T(8,128)(2,1)S(1)}, u32[]{:S(2)}, u32[]{:S(2)}) collective-permute-start(bf16[64,512]{1,0:T(8,128)(2,1)S(1)} %collective-permute-done.26.refs_2_), channel_id=1, source_target_pairs={{0,4},{4,0},{8,12},{12,8},{16,20},{20,16},{24,28},{28,24},{1,5},{5... | collective-permute-start | bytes 196616 | tf_op jit(solution)/shard_map/ppermute | solution.py:662

commit v6 on v5

--- a/solution.py
+++ b/solution.py
@@ -607,7 +607,7 @@
 
 
 def unpack_body(tail_ref, *refs, tokens):
-    pieces, (gb_ref, gc_ref, gg_ref, b_scr, c_scr) = refs[:-5], refs[-5:]
+    pieces, (gb_hbm, gc_hbm, gg_hbm, b_scr, c_scr, sems) = refs[:-6], refs[-6:]
     scale = scale_of(tail_ref[...], tokens)
     S = len(pieces)
     b_rows, c_rows = b_scr.shape[0] // S, c_scr.shape[0] // S
@@ -618,14 +618,16 @@
         c_at = s % 2 * (c_scr.shape[0] // 2) + s // 2 * c_rows
         b_scr[pl.ds(pl.multiple_of(b_at, 8), b_rows), :] = v[:b_rows, :]
         c_scr[pl.ds(pl.multiple_of(c_at, 8), c_rows), :] = v[b_rows:, :]
-    shard, cols = gb_ref.shape
+    shard, cols = gb_hbm.shape
     width = b_scr.shape[1]
-    half = shard // 2
-    gb_ref[:, :width] = b_scr[:shard, :]
-    gb_ref[:half, width:] = b_scr[shard:, : cols - width]
-    gb_ref[half:, width:] = b_scr[shard:, cols - width :]
-    gc_ref[...] = c_scr[: gc_ref.shape[0], :]
-    gg_ref[...] = c_scr[gc_ref.shape[0] :, :]
+    half, c_shard = shard // 2, gc_hbm.shape[0]
+    fetch([
+        (c_scr.at[:c_shard, :], gc_hbm),
+        (c_scr.at[c_shard:, :], gg_hbm),
+        (b_scr.at[:shard, :], gb_hbm.at[:, :width]),
+        (b_scr.at[shard:, : cols - width], gb_hbm.at[:half, width:]),
+        (b_scr.at[shard:, cols - width :], gb_hbm.at[half:, width:]),
+    ], sems)
 
 
 def whole(n, far=()):
@@ -755,7 +757,7 @@
         for k in range(1, deal):
             pieces[2 * k] = swap(piece, "seq", 2 * k, S)
         for k in range(deal):
-            pieces[2 * k + 1] = swap(pieces[2 * k], "seq", 1, S)
+            pieces[2 * k + 1] = swap(pieces[2 * k] if k else after(piece, pieces[2]), "seq", 1, S)
         pieces = [pieces[k] for k in range(S)]
     else:
         piece, tail, pieces = sum_by_all_to_all(part_b, c_sum, S, s_at)
@@ -768,7 +770,7 @@
         functools.partial(unpack_body, tokens=tokens),
         [((shard, 2 * states), F32), ((c_shard, width), F32), ((g_shard, width), F32)],
         [((b_bulk, width), F32), ((c_bulk, width), F32)],
-        tail, *pieces, limit=8,
+        tail, *pieces, limit=8, far_outs=range(3), copies=5,
     )
     gain, bias, skip, gate, real, imag, step = (v[0] for v in lines)
     return (

time: 83.7 us -> 83.4 us (level)
  starting transfers between devices: 37.3 us -> 35.4 us
  waiting for transfers between devices: 23.3 us -> 24.7 us
    ppermute x22, starting transfers between devices: 25.6 us -> 23.8 us  [swap(): return lax.ppermute(v, axis, [(i, i ^ bit) for i in range(n)])]
    ppermute x22, waiting for transfers between devices: 10.1 us -> 11.6 us  [swap(): return lax.ppermute(v, axis, [(i, i ^ bit) for i in range(n)])]
  transfers between devices with their start and end apart: 32 -> 32, of which waited for: 18 -> 20; matrix products, arithmetic and copies ran while one was open for 0% -> 0% of each run, Pallas kernels for 12% -> 12%
where the time goes in v6:
time: 83.4 us; the launch traced here: 83.3 us
  starting transfers between devices  35.4 us (42%)
  waiting for transfers between devices  24.7 us (30%)
  Pallas kernels  22.1 us (26%)
  between operations  1.04 us (1%)
    ppermute x22, starting transfers between devices, swap(): return lax.ppermute(v, axis, [(i, i ^ bit) for i in range(n)])  23.8 us
    pallas_call x13, Pallas kernels, call(): pl.pallas_call(body, out_shape=[jax.ShapeDtypeStruct(*o) for o in outs],...  22.1 us
    ppermute x22, waiting for transfers between devices, swap(): return lax.ppermute(v, axis, [(i, i ^ bit) for i in range(n)])  11.6 us
    ppermute x6, waiting for transfers between devices, cross(): lax.ppermute(v, ('seq', 'wy'), [(2 * a + b, 2 * (a ^ flip_x) + (b ^ flip_...  7.78 us
    ppermute x6, starting transfers between devices, cross(): lax.ppermute(v, ('seq', 'wy'), [(2 * a + b, 2 * (a ^ flip_x) + (b ^ flip_...  6.31 us
    ppermute x2, waiting for transfers between devices, per_device(): lax.ppermute(fwd, 'seq', [(i, (i + k) % S) for i in range(S)])  4.84 us
    ppermute x2, starting transfers between devices, per_device(): lax.ppermute(fwd, 'seq', [(i, (i + k) % S) for i in range(S)])  3.03 us
    ppermute x2, starting transfers between devices, per_device(): lax.ppermute(bwd, 'seq', [((i + k) % S, i) for i in range(S)])  2.35 us
  transfers between devices with their start and end apart: 32, of which 20 were waited for; matrix products, arithmetic and copies ran while one was open for 0% of the time, Pallas kernels for 12%

profile of v6, /device:TPU:0, one launch (start us, length us, event | category | flops | bytes accessed | tf_op | source)
XLA Modules:
  0.0 83.3 jit_solution(13175492686154261443)
XLA Ops:
  0.7 1.8 %shard_map.237 = (bf16[144,768]{1,0:T(8,128)(2,1)}, f32[8,384]{1,0:T(8,128)}) custom-call(bf16[128,768]{1,0:T(8,128)(2,1)} %b_ref.1, bf16[1,128]{1,0:T(2,128)(2,1)} %bitcast.23, bf16[1,128]{1,0:T(2,128)(2,1)} %bitcast.24, bf16[1,128]{1,0:T(2,128)(2,1)} %bitcast.25, bf16[1,128]{1,0:T(2,128)(2,1)} %bitcast.26, f32[1,48]{1,0:T(1,128)} %bitcast.27, ...), custom_call_target="tpu_custom_call" | custom-call | flops 1000000000 | bytes 1048576 | tf_op jit(solution)/shard_map/pallas_call | solution.py:638
  2.6 3.0 %collective-permute-start.1 = (bf16[144,768]{1,0:T(8,128)(2,1)}, bf16[144,768]{1,0:T(8,128)(2,1)S(1)}, u32[]{:S(2)}, u32[]{:S(2)}) collective-permute-start(bf16[144,768]{1,0:T(8,128)(2,1)} %get-tuple-element.75.b0), channel_id=1, source_target_pairs={{0,2},{2,0},{1,3},{3,1},{4,6},{6,4},{5,7},{7,5},{8,10},{10,8},{9,1... | collective-permute-start | bytes 663560 | tf_op jit(solution)/shard_map/ppermute | solution.py:664
  5.6 2.5 %collective-permute-start.5 = (f32[8,384]{1,0:T(8,128)}, f32[8,384]{1,0:T(8,128)S(1)}, u32[]{:S(2)}, u32[]{:S(2)}) collective-permute-start(f32[8,384]{1,0:T(8,128)} %get-tuple-element.76), channel_id=1, source_target_pairs={{0,12},{4,8},{8,4},{12,0},{16,28},{20,24},{24,20},{28,16},{1,13},{... | collective-permute-start | bytes 36872 | tf_op jit(solution)/shard_map/ppermute | solution.py:664
  8.1 0.4 collective-permute-start.4
  8.5 0.5 collective-permute-start.3
  9.1 0.5 shard_map.239.refs_10_
  9.6 1.7 %collective-permute-done.1.b2 = bf16[144,768]{1,0:T(8,128)(2,1)S(1)} collective-permute-done((bf16[144,768]{1,0:T(8,128)(2,1)}, bf16[144,768]{1,0:T(8,128)(2,1)S(1)}, u32[]{:S(2)}, u32[]{:S(2)}) %collective-permute-start.1) | collective-permute-done | bytes 221216 | tf_op jit(solution)/shard_map/ppermute | solution.py:664
  11.2 1.7 %collective-permute-start.8 = (bf16[320,512]{1,0:T(8,128)(2,1)S(1)}, bf16[320,512]{1,0:T(8,128)(2,1)S(1)}, u32[]{:S(2)}, u32[]{:S(2)}) collective-permute-start(bf16[320,512]{1,0:T(8,128)(2,1)S(1)} %shard_map.239.refs_10_), channel_id=1, source_target_pairs={{0,2},{2,0},{1,3},{3,1},{4,6},{6,4},{5,7},{7,5},{8,10},{10,8},{9,1... | collective-permute-start | bytes 983048 | tf_op jit(solution)/shard_map/ppermute | solution.py:664
  13.0 2.7 %collective-permute-start.6 = (f32[8,384]{1,0:T(8,128)S(1)}, f32[8,384]{1,0:T(8,128)S(1)}, u32[]{:S(2)}, u32[]{:S(2)}) collective-permute-start(f32[8,384]{1,0:T(8,128)S(1)} %add_add_fusion), channel_id=1, source_target_pairs={{0,16},{4,20},{8,24},{12,28},{16,0},{20,4},{24,8},{28,12},{1,17},{... | collective-permute-start | bytes 36872 | tf_op jit(solution)/shard_map/ppermute | solution.py:664
  15.7 0.2 collective-permute-start.7
  15.9 1.8 %collective-permute-done.6 = f32[8,384]{1,0:T(8,128)S(1)} collective-permute-done((f32[8,384]{1,0:T(8,128)S(1)}, f32[8,384]{1,0:T(8,128)S(1)}, u32[]{:S(2)}, u32[]{:S(2)}) %collective-permute-start.6) | collective-permute-done | bytes 12320 | tf_op jit(solution)/shard_map/ppermute | solution.py:664
  17.7 2.2 %shard_map.238 = (bf16[1024,512]{1,0:T(8,128)(2,1)S(1)}, bf16[1024,512]{1,0:T(8,128)(2,1)S(1)}, f32[6,1048,128]{2,1,0:T(8,128)S(1)}, f32[8,512]{1,0:T(8,128)S(1)...) custom-call(bf16[1024,512]{1,0:T(8,128)(2,1)S(1)} %bitcast.20, ...), custom_call_target="tpu_custom_call" | custom-call | flops 2000000000 | bytes 1048576 | tf_op jit(solution)/shard_map/pallas_call | solution.py:638
  20.1 1.5 %collective-permute-start.11 = (f32[2,896]{1,0:T(2,128)S(1)}, f32[2,896]{1,0:T(2,128)S(1)}, u32[]{:S(2)}, u32[]{:S(2)}) collective-permute-start(f32[2,896]{1,0:T(2,128)S(1)} %get-tuple-element.86), channel_id=1, source_target_pairs={{0,8},{4,12},{8,16},{12,20},{16,24},{20,28},{24,0},{28,4},{1,9},{5... | collective-permute-start | bytes 21512 | tf_op jit(solution)/shard_map/ppermute | solution.py:706
  21.7 1.5 %collective-permute-start.10 = (f32[2,896]{1,0:T(2,128)S(1)}, f32[2,896]{1,0:T(2,128)S(1)}, u32[]{:S(2)}, u32[]{:S(2)}) collective-permute-start(f32[2,896]{1,0:T(2,128)S(1)} %get-tuple-element.86), channel_id=1, source_target_pairs={{0,4},{4,8},{8,12},{12,16},{16,20},{20,24},{24,28},{28,0},{1,5},{5... | collective-permute-start | bytes 21512 | tf_op jit(solution)/shard_map/ppermute | solution.py:706
  23.2 2.4 %collective-permute-done.11.refs_15_ = f32[2,896]{1,0:T(2,128)S(1)} collective-permute-done((f32[2,896]{1,0:T(2,128)S(1)}, f32[2,896]{1,0:T(2,128)S(1)}, u32[]{:S(2)}, u32[]{:S(2)}) %collective-permute-start.11) | collective-permute-done | bytes 7200 | tf_op jit(solution)/shard_map/ppermute | solution.py:706
  25.6 2.4 %collective-permute-done.10.refs_14_ = f32[2,896]{1,0:T(2,128)S(1)} collective-permute-done((f32[2,896]{1,0:T(2,128)S(1)}, f32[2,896]{1,0:T(2,128)S(1)}, u32[]{:S(2)}, u32[]{:S(2)}) %collective-permute-start.10) | collective-permute-done | bytes 7200 | tf_op jit(solution)/shard_map/ppermute | solution.py:706
  28.0 8.9 %shard_map.240 = (bf16[1024,512]{1,0:T(8,128)(2,1)}, f32[6,1048,128]{2,1,0:T(8,128)S(1)}, f32[6,1048,128]{2,1,0:T(8,128)S(1)}, bf16[1024,512]{1,0:T(8,128)(2,1)S...) custom-call(bf16[1024,512]{1,0:T(8,128)(2,1)S(1)} %bitcast.21, ...), custom_call_target="tpu_custom_call" | custom-call | flops 10000000000 | bytes 1048576 | tf_op jit(solution)/shard_map/pallas_call | solution.py:638
  37.0 0.5 collective-permute-start.13
  37.6 1.8 %collective-permute-start.12 = (f32[2,896]{1,0:T(2,128)S(1)}, f32[2,896]{1,0:T(2,128)S(1)}, u32[]{:S(2)}, u32[]{:S(2)}) collective-permute-start(f32[2,896]{1,0:T(2,128)S(1)} %get-tuple-element.95), channel_id=1, source_target_pairs={{4,0},{8,4},{12,8},{16,12},{20,16},{24,20},{28,24},{0,28},{5,1},{9... | collective-permute-start | bytes 21512 | tf_op jit(solution)/shard_map/ppermute | solution.py:717
  39.6 1.1 %collective-permute-start.15 = (bf16[176,512]{1,0:T(8,128)(2,1)S(1)}, bf16[176,512]{1,0:T(8,128)(2,1)S(1)}, u32[]{:S(2)}, u32[]{:S(2)}) collective-permute-start(bf16[176,512]{1,0:T(8,128)(2,1)S(1)} %get-tuple-element.101), channel_id=1, source_target_pairs={{0,6},{2,4},{4,2},{6,0},{8,14},{10,12},{12,10},{14,8},{16,22},{18,... | collective-permute-start | bytes 540680 | tf_op jit(solution)/shard_map/ppermute | solution.py:719
  40.7 0.5 collective-permute-done.12.refs_12_
  41.2 4.0 %shard_map.242 = (bf16[1024,512]{1,0:T(8,128)(2,1)S(1)}, bf16[2,208,512]{2,1,0:T(8,128)(2,1)S(1)}, bf16[2,208,512]{2,1,0:T(8,128)(2,1)S(1)}) custom-call(bf16[1024,512]{1,0:T(8,128)(2,1)S(1)} %get-tuple-element.89.refs_0_, f32[1048,128]{1,0:T(8,128)S(1)} %get-tuple-element.77.refs_2_.refs_1_, f32[4,128]{1,0:T(4,128)S(1)} %get-tuple-element.79.refs_4_.refs_2_, ...), custom_call_target="tpu_custom_call" | custom-call | flops 8000000000 | bytes 1048576 | tf_op jit(solution)/shard_map/pallas_call | solution.py:638
  45.2 1.7 %collective-permute-done.15.c3 = bf16[176,512]{1,0:T(8,128)(2,1)S(1)} collective-permute-done((bf16[176,512]{1,0:T(8,128)(2,1)S(1)}, bf16[176,512]{1,0:T(8,128)(2,1)S(1)}, u32[]{:S(2)}, u32[]{:S(2)}) %collective-permute-start.15) | collective-permute-done | bytes 180256 | tf_op jit(solution)/shard_map/ppermute | solution.py:719
  46.9 1.5 %collective-permute-start.20 = (bf16[176,512]{1,0:T(8,128)(2,1)S(1)}, bf16[176,512]{1,0:T(8,128)(2,1)S(1)}, u32[]{:S(2)}, u32[]{:S(2)}) collective-permute-start(bf16[176,512]{1,0:T(8,128)(2,1)S(1)} %get-tuple-element.99), channel_id=1, source_target_pairs={{0,2},{2,0},{4,6},{6,4},{8,10},{10,8},{12,14},{14,12},{16,18},{18,... | collective-permute-start | bytes 540680 | tf_op jit(solution)/shard_map/ppermute | solution.py:719
  48.8 1.5 %collective-permute-start.17 = (bf16[112,512]{1,0:T(8,128)(2,1)S(1)}, bf16[112,512]{1,0:T(8,128)(2,1)S(1)}, u32[]{:S(2)}, u32[]{:S(2)}) collective-permute-start(bf16[112,512]{1,0:T(8,128)(2,1)S(1)} %get-tuple-element.108), channel_id=1, source_target_pairs={{0,2},{2,0},{4,6},{6,4},{8,10},{10,8},{12,14},{14,12},{16,18},{18,... | collective-permute-start | bytes 344072 | tf_op jit(solution)/shard_map/ppermute | solution.py:719
  50.3 0.8 collective-permute-start.18
  51.2 1.2 %collective-permute-start.19 = (bf16[112,512]{1,0:T(8,128)(2,1)S(1)}, bf16[112,512]{1,0:T(8,128)(2,1)S(1)}, u32[]{:S(2)}, u32[]{:S(2)}) collective-permute-start(bf16[112,512]{1,0:T(8,128)(2,1)S(1)} %get-tuple-element.110), channel_id=1, source_target_pairs={{0,6},{2,4},{4,2},{6,0},{8,14},{10,12},{12,10},{14,8},{16,22},{18,... | collective-permute-start | bytes 344072 | tf_op jit(solution)/shard_map/ppermute | solution.py:719
  52.4 1.4 %shard_map.244.ig_ref = bf16[1024,512]{1,0:T(8,128)(2,1)S(1)} custom-call(bf16[1024,512]{1,0:T(8,128)(2,1)S(1)} %bitcast.22, bf16[1024,512]{1,0:T(8,128)(2,1)S(1)} %get-tuple-element.111.gn_ref, bf16[1024,512]{1,0:T(8,128)(2,1)S(1)} %get-tuple-element.112.gres_ref, f32[8,512]{1,0:T(8,128)S(1)} %get-tuple-element.84.refs_9_.refs_10_.vec_ref), custom_call_target="tpu_custom_call" | custom-call | flops 3000000000 | bytes 1048576 | tf_op jit(solution)/shard_map/pallas_call | solution.py:638
  53.8 0.5 collective-permute-done.20.c1
  54.3 1.5 %collective-permute-done.21.c2 = bf16[176,512]{1,0:T(8,128)(2,1)S(1)} collective-permute-done((bf16[176,512]{1,0:T(8,128)(2,1)S(1)}, bf16[176,512]{1,0:T(8,128)(2,1)S(1)}, u32[]{:S(2)}, u32[]{:S(2)}) %collective-permute-start.21) | collective-permute-done | bytes 180256 | tf_op jit(solution)/shard_map/ppermute | solution.py:719
  55.9 0.5 collective-permute-done.17.refs_1_
  56.3 1.9 %collective-permute-done.18.refs_2_ = bf16[112,512]{1,0:T(8,128)(2,1)S(1)} collective-permute-done((bf16[112,512]{1,0:T(8,128)(2,1)S(1)}, bf16[112,512]{1,0:T(8,128)(2,1)S(1)}, u32[]{:S(2)}, u32[]{:S(2)}) %collective-permute-start.18) | collective-permute-done | bytes 114720 | tf_op jit(solution)/shard_map/ppermute | solution.py:719
  58.2 1.8 %collective-permute-done.19.refs_3_ = bf16[112,512]{1,0:T(8,128)(2,1)S(1)} collective-permute-done((bf16[112,512]{1,0:T(8,128)(2,1)S(1)}, bf16[112,512]{1,0:T(8,128)(2,1)S(1)}, u32[]{:S(2)}, u32[]{:S(2)}) %collective-permute-start.19) | collective-permute-done | bytes 114720 | tf_op jit(solution)/shard_map/ppermute | solution.py:719
  60.1 0.3 collective-permute-start.22
  60.4 2.1 %collective-permute-start.23 = (bf16[72,512]{1,0:T(8,128)(2,1)S(1)}, bf16[72,512]{1,0:T(8,128)(2,1)S(1)}, u32[]{:S(2)}, u32[]{:S(2)}) collective-permute-start(bf16[72,512]{1,0:T(8,128)(2,1)S(1)} %get-tuple-element.119), channel_id=1, source_target_pairs={{0,16},{4,20},{8,24},{12,28},{16,0},{20,4},{24,8},{28,12},{1,17},{... | collective-permute-start | bytes 221192 | tf_op jit(solution)/shard_map/ppermute | solution.py:664
  62.5 2.0 %collective-permute-start.24 = (bf16[72,512]{1,0:T(8,128)(2,1)S(1)}, bf16[72,512]{1,0:T(8,128)(2,1)S(1)}, u32[]{:S(2)}, u32[]{:S(2)}) collective-permute-start(bf16[72,512]{1,0:T(8,128)(2,1)S(1)} %get-tuple-element.120), channel_id=1, source_target_pairs={{0,24},{4,28},{8,16},{12,20},{16,8},{20,12},{24,0},{28,4},{1,25},{... | collective-permute-start | bytes 221192 | tf_op jit(solution)/shard_map/ppermute | solution.py:664
  64.7 4.1 %collective-permute-done.23.refs_2_ = bf16[72,512]{1,0:T(8,128)(2,1)S(1)} collective-permute-done((bf16[72,512]{1,0:T(8,128)(2,1)S(1)}, bf16[72,512]{1,0:T(8,128)(2,1)S(1)}, u32[]{:S(2)}, u32[]{:S(2)}) %collective-permute-start.23) | collective-permute-done | bytes 73760 | tf_op jit(solution)/shard_map/ppermute | solution.py:664
  68.8 1.4 %collective-permute-start.25 = (bf16[64,512]{1,0:T(8,128)(2,1)S(1)}, bf16[64,512]{1,0:T(8,128)(2,1)S(1)}, u32[]{:S(2)}, u32[]{:S(2)}) collective-permute-start(bf16[64,512]{1,0:T(8,128)(2,1)S(1)} %get-tuple-element.128.refs_0_), channel_id=1, source_target_pairs={{0,8},{4,12},{8,0},{12,4},{16,24},{20,28},{24,16},{28,20},{1,9},{5... | collective-permute-start | bytes 196616 | tf_op jit(solution)/shard_map/ppermute | solution.py:664
  70.2 2.0 %collective-permute-start.30 = (bf16[64,512]{1,0:T(8,128)(2,1)S(1)}, bf16[64,512]{1,0:T(8,128)(2,1)S(1)}, u32[]{:S(2)}, u32[]{:S(2)}) collective-permute-start(bf16[64,512]{1,0:T(8,128)(2,1)S(1)} %get-tuple-element.128.refs_0_), channel_id=1, source_target_pairs={{0,24},{4,28},{8,16},{12,20},{16,8},{20,12},{24,0},{28,4},{1,25},{... | collective-permute-start | bytes 196616 | tf_op jit(solution)/shard_map/ppermute | solution.py:664
  72.4 1.1 %collective-permute-done.25.refs_2_ = bf16[64,512]{1,0:T(8,128)(2,1)S(1)} collective-permute-done((bf16[64,512]{1,0:T(8,128)(2,1)S(1)}, bf16[64,512]{1,0:T(8,128)(2,1)S(1)}, u32[]{:S(2)}, u32[]{:S(2)}) %collective-permute-start.25) | collective-permute-done | bytes 65568 | tf_op jit(solution)/shard_map/ppermute | solution.py:664
  73.5 1.4 %collective-permute-start.26 = (bf16[64,512]{1,0:T(8,128)(2,1)S(1)}, bf16[64,512]{1,0:T(8,128)(2,1)S(1)}, u32[]{:S(2)}, u32[]{:S(2)}) collective-permute-start(bf16[64,512]{1,0:T(8,128)(2,1)S(1)} %get-tuple-element.128.refs_0_), channel_id=1, source_target_pairs={{0,4},{4,0},{8,12},{12,8},{16,20},{20,16},{24,28},{28,24},{1,5},{5... | collective-permute-start | bytes 196616 | tf_op jit(solution)/shard_map/ppermute | solution.py:664
  74.9 0.6 collective-permute-start.27
  75.5 0.8 collective-permute-done.30.refs_6_
  76.3 1.3 %collective-permute-start.31 = (bf16[64,512]{1,0:T(8,128)(2,1)S(1)}, bf16[64,512]{1,0:T(8,128)(2,1)S(1)}, u32[]{:S(2)}, u32[]{:S(2)}) collective-permute-start(bf16[64,512]{1,0:T(8,128)(2,1)S(1)} %collective-permute-done.30.refs_6_), channel_id=1, source_target_pairs={{0,4},{4,0},{8,12},{12,8},{16,20},{20,16},{24,28},{28,24},{1,5},{5... | collective-permute-start | bytes 196616 | tf_op jit(solution)/shard_map/ppermute | solution.py:664
  77.7 1.3 %collective-permute-start.29 = (bf16[64,512]{1,0:T(8,128)(2,1)S(1)}, bf16[64,512]{1,0:T(8,128)(2,1)S(1)}, u32[]{:S(2)}, u32[]{:S(2)}) collective-permute-start(bf16[64,512]{1,0:T(8,128)(2,1)S(1)} %collective-permute-done.28.refs_4_), channel_id=1, source_target_pairs={{0,4},{4,0},{8,12},{12,8},{16,20},{20,16},{24,28},{28,24},{1,5},{5... | collective-permute-start | bytes 196616 | tf_op jit(solution)/shard_map/ppermute | solution.py:664
  79.0 1.5 %shard_map.248 = (f32[1024,512]{1,0:T(8,128)}, f32[1,1]{1,0:T(1,128)}, f32[1,128]{1,0:T(1,128)}, f32[1,128]{1,0:T(1,128)}, f32[1,128]{1,0:T(1,128)}, /*index=5*/...) custom-call(f32[8,512]{1,0:T(8,128)S(1)} %get-tuple-element.121.tail_ref, ...), custom_call_target="tpu_custom_call" | custom-call | flops 1000000000 | bytes 1048576 | tf_op jit(solution)/shard_map/pallas_call | solution.py:638
  80.6 1.4 %collective-permute-done.29.refs_5_ = bf16[64,512]{1,0:T(8,128)(2,1)S(1)} collective-permute-done((bf16[64,512]{1,0:T(8,128)(2,1)S(1)}, bf16[64,512]{1,0:T(8,128)(2,1)S(1)}, u32[]{:S(2)}, u32[]{:S(2)}) %collective-permute-start.29) | collective-permute-done | bytes 65568 | tf_op jit(solution)/shard_map/ppermute | solution.py:664
  82.0 1.1 %shard_map.249 = (f32[128,768]{1,0:T(8,128)}, f32[192,512]{1,0:T(8,128)}, f32[128,512]{1,0:T(8,128)}) custom-call(f32[8,512]{1,0:T(8,128)S(1)} %get-tuple-element.121.tail_ref, bf16[64,512]{1,0:T(8,128)(2,1)S(1)} %get-tuple-element.128.refs_0_, bf16[64,512]{1,0:T(8,128)(2,1)S(1)} %collective-permute-done.26.refs_1_, ...), custom_call_target="tpu_custom_call" | custom-call | flops 1000000000 | bytes 1048576 | tf_op jit(solution)/shard_map/pallas_call | solution.py:638
  (47 shorter events, 1.7 us)
Async XLA Ops:
  0.6 8.4 %copy-start.4 = (bf16[128,512]{1,0:T(8,128)(2,1)S(1)}, bf16[128,512]{1,0:T(8,128)(2,1)}, u32[]{:S(2)}) copy-start(bf16[128,512]{1,0:T(8,128)(2,1)} %g_ref.1) | copy-start | bytes 393220
  0.7 8.4 %copy-start.3 = (bf16[192,512]{1,0:T(8,128)(2,1)S(1)}, bf16[192,512]{1,0:T(8,128)(2,1)}, u32[]{:S(2)}) copy-start(bf16[192,512]{1,0:T(8,128)(2,1)} %c_ref.1) | copy-start | bytes 589828
  0.7 17.0 %copy-start.1 = (bf16[2,512,512]{2,1,0:T(8,128)(2,1)S(1)}, bf16[2,512,512]{2,1,0:T(8,128)(2,1)}, u32[]{:S(2)}) copy-start(bf16[2,512,512]{2,1,0:T(8,128)(2,1)} %param.14) | copy-start | bytes 3145732
  0.7 17.0 %copy-start.5 = (s32[2,512]{1,0:T(2,128)S(1)}, s32[2,512]{1,0:T(2,128)}, u32[]{:S(2)}) copy-start(s32[2,512]{1,0:T(2,128)} %seg_ref.1) | copy-start | bytes 12292
  0.7 17.0 %copy-start.6 = (s32[2,512]{1,0:T(2,128)S(1)}, s32[2,512]{1,0:T(2,128)}, u32[]{:S(2)}) copy-start(s32[2,512]{1,0:T(2,128)} %mask_ref.1) | copy-start | bytes 12292
  2.5 10.5 %copy-start.7 = (f32[8,384]{1,0:T(8,128)S(1)}, f32[8,384]{1,0:T(8,128)}, u32[]{:S(2)}) copy-start(f32[8,384]{1,0:T(8,128)} %get-tuple-element.76) | copy-start | bytes 36868
  2.5 15.2 %copy-start.2 = (bf16[144,768]{1,0:T(8,128)(2,1)S(1)}, bf16[144,768]{1,0:T(8,128)(2,1)}, u32[]{:S(2)}) copy-start(bf16[144,768]{1,0:T(8,128)(2,1)} %get-tuple-element.75.b0) | copy-start | bytes 663556
  2.6 8.7 %collective-permute-start.1 = (bf16[144,768]{1,0:T(8,128)(2,1)}, bf16[144,768]{1,0:T(8,128)(2,1)S(1)}, u32[]{:S(2)}, u32[]{:S(2)}) collective-permute-start(bf16[144,768]{1,0:T(8,128)(2,1)} %get-tuple-element.75.b0), channel_id=1, source_target_pairs={{0,2},{2,0},{1,3},{3,1},{4,6},{6,4},{5,7},{7,5},{8,10},{10,8},{9,1... | collective-permute-start | bytes 663560 | tf_op jit(solution)/shard_map/ppermute | solution.py:664
  5.6 7.4 %collective-permute-start.5 = (f32[8,384]{1,0:T(8,128)}, f32[8,384]{1,0:T(8,128)S(1)}, u32[]{:S(2)}, u32[]{:S(2)}) collective-permute-start(f32[8,384]{1,0:T(8,128)} %get-tuple-element.76), channel_id=1, source_target_pairs={{0,12},{4,8},{8,4},{12,0},{16,28},{20,24},{24,20},{28,16},{1,13},{... | collective-permute-start | bytes 36872 | tf_op jit(solution)/shard_map/ppermute | solution.py:664
  8.1 4.9 %collective-permute-start.4 = (f32[8,384]{1,0:T(8,128)}, f32[8,384]{1,0:T(8,128)S(1)}, u32[]{:S(2)}, u32[]{:S(2)}) collective-permute-start(f32[8,384]{1,0:T(8,128)} %get-tuple-element.76), channel_id=1, source_target_pairs={{0,8},{4,12},{8,0},{12,4},{16,24},{20,28},{24,16},{28,20},{1,9},{5... | collective-permute-start | bytes 36872 | tf_op jit(solution)/shard_map/ppermute | solution.py:664
  8.5 4.4 %collective-permute-start.3 = (f32[8,384]{1,0:T(8,128)}, f32[8,384]{1,0:T(8,128)S(1)}, u32[]{:S(2)}, u32[]{:S(2)}) collective-permute-start(f32[8,384]{1,0:T(8,128)} %get-tuple-element.76), channel_id=1, source_target_pairs={{0,4},{4,0},{8,12},{12,8},{16,20},{20,16},{24,28},{28,24},{1,5},{5... | collective-permute-start | bytes 36872 | tf_op jit(solution)/shard_map/ppermute | solution.py:664
  9.1 8.6 %collective-permute-start = (bf16[144,768]{1,0:T(8,128)(2,1)}, bf16[144,768]{1,0:T(8,128)(2,1)S(1)}, u32[]{:S(2)}, u32[]{:S(2)}) collective-permute-start(bf16[144,768]{1,0:T(8,128)(2,1)} %get-tuple-element.75.b0), channel_id=1, source_target_pairs={{0,1},{1,0},{2,3},{3,2},{4,5},{5,4},{6,7},{7,6},{8,9},{9,8},{10,11... | collective-permute-start | bytes 663560 | tf_op jit(solution)/shard_map/ppermute | solution.py:664
  11.2 8.9 %collective-permute-start.8 = (bf16[320,512]{1,0:T(8,128)(2,1)S(1)}, bf16[320,512]{1,0:T(8,128)(2,1)S(1)}, u32[]{:S(2)}, u32[]{:S(2)}) collective-permute-start(bf16[320,512]{1,0:T(8,128)(2,1)S(1)} %shard_map.239.refs_10_), channel_id=1, source_target_pairs={{0,2},{2,0},{1,3},{3,1},{4,6},{6,4},{5,7},{7,5},{8,10},{10,8},{9,1... | collective-permute-start | bytes 983048 | tf_op jit(solution)/shard_map/ppermute | solution.py:664
  13.0 4.7 %collective-permute-start.2 = (bf16[144,768]{1,0:T(8,128)(2,1)S(1)}, bf16[144,768]{1,0:T(8,128)(2,1)S(1)}, u32[]{:S(2)}, u32[]{:S(2)}) collective-permute-start(bf16[144,768]{1,0:T(8,128)(2,1)S(1)} %collective-permute-done.1.b2), channel_id=1, source_target_pairs={{0,1},{1,0},{2,3},{3,2},{4,5},{5,4},{6,7},{7,6},{8,9},{9,8},{10,11... | collective-permute-start | bytes 663560 | tf_op jit(solution)/shard_map/ppermute | solution.py:664
  13.0 4.7 %collective-permute-start.6 = (f32[8,384]{1,0:T(8,128)S(1)}, f32[8,384]{1,0:T(8,128)S(1)}, u32[]{:S(2)}, u32[]{:S(2)}) collective-permute-start(f32[8,384]{1,0:T(8,128)S(1)} %add_add_fusion), channel_id=1, source_target_pairs={{0,16},{4,20},{8,24},{12,28},{16,0},{20,4},{24,8},{28,12},{1,17},{... | collective-permute-start | bytes 36872 | tf_op jit(solution)/shard_map/ppermute | solution.py:664
  15.7 7.5 %collective-permute-start.7 = (bf16[320,512]{1,0:T(8,128)(2,1)S(1)}, bf16[320,512]{1,0:T(8,128)(2,1)S(1)}, u32[]{:S(2)}, u32[]{:S(2)}) collective-permute-start(bf16[320,512]{1,0:T(8,128)(2,1)S(1)} %shard_map.239.refs_10_), channel_id=1, source_target_pairs={{0,1},{1,0},{2,3},{3,2},{4,5},{5,4},{6,7},{7,6},{8,9},{9,8},{10,11... | collective-permute-start | bytes 983048 | tf_op jit(solution)/shard_map/ppermute | solution.py:664
  17.7 10.3 %copy-start = (bf16[2,512,512]{2,1,0:T(8,128)(2,1)S(1)}, bf16[2,512,512]{2,1,0:T(8,128)(2,1)}, u32[]{:S(2)}) copy-start(bf16[2,512,512]{2,1,0:T(8,128)(2,1)} %param.15) | copy-start | bytes 3145732
  20.1 7.9 %collective-permute-start.9 = (bf16[320,512]{1,0:T(8,128)(2,1)S(1)}, bf16[320,512]{1,0:T(8,128)(2,1)S(1)}, u32[]{:S(2)}, u32[]{:S(2)}) collective-permute-start(bf16[320,512]{1,0:T(8,128)(2,1)S(1)} %collective-permute-done.8.refs_12_), channel_id=1, source_target_pairs={{0,1},{1,0},{2,3},{3,2},{4,5},{5,4},{6,7},{7,6},{8,9},{9,8},{10,11... | collective-permute-start | bytes 983048 | tf_op jit(solution)/shard_map/ppermute | solution.py:664
  20.1 5.4 %collective-permute-start.11 = (f32[2,896]{1,0:T(2,128)S(1)}, f32[2,896]{1,0:T(2,128)S(1)}, u32[]{:S(2)}, u32[]{:S(2)}) collective-permute-start(f32[2,896]{1,0:T(2,128)S(1)} %get-tuple-element.86), channel_id=1, source_target_pairs={{0,8},{4,12},{8,16},{12,20},{16,24},{20,28},{24,0},{28,4},{1,9},{5... | collective-permute-start | bytes 21512 | tf_op jit(solution)/shard_map/ppermute | solution.py:706
  21.7 6.3 %collective-permute-start.10 = (f32[2,896]{1,0:T(2,128)S(1)}, f32[2,896]{1,0:T(2,128)S(1)}, u32[]{:S(2)}, u32[]{:S(2)}) collective-permute-start(f32[2,896]{1,0:T(2,128)S(1)} %get-tuple-element.86), channel_id=1, source_target_pairs={{0,4},{4,8},{8,12},{12,16},{16,20},{20,24},{24,28},{28,0},{1,5},{5... | collective-permute-start | bytes 21512 | tf_op jit(solution)/shard_map/ppermute | solution.py:706
  37.0 2.4 %collective-permute-start.14 = (bf16[2,336,512]{2,1,0:T(8,128)(2,1)S(1)}, bf16[2,336,512]{2,1,0:T(8,128)(2,1)S(1)}, u32[]{:S(2)}, u32[]{:S(2)}) collective-permute-start(bf16[2,336,512]{2,1,0:T(8,128)(2,1)S(1)} %get-tuple-element.97), channel_id=1, source_target_pairs={{0,1},{1,0},{2,3},{3,2},{4,5},{5,4},{6,7},{7,6},{8,9},{9,8},{10,11... | collective-permute-start | bytes 2064392 | tf_op jit(solution)/shard_map/ppermute | solution.py:664
  37.0 3.7 %collective-permute-start.13 = (f32[2,896]{1,0:T(2,128)S(1)}, f32[2,896]{1,0:T(2,128)S(1)}, u32[]{:S(2)}, u32[]{:S(2)}) collective-permute-start(f32[2,896]{1,0:T(2,128)S(1)} %get-tuple-element.95), channel_id=1, source_target_pairs={{8,0},{12,4},{16,8},{20,12},{24,16},{28,20},{0,24},{4,28},{9,1},{1... | collective-permute-start | bytes 21512 | tf_op jit(solution)/shard_map/ppermute | solution.py:717
  37.6 3.6 %collective-permute-start.12 = (f32[2,896]{1,0:T(2,128)S(1)}, f32[2,896]{1,0:T(2,128)S(1)}, u32[]{:S(2)}, u32[]{:S(2)}) collective-permute-start(f32[2,896]{1,0:T(2,128)S(1)} %get-tuple-element.95), channel_id=1, source_target_pairs={{4,0},{8,4},{12,8},{16,12},{20,16},{24,20},{28,24},{0,28},{5,1},{9... | collective-permute-start | bytes 21512 | tf_op jit(solution)/shard_map/ppermute | solution.py:717
  39.6 7.3 %collective-permute-start.15 = (bf16[176,512]{1,0:T(8,128)(2,1)S(1)}, bf16[176,512]{1,0:T(8,128)(2,1)S(1)}, u32[]{:S(2)}, u32[]{:S(2)}) collective-permute-start(bf16[176,512]{1,0:T(8,128)(2,1)S(1)} %get-tuple-element.101), channel_id=1, source_target_pairs={{0,6},{2,4},{4,2},{6,0},{8,14},{10,12},{12,10},{14,8},{16,22},{18,... | collective-permute-start | bytes 540680 | tf_op jit(solution)/shard_map/ppermute | solution.py:719
  46.9 1.8 %collective-permute-start.16 = (bf16[2,208,512]{2,1,0:T(8,128)(2,1)S(1)}, bf16[2,208,512]{2,1,0:T(8,128)(2,1)S(1)}, u32[]{:S(2)}, u32[]{:S(2)}) collective-permute-start(bf16[2,208,512]{2,1,0:T(8,128)(2,1)S(1)} %get-tuple-element.106), channel_id=1, source_target_pairs={{0,1},{1,0},{2,3},{3,2},{4,5},{5,4},{6,7},{7,6},{8,9},{9,8},{10,11... | collective-permute-start | bytes 1277960 | tf_op jit(solution)/shard_map/ppermute | solution.py:664
  46.9 7.3 %collective-permute-start.20 = (bf16[176,512]{1,0:T(8,128)(2,1)S(1)}, bf16[176,512]{1,0:T(8,128)(2,1)S(1)}, u32[]{:S(2)}, u32[]{:S(2)}) collective-permute-start(bf16[176,512]{1,0:T(8,128)(2,1)S(1)} %get-tuple-element.99), channel_id=1, source_target_pairs={{0,2},{2,0},{4,6},{6,4},{8,10},{10,8},{12,14},{14,12},{16,18},{18,... | collective-permute-start | bytes 540680 | tf_op jit(solution)/shard_map/ppermute | solution.py:719
  48.4 7.4 %collective-permute-start.21 = (bf16[176,512]{1,0:T(8,128)(2,1)S(1)}, bf16[176,512]{1,0:T(8,128)(2,1)S(1)}, u32[]{:S(2)}, u32[]{:S(2)}) collective-permute-start(bf16[176,512]{1,0:T(8,128)(2,1)S(1)} %get-tuple-element.100), channel_id=1, source_target_pairs={{0,4},{2,6},{4,0},{6,2},{8,12},{10,14},{12,8},{14,10},{16,20},{18,... | collective-permute-start | bytes 540680 | tf_op jit(solution)/shard_map/ppermute | solution.py:719
  48.8 7.5 %collective-permute-start.17 = (bf16[112,512]{1,0:T(8,128)(2,1)S(1)}, bf16[112,512]{1,0:T(8,128)(2,1)S(1)}, u32[]{:S(2)}, u32[]{:S(2)}) collective-permute-start(bf16[112,512]{1,0:T(8,128)(2,1)S(1)} %get-tuple-element.108), channel_id=1, source_target_pairs={{0,2},{2,0},{4,6},{6,4},{8,10},{10,8},{12,14},{14,12},{16,18},{18,... | collective-permute-start | bytes 344072 | tf_op jit(solution)/shard_map/ppermute | solution.py:719
  50.3 7.9 %collective-permute-start.18 = (bf16[112,512]{1,0:T(8,128)(2,1)S(1)}, bf16[112,512]{1,0:T(8,128)(2,1)S(1)}, u32[]{:S(2)}, u32[]{:S(2)}) collective-permute-start(bf16[112,512]{1,0:T(8,128)(2,1)S(1)} %get-tuple-element.109), channel_id=1, source_target_pairs={{0,4},{2,6},{4,0},{6,2},{8,12},{10,14},{12,8},{14,10},{16,20},{18,... | collective-permute-start | bytes 344072 | tf_op jit(solution)/shard_map/ppermute | solution.py:719
  51.2 8.8 %collective-permute-start.19 = (bf16[112,512]{1,0:T(8,128)(2,1)S(1)}, bf16[112,512]{1,0:T(8,128)(2,1)S(1)}, u32[]{:S(2)}, u32[]{:S(2)}) collective-permute-start(bf16[112,512]{1,0:T(8,128)(2,1)S(1)} %get-tuple-element.110), channel_id=1, source_target_pairs={{0,6},{2,4},{4,2},{6,0},{8,14},{10,12},{12,10},{14,8},{16,22},{18,... | collective-permute-start | bytes 344072 | tf_op jit(solution)/shard_map/ppermute | solution.py:719
  60.1 4.6 %collective-permute-start.22 = (bf16[72,512]{1,0:T(8,128)(2,1)S(1)}, bf16[72,512]{1,0:T(8,128)(2,1)S(1)}, u32[]{:S(2)}, u32[]{:S(2)}) collective-permute-start(bf16[72,512]{1,0:T(8,128)(2,1)S(1)} %get-tuple-element.118), channel_id=1, source_target_pairs={{0,8},{4,12},{8,0},{12,4},{16,24},{20,28},{24,16},{28,20},{1,9},{5... | collective-permute-start | bytes 221192 | tf_op jit(solution)/shard_map/ppermute | solution.py:664
  60.4 8.4 %collective-permute-start.23 = (bf16[72,512]{1,0:T(8,128)(2,1)S(1)}, bf16[72,512]{1,0:T(8,128)(2,1)S(1)}, u32[]{:S(2)}, u32[]{:S(2)}) collective-permute-start(bf16[72,512]{1,0:T(8,128)(2,1)S(1)} %get-tuple-element.119), channel_id=1, source_target_pairs={{0,16},{4,20},{8,24},{12,28},{16,0},{20,4},{24,8},{28,12},{1,17},{... | collective-permute-start | bytes 221192 | tf_op jit(solution)/shard_map/ppermute | solution.py:664
  62.5 6.2 %collective-permute-start.24 = (bf16[72,512]{1,0:T(8,128)(2,1)S(1)}, bf16[72,512]{1,0:T(8,128)(2,1)S(1)}, u32[]{:S(2)}, u32[]{:S(2)}) collective-permute-start(bf16[72,512]{1,0:T(8,128)(2,1)S(1)} %get-tuple-element.120), channel_id=1, source_target_pairs={{0,24},{4,28},{8,16},{12,20},{16,8},{20,12},{24,0},{28,4},{1,25},{... | collective-permute-start | bytes 221192 | tf_op jit(solution)/shard_map/ppermute | solution.py:664
  68.8 4.7 %collective-permute-start.25 = (bf16[64,512]{1,0:T(8,128)(2,1)S(1)}, bf16[64,512]{1,0:T(8,128)(2,1)S(1)}, u32[]{:S(2)}, u32[]{:S(2)}) collective-permute-start(bf16[64,512]{1,0:T(8,128)(2,1)S(1)} %get-tuple-element.128.refs_0_), channel_id=1, source_target_pairs={{0,8},{4,12},{8,0},{12,4},{16,24},{20,28},{24,16},{28,20},{1,9},{5... | collective-permute-start | bytes 196616 | tf_op jit(solution)/shard_map/ppermute | solution.py:664
  70.2 6.1 %collective-permute-start.30 = (bf16[64,512]{1,0:T(8,128)(2,1)S(1)}, bf16[64,512]{1,0:T(8,128)(2,1)S(1)}, u32[]{:S(2)}, u32[]{:S(2)}) collective-permute-start(bf16[64,512]{1,0:T(8,128)(2,1)S(1)} %get-tuple-element.128.refs_0_), channel_id=1, source_target_pairs={{0,24},{4,28},{8,16},{12,20},{16,8},{20,12},{24,0},{28,4},{1,25},{... | collective-permute-start | bytes 196616 | tf_op jit(solution)/shard_map/ppermute | solution.py:664
  72.2 5.5 %collective-permute-start.28 = (bf16[64,512]{1,0:T(8,128)(2,1)S(1)}, bf16[64,512]{1,0:T(8,128)(2,1)S(1)}, u32[]{:S(2)}, u32[]{:S(2)}) collective-permute-start(bf16[64,512]{1,0:T(8,128)(2,1)S(1)} %get-tuple-element.128.refs_0_), channel_id=1, source_target_pairs={{0,16},{4,20},{8,24},{12,28},{16,0},{20,4},{24,8},{28,12},{1,17},{... | collective-permute-start | bytes 196616 | tf_op jit(solution)/shard_map/ppermute | solution.py:664
  73.5 8.5 %collective-permute-start.26 = (bf16[64,512]{1,0:T(8,128)(2,1)S(1)}, bf16[64,512]{1,0:T(8,128)(2,1)S(1)}, u32[]{:S(2)}, u32[]{:S(2)}) collective-permute-start(bf16[64,512]{1,0:T(8,128)(2,1)S(1)} %get-tuple-element.128.refs_0_), channel_id=1, source_target_pairs={{0,4},{4,0},{8,12},{12,8},{16,20},{20,16},{24,28},{28,24},{1,5},{5... | collective-permute-start | bytes 196616 | tf_op jit(solution)/shard_map/ppermute | solution.py:664
  74.9 7.1 %collective-permute-start.27 = (bf16[64,512]{1,0:T(8,128)(2,1)S(1)}, bf16[64,512]{1,0:T(8,128)(2,1)S(1)}, u32[]{:S(2)}, u32[]{:S(2)}) collective-permute-start(bf16[64,512]{1,0:T(8,128)(2,1)S(1)} %collective-permute-done.25.refs_2_), channel_id=1, source_target_pairs={{0,4},{4,0},{8,12},{12,8},{16,20},{20,16},{24,28},{28,24},{1,5},{5... | collective-permute-start | bytes 196616 | tf_op jit(solution)/shard_map/ppermute | solution.py:664
  76.3 4.3 %collective-permute-start.31 = (bf16[64,512]{1,0:T(8,128)(2,1)S(1)}, bf16[64,512]{1,0:T(8,128)(2,1)S(1)}, u32[]{:S(2)}, u32[]{:S(2)}) collective-permute-start(bf16[64,512]{1,0:T(8,128)(2,1)S(1)} %collective-permute-done.30.refs_6_), channel_id=1, source_target_pairs={{0,4},{4,0},{8,12},{12,8},{16,20},{20,16},{24,28},{28,24},{1,5},{5... | collective-permute-start | bytes 196616 | tf_op jit(solution)/shard_map/ppermute | solution.py:664
  77.7 4.3 %collective-permute-start.29 = (bf16[64,512]{1,0:T(8,128)(2,1)S(1)}, bf16[64,512]{1,0:T(8,128)(2,1)S(1)}, u32[]{:S(2)}, u32[]{:S(2)}) collective-permute-start(bf16[64,512]{1,0:T(8,128)(2,1)S(1)} %collective-permute-done.28.refs_4_), channel_id=1, source_target_pairs={{0,4},{4,0},{8,12},{12,8},{16,20},{20,16},{24,28},{28,24},{1,5},{5... | collective-permute-start | bytes 196616 | tf_op jit(solution)/shard_map/ppermute | solution.py:664

commit v7 on v6

--- a/solution.py
+++ b/solution.py
@@ -286,8 +286,8 @@
     (x_ref, t_ref, link_ref, valid_ref, ids_ref, low_ref, proj_ref, s1_ref, rates_ref, vec_ref,
      c0, c1, c2, c3) = refs[:14]
     recvs = refs[14 : 14 + hops]
-    (out_hbm, state_ref, gs_ref, gres_ref, gssm_ref, s2_ref, msg_ref, send_ref, keep_ref,
-     wc_scr, wg_scr, gc_scr, gg_scr, sum_scr, out_ref, sems) = refs[14 + hops :]
+    (out_hbm, state_ref, gs_ref, gres_ref, gssm_ref, s2_ref, msg_ref, send_ref, keep_ref, sums_ref,
+     wc_scr, wg_scr, gc_scr, gg_scr, out_ref, sems) = refs[14 + hops :]
     rows, width = x_ref.shape
     states = rates_ref.shape[1]
     groups = states // LANES
@@ -379,10 +379,11 @@
         put(gs_ref, pad_at, 0, nt_dot(ssl, wc_scr[...]).astype(BF16).astype(F32))
         add_to(gc_scr, i, tn_dot(sl, ssl))
     clear_pads(gs_ref, seqs, pitch)
-    sum_scr[0:1, :] = one_row(skip_acc)
-    sum_scr[1:2, :] = one_row(gbias_acc)
-    loss = jnp.sum(one_row(loss_acc), axis=1, keepdims=True)
-    count = one_row(fold_rows(valid_ref[...]))
+    sums_ref[0:1, :] = one_row(skip_acc)
+    sums_ref[1:2, :] = one_row(gbias_acc)
+    sums_ref[2:3, :] = jnp.broadcast_to(jnp.sum(one_row(loss_acc), axis=1, keepdims=True), (1, width))
+    sums_ref[3:4, :] = wide(one_row(fold_rows(valid_ref[...])), width // LANES)
+    sums_ref[4:8, :] = jnp.zeros((4, width), F32)
 
     def back(i, carry):
         j = steps - 1 - i
@@ -417,10 +418,6 @@
         dst[slot, :c_shard, :] = gc_scr[pl.ds(pl.multiple_of(q * c_shard, c_shard), c_shard), :].astype(BF16)
         lanes = pl.multiple_of(q * g_shard, g_shard)
         dst[slot, c_shard : c_shard + g_shard, :] = gg_scr[pl.ds(lanes, g_shard), :].astype(BF16)
-        line = jnp.concatenate(
-            [sum_scr[v : v + 1, pl.ds(lanes, g_shard)] for v in range(2)]
-            + [jnp.broadcast_to(loss, (1, LANES)), count], axis=1)
-        dst[slot, c_shard + g_shard :, :] = split_rows([jnp.zeros((3, width), F32), line])
     for copy in leaving:
         copy.wait()
 
@@ -439,10 +436,10 @@
 
 
 def k3_body(*refs, seqs, hops, blocks):
-    (n_ref, link_ref, ids_ref, low_ref, proj_ref, state_ref, gs_ref, gssm_ref,
-     s2_ref, rates_ref, vec_ref, w_full) = refs[:12]
-    recvs = refs[12 : 12 + hops]
-    (gn_ref, send_ref, keep_ref, gp_scr, gpl_scr, gb_scr, vec_scr) = refs[12 + hops :]
+    (n_ref, sums_ref, link_ref, ids_ref, low_ref, proj_ref, state_ref, gs_ref, gssm_ref,
+     s2_ref, rates_ref, vec_ref, w_full) = refs[:13]
+    recvs = refs[13 : 13 + hops]
+    (gn_ref, send_ref, keep_ref, gp_scr, gpl_scr, gb_scr, vec_scr) = refs[13 + hops :]
     rows, width = n_ref.shape
     states = rates_ref.shape[1]
     groups = states // LANES
@@ -517,7 +514,9 @@
         dst[slot, shard:extra, : width // 2] = gb_scr[pl.ds(q, half), width:].astype(BF16)
         dst[slot, shard:extra, width // 2 :] = gb_scr[pl.ds(q + half, half), width:].astype(BF16)
         mine = [vec_scr[v : v + 1, pl.ds(q, shard)] for v in range(2)] + [jnp.zeros((1, shard), F32)]
-        dst[slot, extra:, :] = split_rows([jnp.concatenate(p, axis=1) for p in zip(rate_grads, mine)])
+        others = [sums_ref[v : v + 1, pl.ds(q, shard)] for v in range(2)] + [sums_ref[v : v + 1, :shard] for v in (2, 3)]
+        lines = [jnp.concatenate(p, axis=1) for p in [*zip(rate_grads, mine), others]]
+        dst[slot, extra:, :] = split_rows(lines)
 
 
 def centre(values):
@@ -531,16 +530,17 @@
     sum_ref[...] = total((c0, c1, c2, c3), slice(0, sum_ref.shape[0]))
 
 
-def quarter_body(keep_ref, got_ref, *outs):
-    half = outs[0].shape[0] - 16
+def quarter_body(keep_ref, got_ref, *outs, extra):
+    half = outs[0].shape[0] - extra
     x, y = lax.axis_index("seq") % 2, lax.axis_index("wy")
     for out, slot, side in zip(outs, (y, 1 - y, y, 1 - y), (x, x, 1 - x, 1 - x)):
         def both(rows):
             return keep_ref[slot, rows, :].astype(F32) + got_ref[slot, rows, :].astype(F32)
 
         out[:half, :] = both(pl.ds(pl.multiple_of(side * half, half), half)).astype(BF16)
-        v = both(slice(2 * half, 2 * half + 16))
-        out[half:, :] = split_rows([v[:8] + v[8:]])
+        if extra:
+            v = both(slice(2 * half, 2 * half + 16))
+            out[half:, :] = split_rows([v[:8] + v[8:]])
 
 
 def total(refs, rows):
@@ -550,10 +550,10 @@
 def deal_body(*refs):
     n = len(refs) - 6
     bs, c_sum, outs, b_scr = refs[:4], refs[4], refs[5 : 5 + n], refs[5 + n]
-    b_half, c_half = b_scr.shape[0], c_sum.shape[0] - 16
+    b_half, c_half = b_scr.shape[0], c_sum.shape[0]
     b_part, c_part = b_half // n, c_half // n
     b_scr[...] = total(bs, slice(0, b_half))
-    tail = total(bs, slice(b_half, b_half + 16)) + c_sum[c_half:, :]
+    tail = total(bs, slice(b_half, b_half + 16))
     ends = split_rows([tail[:8] + tail[8:]]).astype(F32)
     for k, out in enumerate(outs):
         at = (lax.axis_index("seq") // 2) ^ k
@@ -705,13 +705,13 @@
     cs = (c_msg, swap(c_msg, "wc"), c_far, swap(after(c_far, fwd), "wc"))
     fwds = [lax.ppermute(fwd, "seq", [(i, (i + k) % S) for i in range(S)]) for k in range(1, hops + 1)]
     c_bulk = c_shard + g_shard
-    out, state, gs, gres, gssm, s2, bwd, send_c, keep_c = call(
+    out, state, gs, gres, gssm, s2, bwd, send_c, keep_c, sums = call(
         functools.partial(k2_body, seqs=seqs, hops=hops),
         [((rows, width), BF16), (slab, F32), (slab, F32),
          ((rows, width), BF16), ((rows, width), F32), ((R, 4 * states), F32), msg_shape,
-         ((2, c_bulk + 16, width), BF16), ((2, c_bulk + 16, width), BF16)],
+         ((2, c_bulk, width), BF16), ((2, c_bulk, width), BF16), ((8, width), F32)],
         [((2 * states, width), BF16), ((width, width), BF16), ((2 * states, width), F32), ((width, width), F32),
-         ((8, width), F32), ((rows, width), BF16)],
+         ((rows, width), BF16)],
         x, teach, link, valid, ids, low, proj, s1, rates, vec, *cs, *fwds, us=10, limit=20, far_outs=(0,), copies=rows // TILE,
     )
     bwds = [lax.ppermute(bwd, "seq", [((i + k) % S, i) for i in range(S)]) for k in range(1, hops + 1)]
@@ -719,14 +719,14 @@
         return lax.ppermute(
             v, ("seq", "wy"), [(2 * a + b, 2 * (a ^ flip_x) + (b ^ flip_y)) for a in range(S) for b in range(2)])
 
-    def quarters(keep, got):
-        shape = ((keep.shape[1] - 16) // 2 + 16, width)
-        return call(quarter_body, [(shape, BF16)] * 4, [], keep, got, limit=4)
+    def quarters(keep, got, extra):
+        shape = ((keep.shape[1] - extra) // 2 + extra, width)
+        return call(functools.partial(quarter_body, extra=extra), [(shape, BF16)] * 4, [], keep, got, limit=4)
 
     def exchange(q):
         return (q[0], cross(q[1], 0, 1), cross(q[2], 1, 0), cross(q[3], 1, 1))
 
-    q_c = quarters(keep_c, swap(send_c, "wc"))
+    q_c = quarters(keep_c, swap(send_c, "wc"), 0)
     bwds = lax.optimization_barrier((bwds, q_c))[0]
     part_c = exchange(q_c)
     b_bulk = 3 * shard // 2
@@ -735,11 +735,11 @@
         functools.partial(k3_body, seqs=seqs, hops=hops, blocks=S),
         [((rows, width), BF16), ((2, b_bulk + 16, width), BF16), ((2, b_bulk + 16, width), BF16)],
         [(slab, F32), ((rows, 2 * states), BF16), ((width, 2 * states), F32), ((8, width), F32)],
-        norm, link, ids, low, proj, state, gs, gssm, s2, rates, vec, w_full, *bwds, us=8, limit=14,
-    )
-    (c_sum,) = call(sum_body, [((c_bulk // 2 + 16, width), F32)], [], *part_c, limit=4)
+        norm, sums, link, ids, low, proj, state, gs, gssm, s2, rates, vec, w_full, *bwds, us=8, limit=14,
+    )
+    (c_sum,) = call(sum_body, [((c_bulk // 2, width), F32)], [], *part_c, limit=4)
     got_b = swap(after(send_b, part_c[3]), "wc")
-    part_b = exchange(quarters(keep_b, got_b))
+    part_b = exchange(quarters(keep_b, got_b, 16))
     (ig,) = call(norm_body, [((rows, width), BF16)], [], x, gn, gres, vec, us=3, limit=8)
     part_b, ig = lax.optimization_barrier((part_b, ig))
     tokens = float(length * seqs * lax.axis_size(("wy", "wc")))
@@ -782,10 +782,10 @@
 def sum_by_all_to_all(part_b, v_c, S, s_at):
     v_b = sum([p.astype(F32) for p in part_b[1:]], part_b[0].astype(F32))
     width = v_b.shape[1]
-    tail = v_b[-16:-8] + v_b[-8:] + v_c[-16:-8] + v_c[-8:]
+    tail = v_b[-16:-8] + v_b[-8:]
     high = lax.reduce_precision(tail, 8, 7)
     ends = jnp.concatenate([high, tail - high], 0).astype(BF16)
-    both = jnp.concatenate([v[:-16].astype(BF16).reshape(S // 2, -1, width) for v in (v_b, v_c)], 1)
+    both = jnp.concatenate([v.astype(BF16).reshape(S // 2, -1, width) for v in (v_b[:-16], v_c)], 1)
     bulk = both.shape[1]
     both = jnp.concatenate([both, jnp.broadcast_to(ends[None], (S // 2, 16, width))], 1)
     empty = jnp.zeros_like(both)

time: 83.4 us -> 82.7 us (level)
    ppermute x6, waiting for transfers between devices: 7.78 us -> 6.92 us  [cross(): lax.ppermute(v, ('seq', 'wy'), [(2 * a + b, 2 * (a ^ flip_x) + (b ^ flip_...]
  transfers between devices with their start and end apart: 32 -> 32, of which waited for: 20 -> 18; matrix products, arithmetic and copies ran while one was open for 0% -> 0% of each run, Pallas kernels for 12% -> 12%
where the time goes in v7:
time: 82.7 us; the launch traced here: 82.6 us
  starting transfers between devices  35.4 us (43%)
  waiting for transfers between devices  24.1 us (29%)
  Pallas kernels  22 us (27%)
  between operations  1.04 us (1%)
    ppermute x22, starting transfers between devices, swap(): return lax.ppermute(v, axis, [(i, i ^ bit) for i in range(n)])  23.5 us
    pallas_call x13, Pallas kernels, call(): pl.pallas_call(body, out_shape=[jax.ShapeDtypeStruct(*o) for o in outs],...  22 us
    ppermute x22, waiting for transfers between devices, swap(): return lax.ppermute(v, axis, [(i, i ^ bit) for i in range(n)])  11.8 us
    ppermute x6, waiting for transfers between devices, cross(): lax.ppermute(v, ('seq', 'wy'), [(2 * a + b, 2 * (a ^ flip_x) + (b ^ flip_...  6.92 us
    ppermute x6, starting transfers between devices, cross(): lax.ppermute(v, ('seq', 'wy'), [(2 * a + b, 2 * (a ^ flip_x) + (b ^ flip_...  6.57 us
    ppermute x2, waiting for transfers between devices, per_device(): lax.ppermute(fwd, 'seq', [(i, (i + k) % S) for i in range(S)])  4.84 us
    ppermute x2, starting transfers between devices, per_device(): lax.ppermute(fwd, 'seq', [(i, (i + k) % S) for i in range(S)])  3.03 us
    ppermute x2, starting transfers between devices, per_device(): lax.ppermute(bwd, 'seq', [((i + k) % S, i) for i in range(S)])  2.35 us
  transfers between devices with their start and end apart: 32, of which 18 were waited for; matrix products, arithmetic and copies ran while one was open for 0% of the time, Pallas kernels for 12%

profile of v7, /device:TPU:0, one launch (start us, length us, event | category | flops | bytes accessed | tf_op | source)
XLA Modules:
  0.0 82.6 jit_solution(16671261856422811069)
XLA Ops:
  0.7 1.8 %shard_map.237 = (bf16[144,768]{1,0:T(8,128)(2,1)}, f32[8,384]{1,0:T(8,128)}) custom-call(bf16[128,768]{1,0:T(8,128)(2,1)} %b_ref.1, bf16[1,128]{1,0:T(2,128)(2,1)} %bitcast.23, bf16[1,128]{1,0:T(2,128)(2,1)} %bitcast.24, bf16[1,128]{1,0:T(2,128)(2,1)} %bitcast.25, bf16[1,128]{1,0:T(2,128)(2,1)} %bitcast.26, f32[1,48]{1,0:T(1,128)} %bitcast.27, ...), custom_call_target="tpu_custom_call" | custom-call | flops 1000000000 | bytes 1048576 | tf_op jit(solution)/shard_map/pallas_call | solution.py:638
  2.6 3.0 %collective-permute-start.1 = (bf16[144,768]{1,0:T(8,128)(2,1)}, bf16[144,768]{1,0:T(8,128)(2,1)S(1)}, u32[]{:S(2)}, u32[]{:S(2)}) collective-permute-start(bf16[144,768]{1,0:T(8,128)(2,1)} %get-tuple-element.76.b0), channel_id=1, source_target_pairs={{0,2},{2,0},{1,3},{3,1},{4,6},{6,4},{5,7},{7,5},{8,10},{10,8},{9,1... | collective-permute-start | bytes 663560 | tf_op jit(solution)/shard_map/ppermute | solution.py:664
  5.6 2.5 %collective-permute-start.5 = (f32[8,384]{1,0:T(8,128)}, f32[8,384]{1,0:T(8,128)S(1)}, u32[]{:S(2)}, u32[]{:S(2)}) collective-permute-start(f32[8,384]{1,0:T(8,128)} %get-tuple-element.77), channel_id=1, source_target_pairs={{0,12},{4,8},{8,4},{12,0},{16,28},{20,24},{24,20},{28,16},{1,13},{... | collective-permute-start | bytes 36872 | tf_op jit(solution)/shard_map/ppermute | solution.py:664
  8.1 0.4 collective-permute-start.4
  8.5 0.5 collective-permute-start.3
  9.1 0.5 shard_map.239.refs_10_
  9.6 1.7 %collective-permute-done.1.b2 = bf16[144,768]{1,0:T(8,128)(2,1)S(1)} collective-permute-done((bf16[144,768]{1,0:T(8,128)(2,1)}, bf16[144,768]{1,0:T(8,128)(2,1)S(1)}, u32[]{:S(2)}, u32[]{:S(2)}) %collective-permute-start.1) | collective-permute-done | bytes 221216 | tf_op jit(solution)/shard_map/ppermute | solution.py:664
  11.2 1.7 %collective-permute-start.8 = (bf16[320,512]{1,0:T(8,128)(2,1)S(1)}, bf16[320,512]{1,0:T(8,128)(2,1)S(1)}, u32[]{:S(2)}, u32[]{:S(2)}) collective-permute-start(bf16[320,512]{1,0:T(8,128)(2,1)S(1)} %shard_map.239.refs_10_), channel_id=1, source_target_pairs={{0,2},{2,0},{1,3},{3,1},{4,6},{6,4},{5,7},{7,5},{8,10},{10,8},{9,1... | collective-permute-start | bytes 983048 | tf_op jit(solution)/shard_map/ppermute | solution.py:664
  13.0 2.7 %collective-permute-start.6 = (f32[8,384]{1,0:T(8,128)S(1)}, f32[8,384]{1,0:T(8,128)S(1)}, u32[]{:S(2)}, u32[]{:S(2)}) collective-permute-start(f32[8,384]{1,0:T(8,128)S(1)} %add_add_fusion), channel_id=1, source_target_pairs={{0,16},{4,20},{8,24},{12,28},{16,0},{20,4},{24,8},{28,12},{1,17},{... | collective-permute-start | bytes 36872 | tf_op jit(solution)/shard_map/ppermute | solution.py:664
  15.9 1.8 %collective-permute-done.6 = f32[8,384]{1,0:T(8,128)S(1)} collective-permute-done((f32[8,384]{1,0:T(8,128)S(1)}, f32[8,384]{1,0:T(8,128)S(1)}, u32[]{:S(2)}, u32[]{:S(2)}) %collective-permute-start.6) | collective-permute-done | bytes 12320 | tf_op jit(solution)/shard_map/ppermute | solution.py:664
  17.7 2.2 %shard_map.238 = (bf16[1024,512]{1,0:T(8,128)(2,1)S(1)}, bf16[1024,512]{1,0:T(8,128)(2,1)S(1)}, f32[6,1048,128]{2,1,0:T(8,128)S(1)}, f32[8,512]{1,0:T(8,128)S(1)...) custom-call(bf16[1024,512]{1,0:T(8,128)(2,1)S(1)} %bitcast.20, ...), custom_call_target="tpu_custom_call" | custom-call | flops 2000000000 | bytes 1048576 | tf_op jit(solution)/shard_map/pallas_call | solution.py:638
  20.1 1.5 %collective-permute-start.11 = (f32[2,896]{1,0:T(2,128)S(1)}, f32[2,896]{1,0:T(2,128)S(1)}, u32[]{:S(2)}, u32[]{:S(2)}) collective-permute-start(f32[2,896]{1,0:T(2,128)S(1)} %get-tuple-element.87), channel_id=1, source_target_pairs={{0,8},{4,12},{8,16},{12,20},{16,24},{20,28},{24,0},{28,4},{1,9},{5... | collective-permute-start | bytes 21512 | tf_op jit(solution)/shard_map/ppermute | solution.py:706
  21.7 1.5 %collective-permute-start.10 = (f32[2,896]{1,0:T(2,128)S(1)}, f32[2,896]{1,0:T(2,128)S(1)}, u32[]{:S(2)}, u32[]{:S(2)}) collective-permute-start(f32[2,896]{1,0:T(2,128)S(1)} %get-tuple-element.87), channel_id=1, source_target_pairs={{0,4},{4,8},{8,12},{12,16},{16,20},{20,24},{24,28},{28,0},{1,5},{5... | collective-permute-start | bytes 21512 | tf_op jit(solution)/shard_map/ppermute | solution.py:706
  23.2 2.4 %collective-permute-done.11.refs_15_ = f32[2,896]{1,0:T(2,128)S(1)} collective-permute-done((f32[2,896]{1,0:T(2,128)S(1)}, f32[2,896]{1,0:T(2,128)S(1)}, u32[]{:S(2)}, u32[]{:S(2)}) %collective-permute-start.11) | collective-permute-done | bytes 7200 | tf_op jit(solution)/shard_map/ppermute | solution.py:706
  25.6 2.4 %collective-permute-done.10.refs_14_ = f32[2,896]{1,0:T(2,128)S(1)} collective-permute-done((f32[2,896]{1,0:T(2,128)S(1)}, f32[2,896]{1,0:T(2,128)S(1)}, u32[]{:S(2)}, u32[]{:S(2)}) %collective-permute-start.10) | collective-permute-done | bytes 7200 | tf_op jit(solution)/shard_map/ppermute | solution.py:706
  28.0 8.9 %shard_map.240 = (bf16[1024,512]{1,0:T(8,128)(2,1)}, f32[6,1048,128]{2,1,0:T(8,128)S(1)}, f32[6,1048,128]{2,1,0:T(8,128)S(1)}, bf16[1024,512]{1,0:T(8,128)(2,1)S...) custom-call(bf16[1024,512]{1,0:T(8,128)(2,1)S(1)} %bitcast.21, ...), custom_call_target="tpu_custom_call" | custom-call | flops 10000000000 | bytes 1048576 | tf_op jit(solution)/shard_map/pallas_call | solution.py:638
  37.0 0.5 collective-permute-start.13
  37.5 1.8 %collective-permute-start.12 = (f32[2,896]{1,0:T(2,128)S(1)}, f32[2,896]{1,0:T(2,128)S(1)}, u32[]{:S(2)}, u32[]{:S(2)}) collective-permute-start(f32[2,896]{1,0:T(2,128)S(1)} %get-tuple-element.97), channel_id=1, source_target_pairs={{4,0},{8,4},{12,8},{16,12},{20,16},{24,20},{28,24},{0,28},{5,1},{9... | collective-permute-start | bytes 21512 | tf_op jit(solution)/shard_map/ppermute | solution.py:717
  39.5 1.1 %collective-permute-start.15 = (bf16[160,512]{1,0:T(8,128)(2,1)S(1)}, bf16[160,512]{1,0:T(8,128)(2,1)S(1)}, u32[]{:S(2)}, u32[]{:S(2)}) collective-permute-start(bf16[160,512]{1,0:T(8,128)(2,1)S(1)} %get-tuple-element.103), channel_id=1, source_target_pairs={{0,6},{2,4},{4,2},{6,0},{8,14},{10,12},{12,10},{14,8},{16,22},{18,... | collective-permute-start | bytes 491528 | tf_op jit(solution)/shard_map/ppermute | solution.py:719
  40.7 0.5 collective-permute-done.12.refs_13_
  41.1 4.0 %shard_map.242 = (bf16[1024,512]{1,0:T(8,128)(2,1)S(1)}, bf16[2,208,512]{2,1,0:T(8,128)(2,1)S(1)}, bf16[2,208,512]{2,1,0:T(8,128)(2,1)S(1)}) custom-call(bf16[1024,512]{1,0:T(8,128)(2,1)S(1)} %get-tuple-element.90.refs_0_, f32[8,512]{1,0:T(8,128)S(1)} %get-tuple-element.91.refs_1_, f32[1048,128]{1,0:T(8,128)S(1)} %get-tuple-element.78.refs_2_, ...), custom_call_target="tpu_custom_call" | custom-call | flops 8000000000 | bytes 1048576 | tf_op jit(solution)/shard_map/pallas_call | solution.py:638
  45.2 1.3 %collective-permute-done.15.c3 = bf16[160,512]{1,0:T(8,128)(2,1)S(1)} collective-permute-done((bf16[160,512]{1,0:T(8,128)(2,1)S(1)}, bf16[160,512]{1,0:T(8,128)(2,1)S(1)}, u32[]{:S(2)}, u32[]{:S(2)}) %collective-permute-start.15) | collective-permute-done | bytes 163872 | tf_op jit(solution)/shard_map/ppermute | solution.py:719
  46.5 1.4 %collective-permute-start.20 = (bf16[160,512]{1,0:T(8,128)(2,1)S(1)}, bf16[160,512]{1,0:T(8,128)(2,1)S(1)}, u32[]{:S(2)}, u32[]{:S(2)}) collective-permute-start(bf16[160,512]{1,0:T(8,128)(2,1)S(1)} %get-tuple-element.101), channel_id=1, source_target_pairs={{0,2},{2,0},{4,6},{6,4},{8,10},{10,8},{12,14},{14,12},{16,18},{18,... | collective-permute-start | bytes 491528 | tf_op jit(solution)/shard_map/ppermute | solution.py:719
  47.9 0.4 collective-permute-start.21
  48.5 1.4 %collective-permute-start.17 = (bf16[112,512]{1,0:T(8,128)(2,1)S(1)}, bf16[112,512]{1,0:T(8,128)(2,1)S(1)}, u32[]{:S(2)}, u32[]{:S(2)}) collective-permute-start(bf16[112,512]{1,0:T(8,128)(2,1)S(1)} %get-tuple-element.110), channel_id=1, source_target_pairs={{0,2},{2,0},{4,6},{6,4},{8,10},{10,8},{12,14},{14,12},{16,18},{18,... | collective-permute-start | bytes 344072 | tf_op jit(solution)/shard_map/ppermute | solution.py:719
  49.9 0.8 %collective-permute-start.18 = (bf16[112,512]{1,0:T(8,128)(2,1)S(1)}, bf16[112,512]{1,0:T(8,128)(2,1)S(1)}, u32[]{:S(2)}, u32[]{:S(2)}) collective-permute-start(bf16[112,512]{1,0:T(8,128)(2,1)S(1)} %get-tuple-element.111), channel_id=1, source_target_pairs={{0,4},{2,6},{4,0},{6,2},{8,12},{10,14},{12,8},{14,10},{16,20},{18,... | collective-permute-start | bytes 344072 | tf_op jit(solution)/shard_map/ppermute | solution.py:719
  50.7 1.3 %collective-permute-start.19 = (bf16[112,512]{1,0:T(8,128)(2,1)S(1)}, bf16[112,512]{1,0:T(8,128)(2,1)S(1)}, u32[]{:S(2)}, u32[]{:S(2)}) collective-permute-start(bf16[112,512]{1,0:T(8,128)(2,1)S(1)} %get-tuple-element.112), channel_id=1, source_target_pairs={{0,6},{2,4},{4,2},{6,0},{8,14},{10,12},{12,10},{14,8},{16,22},{18,... | collective-permute-start | bytes 344072 | tf_op jit(solution)/shard_map/ppermute | solution.py:719
  52.0 1.4 %shard_map.244.ig_ref = bf16[1024,512]{1,0:T(8,128)(2,1)S(1)} custom-call(bf16[1024,512]{1,0:T(8,128)(2,1)S(1)} %bitcast.22, bf16[1024,512]{1,0:T(8,128)(2,1)S(1)} %get-tuple-element.113.gn_ref, bf16[1024,512]{1,0:T(8,128)(2,1)S(1)} %get-tuple-element.114.gres_ref, f32[8,512]{1,0:T(8,128)S(1)} %get-tuple-element.85.refs_9_.refs_11_.vec_ref), custom_call_target="tpu_custom_call" | custom-call | flops 3000000000 | bytes 1048576 | tf_op jit(solution)/shard_map/pallas_call | solution.py:638
  53.5 1.5 %collective-permute-done.21.c2 = bf16[160,512]{1,0:T(8,128)(2,1)S(1)} collective-permute-done((bf16[160,512]{1,0:T(8,128)(2,1)S(1)}, bf16[160,512]{1,0:T(8,128)(2,1)S(1)}, u32[]{:S(2)}, u32[]{:S(2)}) %collective-permute-start.21) | collective-permute-done | bytes 163872 | tf_op jit(solution)/shard_map/ppermute | solution.py:719
  55.0 0.5 collective-permute-done.17.refs_1_
  55.5 1.9 %collective-permute-done.18.refs_2_ = bf16[112,512]{1,0:T(8,128)(2,1)S(1)} collective-permute-done((bf16[112,512]{1,0:T(8,128)(2,1)S(1)}, bf16[112,512]{1,0:T(8,128)(2,1)S(1)}, u32[]{:S(2)}, u32[]{:S(2)}) %collective-permute-start.18) | collective-permute-done | bytes 114720 | tf_op jit(solution)/shard_map/ppermute | solution.py:719
  57.4 1.8 %collective-permute-done.19.refs_3_ = bf16[112,512]{1,0:T(8,128)(2,1)S(1)} collective-permute-done((bf16[112,512]{1,0:T(8,128)(2,1)S(1)}, bf16[112,512]{1,0:T(8,128)(2,1)S(1)}, u32[]{:S(2)}, u32[]{:S(2)}) %collective-permute-start.19) | collective-permute-done | bytes 114720 | tf_op jit(solution)/shard_map/ppermute | solution.py:719
  59.7 2.5 %collective-permute-start.23 = (bf16[72,512]{1,0:T(8,128)(2,1)S(1)}, bf16[72,512]{1,0:T(8,128)(2,1)S(1)}, u32[]{:S(2)}, u32[]{:S(2)}) collective-permute-start(bf16[72,512]{1,0:T(8,128)(2,1)S(1)} %get-tuple-element.121), channel_id=1, source_target_pairs={{0,16},{4,20},{8,24},{12,28},{16,0},{20,4},{24,8},{28,12},{1,17},{... | collective-permute-start | bytes 221192 | tf_op jit(solution)/shard_map/ppermute | solution.py:664
  62.1 1.6 %collective-permute-start.24 = (bf16[72,512]{1,0:T(8,128)(2,1)S(1)}, bf16[72,512]{1,0:T(8,128)(2,1)S(1)}, u32[]{:S(2)}, u32[]{:S(2)}) collective-permute-start(bf16[72,512]{1,0:T(8,128)(2,1)S(1)} %get-tuple-element.122), channel_id=1, source_target_pairs={{0,24},{4,28},{8,16},{12,20},{16,8},{20,12},{24,0},{28,4},{1,25},{... | collective-permute-start | bytes 221192 | tf_op jit(solution)/shard_map/ppermute | solution.py:664
  63.9 3.4 %collective-permute-done.23.refs_2_ = bf16[72,512]{1,0:T(8,128)(2,1)S(1)} collective-permute-done((bf16[72,512]{1,0:T(8,128)(2,1)S(1)}, bf16[72,512]{1,0:T(8,128)(2,1)S(1)}, u32[]{:S(2)}, u32[]{:S(2)}) %collective-permute-start.23) | collective-permute-done | bytes 73760 | tf_op jit(solution)/shard_map/ppermute | solution.py:664
  67.3 1.1 %collective-permute-done.24.refs_3_ = bf16[72,512]{1,0:T(8,128)(2,1)S(1)} collective-permute-done((bf16[72,512]{1,0:T(8,128)(2,1)S(1)}, bf16[72,512]{1,0:T(8,128)(2,1)S(1)}, u32[]{:S(2)}, u32[]{:S(2)}) %collective-permute-start.24) | collective-permute-done | bytes 73760 | tf_op jit(solution)/shard_map/ppermute | solution.py:664
  68.4 1.1 %collective-permute-start.25 = (bf16[64,512]{1,0:T(8,128)(2,1)S(1)}, bf16[64,512]{1,0:T(8,128)(2,1)S(1)}, u32[]{:S(2)}, u32[]{:S(2)}) collective-permute-start(bf16[64,512]{1,0:T(8,128)(2,1)S(1)} %get-tuple-element.130.refs_0_), channel_id=1, source_target_pairs={{0,8},{4,12},{8,0},{12,4},{16,24},{20,28},{24,16},{28,20},{1,9},{5... | collective-permute-start | bytes 196616 | tf_op jit(solution)/shard_map/ppermute | solution.py:664
  69.6 2.0 %collective-permute-start.30 = (bf16[64,512]{1,0:T(8,128)(2,1)S(1)}, bf16[64,512]{1,0:T(8,128)(2,1)S(1)}, u32[]{:S(2)}, u32[]{:S(2)}) collective-permute-start(bf16[64,512]{1,0:T(8,128)(2,1)S(1)} %get-tuple-element.130.refs_0_), channel_id=1, source_target_pairs={{0,24},{4,28},{8,16},{12,20},{16,8},{20,12},{24,0},{28,4},{1,25},{... | collective-permute-start | bytes 196616 | tf_op jit(solution)/shard_map/ppermute | solution.py:664
  71.5 0.5 collective-permute-start.28
  72.0 0.8 %collective-permute-done.25.refs_2_ = bf16[64,512]{1,0:T(8,128)(2,1)S(1)} collective-permute-done((bf16[64,512]{1,0:T(8,128)(2,1)S(1)}, bf16[64,512]{1,0:T(8,128)(2,1)S(1)}, u32[]{:S(2)}, u32[]{:S(2)}) %collective-permute-start.25) | collective-permute-done | bytes 65568 | tf_op jit(solution)/shard_map/ppermute | solution.py:664
  72.8 1.7 %collective-permute-start.26 = (bf16[64,512]{1,0:T(8,128)(2,1)S(1)}, bf16[64,512]{1,0:T(8,128)(2,1)S(1)}, u32[]{:S(2)}, u32[]{:S(2)}) collective-permute-start(bf16[64,512]{1,0:T(8,128)(2,1)S(1)} %get-tuple-element.130.refs_0_), channel_id=1, source_target_pairs={{0,4},{4,0},{8,12},{12,8},{16,20},{20,16},{24,28},{28,24},{1,5},{5... | collective-permute-start | bytes 196616 | tf_op jit(solution)/shard_map/ppermute | solution.py:664
  74.9 0.8 collective-permute-done.30.refs_6_
  75.6 0.9 %collective-permute-start.31 = (bf16[64,512]{1,0:T(8,128)(2,1)S(1)}, bf16[64,512]{1,0:T(8,128)(2,1)S(1)}, u32[]{:S(2)}, u32[]{:S(2)}) collective-permute-start(bf16[64,512]{1,0:T(8,128)(2,1)S(1)} %collective-permute-done.30.refs_6_), channel_id=1, source_target_pairs={{0,4},{4,0},{8,12},{12,8},{16,20},{20,16},{24,28},{28,24},{1,5},{5... | collective-permute-start | bytes 196616 | tf_op jit(solution)/shard_map/ppermute | solution.py:664
  76.5 0.5 collective-permute-done.28.refs_4_
  77.0 1.4 %collective-permute-start.29 = (bf16[64,512]{1,0:T(8,128)(2,1)S(1)}, bf16[64,512]{1,0:T(8,128)(2,1)S(1)}, u32[]{:S(2)}, u32[]{:S(2)}) collective-permute-start(bf16[64,512]{1,0:T(8,128)(2,1)S(1)} %collective-permute-done.28.refs_4_), channel_id=1, source_target_pairs={{0,4},{4,0},{8,12},{12,8},{16,20},{20,16},{24,28},{28,24},{1,5},{5... | collective-permute-start | bytes 196616 | tf_op jit(solution)/shard_map/ppermute | solution.py:664
  78.4 1.5 %shard_map.248 = (f32[1024,512]{1,0:T(8,128)}, f32[1,1]{1,0:T(1,128)}, f32[1,128]{1,0:T(1,128)}, f32[1,128]{1,0:T(1,128)}, f32[1,128]{1,0:T(1,128)}, /*index=5*/...) custom-call(f32[8,512]{1,0:T(8,128)S(1)} %get-tuple-element.123.tail_ref, ...), custom_call_target="tpu_custom_call" | custom-call | flops 1000000000 | bytes 1048576 | tf_op jit(solution)/shard_map/pallas_call | solution.py:638
  79.9 1.4 %collective-permute-done.29.refs_5_ = bf16[64,512]{1,0:T(8,128)(2,1)S(1)} collective-permute-done((bf16[64,512]{1,0:T(8,128)(2,1)S(1)}, bf16[64,512]{1,0:T(8,128)(2,1)S(1)}, u32[]{:S(2)}, u32[]{:S(2)}) %collective-permute-start.29) | collective-permute-done | bytes 65568 | tf_op jit(solution)/shard_map/ppermute | solution.py:664
  81.3 1.1 %shard_map.249 = (f32[128,768]{1,0:T(8,128)}, f32[192,512]{1,0:T(8,128)}, f32[128,512]{1,0:T(8,128)}) custom-call(f32[8,512]{1,0:T(8,128)S(1)} %get-tuple-element.123.tail_ref, bf16[64,512]{1,0:T(8,128)(2,1)S(1)} %get-tuple-element.130.refs_0_, bf16[64,512]{1,0:T(8,128)(2,1)S(1)} %collective-permute-done.26.refs_1_, ...), custom_call_target="tpu_custom_call" | custom-call | flops 1000000000 | bytes 1048576 | tf_op jit(solution)/shard_map/pallas_call | solution.py:638
  (47 shorter events, 2.0 us)
Async XLA Ops:
  0.6 8.4 %copy-start.4 = (bf16[128,512]{1,0:T(8,128)(2,1)S(1)}, bf16[128,512]{1,0:T(8,128)(2,1)}, u32[]{:S(2)}) copy-start(bf16[128,512]{1,0:T(8,128)(2,1)} %g_ref.1) | copy-start | bytes 393220
  0.7 8.4 %copy-start.3 = (bf16[192,512]{1,0:T(8,128)(2,1)S(1)}, bf16[192,512]{1,0:T(8,128)(2,1)}, u32[]{:S(2)}) copy-start(bf16[192,512]{1,0:T(8,128)(2,1)} %c_ref.1) | copy-start | bytes 589828
  0.7 17.0 %copy-start.1 = (bf16[2,512,512]{2,1,0:T(8,128)(2,1)S(1)}, bf16[2,512,512]{2,1,0:T(8,128)(2,1)}, u32[]{:S(2)}) copy-start(bf16[2,512,512]{2,1,0:T(8,128)(2,1)} %param.14) | copy-start | bytes 3145732
  0.7 17.0 %copy-start.5 = (s32[2,512]{1,0:T(2,128)S(1)}, s32[2,512]{1,0:T(2,128)}, u32[]{:S(2)}) copy-start(s32[2,512]{1,0:T(2,128)} %seg_ref.1) | copy-start | bytes 12292
  0.7 17.0 %copy-start.6 = (s32[2,512]{1,0:T(2,128)S(1)}, s32[2,512]{1,0:T(2,128)}, u32[]{:S(2)}) copy-start(s32[2,512]{1,0:T(2,128)} %mask_ref.1) | copy-start | bytes 12292
  2.5 10.5 %copy-start.7 = (f32[8,384]{1,0:T(8,128)S(1)}, f32[8,384]{1,0:T(8,128)}, u32[]{:S(2)}) copy-start(f32[8,384]{1,0:T(8,128)} %get-tuple-element.77) | copy-start | bytes 36868
  2.5 15.2 %copy-start.2 = (bf16[144,768]{1,0:T(8,128)(2,1)S(1)}, bf16[144,768]{1,0:T(8,128)(2,1)}, u32[]{:S(2)}) copy-start(bf16[144,768]{1,0:T(8,128)(2,1)} %get-tuple-element.76.b0) | copy-start | bytes 663556
  2.6 8.7 %collective-permute-start.1 = (bf16[144,768]{1,0:T(8,128)(2,1)}, bf16[144,768]{1,0:T(8,128)(2,1)S(1)}, u32[]{:S(2)}, u32[]{:S(2)}) collective-permute-start(bf16[144,768]{1,0:T(8,128)(2,1)} %get-tuple-element.76.b0), channel_id=1, source_target_pairs={{0,2},{2,0},{1,3},{3,1},{4,6},{6,4},{5,7},{7,5},{8,10},{10,8},{9,1... | collective-permute-start | bytes 663560 | tf_op jit(solution)/shard_map/ppermute | solution.py:664
  5.6 7.4 %collective-permute-start.5 = (f32[8,384]{1,0:T(8,128)}, f32[8,384]{1,0:T(8,128)S(1)}, u32[]{:S(2)}, u32[]{:S(2)}) collective-permute-start(f32[8,384]{1,0:T(8,128)} %get-tuple-element.77), channel_id=1, source_target_pairs={{0,12},{4,8},{8,4},{12,0},{16,28},{20,24},{24,20},{28,16},{1,13},{... | collective-permute-start | bytes 36872 | tf_op jit(solution)/shard_map/ppermute | solution.py:664
  8.1 4.9 %collective-permute-start.4 = (f32[8,384]{1,0:T(8,128)}, f32[8,384]{1,0:T(8,128)S(1)}, u32[]{:S(2)}, u32[]{:S(2)}) collective-permute-start(f32[8,384]{1,0:T(8,128)} %get-tuple-element.77), channel_id=1, source_target_pairs={{0,8},{4,12},{8,0},{12,4},{16,24},{20,28},{24,16},{28,20},{1,9},{5... | collective-permute-start | bytes 36872 | tf_op jit(solution)/shard_map/ppermute | solution.py:664
  8.5 4.4 %collective-permute-start.3 = (f32[8,384]{1,0:T(8,128)}, f32[8,384]{1,0:T(8,128)S(1)}, u32[]{:S(2)}, u32[]{:S(2)}) collective-permute-start(f32[8,384]{1,0:T(8,128)} %get-tuple-element.77), channel_id=1, source_target_pairs={{0,4},{4,0},{8,12},{12,8},{16,20},{20,16},{24,28},{28,24},{1,5},{5... | collective-permute-start | bytes 36872 | tf_op jit(solution)/shard_map/ppermute | solution.py:664
  9.1 8.6 %collective-permute-start = (bf16[144,768]{1,0:T(8,128)(2,1)}, bf16[144,768]{1,0:T(8,128)(2,1)S(1)}, u32[]{:S(2)}, u32[]{:S(2)}) collective-permute-start(bf16[144,768]{1,0:T(8,128)(2,1)} %get-tuple-element.76.b0), channel_id=1, source_target_pairs={{0,1},{1,0},{2,3},{3,2},{4,5},{5,4},{6,7},{7,6},{8,9},{9,8},{10,11... | collective-permute-start | bytes 663560 | tf_op jit(solution)/shard_map/ppermute | solution.py:664
  11.2 8.9 %collective-permute-start.8 = (bf16[320,512]{1,0:T(8,128)(2,1)S(1)}, bf16[320,512]{1,0:T(8,128)(2,1)S(1)}, u32[]{:S(2)}, u32[]{:S(2)}) collective-permute-start(bf16[320,512]{1,0:T(8,128)(2,1)S(1)} %shard_map.239.refs_10_), channel_id=1, source_target_pairs={{0,2},{2,0},{1,3},{3,1},{4,6},{6,4},{5,7},{7,5},{8,10},{10,8},{9,1... | collective-permute-start | bytes 983048 | tf_op jit(solution)/shard_map/ppermute | solution.py:664
  13.0 4.7 %collective-permute-start.2 = (bf16[144,768]{1,0:T(8,128)(2,1)S(1)}, bf16[144,768]{1,0:T(8,128)(2,1)S(1)}, u32[]{:S(2)}, u32[]{:S(2)}) collective-permute-start(bf16[144,768]{1,0:T(8,128)(2,1)S(1)} %collective-permute-done.1.b2), channel_id=1, source_target_pairs={{0,1},{1,0},{2,3},{3,2},{4,5},{5,4},{6,7},{7,6},{8,9},{9,8},{10,11... | collective-permute-start | bytes 663560 | tf_op jit(solution)/shard_map/ppermute | solution.py:664
  13.0 4.7 %collective-permute-start.6 = (f32[8,384]{1,0:T(8,128)S(1)}, f32[8,384]{1,0:T(8,128)S(1)}, u32[]{:S(2)}, u32[]{:S(2)}) collective-permute-start(f32[8,384]{1,0:T(8,128)S(1)} %add_add_fusion), channel_id=1, source_target_pairs={{0,16},{4,20},{8,24},{12,28},{16,0},{20,4},{24,8},{28,12},{1,17},{... | collective-permute-start | bytes 36872 | tf_op jit(solution)/shard_map/ppermute | solution.py:664
  15.7 7.5 %collective-permute-start.7 = (bf16[320,512]{1,0:T(8,128)(2,1)S(1)}, bf16[320,512]{1,0:T(8,128)(2,1)S(1)}, u32[]{:S(2)}, u32[]{:S(2)}) collective-permute-start(bf16[320,512]{1,0:T(8,128)(2,1)S(1)} %shard_map.239.refs_10_), channel_id=1, source_target_pairs={{0,1},{1,0},{2,3},{3,2},{4,5},{5,4},{6,7},{7,6},{8,9},{9,8},{10,11... | collective-permute-start | bytes 983048 | tf_op jit(solution)/shard_map/ppermute | solution.py:664
  17.7 10.3 %copy-start = (bf16[2,512,512]{2,1,0:T(8,128)(2,1)S(1)}, bf16[2,512,512]{2,1,0:T(8,128)(2,1)}, u32[]{:S(2)}) copy-start(bf16[2,512,512]{2,1,0:T(8,128)(2,1)} %param.15) | copy-start | bytes 3145732
  20.1 7.9 %collective-permute-start.9 = (bf16[320,512]{1,0:T(8,128)(2,1)S(1)}, bf16[320,512]{1,0:T(8,128)(2,1)S(1)}, u32[]{:S(2)}, u32[]{:S(2)}) collective-permute-start(bf16[320,512]{1,0:T(8,128)(2,1)S(1)} %collective-permute-done.8.refs_12_), channel_id=1, source_target_pairs={{0,1},{1,0},{2,3},{3,2},{4,5},{5,4},{6,7},{7,6},{8,9},{9,8},{10,11... | collective-permute-start | bytes 983048 | tf_op jit(solution)/shard_map/ppermute | solution.py:664
  20.1 5.4 %collective-permute-start.11 = (f32[2,896]{1,0:T(2,128)S(1)}, f32[2,896]{1,0:T(2,128)S(1)}, u32[]{:S(2)}, u32[]{:S(2)}) collective-permute-start(f32[2,896]{1,0:T(2,128)S(1)} %get-tuple-element.87), channel_id=1, source_target_pairs={{0,8},{4,12},{8,16},{12,20},{16,24},{20,28},{24,0},{28,4},{1,9},{5... | collective-permute-start | bytes 21512 | tf_op jit(solution)/shard_map/ppermute | solution.py:706
  21.7 6.3 %collective-permute-start.10 = (f32[2,896]{1,0:T(2,128)S(1)}, f32[2,896]{1,0:T(2,128)S(1)}, u32[]{:S(2)}, u32[]{:S(2)}) collective-permute-start(f32[2,896]{1,0:T(2,128)S(1)} %get-tuple-element.87), channel_id=1, source_target_pairs={{0,4},{4,8},{8,12},{12,16},{16,20},{20,24},{24,28},{28,0},{1,5},{5... | collective-permute-start | bytes 21512 | tf_op jit(solution)/shard_map/ppermute | solution.py:706
  36.9 2.4 %collective-permute-start.14 = (bf16[2,320,512]{2,1,0:T(8,128)(2,1)S(1)}, bf16[2,320,512]{2,1,0:T(8,128)(2,1)S(1)}, u32[]{:S(2)}, u32[]{:S(2)}) collective-permute-start(bf16[2,320,512]{2,1,0:T(8,128)(2,1)S(1)} %get-tuple-element.99), channel_id=1, source_target_pairs={{0,1},{1,0},{2,3},{3,2},{4,5},{5,4},{6,7},{7,6},{8,9},{9,8},{10,11... | collective-permute-start | bytes 1966088 | tf_op jit(solution)/shard_map/ppermute | solution.py:664
  37.0 3.7 %collective-permute-start.13 = (f32[2,896]{1,0:T(2,128)S(1)}, f32[2,896]{1,0:T(2,128)S(1)}, u32[]{:S(2)}, u32[]{:S(2)}) collective-permute-start(f32[2,896]{1,0:T(2,128)S(1)} %get-tuple-element.97), channel_id=1, source_target_pairs={{8,0},{12,4},{16,8},{20,12},{24,16},{28,20},{0,24},{4,28},{9,1},{1... | collective-permute-start | bytes 21512 | tf_op jit(solution)/shard_map/ppermute | solution.py:717
  37.5 3.6 %collective-permute-start.12 = (f32[2,896]{1,0:T(2,128)S(1)}, f32[2,896]{1,0:T(2,128)S(1)}, u32[]{:S(2)}, u32[]{:S(2)}) collective-permute-start(f32[2,896]{1,0:T(2,128)S(1)} %get-tuple-element.97), channel_id=1, source_target_pairs={{4,0},{8,4},{12,8},{16,12},{20,16},{24,20},{28,24},{0,28},{5,1},{9... | collective-permute-start | bytes 21512 | tf_op jit(solution)/shard_map/ppermute | solution.py:717
  39.5 7.0 %collective-permute-start.15 = (bf16[160,512]{1,0:T(8,128)(2,1)S(1)}, bf16[160,512]{1,0:T(8,128)(2,1)S(1)}, u32[]{:S(2)}, u32[]{:S(2)}) collective-permute-start(bf16[160,512]{1,0:T(8,128)(2,1)S(1)} %get-tuple-element.103), channel_id=1, source_target_pairs={{0,6},{2,4},{4,2},{6,0},{8,14},{10,12},{12,10},{14,8},{16,22},{18,... | collective-permute-start | bytes 491528 | tf_op jit(solution)/shard_map/ppermute | solution.py:719
  46.5 1.9 %collective-permute-start.16 = (bf16[2,208,512]{2,1,0:T(8,128)(2,1)S(1)}, bf16[2,208,512]{2,1,0:T(8,128)(2,1)S(1)}, u32[]{:S(2)}, u32[]{:S(2)}) collective-permute-start(bf16[2,208,512]{2,1,0:T(8,128)(2,1)S(1)} %get-tuple-element.108), channel_id=1, source_target_pairs={{0,1},{1,0},{2,3},{3,2},{4,5},{5,4},{6,7},{7,6},{8,9},{9,8},{10,11... | collective-permute-start | bytes 1277960 | tf_op jit(solution)/shard_map/ppermute | solution.py:664
  46.5 7.0 %collective-permute-start.20 = (bf16[160,512]{1,0:T(8,128)(2,1)S(1)}, bf16[160,512]{1,0:T(8,128)(2,1)S(1)}, u32[]{:S(2)}, u32[]{:S(2)}) collective-permute-start(bf16[160,512]{1,0:T(8,128)(2,1)S(1)} %get-tuple-element.101), channel_id=1, source_target_pairs={{0,2},{2,0},{4,6},{6,4},{8,10},{10,8},{12,14},{14,12},{16,18},{18,... | collective-permute-start | bytes 491528 | tf_op jit(solution)/shard_map/ppermute | solution.py:719
  47.9 7.0 %collective-permute-start.21 = (bf16[160,512]{1,0:T(8,128)(2,1)S(1)}, bf16[160,512]{1,0:T(8,128)(2,1)S(1)}, u32[]{:S(2)}, u32[]{:S(2)}) collective-permute-start(bf16[160,512]{1,0:T(8,128)(2,1)S(1)} %get-tuple-element.102), channel_id=1, source_target_pairs={{0,4},{2,6},{4,0},{6,2},{8,12},{10,14},{12,8},{14,10},{16,20},{18,... | collective-permute-start | bytes 491528 | tf_op jit(solution)/shard_map/ppermute | solution.py:719
  48.5 7.1 %collective-permute-start.17 = (bf16[112,512]{1,0:T(8,128)(2,1)S(1)}, bf16[112,512]{1,0:T(8,128)(2,1)S(1)}, u32[]{:S(2)}, u32[]{:S(2)}) collective-permute-start(bf16[112,512]{1,0:T(8,128)(2,1)S(1)} %get-tuple-element.110), channel_id=1, source_target_pairs={{0,2},{2,0},{4,6},{6,4},{8,10},{10,8},{12,14},{14,12},{16,18},{18,... | collective-permute-start | bytes 344072 | tf_op jit(solution)/shard_map/ppermute | solution.py:719
  49.9 7.5 %collective-permute-start.18 = (bf16[112,512]{1,0:T(8,128)(2,1)S(1)}, bf16[112,512]{1,0:T(8,128)(2,1)S(1)}, u32[]{:S(2)}, u32[]{:S(2)}) collective-permute-start(bf16[112,512]{1,0:T(8,128)(2,1)S(1)} %get-tuple-element.111), channel_id=1, source_target_pairs={{0,4},{2,6},{4,0},{6,2},{8,12},{10,14},{12,8},{14,10},{16,20},{18,... | collective-permute-start | bytes 344072 | tf_op jit(solution)/shard_map/ppermute | solution.py:719
  50.7 8.5 %collective-permute-start.19 = (bf16[112,512]{1,0:T(8,128)(2,1)S(1)}, bf16[112,512]{1,0:T(8,128)(2,1)S(1)}, u32[]{:S(2)}, u32[]{:S(2)}) collective-permute-start(bf16[112,512]{1,0:T(8,128)(2,1)S(1)} %get-tuple-element.112), channel_id=1, source_target_pairs={{0,6},{2,4},{4,2},{6,0},{8,14},{10,12},{12,10},{14,8},{16,22},{18,... | collective-permute-start | bytes 344072 | tf_op jit(solution)/shard_map/ppermute | solution.py:719
  59.3 4.6 %collective-permute-start.22 = (bf16[72,512]{1,0:T(8,128)(2,1)S(1)}, bf16[72,512]{1,0:T(8,128)(2,1)S(1)}, u32[]{:S(2)}, u32[]{:S(2)}) collective-permute-start(bf16[72,512]{1,0:T(8,128)(2,1)S(1)} %get-tuple-element.120), channel_id=1, source_target_pairs={{0,8},{4,12},{8,0},{12,4},{16,24},{20,28},{24,16},{28,20},{1,9},{5... | collective-permute-start | bytes 221192 | tf_op jit(solution)/shard_map/ppermute | solution.py:664
  59.7 7.6 %collective-permute-start.23 = (bf16[72,512]{1,0:T(8,128)(2,1)S(1)}, bf16[72,512]{1,0:T(8,128)(2,1)S(1)}, u32[]{:S(2)}, u32[]{:S(2)}) collective-permute-start(bf16[72,512]{1,0:T(8,128)(2,1)S(1)} %get-tuple-element.121), channel_id=1, source_target_pairs={{0,16},{4,20},{8,24},{12,28},{16,0},{20,4},{24,8},{28,12},{1,17},{... | collective-permute-start | bytes 221192 | tf_op jit(solution)/shard_map/ppermute | solution.py:664
  62.1 6.3 %collective-permute-start.24 = (bf16[72,512]{1,0:T(8,128)(2,1)S(1)}, bf16[72,512]{1,0:T(8,128)(2,1)S(1)}, u32[]{:S(2)}, u32[]{:S(2)}) collective-permute-start(bf16[72,512]{1,0:T(8,128)(2,1)S(1)} %get-tuple-element.122), channel_id=1, source_target_pairs={{0,24},{4,28},{8,16},{12,20},{16,8},{20,12},{24,0},{28,4},{1,25},{... | collective-permute-start | bytes 221192 | tf_op jit(solution)/shard_map/ppermute | solution.py:664
  68.4 4.4 %collective-permute-start.25 = (bf16[64,512]{1,0:T(8,128)(2,1)S(1)}, bf16[64,512]{1,0:T(8,128)(2,1)S(1)}, u32[]{:S(2)}, u32[]{:S(2)}) collective-permute-start(bf16[64,512]{1,0:T(8,128)(2,1)S(1)} %get-tuple-element.130.refs_0_), channel_id=1, source_target_pairs={{0,8},{4,12},{8,0},{12,4},{16,24},{20,28},{24,16},{28,20},{1,9},{5... | collective-permute-start | bytes 196616 | tf_op jit(solution)/shard_map/ppermute | solution.py:664
  69.6 6.1 %collective-permute-start.30 = (bf16[64,512]{1,0:T(8,128)(2,1)S(1)}, bf16[64,512]{1,0:T(8,128)(2,1)S(1)}, u32[]{:S(2)}, u32[]{:S(2)}) collective-permute-start(bf16[64,512]{1,0:T(8,128)(2,1)S(1)} %get-tuple-element.130.refs_0_), channel_id=1, source_target_pairs={{0,24},{4,28},{8,16},{12,20},{16,8},{20,12},{24,0},{28,4},{1,25},{... | collective-permute-start | bytes 196616 | tf_op jit(solution)/shard_map/ppermute | solution.py:664
  71.5 5.5 %collective-permute-start.28 = (bf16[64,512]{1,0:T(8,128)(2,1)S(1)}, bf16[64,512]{1,0:T(8,128)(2,1)S(1)}, u32[]{:S(2)}, u32[]{:S(2)}) collective-permute-start(bf16[64,512]{1,0:T(8,128)(2,1)S(1)} %get-tuple-element.130.refs_0_), channel_id=1, source_target_pairs={{0,16},{4,20},{8,24},{12,28},{16,0},{20,4},{24,8},{28,12},{1,17},{... | collective-permute-start | bytes 196616 | tf_op jit(solution)/shard_map/ppermute | solution.py:664
  72.8 8.5 %collective-permute-start.26 = (bf16[64,512]{1,0:T(8,128)(2,1)S(1)}, bf16[64,512]{1,0:T(8,128)(2,1)S(1)}, u32[]{:S(2)}, u32[]{:S(2)}) collective-permute-start(bf16[64,512]{1,0:T(8,128)(2,1)S(1)} %get-tuple-element.130.refs_0_), channel_id=1, source_target_pairs={{0,4},{4,0},{8,12},{12,8},{16,20},{20,16},{24,28},{28,24},{1,5},{5... | collective-permute-start | bytes 196616 | tf_op jit(solution)/shard_map/ppermute | solution.py:664
  74.5 6.8 %collective-permute-start.27 = (bf16[64,512]{1,0:T(8,128)(2,1)S(1)}, bf16[64,512]{1,0:T(8,128)(2,1)S(1)}, u32[]{:S(2)}, u32[]{:S(2)}) collective-permute-start(bf16[64,512]{1,0:T(8,128)(2,1)S(1)} %collective-permute-done.25.refs_2_), channel_id=1, source_target_pairs={{0,4},{4,0},{8,12},{12,8},{16,20},{20,16},{24,28},{28,24},{1,5},{5... | collective-permute-start | bytes 196616 | tf_op jit(solution)/shard_map/ppermute | solution.py:664
  75.6 4.3 %collective-permute-start.31 = (bf16[64,512]{1,0:T(8,128)(2,1)S(1)}, bf16[64,512]{1,0:T(8,128)(2,1)S(1)}, u32[]{:S(2)}, u32[]{:S(2)}) collective-permute-start(bf16[64,512]{1,0:T(8,128)(2,1)S(1)} %collective-permute-done.30.refs_6_), channel_id=1, source_target_pairs={{0,4},{4,0},{8,12},{12,8},{16,20},{20,16},{24,28},{28,24},{1,5},{5... | collective-permute-start | bytes 196616 | tf_op jit(solution)/shard_map/ppermute | solution.py:664
  77.0 4.3 %collective-permute-start.29 = (bf16[64,512]{1,0:T(8,128)(2,1)S(1)}, bf16[64,512]{1,0:T(8,128)(2,1)S(1)}, u32[]{:S(2)}, u32[]{:S(2)}) collective-permute-start(bf16[64,512]{1,0:T(8,128)(2,1)S(1)} %collective-permute-done.28.refs_4_), channel_id=1, source_target_pairs={{0,4},{4,0},{8,12},{12,8},{16,20},{20,16},{24,28},{28,24},{1,5},{5... | collective-permute-start | bytes 196616 | tf_op jit(solution)/shard_map/ppermute | solution.py:664

commit v8 on v7

--- a/solution.py
+++ b/solution.py
@@ -339,7 +339,7 @@
         put(state_ref, at, 0, sr)
         put(state_ref, at, groups, si)
         entry[s] = (ur, ui)
-    run(steps - PAD, lambda i, c: step(i + PAD, c), tuple(entry), 8)
+    run(steps - PAD, lambda i, c: step(i + PAD, c), tuple(entry), 19)
 
     skip = vec_ref[2:3, :]
     gbias = 0.5 * vec_ref[3:4, :]
@@ -399,7 +399,7 @@
 
     zero = jnp.zeros((CHUNKS, states), F32)
     init = tuple((zero, zero, jnp.ones((CHUNKS, LANES), F32)) for _ in range(seqs))
-    firsts = run(steps - PAD, back, init, 8)
+    firsts = run(steps - PAD, back, init, 19)
     ends = run(PAD, lambda i, c: back(i + steps - PAD, c), firsts, PAD)
     pr, pi = chunk_powers(ar, -ai, steps)
     for s in range(seqs):

time: 82.7 us -> 82.6 us (level)
  no operation moved by 1% of the time
where the time goes in v8:
time: 82.6 us; the launch traced here: 82.5 us
  starting transfers between devices  35.5 us (43%)
  waiting for transfers between devices  24 us (29%)
  Pallas kernels  21.9 us (27%)
  between operations  1.05 us (1%)
    ppermute x22, starting transfers between devices, swap(): return lax.ppermute(v, axis, [(i, i ^ bit) for i in range(n)])  23.5 us
    pallas_call x13, Pallas kernels, call(): pl.pallas_call(body, out_shape=[jax.ShapeDtypeStruct(*o) for o in outs],...  21.9 us
    ppermute x22, waiting for transfers between devices, swap(): return lax.ppermute(v, axis, [(i, i ^ bit) for i in range(n)])  11.7 us
    ppermute x6, waiting for transfers between devices, cross(): lax.ppermute(v, ('seq', 'wy'), [(2 * a + b, 2 * (a ^ flip_x) + (b ^ flip_...  6.91 us
    ppermute x6, starting transfers between devices, cross(): lax.ppermute(v, ('seq', 'wy'), [(2 * a + b, 2 * (a ^ flip_x) + (b ^ flip_...  6.58 us
    ppermute x2, waiting for transfers between devices, per_device(): lax.ppermute(fwd, 'seq', [(i, (i + k) % S) for i in range(S)])  4.84 us
    ppermute x2, starting transfers between devices, per_device(): lax.ppermute(fwd, 'seq', [(i, (i + k) % S) for i in range(S)])  3.03 us
    ppermute x2, starting transfers between devices, per_device(): lax.ppermute(bwd, 'seq', [((i + k) % S, i) for i in range(S)])  2.36 us
  transfers between devices with their start and end apart: 32, of which 18 were waited for; matrix products, arithmetic and copies ran while one was open for 0% of the time, Pallas kernels for 12%

profile of v8, /device:TPU:0, one launch (start us, length us, event | category | flops | bytes accessed | tf_op | source)
XLA Modules:
  0.0 82.5 jit_solution(4303979436031604163)
XLA Ops:
  0.7 1.8 %shard_map.237 = (bf16[144,768]{1,0:T(8,128)(2,1)}, f32[8,384]{1,0:T(8,128)}) custom-call(bf16[128,768]{1,0:T(8,128)(2,1)} %b_ref.1, bf16[1,128]{1,0:T(2,128)(2,1)} %bitcast.23, bf16[1,128]{1,0:T(2,128)(2,1)} %bitcast.24, bf16[1,128]{1,0:T(2,128)(2,1)} %bitcast.25, bf16[1,128]{1,0:T(2,128)(2,1)} %bitcast.26, f32[1,48]{1,0:T(1,128)} %bitcast.27, ...), custom_call_target="tpu_custom_call" | custom-call | flops 1000000000 | bytes 1048576 | tf_op jit(solution)/shard_map/pallas_call | solution.py:638
  2.6 3.0 %collective-permute-start.1 = (bf16[144,768]{1,0:T(8,128)(2,1)}, bf16[144,768]{1,0:T(8,128)(2,1)S(1)}, u32[]{:S(2)}, u32[]{:S(2)}) collective-permute-start(bf16[144,768]{1,0:T(8,128)(2,1)} %get-tuple-element.76.b0), channel_id=1, source_target_pairs={{0,2},{2,0},{1,3},{3,1},{4,6},{6,4},{5,7},{7,5},{8,10},{10,8},{9,1... | collective-permute-start | bytes 663560 | tf_op jit(solution)/shard_map/ppermute | solution.py:664
  5.6 2.5 %collective-permute-start.5 = (f32[8,384]{1,0:T(8,128)}, f32[8,384]{1,0:T(8,128)S(1)}, u32[]{:S(2)}, u32[]{:S(2)}) collective-permute-start(f32[8,384]{1,0:T(8,128)} %get-tuple-element.77), channel_id=1, source_target_pairs={{0,12},{4,8},{8,4},{12,0},{16,28},{20,24},{24,20},{28,16},{1,13},{... | collective-permute-start | bytes 36872 | tf_op jit(solution)/shard_map/ppermute | solution.py:664
  8.1 0.4 collective-permute-start.4
  8.5 0.5 collective-permute-start.3
  9.1 0.5 shard_map.239.refs_10_
  9.6 1.7 %collective-permute-done.1.b2 = bf16[144,768]{1,0:T(8,128)(2,1)S(1)} collective-permute-done((bf16[144,768]{1,0:T(8,128)(2,1)}, bf16[144,768]{1,0:T(8,128)(2,1)S(1)}, u32[]{:S(2)}, u32[]{:S(2)}) %collective-permute-start.1) | collective-permute-done | bytes 221216 | tf_op jit(solution)/shard_map/ppermute | solution.py:664
  11.2 1.7 %collective-permute-start.8 = (bf16[320,512]{1,0:T(8,128)(2,1)S(1)}, bf16[320,512]{1,0:T(8,128)(2,1)S(1)}, u32[]{:S(2)}, u32[]{:S(2)}) collective-permute-start(bf16[320,512]{1,0:T(8,128)(2,1)S(1)} %shard_map.239.refs_10_), channel_id=1, source_target_pairs={{0,2},{2,0},{1,3},{3,1},{4,6},{6,4},{5,7},{7,5},{8,10},{10,8},{9,1... | collective-permute-start | bytes 983048 | tf_op jit(solution)/shard_map/ppermute | solution.py:664
  13.0 2.7 %collective-permute-start.6 = (f32[8,384]{1,0:T(8,128)S(1)}, f32[8,384]{1,0:T(8,128)S(1)}, u32[]{:S(2)}, u32[]{:S(2)}) collective-permute-start(f32[8,384]{1,0:T(8,128)S(1)} %add_add_fusion), channel_id=1, source_target_pairs={{0,16},{4,20},{8,24},{12,28},{16,0},{20,4},{24,8},{28,12},{1,17},{... | collective-permute-start | bytes 36872 | tf_op jit(solution)/shard_map/ppermute | solution.py:664
  15.9 1.8 %collective-permute-done.6 = f32[8,384]{1,0:T(8,128)S(1)} collective-permute-done((f32[8,384]{1,0:T(8,128)S(1)}, f32[8,384]{1,0:T(8,128)S(1)}, u32[]{:S(2)}, u32[]{:S(2)}) %collective-permute-start.6) | collective-permute-done | bytes 12320 | tf_op jit(solution)/shard_map/ppermute | solution.py:664
  17.7 2.2 %shard_map.238 = (bf16[1024,512]{1,0:T(8,128)(2,1)S(1)}, bf16[1024,512]{1,0:T(8,128)(2,1)S(1)}, f32[6,1048,128]{2,1,0:T(8,128)S(1)}, f32[8,512]{1,0:T(8,128)S(1)...) custom-call(bf16[1024,512]{1,0:T(8,128)(2,1)S(1)} %bitcast.20, ...), custom_call_target="tpu_custom_call" | custom-call | flops 2000000000 | bytes 1048576 | tf_op jit(solution)/shard_map/pallas_call | solution.py:638
  20.1 1.5 %collective-permute-start.11 = (f32[2,896]{1,0:T(2,128)S(1)}, f32[2,896]{1,0:T(2,128)S(1)}, u32[]{:S(2)}, u32[]{:S(2)}) collective-permute-start(f32[2,896]{1,0:T(2,128)S(1)} %get-tuple-element.87), channel_id=1, source_target_pairs={{0,8},{4,12},{8,16},{12,20},{16,24},{20,28},{24,0},{28,4},{1,9},{5... | collective-permute-start | bytes 21512 | tf_op jit(solution)/shard_map/ppermute | solution.py:706
  21.7 1.5 %collective-permute-start.10 = (f32[2,896]{1,0:T(2,128)S(1)}, f32[2,896]{1,0:T(2,128)S(1)}, u32[]{:S(2)}, u32[]{:S(2)}) collective-permute-start(f32[2,896]{1,0:T(2,128)S(1)} %get-tuple-element.87), channel_id=1, source_target_pairs={{0,4},{4,8},{8,12},{12,16},{16,20},{20,24},{24,28},{28,0},{1,5},{5... | collective-permute-start | bytes 21512 | tf_op jit(solution)/shard_map/ppermute | solution.py:706
  23.2 2.4 %collective-permute-done.11.refs_15_ = f32[2,896]{1,0:T(2,128)S(1)} collective-permute-done((f32[2,896]{1,0:T(2,128)S(1)}, f32[2,896]{1,0:T(2,128)S(1)}, u32[]{:S(2)}, u32[]{:S(2)}) %collective-permute-start.11) | collective-permute-done | bytes 7200 | tf_op jit(solution)/shard_map/ppermute | solution.py:706
  25.6 2.4 %collective-permute-done.10.refs_14_ = f32[2,896]{1,0:T(2,128)S(1)} collective-permute-done((f32[2,896]{1,0:T(2,128)S(1)}, f32[2,896]{1,0:T(2,128)S(1)}, u32[]{:S(2)}, u32[]{:S(2)}) %collective-permute-start.10) | collective-permute-done | bytes 7200 | tf_op jit(solution)/shard_map/ppermute | solution.py:706
  28.0 8.8 %shard_map.240 = (bf16[1024,512]{1,0:T(8,128)(2,1)}, f32[6,1048,128]{2,1,0:T(8,128)S(1)}, f32[6,1048,128]{2,1,0:T(8,128)S(1)}, bf16[1024,512]{1,0:T(8,128)(2,1)S...) custom-call(bf16[1024,512]{1,0:T(8,128)(2,1)S(1)} %bitcast.21, ...), custom_call_target="tpu_custom_call" | custom-call | flops 10000000000 | bytes 1048576 | tf_op jit(solution)/shard_map/pallas_call | solution.py:638
  36.9 0.5 collective-permute-start.13
  37.5 1.8 %collective-permute-start.12 = (f32[2,896]{1,0:T(2,128)S(1)}, f32[2,896]{1,0:T(2,128)S(1)}, u32[]{:S(2)}, u32[]{:S(2)}) collective-permute-start(f32[2,896]{1,0:T(2,128)S(1)} %get-tuple-element.97), channel_id=1, source_target_pairs={{4,0},{8,4},{12,8},{16,12},{20,16},{24,20},{28,24},{0,28},{5,1},{9... | collective-permute-start | bytes 21512 | tf_op jit(solution)/shard_map/ppermute | solution.py:717
  39.4 1.1 %collective-permute-start.15 = (bf16[160,512]{1,0:T(8,128)(2,1)S(1)}, bf16[160,512]{1,0:T(8,128)(2,1)S(1)}, u32[]{:S(2)}, u32[]{:S(2)}) collective-permute-start(bf16[160,512]{1,0:T(8,128)(2,1)S(1)} %get-tuple-element.103), channel_id=1, source_target_pairs={{0,6},{2,4},{4,2},{6,0},{8,14},{10,12},{12,10},{14,8},{16,22},{18,... | collective-permute-start | bytes 491528 | tf_op jit(solution)/shard_map/ppermute | solution.py:719
  40.6 0.5 collective-permute-done.12.refs_13_
  41.1 4.0 %shard_map.242 = (bf16[1024,512]{1,0:T(8,128)(2,1)S(1)}, bf16[2,208,512]{2,1,0:T(8,128)(2,1)S(1)}, bf16[2,208,512]{2,1,0:T(8,128)(2,1)S(1)}) custom-call(bf16[1024,512]{1,0:T(8,128)(2,1)S(1)} %get-tuple-element.90.refs_0_, f32[8,512]{1,0:T(8,128)S(1)} %get-tuple-element.91.refs_1_, f32[1048,128]{1,0:T(8,128)S(1)} %get-tuple-element.78.refs_2_, ...), custom_call_target="tpu_custom_call" | custom-call | flops 8000000000 | bytes 1048576 | tf_op jit(solution)/shard_map/pallas_call | solution.py:638
  45.1 1.3 %collective-permute-done.15.c3 = bf16[160,512]{1,0:T(8,128)(2,1)S(1)} collective-permute-done((bf16[160,512]{1,0:T(8,128)(2,1)S(1)}, bf16[160,512]{1,0:T(8,128)(2,1)S(1)}, u32[]{:S(2)}, u32[]{:S(2)}) %collective-permute-start.15) | collective-permute-done | bytes 163872 | tf_op jit(solution)/shard_map/ppermute | solution.py:719
  46.4 1.4 %collective-permute-start.20 = (bf16[160,512]{1,0:T(8,128)(2,1)S(1)}, bf16[160,512]{1,0:T(8,128)(2,1)S(1)}, u32[]{:S(2)}, u32[]{:S(2)}) collective-permute-start(bf16[160,512]{1,0:T(8,128)(2,1)S(1)} %get-tuple-element.101), channel_id=1, source_target_pairs={{0,2},{2,0},{4,6},{6,4},{8,10},{10,8},{12,14},{14,12},{16,18},{18,... | collective-permute-start | bytes 491528 | tf_op jit(solution)/shard_map/ppermute | solution.py:719
  47.8 0.4 collective-permute-start.21
  48.4 1.4 %collective-permute-start.17 = (bf16[112,512]{1,0:T(8,128)(2,1)S(1)}, bf16[112,512]{1,0:T(8,128)(2,1)S(1)}, u32[]{:S(2)}, u32[]{:S(2)}) collective-permute-start(bf16[112,512]{1,0:T(8,128)(2,1)S(1)} %get-tuple-element.110), channel_id=1, source_target_pairs={{0,2},{2,0},{4,6},{6,4},{8,10},{10,8},{12,14},{14,12},{16,18},{18,... | collective-permute-start | bytes 344072 | tf_op jit(solution)/shard_map/ppermute | solution.py:719
  49.8 0.8 %collective-permute-start.18 = (bf16[112,512]{1,0:T(8,128)(2,1)S(1)}, bf16[112,512]{1,0:T(8,128)(2,1)S(1)}, u32[]{:S(2)}, u32[]{:S(2)}) collective-permute-start(bf16[112,512]{1,0:T(8,128)(2,1)S(1)} %get-tuple-element.111), channel_id=1, source_target_pairs={{0,4},{2,6},{4,0},{6,2},{8,12},{10,14},{12,8},{14,10},{16,20},{18,... | collective-permute-start | bytes 344072 | tf_op jit(solution)/shard_map/ppermute | solution.py:719
  50.6 1.3 %collective-permute-start.19 = (bf16[112,512]{1,0:T(8,128)(2,1)S(1)}, bf16[112,512]{1,0:T(8,128)(2,1)S(1)}, u32[]{:S(2)}, u32[]{:S(2)}) collective-permute-start(bf16[112,512]{1,0:T(8,128)(2,1)S(1)} %get-tuple-element.112), channel_id=1, source_target_pairs={{0,6},{2,4},{4,2},{6,0},{8,14},{10,12},{12,10},{14,8},{16,22},{18,... | collective-permute-start | bytes 344072 | tf_op jit(solution)/shard_map/ppermute | solution.py:719
  52.0 1.4 %shard_map.244.ig_ref = bf16[1024,512]{1,0:T(8,128)(2,1)S(1)} custom-call(bf16[1024,512]{1,0:T(8,128)(2,1)S(1)} %bitcast.22, bf16[1024,512]{1,0:T(8,128)(2,1)S(1)} %get-tuple-element.113.gn_ref, bf16[1024,512]{1,0:T(8,128)(2,1)S(1)} %get-tuple-element.114.gres_ref, f32[8,512]{1,0:T(8,128)S(1)} %get-tuple-element.85.refs_9_.refs_11_.vec_ref), custom_call_target="tpu_custom_call" | custom-call | flops 3000000000 | bytes 1048576 | tf_op jit(solution)/shard_map/pallas_call | solution.py:638
  53.4 1.5 %collective-permute-done.21.c2 = bf16[160,512]{1,0:T(8,128)(2,1)S(1)} collective-permute-done((bf16[160,512]{1,0:T(8,128)(2,1)S(1)}, bf16[160,512]{1,0:T(8,128)(2,1)S(1)}, u32[]{:S(2)}, u32[]{:S(2)}) %collective-permute-start.21) | collective-permute-done | bytes 163872 | tf_op jit(solution)/shard_map/ppermute | solution.py:719
  55.0 0.5 collective-permute-done.17.refs_1_
  55.5 1.9 %collective-permute-done.18.refs_2_ = bf16[112,512]{1,0:T(8,128)(2,1)S(1)} collective-permute-done((bf16[112,512]{1,0:T(8,128)(2,1)S(1)}, bf16[112,512]{1,0:T(8,128)(2,1)S(1)}, u32[]{:S(2)}, u32[]{:S(2)}) %collective-permute-start.18) | collective-permute-done | bytes 114720 | tf_op jit(solution)/shard_map/ppermute | solution.py:719
  57.3 1.8 %collective-permute-done.19.refs_3_ = bf16[112,512]{1,0:T(8,128)(2,1)S(1)} collective-permute-done((bf16[112,512]{1,0:T(8,128)(2,1)S(1)}, bf16[112,512]{1,0:T(8,128)(2,1)S(1)}, u32[]{:S(2)}, u32[]{:S(2)}) %collective-permute-start.19) | collective-permute-done | bytes 114720 | tf_op jit(solution)/shard_map/ppermute | solution.py:719
  59.6 2.5 %collective-permute-start.23 = (bf16[72,512]{1,0:T(8,128)(2,1)S(1)}, bf16[72,512]{1,0:T(8,128)(2,1)S(1)}, u32[]{:S(2)}, u32[]{:S(2)}) collective-permute-start(bf16[72,512]{1,0:T(8,128)(2,1)S(1)} %get-tuple-element.121), channel_id=1, source_target_pairs={{0,16},{4,20},{8,24},{12,28},{16,0},{20,4},{24,8},{28,12},{1,17},{... | collective-permute-start | bytes 221192 | tf_op jit(solution)/shard_map/ppermute | solution.py:664
  62.1 1.6 %collective-permute-start.24 = (bf16[72,512]{1,0:T(8,128)(2,1)S(1)}, bf16[72,512]{1,0:T(8,128)(2,1)S(1)}, u32[]{:S(2)}, u32[]{:S(2)}) collective-permute-start(bf16[72,512]{1,0:T(8,128)(2,1)S(1)} %get-tuple-element.122), channel_id=1, source_target_pairs={{0,24},{4,28},{8,16},{12,20},{16,8},{20,12},{24,0},{28,4},{1,25},{... | collective-permute-start | bytes 221192 | tf_op jit(solution)/shard_map/ppermute | solution.py:664
  63.8 3.4 %collective-permute-done.23.refs_2_ = bf16[72,512]{1,0:T(8,128)(2,1)S(1)} collective-permute-done((bf16[72,512]{1,0:T(8,128)(2,1)S(1)}, bf16[72,512]{1,0:T(8,128)(2,1)S(1)}, u32[]{:S(2)}, u32[]{:S(2)}) %collective-permute-start.23) | collective-permute-done | bytes 73760 | tf_op jit(solution)/shard_map/ppermute | solution.py:664
  67.2 1.1 %collective-permute-done.24.refs_3_ = bf16[72,512]{1,0:T(8,128)(2,1)S(1)} collective-permute-done((bf16[72,512]{1,0:T(8,128)(2,1)S(1)}, bf16[72,512]{1,0:T(8,128)(2,1)S(1)}, u32[]{:S(2)}, u32[]{:S(2)}) %collective-permute-start.24) | collective-permute-done | bytes 73760 | tf_op jit(solution)/shard_map/ppermute | solution.py:664
  68.4 1.1 %collective-permute-start.25 = (bf16[64,512]{1,0:T(8,128)(2,1)S(1)}, bf16[64,512]{1,0:T(8,128)(2,1)S(1)}, u32[]{:S(2)}, u32[]{:S(2)}) collective-permute-start(bf16[64,512]{1,0:T(8,128)(2,1)S(1)} %get-tuple-element.130.refs_0_), channel_id=1, source_target_pairs={{0,8},{4,12},{8,0},{12,4},{16,24},{20,28},{24,16},{28,20},{1,9},{5... | collective-permute-start | bytes 196616 | tf_op jit(solution)/shard_map/ppermute | solution.py:664
  69.5 2.0 %collective-permute-start.30 = (bf16[64,512]{1,0:T(8,128)(2,1)S(1)}, bf16[64,512]{1,0:T(8,128)(2,1)S(1)}, u32[]{:S(2)}, u32[]{:S(2)}) collective-permute-start(bf16[64,512]{1,0:T(8,128)(2,1)S(1)} %get-tuple-element.130.refs_0_), channel_id=1, source_target_pairs={{0,24},{4,28},{8,16},{12,20},{16,8},{20,12},{24,0},{28,4},{1,25},{... | collective-permute-start | bytes 196616 | tf_op jit(solution)/shard_map/ppermute | solution.py:664
  71.4 0.5 collective-permute-start.28
  71.9 0.8 %collective-permute-done.25.refs_2_ = bf16[64,512]{1,0:T(8,128)(2,1)S(1)} collective-permute-done((bf16[64,512]{1,0:T(8,128)(2,1)S(1)}, bf16[64,512]{1,0:T(8,128)(2,1)S(1)}, u32[]{:S(2)}, u32[]{:S(2)}) %collective-permute-start.25) | collective-permute-done | bytes 65568 | tf_op jit(solution)/shard_map/ppermute | solution.py:664
  72.8 1.6 %collective-permute-start.26 = (bf16[64,512]{1,0:T(8,128)(2,1)S(1)}, bf16[64,512]{1,0:T(8,128)(2,1)S(1)}, u32[]{:S(2)}, u32[]{:S(2)}) collective-permute-start(bf16[64,512]{1,0:T(8,128)(2,1)S(1)} %get-tuple-element.130.refs_0_), channel_id=1, source_target_pairs={{0,4},{4,0},{8,12},{12,8},{16,20},{20,16},{24,28},{28,24},{1,5},{5... | collective-permute-start | bytes 196616 | tf_op jit(solution)/shard_map/ppermute | solution.py:664
  74.8 0.7 collective-permute-done.30.refs_6_
  75.5 0.9 %collective-permute-start.31 = (bf16[64,512]{1,0:T(8,128)(2,1)S(1)}, bf16[64,512]{1,0:T(8,128)(2,1)S(1)}, u32[]{:S(2)}, u32[]{:S(2)}) collective-permute-start(bf16[64,512]{1,0:T(8,128)(2,1)S(1)} %collective-permute-done.30.refs_6_), channel_id=1, source_target_pairs={{0,4},{4,0},{8,12},{12,8},{16,20},{20,16},{24,28},{28,24},{1,5},{5... | collective-permute-start | bytes 196616 | tf_op jit(solution)/shard_map/ppermute | solution.py:664
  76.4 0.5 collective-permute-done.28.refs_4_
  76.9 1.4 %collective-permute-start.29 = (bf16[64,512]{1,0:T(8,128)(2,1)S(1)}, bf16[64,512]{1,0:T(8,128)(2,1)S(1)}, u32[]{:S(2)}, u32[]{:S(2)}) collective-permute-start(bf16[64,512]{1,0:T(8,128)(2,1)S(1)} %collective-permute-done.28.refs_4_), channel_id=1, source_target_pairs={{0,4},{4,0},{8,12},{12,8},{16,20},{20,16},{24,28},{28,24},{1,5},{5... | collective-permute-start | bytes 196616 | tf_op jit(solution)/shard_map/ppermute | solution.py:664
  78.3 1.5 %shard_map.248 = (f32[1024,512]{1,0:T(8,128)}, f32[1,1]{1,0:T(1,128)}, f32[1,128]{1,0:T(1,128)}, f32[1,128]{1,0:T(1,128)}, f32[1,128]{1,0:T(1,128)}, /*index=5*/...) custom-call(f32[8,512]{1,0:T(8,128)S(1)} %get-tuple-element.123.tail_ref, ...), custom_call_target="tpu_custom_call" | custom-call | flops 1000000000 | bytes 1048576 | tf_op jit(solution)/shard_map/pallas_call | solution.py:638
  79.9 1.3 %collective-permute-done.29.refs_5_ = bf16[64,512]{1,0:T(8,128)(2,1)S(1)} collective-permute-done((bf16[64,512]{1,0:T(8,128)(2,1)S(1)}, bf16[64,512]{1,0:T(8,128)(2,1)S(1)}, u32[]{:S(2)}, u32[]{:S(2)}) %collective-permute-start.29) | collective-permute-done | bytes 65568 | tf_op jit(solution)/shard_map/ppermute | solution.py:664
  81.2 1.1 %shard_map.249 = (f32[128,768]{1,0:T(8,128)}, f32[192,512]{1,0:T(8,128)}, f32[128,512]{1,0:T(8,128)}) custom-call(f32[8,512]{1,0:T(8,128)S(1)} %get-tuple-element.123.tail_ref, bf16[64,512]{1,0:T(8,128)(2,1)S(1)} %get-tuple-element.130.refs_0_, bf16[64,512]{1,0:T(8,128)(2,1)S(1)} %collective-permute-done.26.refs_1_, ...), custom_call_target="tpu_custom_call" | custom-call | flops 1000000000 | bytes 1048576 | tf_op jit(solution)/shard_map/pallas_call | solution.py:638
  (47 shorter events, 2.0 us)
Async XLA Ops:
  0.6 8.4 %copy-start.4 = (bf16[128,512]{1,0:T(8,128)(2,1)S(1)}, bf16[128,512]{1,0:T(8,128)(2,1)}, u32[]{:S(2)}) copy-start(bf16[128,512]{1,0:T(8,128)(2,1)} %g_ref.1) | copy-start | bytes 393220
  0.7 8.4 %copy-start.3 = (bf16[192,512]{1,0:T(8,128)(2,1)S(1)}, bf16[192,512]{1,0:T(8,128)(2,1)}, u32[]{:S(2)}) copy-start(bf16[192,512]{1,0:T(8,128)(2,1)} %c_ref.1) | copy-start | bytes 589828
  0.7 17.0 %copy-start.1 = (bf16[2,512,512]{2,1,0:T(8,128)(2,1)S(1)}, bf16[2,512,512]{2,1,0:T(8,128)(2,1)}, u32[]{:S(2)}) copy-start(bf16[2,512,512]{2,1,0:T(8,128)(2,1)} %param.14) | copy-start | bytes 3145732
  0.7 17.0 %copy-start.5 = (s32[2,512]{1,0:T(2,128)S(1)}, s32[2,512]{1,0:T(2,128)}, u32[]{:S(2)}) copy-start(s32[2,512]{1,0:T(2,128)} %seg_ref.1) | copy-start | bytes 12292
  0.7 17.0 %copy-start.6 = (s32[2,512]{1,0:T(2,128)S(1)}, s32[2,512]{1,0:T(2,128)}, u32[]{:S(2)}) copy-start(s32[2,512]{1,0:T(2,128)} %mask_ref.1) | copy-start | bytes 12292
  2.5 10.5 %copy-start.7 = (f32[8,384]{1,0:T(8,128)S(1)}, f32[8,384]{1,0:T(8,128)}, u32[]{:S(2)}) copy-start(f32[8,384]{1,0:T(8,128)} %get-tuple-element.77) | copy-start | bytes 36868
  2.5 15.2 %copy-start.2 = (bf16[144,768]{1,0:T(8,128)(2,1)S(1)}, bf16[144,768]{1,0:T(8,128)(2,1)}, u32[]{:S(2)}) copy-start(bf16[144,768]{1,0:T(8,128)(2,1)} %get-tuple-element.76.b0) | copy-start | bytes 663556
  2.6 8.7 %collective-permute-start.1 = (bf16[144,768]{1,0:T(8,128)(2,1)}, bf16[144,768]{1,0:T(8,128)(2,1)S(1)}, u32[]{:S(2)}, u32[]{:S(2)}) collective-permute-start(bf16[144,768]{1,0:T(8,128)(2,1)} %get-tuple-element.76.b0), channel_id=1, source_target_pairs={{0,2},{2,0},{1,3},{3,1},{4,6},{6,4},{5,7},{7,5},{8,10},{10,8},{9,1... | collective-permute-start | bytes 663560 | tf_op jit(solution)/shard_map/ppermute | solution.py:664
  5.6 7.4 %collective-permute-start.5 = (f32[8,384]{1,0:T(8,128)}, f32[8,384]{1,0:T(8,128)S(1)}, u32[]{:S(2)}, u32[]{:S(2)}) collective-permute-start(f32[8,384]{1,0:T(8,128)} %get-tuple-element.77), channel_id=1, source_target_pairs={{0,12},{4,8},{8,4},{12,0},{16,28},{20,24},{24,20},{28,16},{1,13},{... | collective-permute-start | bytes 36872 | tf_op jit(solution)/shard_map/ppermute | solution.py:664
  8.1 4.9 %collective-permute-start.4 = (f32[8,384]{1,0:T(8,128)}, f32[8,384]{1,0:T(8,128)S(1)}, u32[]{:S(2)}, u32[]{:S(2)}) collective-permute-start(f32[8,384]{1,0:T(8,128)} %get-tuple-element.77), channel_id=1, source_target_pairs={{0,8},{4,12},{8,0},{12,4},{16,24},{20,28},{24,16},{28,20},{1,9},{5... | collective-permute-start | bytes 36872 | tf_op jit(solution)/shard_map/ppermute | solution.py:664
  8.5 4.4 %collective-permute-start.3 = (f32[8,384]{1,0:T(8,128)}, f32[8,384]{1,0:T(8,128)S(1)}, u32[]{:S(2)}, u32[]{:S(2)}) collective-permute-start(f32[8,384]{1,0:T(8,128)} %get-tuple-element.77), channel_id=1, source_target_pairs={{0,4},{4,0},{8,12},{12,8},{16,20},{20,16},{24,28},{28,24},{1,5},{5... | collective-permute-start | bytes 36872 | tf_op jit(solution)/shard_map/ppermute | solution.py:664
  9.1 8.6 %collective-permute-start = (bf16[144,768]{1,0:T(8,128)(2,1)}, bf16[144,768]{1,0:T(8,128)(2,1)S(1)}, u32[]{:S(2)}, u32[]{:S(2)}) collective-permute-start(bf16[144,768]{1,0:T(8,128)(2,1)} %get-tuple-element.76.b0), channel_id=1, source_target_pairs={{0,1},{1,0},{2,3},{3,2},{4,5},{5,4},{6,7},{7,6},{8,9},{9,8},{10,11... | collective-permute-start | bytes 663560 | tf_op jit(solution)/shard_map/ppermute | solution.py:664
  11.2 8.9 %collective-permute-start.8 = (bf16[320,512]{1,0:T(8,128)(2,1)S(1)}, bf16[320,512]{1,0:T(8,128)(2,1)S(1)}, u32[]{:S(2)}, u32[]{:S(2)}) collective-permute-start(bf16[320,512]{1,0:T(8,128)(2,1)S(1)} %shard_map.239.refs_10_), channel_id=1, source_target_pairs={{0,2},{2,0},{1,3},{3,1},{4,6},{6,4},{5,7},{7,5},{8,10},{10,8},{9,1... | collective-permute-start | bytes 983048 | tf_op jit(solution)/shard_map/ppermute | solution.py:664
  13.0 4.7 %collective-permute-start.2 = (bf16[144,768]{1,0:T(8,128)(2,1)S(1)}, bf16[144,768]{1,0:T(8,128)(2,1)S(1)}, u32[]{:S(2)}, u32[]{:S(2)}) collective-permute-start(bf16[144,768]{1,0:T(8,128)(2,1)S(1)} %collective-permute-done.1.b2), channel_id=1, source_target_pairs={{0,1},{1,0},{2,3},{3,2},{4,5},{5,4},{6,7},{7,6},{8,9},{9,8},{10,11... | collective-permute-start | bytes 663560 | tf_op jit(solution)/shard_map/ppermute | solution.py:664
  13.0 4.7 %collective-permute-start.6 = (f32[8,384]{1,0:T(8,128)S(1)}, f32[8,384]{1,0:T(8,128)S(1)}, u32[]{:S(2)}, u32[]{:S(2)}) collective-permute-start(f32[8,384]{1,0:T(8,128)S(1)} %add_add_fusion), channel_id=1, source_target_pairs={{0,16},{4,20},{8,24},{12,28},{16,0},{20,4},{24,8},{28,12},{1,17},{... | collective-permute-start | bytes 36872 | tf_op jit(solution)/shard_map/ppermute | solution.py:664
  15.7 7.5 %collective-permute-start.7 = (bf16[320,512]{1,0:T(8,128)(2,1)S(1)}, bf16[320,512]{1,0:T(8,128)(2,1)S(1)}, u32[]{:S(2)}, u32[]{:S(2)}) collective-permute-start(bf16[320,512]{1,0:T(8,128)(2,1)S(1)} %shard_map.239.refs_10_), channel_id=1, source_target_pairs={{0,1},{1,0},{2,3},{3,2},{4,5},{5,4},{6,7},{7,6},{8,9},{9,8},{10,11... | collective-permute-start | bytes 983048 | tf_op jit(solution)/shard_map/ppermute | solution.py:664
  17.7 10.3 %copy-start = (bf16[2,512,512]{2,1,0:T(8,128)(2,1)S(1)}, bf16[2,512,512]{2,1,0:T(8,128)(2,1)}, u32[]{:S(2)}) copy-start(bf16[2,512,512]{2,1,0:T(8,128)(2,1)} %param.15) | copy-start | bytes 3145732
  20.1 7.9 %collective-permute-start.9 = (bf16[320,512]{1,0:T(8,128)(2,1)S(1)}, bf16[320,512]{1,0:T(8,128)(2,1)S(1)}, u32[]{:S(2)}, u32[]{:S(2)}) collective-permute-start(bf16[320,512]{1,0:T(8,128)(2,1)S(1)} %collective-permute-done.8.refs_12_), channel_id=1, source_target_pairs={{0,1},{1,0},{2,3},{3,2},{4,5},{5,4},{6,7},{7,6},{8,9},{9,8},{10,11... | collective-permute-start | bytes 983048 | tf_op jit(solution)/shard_map/ppermute | solution.py:664
  20.1 5.4 %collective-permute-start.11 = (f32[2,896]{1,0:T(2,128)S(1)}, f32[2,896]{1,0:T(2,128)S(1)}, u32[]{:S(2)}, u32[]{:S(2)}) collective-permute-start(f32[2,896]{1,0:T(2,128)S(1)} %get-tuple-element.87), channel_id=1, source_target_pairs={{0,8},{4,12},{8,16},{12,20},{16,24},{20,28},{24,0},{28,4},{1,9},{5... | collective-permute-start | bytes 21512 | tf_op jit(solution)/shard_map/ppermute | solution.py:706
  21.7 6.3 %collective-permute-start.10 = (f32[2,896]{1,0:T(2,128)S(1)}, f32[2,896]{1,0:T(2,128)S(1)}, u32[]{:S(2)}, u32[]{:S(2)}) collective-permute-start(f32[2,896]{1,0:T(2,128)S(1)} %get-tuple-element.87), channel_id=1, source_target_pairs={{0,4},{4,8},{8,12},{12,16},{16,20},{20,24},{24,28},{28,0},{1,5},{5... | collective-permute-start | bytes 21512 | tf_op jit(solution)/shard_map/ppermute | solution.py:706
  36.8 2.4 %collective-permute-start.14 = (bf16[2,320,512]{2,1,0:T(8,128)(2,1)S(1)}, bf16[2,320,512]{2,1,0:T(8,128)(2,1)S(1)}, u32[]{:S(2)}, u32[]{:S(2)}) collective-permute-start(bf16[2,320,512]{2,1,0:T(8,128)(2,1)S(1)} %get-tuple-element.99), channel_id=1, source_target_pairs={{0,1},{1,0},{2,3},{3,2},{4,5},{5,4},{6,7},{7,6},{8,9},{9,8},{10,11... | collective-permute-start | bytes 1966088 | tf_op jit(solution)/shard_map/ppermute | solution.py:664
  36.9 3.7 %collective-permute-start.13 = (f32[2,896]{1,0:T(2,128)S(1)}, f32[2,896]{1,0:T(2,128)S(1)}, u32[]{:S(2)}, u32[]{:S(2)}) collective-permute-start(f32[2,896]{1,0:T(2,128)S(1)} %get-tuple-element.97), channel_id=1, source_target_pairs={{8,0},{12,4},{16,8},{20,12},{24,16},{28,20},{0,24},{4,28},{9,1},{1... | collective-permute-start | bytes 21512 | tf_op jit(solution)/shard_map/ppermute | solution.py:717
  37.5 3.6 %collective-permute-start.12 = (f32[2,896]{1,0:T(2,128)S(1)}, f32[2,896]{1,0:T(2,128)S(1)}, u32[]{:S(2)}, u32[]{:S(2)}) collective-permute-start(f32[2,896]{1,0:T(2,128)S(1)} %get-tuple-element.97), channel_id=1, source_target_pairs={{4,0},{8,4},{12,8},{16,12},{20,16},{24,20},{28,24},{0,28},{5,1},{9... | collective-permute-start | bytes 21512 | tf_op jit(solution)/shard_map/ppermute | solution.py:717
  39.4 7.0 %collective-permute-start.15 = (bf16[160,512]{1,0:T(8,128)(2,1)S(1)}, bf16[160,512]{1,0:T(8,128)(2,1)S(1)}, u32[]{:S(2)}, u32[]{:S(2)}) collective-permute-start(bf16[160,512]{1,0:T(8,128)(2,1)S(1)} %get-tuple-element.103), channel_id=1, source_target_pairs={{0,6},{2,4},{4,2},{6,0},{8,14},{10,12},{12,10},{14,8},{16,22},{18,... | collective-permute-start | bytes 491528 | tf_op jit(solution)/shard_map/ppermute | solution.py:719
  46.4 1.9 %collective-permute-start.16 = (bf16[2,208,512]{2,1,0:T(8,128)(2,1)S(1)}, bf16[2,208,512]{2,1,0:T(8,128)(2,1)S(1)}, u32[]{:S(2)}, u32[]{:S(2)}) collective-permute-start(bf16[2,208,512]{2,1,0:T(8,128)(2,1)S(1)} %get-tuple-element.108), channel_id=1, source_target_pairs={{0,1},{1,0},{2,3},{3,2},{4,5},{5,4},{6,7},{7,6},{8,9},{9,8},{10,11... | collective-permute-start | bytes 1277960 | tf_op jit(solution)/shard_map/ppermute | solution.py:664
  46.4 7.0 %collective-permute-start.20 = (bf16[160,512]{1,0:T(8,128)(2,1)S(1)}, bf16[160,512]{1,0:T(8,128)(2,1)S(1)}, u32[]{:S(2)}, u32[]{:S(2)}) collective-permute-start(bf16[160,512]{1,0:T(8,128)(2,1)S(1)} %get-tuple-element.101), channel_id=1, source_target_pairs={{0,2},{2,0},{4,6},{6,4},{8,10},{10,8},{12,14},{14,12},{16,18},{18,... | collective-permute-start | bytes 491528 | tf_op jit(solution)/shard_map/ppermute | solution.py:719
  47.8 7.0 %collective-permute-start.21 = (bf16[160,512]{1,0:T(8,128)(2,1)S(1)}, bf16[160,512]{1,0:T(8,128)(2,1)S(1)}, u32[]{:S(2)}, u32[]{:S(2)}) collective-permute-start(bf16[160,512]{1,0:T(8,128)(2,1)S(1)} %get-tuple-element.102), channel_id=1, source_target_pairs={{0,4},{2,6},{4,0},{6,2},{8,12},{10,14},{12,8},{14,10},{16,20},{18,... | collective-permute-start | bytes 491528 | tf_op jit(solution)/shard_map/ppermute | solution.py:719
  48.4 7.1 %collective-permute-start.17 = (bf16[112,512]{1,0:T(8,128)(2,1)S(1)}, bf16[112,512]{1,0:T(8,128)(2,1)S(1)}, u32[]{:S(2)}, u32[]{:S(2)}) collective-permute-start(bf16[112,512]{1,0:T(8,128)(2,1)S(1)} %get-tuple-element.110), channel_id=1, source_target_pairs={{0,2},{2,0},{4,6},{6,4},{8,10},{10,8},{12,14},{14,12},{16,18},{18,... | collective-permute-start | bytes 344072 | tf_op jit(solution)/shard_map/ppermute | solution.py:719
  49.8 7.5 %collective-permute-start.18 = (bf16[112,512]{1,0:T(8,128)(2,1)S(1)}, bf16[112,512]{1,0:T(8,128)(2,1)S(1)}, u32[]{:S(2)}, u32[]{:S(2)}) collective-permute-start(bf16[112,512]{1,0:T(8,128)(2,1)S(1)} %get-tuple-element.111), channel_id=1, source_target_pairs={{0,4},{2,6},{4,0},{6,2},{8,12},{10,14},{12,8},{14,10},{16,20},{18,... | collective-permute-start | bytes 344072 | tf_op jit(solution)/shard_map/ppermute | solution.py:719
  50.6 8.5 %collective-permute-start.19 = (bf16[112,512]{1,0:T(8,128)(2,1)S(1)}, bf16[112,512]{1,0:T(8,128)(2,1)S(1)}, u32[]{:S(2)}, u32[]{:S(2)}) collective-permute-start(bf16[112,512]{1,0:T(8,128)(2,1)S(1)} %get-tuple-element.112), channel_id=1, source_target_pairs={{0,6},{2,4},{4,2},{6,0},{8,14},{10,12},{12,10},{14,8},{16,22},{18,... | collective-permute-start | bytes 344072 | tf_op jit(solution)/shard_map/ppermute | solution.py:719
  59.2 4.6 %collective-permute-start.22 = (bf16[72,512]{1,0:T(8,128)(2,1)S(1)}, bf16[72,512]{1,0:T(8,128)(2,1)S(1)}, u32[]{:S(2)}, u32[]{:S(2)}) collective-permute-start(bf16[72,512]{1,0:T(8,128)(2,1)S(1)} %get-tuple-element.120), channel_id=1, source_target_pairs={{0,8},{4,12},{8,0},{12,4},{16,24},{20,28},{24,16},{28,20},{1,9},{5... | collective-permute-start | bytes 221192 | tf_op jit(solution)/shard_map/ppermute | solution.py:664
  59.6 7.6 %collective-permute-start.23 = (bf16[72,512]{1,0:T(8,128)(2,1)S(1)}, bf16[72,512]{1,0:T(8,128)(2,1)S(1)}, u32[]{:S(2)}, u32[]{:S(2)}) collective-permute-start(bf16[72,512]{1,0:T(8,128)(2,1)S(1)} %get-tuple-element.121), channel_id=1, source_target_pairs={{0,16},{4,20},{8,24},{12,28},{16,0},{20,4},{24,8},{28,12},{1,17},{... | collective-permute-start | bytes 221192 | tf_op jit(solution)/shard_map/ppermute | solution.py:664
  62.1 6.3 %collective-permute-start.24 = (bf16[72,512]{1,0:T(8,128)(2,1)S(1)}, bf16[72,512]{1,0:T(8,128)(2,1)S(1)}, u32[]{:S(2)}, u32[]{:S(2)}) collective-permute-start(bf16[72,512]{1,0:T(8,128)(2,1)S(1)} %get-tuple-element.122), channel_id=1, source_target_pairs={{0,24},{4,28},{8,16},{12,20},{16,8},{20,12},{24,0},{28,4},{1,25},{... | collective-permute-start | bytes 221192 | tf_op jit(solution)/shard_map/ppermute | solution.py:664
  68.4 4.4 %collective-permute-start.25 = (bf16[64,512]{1,0:T(8,128)(2,1)S(1)}, bf16[64,512]{1,0:T(8,128)(2,1)S(1)}, u32[]{:S(2)}, u32[]{:S(2)}) collective-permute-start(bf16[64,512]{1,0:T(8,128)(2,1)S(1)} %get-tuple-element.130.refs_0_), channel_id=1, source_target_pairs={{0,8},{4,12},{8,0},{12,4},{16,24},{20,28},{24,16},{28,20},{1,9},{5... | collective-permute-start | bytes 196616 | tf_op jit(solution)/shard_map/ppermute | solution.py:664
  69.5 6.1 %collective-permute-start.30 = (bf16[64,512]{1,0:T(8,128)(2,1)S(1)}, bf16[64,512]{1,0:T(8,128)(2,1)S(1)}, u32[]{:S(2)}, u32[]{:S(2)}) collective-permute-start(bf16[64,512]{1,0:T(8,128)(2,1)S(1)} %get-tuple-element.130.refs_0_), channel_id=1, source_target_pairs={{0,24},{4,28},{8,16},{12,20},{16,8},{20,12},{24,0},{28,4},{1,25},{... | collective-permute-start | bytes 196616 | tf_op jit(solution)/shard_map/ppermute | solution.py:664
  71.4 5.5 %collective-permute-start.28 = (bf16[64,512]{1,0:T(8,128)(2,1)S(1)}, bf16[64,512]{1,0:T(8,128)(2,1)S(1)}, u32[]{:S(2)}, u32[]{:S(2)}) collective-permute-start(bf16[64,512]{1,0:T(8,128)(2,1)S(1)} %get-tuple-element.130.refs_0_), channel_id=1, source_target_pairs={{0,16},{4,20},{8,24},{12,28},{16,0},{20,4},{24,8},{28,12},{1,17},{... | collective-permute-start | bytes 196616 | tf_op jit(solution)/shard_map/ppermute | solution.py:664
  72.8 8.4 %collective-permute-start.26 = (bf16[64,512]{1,0:T(8,128)(2,1)S(1)}, bf16[64,512]{1,0:T(8,128)(2,1)S(1)}, u32[]{:S(2)}, u32[]{:S(2)}) collective-permute-start(bf16[64,512]{1,0:T(8,128)(2,1)S(1)} %get-tuple-element.130.refs_0_), channel_id=1, source_target_pairs={{0,4},{4,0},{8,12},{12,8},{16,20},{20,16},{24,28},{28,24},{1,5},{5... | collective-permute-start | bytes 196616 | tf_op jit(solution)/shard_map/ppermute | solution.py:664
  74.4 6.8 %collective-permute-start.27 = (bf16[64,512]{1,0:T(8,128)(2,1)S(1)}, bf16[64,512]{1,0:T(8,128)(2,1)S(1)}, u32[]{:S(2)}, u32[]{:S(2)}) collective-permute-start(bf16[64,512]{1,0:T(8,128)(2,1)S(1)} %collective-permute-done.25.refs_2_), channel_id=1, source_target_pairs={{0,4},{4,0},{8,12},{12,8},{16,20},{20,16},{24,28},{28,24},{1,5},{5... | collective-permute-start | bytes 196616 | tf_op jit(solution)/shard_map/ppermute | solution.py:664
  75.5 4.3 %collective-permute-start.31 = (bf16[64,512]{1,0:T(8,128)(2,1)S(1)}, bf16[64,512]{1,0:T(8,128)(2,1)S(1)}, u32[]{:S(2)}, u32[]{:S(2)}) collective-permute-start(bf16[64,512]{1,0:T(8,128)(2,1)S(1)} %collective-permute-done.30.refs_6_), channel_id=1, source_target_pairs={{0,4},{4,0},{8,12},{12,8},{16,20},{20,16},{24,28},{28,24},{1,5},{5... | collective-permute-start | bytes 196616 | tf_op jit(solution)/shard_map/ppermute | solution.py:664
  76.9 4.3 %collective-permute-start.29 = (bf16[64,512]{1,0:T(8,128)(2,1)S(1)}, bf16[64,512]{1,0:T(8,128)(2,1)S(1)}, u32[]{:S(2)}, u32[]{:S(2)}) collective-permute-start(bf16[64,512]{1,0:T(8,128)(2,1)S(1)} %collective-permute-done.28.refs_4_), channel_id=1, source_target_pairs={{0,4},{4,0},{8,12},{12,8},{16,20},{20,16},{24,28},{28,24},{1,5},{5... | collective-permute-start | bytes 196616 | tf_op jit(solution)/shard_map/ppermute | solution.py:664

commit v9 on v7

--- a/solution.py
+++ b/solution.py
@@ -439,7 +439,7 @@
     (n_ref, sums_ref, link_ref, ids_ref, low_ref, proj_ref, state_ref, gs_ref, gssm_ref,
      s2_ref, rates_ref, vec_ref, w_full) = refs[:13]
     recvs = refs[13 : 13 + hops]
-    (gn_ref, send_ref, keep_ref, gp_scr, gpl_scr, gb_scr, vec_scr) = refs[13 + hops :]
+    (gn_ref, send_ref, keep_ref, gp_scr, gb_scr, vec_scr) = refs[13 + hops :]
     rows, width = n_ref.shape
     states = rates_ref.shape[1]
     groups = states // LANES
@@ -493,12 +493,11 @@
     for i in range(rows // TILE):
         at = slice(i * TILE, (i + 1) * TILE)
         gpl = take(gp_scr, padded(i, block_len), 0, 2 * groups).astype(BF16)
-        gpl_scr[at, :] = gpl
+        add_to(gb_scr, i, tn_dot(low_ref[at, :], gpl))
         gn = nt_dot(gpl, w_full[...]) + skip * gssm_ref[at, :]
         gn_ref[at, :] = gn.astype(BF16)
         gain_acc = gain_acc + fold_rows(gn * n_ref[at, :].astype(F32))
         bias_acc = bias_acc + fold_rows(gn)
-    gb_scr[...] = tn_dot(low_ref[...], gpl_scr[...])
     sums4 = [one_row(v) for v in rate_sums]
     rate_grads = []
     for k in range(3):
@@ -734,7 +733,7 @@
     gn, send_b, keep_b = call(
         functools.partial(k3_body, seqs=seqs, hops=hops, blocks=S),
         [((rows, width), BF16), ((2, b_bulk + 16, width), BF16), ((2, b_bulk + 16, width), BF16)],
-        [(slab, F32), ((rows, 2 * states), BF16), ((width, 2 * states), F32), ((8, width), F32)],
+        [(slab, F32), ((width, 2 * states), F32), ((8, width), F32)],
         norm, sums, link, ids, low, proj, state, gs, gssm, s2, rates, vec, w_full, *bwds, us=8, limit=14,
     )
     (c_sum,) = call(sum_body, [((c_bulk // 2, width), F32)], [], *part_c, limit=4)

time: 82.7 us -> 82.7 us (level)
  no operation moved by 1% of the time
where the time goes in v9:
time: 82.7 us; the launch traced here: 82.6 us
  starting transfers between devices  35.5 us (43%)
  waiting for transfers between devices  24.1 us (29%)
  Pallas kernels  22 us (27%)
  between operations  1.04 us (1%)
    ppermute x22, starting transfers between devices, swap(): return lax.ppermute(v, axis, [(i, i ^ bit) for i in range(n)])  23.5 us
    pallas_call x13, Pallas kernels, call(): pl.pallas_call(body, out_shape=[jax.ShapeDtypeStruct(*o) for o in outs],...  22 us
    ppermute x22, waiting for transfers between devices, swap(): return lax.ppermute(v, axis, [(i, i ^ bit) for i in range(n)])  11.8 us
    ppermute x6, waiting for transfers between devices, cross(): lax.ppermute(v, ('seq', 'wy'), [(2 * a + b, 2 * (a ^ flip_x) + (b ^ flip_...  6.92 us
    ppermute x6, starting transfers between devices, cross(): lax.ppermute(v, ('seq', 'wy'), [(2 * a + b, 2 * (a ^ flip_x) + (b ^ flip_...  6.57 us
    ppermute x2, waiting for transfers between devices, per_device(): lax.ppermute(fwd, 'seq', [(i, (i + k) % S) for i in range(S)])  4.84 us
    ppermute x2, starting transfers between devices, per_device(): lax.ppermute(fwd, 'seq', [(i, (i + k) % S) for i in range(S)])  3.03 us
    ppermute x2, starting transfers between devices, per_device(): lax.ppermute(bwd, 'seq', [((i + k) % S, i) for i in range(S)])  2.35 us
  transfers between devices with their start and end apart: 32, of which 18 were waited for; matrix products, arithmetic and copies ran while one was open for 0% of the time, Pallas kernels for 12%

profile of v9, /device:TPU:0, one launch (start us, length us, event | category | flops | bytes accessed | tf_op | source)
XLA Modules:
  0.0 82.6 jit_solution(238643133389093546)
XLA Ops:
  0.7 1.8 %shard_map.237 = (bf16[144,768]{1,0:T(8,128)(2,1)}, f32[8,384]{1,0:T(8,128)}) custom-call(bf16[128,768]{1,0:T(8,128)(2,1)} %b_ref.1, bf16[1,128]{1,0:T(2,128)(2,1)} %bitcast.23, bf16[1,128]{1,0:T(2,128)(2,1)} %bitcast.24, bf16[1,128]{1,0:T(2,128)(2,1)} %bitcast.25, bf16[1,128]{1,0:T(2,128)(2,1)} %bitcast.26, f32[1,48]{1,0:T(1,128)} %bitcast.27, ...), custom_call_target="tpu_custom_call" | custom-call | flops 1000000000 | bytes 1048576 | tf_op jit(solution)/shard_map/pallas_call | solution.py:637
  2.6 3.0 %collective-permute-start.1 = (bf16[144,768]{1,0:T(8,128)(2,1)}, bf16[144,768]{1,0:T(8,128)(2,1)S(1)}, u32[]{:S(2)}, u32[]{:S(2)}) collective-permute-start(bf16[144,768]{1,0:T(8,128)(2,1)} %get-tuple-element.76.b0), channel_id=1, source_target_pairs={{0,2},{2,0},{1,3},{3,1},{4,6},{6,4},{5,7},{7,5},{8,10},{10,8},{9,1... | collective-permute-start | bytes 663560 | tf_op jit(solution)/shard_map/ppermute | solution.py:663
  5.6 2.5 %collective-permute-start.5 = (f32[8,384]{1,0:T(8,128)}, f32[8,384]{1,0:T(8,128)S(1)}, u32[]{:S(2)}, u32[]{:S(2)}) collective-permute-start(f32[8,384]{1,0:T(8,128)} %get-tuple-element.77), channel_id=1, source_target_pairs={{0,12},{4,8},{8,4},{12,0},{16,28},{20,24},{24,20},{28,16},{1,13},{... | collective-permute-start | bytes 36872 | tf_op jit(solution)/shard_map/ppermute | solution.py:663
  8.1 0.4 collective-permute-start.4
  8.5 0.5 collective-permute-start.3
  9.1 0.5 shard_map.239.refs_10_
  9.6 1.7 %collective-permute-done.1.b2 = bf16[144,768]{1,0:T(8,128)(2,1)S(1)} collective-permute-done((bf16[144,768]{1,0:T(8,128)(2,1)}, bf16[144,768]{1,0:T(8,128)(2,1)S(1)}, u32[]{:S(2)}, u32[]{:S(2)}) %collective-permute-start.1) | collective-permute-done | bytes 221216 | tf_op jit(solution)/shard_map/ppermute | solution.py:663
  11.2 1.7 %collective-permute-start.8 = (bf16[320,512]{1,0:T(8,128)(2,1)S(1)}, bf16[320,512]{1,0:T(8,128)(2,1)S(1)}, u32[]{:S(2)}, u32[]{:S(2)}) collective-permute-start(bf16[320,512]{1,0:T(8,128)(2,1)S(1)} %shard_map.239.refs_10_), channel_id=1, source_target_pairs={{0,2},{2,0},{1,3},{3,1},{4,6},{6,4},{5,7},{7,5},{8,10},{10,8},{9,1... | collective-permute-start | bytes 983048 | tf_op jit(solution)/shard_map/ppermute | solution.py:663
  13.0 2.7 %collective-permute-start.6 = (f32[8,384]{1,0:T(8,128)S(1)}, f32[8,384]{1,0:T(8,128)S(1)}, u32[]{:S(2)}, u32[]{:S(2)}) collective-permute-start(f32[8,384]{1,0:T(8,128)S(1)} %add_add_fusion), channel_id=1, source_target_pairs={{0,16},{4,20},{8,24},{12,28},{16,0},{20,4},{24,8},{28,12},{1,17},{... | collective-permute-start | bytes 36872 | tf_op jit(solution)/shard_map/ppermute | solution.py:663
  15.9 1.8 %collective-permute-done.6 = f32[8,384]{1,0:T(8,128)S(1)} collective-permute-done((f32[8,384]{1,0:T(8,128)S(1)}, f32[8,384]{1,0:T(8,128)S(1)}, u32[]{:S(2)}, u32[]{:S(2)}) %collective-permute-start.6) | collective-permute-done | bytes 12320 | tf_op jit(solution)/shard_map/ppermute | solution.py:663
  17.7 2.2 %shard_map.238 = (bf16[1024,512]{1,0:T(8,128)(2,1)S(1)}, bf16[1024,512]{1,0:T(8,128)(2,1)S(1)}, f32[6,1048,128]{2,1,0:T(8,128)S(1)}, f32[8,512]{1,0:T(8,128)S(1)...) custom-call(bf16[1024,512]{1,0:T(8,128)(2,1)S(1)} %bitcast.20, ...), custom_call_target="tpu_custom_call" | custom-call | flops 2000000000 | bytes 1048576 | tf_op jit(solution)/shard_map/pallas_call | solution.py:637
  20.1 1.5 %collective-permute-start.11 = (f32[2,896]{1,0:T(2,128)S(1)}, f32[2,896]{1,0:T(2,128)S(1)}, u32[]{:S(2)}, u32[]{:S(2)}) collective-permute-start(f32[2,896]{1,0:T(2,128)S(1)} %get-tuple-element.87), channel_id=1, source_target_pairs={{0,8},{4,12},{8,16},{12,20},{16,24},{20,28},{24,0},{28,4},{1,9},{5... | collective-permute-start | bytes 21512 | tf_op jit(solution)/shard_map/ppermute | solution.py:705
  21.7 1.5 %collective-permute-start.10 = (f32[2,896]{1,0:T(2,128)S(1)}, f32[2,896]{1,0:T(2,128)S(1)}, u32[]{:S(2)}, u32[]{:S(2)}) collective-permute-start(f32[2,896]{1,0:T(2,128)S(1)} %get-tuple-element.87), channel_id=1, source_target_pairs={{0,4},{4,8},{8,12},{12,16},{16,20},{20,24},{24,28},{28,0},{1,5},{5... | collective-permute-start | bytes 21512 | tf_op jit(solution)/shard_map/ppermute | solution.py:705
  23.2 2.4 %collective-permute-done.11.refs_15_ = f32[2,896]{1,0:T(2,128)S(1)} collective-permute-done((f32[2,896]{1,0:T(2,128)S(1)}, f32[2,896]{1,0:T(2,128)S(1)}, u32[]{:S(2)}, u32[]{:S(2)}) %collective-permute-start.11) | collective-permute-done | bytes 7200 | tf_op jit(solution)/shard_map/ppermute | solution.py:705
  25.6 2.4 %collective-permute-done.10.refs_14_ = f32[2,896]{1,0:T(2,128)S(1)} collective-permute-done((f32[2,896]{1,0:T(2,128)S(1)}, f32[2,896]{1,0:T(2,128)S(1)}, u32[]{:S(2)}, u32[]{:S(2)}) %collective-permute-start.10) | collective-permute-done | bytes 7200 | tf_op jit(solution)/shard_map/ppermute | solution.py:705
  28.0 8.9 %shard_map.240 = (bf16[1024,512]{1,0:T(8,128)(2,1)}, f32[6,1048,128]{2,1,0:T(8,128)S(1)}, f32[6,1048,128]{2,1,0:T(8,128)S(1)}, bf16[1024,512]{1,0:T(8,128)(2,1)S...) custom-call(bf16[1024,512]{1,0:T(8,128)(2,1)S(1)} %bitcast.21, ...), custom_call_target="tpu_custom_call" | custom-call | flops 10000000000 | bytes 1048576 | tf_op jit(solution)/shard_map/pallas_call | solution.py:637
  37.0 0.5 collective-permute-start.13
  37.5 1.8 %collective-permute-start.12 = (f32[2,896]{1,0:T(2,128)S(1)}, f32[2,896]{1,0:T(2,128)S(1)}, u32[]{:S(2)}, u32[]{:S(2)}) collective-permute-start(f32[2,896]{1,0:T(2,128)S(1)} %get-tuple-element.97), channel_id=1, source_target_pairs={{4,0},{8,4},{12,8},{16,12},{20,16},{24,20},{28,24},{0,28},{5,1},{9... | collective-permute-start | bytes 21512 | tf_op jit(solution)/shard_map/ppermute | solution.py:716
  39.5 1.1 %collective-permute-start.15 = (bf16[160,512]{1,0:T(8,128)(2,1)S(1)}, bf16[160,512]{1,0:T(8,128)(2,1)S(1)}, u32[]{:S(2)}, u32[]{:S(2)}) collective-permute-start(bf16[160,512]{1,0:T(8,128)(2,1)S(1)} %get-tuple-element.103), channel_id=1, source_target_pairs={{0,6},{2,4},{4,2},{6,0},{8,14},{10,12},{12,10},{14,8},{16,22},{18,... | collective-permute-start | bytes 491528 | tf_op jit(solution)/shard_map/ppermute | solution.py:718
  40.7 0.5 collective-permute-done.12.refs_13_
  41.1 4.0 %shard_map.242 = (bf16[1024,512]{1,0:T(8,128)(2,1)S(1)}, bf16[2,208,512]{2,1,0:T(8,128)(2,1)S(1)}, bf16[2,208,512]{2,1,0:T(8,128)(2,1)S(1)}) custom-call(bf16[1024,512]{1,0:T(8,128)(2,1)S(1)} %get-tuple-element.90.refs_0_, f32[8,512]{1,0:T(8,128)S(1)} %get-tuple-element.91.refs_1_, f32[1048,128]{1,0:T(8,128)S(1)} %get-tuple-element.78.refs_2_, ...), custom_call_target="tpu_custom_call" | custom-call | flops 8000000000 | bytes 1048576 | tf_op jit(solution)/shard_map/pallas_call | solution.py:637
  45.2 1.3 %collective-permute-done.15.c3 = bf16[160,512]{1,0:T(8,128)(2,1)S(1)} collective-permute-done((bf16[160,512]{1,0:T(8,128)(2,1)S(1)}, bf16[160,512]{1,0:T(8,128)(2,1)S(1)}, u32[]{:S(2)}, u32[]{:S(2)}) %collective-permute-start.15) | collective-permute-done | bytes 163872 | tf_op jit(solution)/shard_map/ppermute | solution.py:718
  46.5 1.4 %collective-permute-start.20 = (bf16[160,512]{1,0:T(8,128)(2,1)S(1)}, bf16[160,512]{1,0:T(8,128)(2,1)S(1)}, u32[]{:S(2)}, u32[]{:S(2)}) collective-permute-start(bf16[160,512]{1,0:T(8,128)(2,1)S(1)} %get-tuple-element.101), channel_id=1, source_target_pairs={{0,2},{2,0},{4,6},{6,4},{8,10},{10,8},{12,14},{14,12},{16,18},{18,... | collective-permute-start | bytes 491528 | tf_op jit(solution)/shard_map/ppermute | solution.py:718
  47.9 0.4 collective-permute-start.21
  48.5 1.4 %collective-permute-start.17 = (bf16[112,512]{1,0:T(8,128)(2,1)S(1)}, bf16[112,512]{1,0:T(8,128)(2,1)S(1)}, u32[]{:S(2)}, u32[]{:S(2)}) collective-permute-start(bf16[112,512]{1,0:T(8,128)(2,1)S(1)} %get-tuple-element.110), channel_id=1, source_target_pairs={{0,2},{2,0},{4,6},{6,4},{8,10},{10,8},{12,14},{14,12},{16,18},{18,... | collective-permute-start | bytes 344072 | tf_op jit(solution)/shard_map/ppermute | solution.py:718
  49.9 0.8 %collective-permute-start.18 = (bf16[112,512]{1,0:T(8,128)(2,1)S(1)}, bf16[112,512]{1,0:T(8,128)(2,1)S(1)}, u32[]{:S(2)}, u32[]{:S(2)}) collective-permute-start(bf16[112,512]{1,0:T(8,128)(2,1)S(1)} %get-tuple-element.111), channel_id=1, source_target_pairs={{0,4},{2,6},{4,0},{6,2},{8,12},{10,14},{12,8},{14,10},{16,20},{18,... | collective-permute-start | bytes 344072 | tf_op jit(solution)/shard_map/ppermute | solution.py:718
  50.7 1.3 %collective-permute-start.19 = (bf16[112,512]{1,0:T(8,128)(2,1)S(1)}, bf16[112,512]{1,0:T(8,128)(2,1)S(1)}, u32[]{:S(2)}, u32[]{:S(2)}) collective-permute-start(bf16[112,512]{1,0:T(8,128)(2,1)S(1)} %get-tuple-element.112), channel_id=1, source_target_pairs={{0,6},{2,4},{4,2},{6,0},{8,14},{10,12},{12,10},{14,8},{16,22},{18,... | collective-permute-start | bytes 344072 | tf_op jit(solution)/shard_map/ppermute | solution.py:718
  52.0 1.4 %shard_map.244.ig_ref = bf16[1024,512]{1,0:T(8,128)(2,1)S(1)} custom-call(bf16[1024,512]{1,0:T(8,128)(2,1)S(1)} %bitcast.22, bf16[1024,512]{1,0:T(8,128)(2,1)S(1)} %get-tuple-element.113.gn_ref, bf16[1024,512]{1,0:T(8,128)(2,1)S(1)} %get-tuple-element.114.gres_ref, f32[8,512]{1,0:T(8,128)S(1)} %get-tuple-element.85.refs_9_.refs_11_.vec_ref), custom_call_target="tpu_custom_call" | custom-call | flops 3000000000 | bytes 1048576 | tf_op jit(solution)/shard_map/pallas_call | solution.py:637
  53.5 1.5 %collective-permute-done.21.c2 = bf16[160,512]{1,0:T(8,128)(2,1)S(1)} collective-permute-done((bf16[160,512]{1,0:T(8,128)(2,1)S(1)}, bf16[160,512]{1,0:T(8,128)(2,1)S(1)}, u32[]{:S(2)}, u32[]{:S(2)}) %collective-permute-start.21) | collective-permute-done | bytes 163872 | tf_op jit(solution)/shard_map/ppermute | solution.py:718
  55.0 0.5 collective-permute-done.17.refs_1_
  55.5 1.9 %collective-permute-done.18.refs_2_ = bf16[112,512]{1,0:T(8,128)(2,1)S(1)} collective-permute-done((bf16[112,512]{1,0:T(8,128)(2,1)S(1)}, bf16[112,512]{1,0:T(8,128)(2,1)S(1)}, u32[]{:S(2)}, u32[]{:S(2)}) %collective-permute-start.18) | collective-permute-done | bytes 114720 | tf_op jit(solution)/shard_map/ppermute | solution.py:718
  57.4 1.8 %collective-permute-done.19.refs_3_ = bf16[112,512]{1,0:T(8,128)(2,1)S(1)} collective-permute-done((bf16[112,512]{1,0:T(8,128)(2,1)S(1)}, bf16[112,512]{1,0:T(8,128)(2,1)S(1)}, u32[]{:S(2)}, u32[]{:S(2)}) %collective-permute-start.19) | collective-permute-done | bytes 114720 | tf_op jit(solution)/shard_map/ppermute | solution.py:718
  59.7 2.5 %collective-permute-start.23 = (bf16[72,512]{1,0:T(8,128)(2,1)S(1)}, bf16[72,512]{1,0:T(8,128)(2,1)S(1)}, u32[]{:S(2)}, u32[]{:S(2)}) collective-permute-start(bf16[72,512]{1,0:T(8,128)(2,1)S(1)} %get-tuple-element.121), channel_id=1, source_target_pairs={{0,16},{4,20},{8,24},{12,28},{16,0},{20,4},{24,8},{28,12},{1,17},{... | collective-permute-start | bytes 221192 | tf_op jit(solution)/shard_map/ppermute | solution.py:663
  62.1 1.6 %collective-permute-start.24 = (bf16[72,512]{1,0:T(8,128)(2,1)S(1)}, bf16[72,512]{1,0:T(8,128)(2,1)S(1)}, u32[]{:S(2)}, u32[]{:S(2)}) collective-permute-start(bf16[72,512]{1,0:T(8,128)(2,1)S(1)} %get-tuple-element.122), channel_id=1, source_target_pairs={{0,24},{4,28},{8,16},{12,20},{16,8},{20,12},{24,0},{28,4},{1,25},{... | collective-permute-start | bytes 221192 | tf_op jit(solution)/shard_map/ppermute | solution.py:663
  63.9 3.4 %collective-permute-done.23.refs_2_ = bf16[72,512]{1,0:T(8,128)(2,1)S(1)} collective-permute-done((bf16[72,512]{1,0:T(8,128)(2,1)S(1)}, bf16[72,512]{1,0:T(8,128)(2,1)S(1)}, u32[]{:S(2)}, u32[]{:S(2)}) %collective-permute-start.23) | collective-permute-done | bytes 73760 | tf_op jit(solution)/shard_map/ppermute | solution.py:663
  67.3 1.1 %collective-permute-done.24.refs_3_ = bf16[72,512]{1,0:T(8,128)(2,1)S(1)} collective-permute-done((bf16[72,512]{1,0:T(8,128)(2,1)S(1)}, bf16[72,512]{1,0:T(8,128)(2,1)S(1)}, u32[]{:S(2)}, u32[]{:S(2)}) %collective-permute-start.24) | collective-permute-done | bytes 73760 | tf_op jit(solution)/shard_map/ppermute | solution.py:663
  68.4 1.1 %collective-permute-start.25 = (bf16[64,512]{1,0:T(8,128)(2,1)S(1)}, bf16[64,512]{1,0:T(8,128)(2,1)S(1)}, u32[]{:S(2)}, u32[]{:S(2)}) collective-permute-start(bf16[64,512]{1,0:T(8,128)(2,1)S(1)} %get-tuple-element.130.refs_0_), channel_id=1, source_target_pairs={{0,8},{4,12},{8,0},{12,4},{16,24},{20,28},{24,16},{28,20},{1,9},{5... | collective-permute-start | bytes 196616 | tf_op jit(solution)/shard_map/ppermute | solution.py:663
  69.5 2.0 %collective-permute-start.30 = (bf16[64,512]{1,0:T(8,128)(2,1)S(1)}, bf16[64,512]{1,0:T(8,128)(2,1)S(1)}, u32[]{:S(2)}, u32[]{:S(2)}) collective-permute-start(bf16[64,512]{1,0:T(8,128)(2,1)S(1)} %get-tuple-element.130.refs_0_), channel_id=1, source_target_pairs={{0,24},{4,28},{8,16},{12,20},{16,8},{20,12},{24,0},{28,4},{1,25},{... | collective-permute-start | bytes 196616 | tf_op jit(solution)/shard_map/ppermute | solution.py:663
  71.5 0.5 collective-permute-start.28
  72.0 0.8 %collective-permute-done.25.refs_2_ = bf16[64,512]{1,0:T(8,128)(2,1)S(1)} collective-permute-done((bf16[64,512]{1,0:T(8,128)(2,1)S(1)}, bf16[64,512]{1,0:T(8,128)(2,1)S(1)}, u32[]{:S(2)}, u32[]{:S(2)}) %collective-permute-start.25) | collective-permute-done | bytes 65568 | tf_op jit(solution)/shard_map/ppermute | solution.py:663
  72.8 1.6 %collective-permute-start.26 = (bf16[64,512]{1,0:T(8,128)(2,1)S(1)}, bf16[64,512]{1,0:T(8,128)(2,1)S(1)}, u32[]{:S(2)}, u32[]{:S(2)}) collective-permute-start(bf16[64,512]{1,0:T(8,128)(2,1)S(1)} %get-tuple-element.130.refs_0_), channel_id=1, source_target_pairs={{0,4},{4,0},{8,12},{12,8},{16,20},{20,16},{24,28},{28,24},{1,5},{5... | collective-permute-start | bytes 196616 | tf_op jit(solution)/shard_map/ppermute | solution.py:663
  74.9 0.8 collective-permute-done.30.refs_6_
  75.6 0.9 %collective-permute-start.31 = (bf16[64,512]{1,0:T(8,128)(2,1)S(1)}, bf16[64,512]{1,0:T(8,128)(2,1)S(1)}, u32[]{:S(2)}, u32[]{:S(2)}) collective-permute-start(bf16[64,512]{1,0:T(8,128)(2,1)S(1)} %collective-permute-done.30.refs_6_), channel_id=1, source_target_pairs={{0,4},{4,0},{8,12},{12,8},{16,20},{20,16},{24,28},{28,24},{1,5},{5... | collective-permute-start | bytes 196616 | tf_op jit(solution)/shard_map/ppermute | solution.py:663
  76.5 0.5 collective-permute-done.28.refs_4_
  77.0 1.4 %collective-permute-start.29 = (bf16[64,512]{1,0:T(8,128)(2,1)S(1)}, bf16[64,512]{1,0:T(8,128)(2,1)S(1)}, u32[]{:S(2)}, u32[]{:S(2)}) collective-permute-start(bf16[64,512]{1,0:T(8,128)(2,1)S(1)} %collective-permute-done.28.refs_4_), channel_id=1, source_target_pairs={{0,4},{4,0},{8,12},{12,8},{16,20},{20,16},{24,28},{28,24},{1,5},{5... | collective-permute-start | bytes 196616 | tf_op jit(solution)/shard_map/ppermute | solution.py:663
  78.4 1.5 %shard_map.248 = (f32[1024,512]{1,0:T(8,128)}, f32[1,1]{1,0:T(1,128)}, f32[1,128]{1,0:T(1,128)}, f32[1,128]{1,0:T(1,128)}, f32[1,128]{1,0:T(1,128)}, /*index=5*/...) custom-call(f32[8,512]{1,0:T(8,128)S(1)} %get-tuple-element.123.tail_ref, ...), custom_call_target="tpu_custom_call" | custom-call | flops 1000000000 | bytes 1048576 | tf_op jit(solution)/shard_map/pallas_call | solution.py:637
  79.9 1.4 %collective-permute-done.29.refs_5_ = bf16[64,512]{1,0:T(8,128)(2,1)S(1)} collective-permute-done((bf16[64,512]{1,0:T(8,128)(2,1)S(1)}, bf16[64,512]{1,0:T(8,128)(2,1)S(1)}, u32[]{:S(2)}, u32[]{:S(2)}) %collective-permute-start.29) | collective-permute-done | bytes 65568 | tf_op jit(solution)/shard_map/ppermute | solution.py:663
  81.3 1.1 %shard_map.249 = (f32[128,768]{1,0:T(8,128)}, f32[192,512]{1,0:T(8,128)}, f32[128,512]{1,0:T(8,128)}) custom-call(f32[8,512]{1,0:T(8,128)S(1)} %get-tuple-element.123.tail_ref, bf16[64,512]{1,0:T(8,128)(2,1)S(1)} %get-tuple-element.130.refs_0_, bf16[64,512]{1,0:T(8,128)(2,1)S(1)} %collective-permute-done.26.refs_1_, ...), custom_call_target="tpu_custom_call" | custom-call | flops 1000000000 | bytes 1048576 | tf_op jit(solution)/shard_map/pallas_call | solution.py:637
  (47 shorter events, 2.0 us)
Async XLA Ops:
  0.6 8.4 %copy-start.4 = (bf16[128,512]{1,0:T(8,128)(2,1)S(1)}, bf16[128,512]{1,0:T(8,128)(2,1)}, u32[]{:S(2)}) copy-start(bf16[128,512]{1,0:T(8,128)(2,1)} %g_ref.1) | copy-start | bytes 393220
  0.7 8.4 %copy-start.3 = (bf16[192,512]{1,0:T(8,128)(2,1)S(1)}, bf16[192,512]{1,0:T(8,128)(2,1)}, u32[]{:S(2)}) copy-start(bf16[192,512]{1,0:T(8,128)(2,1)} %c_ref.1) | copy-start | bytes 589828
  0.7 17.0 %copy-start.1 = (bf16[2,512,512]{2,1,0:T(8,128)(2,1)S(1)}, bf16[2,512,512]{2,1,0:T(8,128)(2,1)}, u32[]{:S(2)}) copy-start(bf16[2,512,512]{2,1,0:T(8,128)(2,1)} %param.14) | copy-start | bytes 3145732
  0.7 17.0 %copy-start.5 = (s32[2,512]{1,0:T(2,128)S(1)}, s32[2,512]{1,0:T(2,128)}, u32[]{:S(2)}) copy-start(s32[2,512]{1,0:T(2,128)} %seg_ref.1) | copy-start | bytes 12292
  0.7 17.0 %copy-start.6 = (s32[2,512]{1,0:T(2,128)S(1)}, s32[2,512]{1,0:T(2,128)}, u32[]{:S(2)}) copy-start(s32[2,512]{1,0:T(2,128)} %mask_ref.1) | copy-start | bytes 12292
  2.5 10.5 %copy-start.7 = (f32[8,384]{1,0:T(8,128)S(1)}, f32[8,384]{1,0:T(8,128)}, u32[]{:S(2)}) copy-start(f32[8,384]{1,0:T(8,128)} %get-tuple-element.77) | copy-start | bytes 36868
  2.5 15.2 %copy-start.2 = (bf16[144,768]{1,0:T(8,128)(2,1)S(1)}, bf16[144,768]{1,0:T(8,128)(2,1)}, u32[]{:S(2)}) copy-start(bf16[144,768]{1,0:T(8,128)(2,1)} %get-tuple-element.76.b0) | copy-start | bytes 663556
  2.6 8.7 %collective-permute-start.1 = (bf16[144,768]{1,0:T(8,128)(2,1)}, bf16[144,768]{1,0:T(8,128)(2,1)S(1)}, u32[]{:S(2)}, u32[]{:S(2)}) collective-permute-start(bf16[144,768]{1,0:T(8,128)(2,1)} %get-tuple-element.76.b0), channel_id=1, source_target_pairs={{0,2},{2,0},{1,3},{3,1},{4,6},{6,4},{5,7},{7,5},{8,10},{10,8},{9,1... | collective-permute-start | bytes 663560 | tf_op jit(solution)/shard_map/ppermute | solution.py:663
  5.6 7.4 %collective-permute-start.5 = (f32[8,384]{1,0:T(8,128)}, f32[8,384]{1,0:T(8,128)S(1)}, u32[]{:S(2)}, u32[]{:S(2)}) collective-permute-start(f32[8,384]{1,0:T(8,128)} %get-tuple-element.77), channel_id=1, source_target_pairs={{0,12},{4,8},{8,4},{12,0},{16,28},{20,24},{24,20},{28,16},{1,13},{... | collective-permute-start | bytes 36872 | tf_op jit(solution)/shard_map/ppermute | solution.py:663
  8.1 4.9 %collective-permute-start.4 = (f32[8,384]{1,0:T(8,128)}, f32[8,384]{1,0:T(8,128)S(1)}, u32[]{:S(2)}, u32[]{:S(2)}) collective-permute-start(f32[8,384]{1,0:T(8,128)} %get-tuple-element.77), channel_id=1, source_target_pairs={{0,8},{4,12},{8,0},{12,4},{16,24},{20,28},{24,16},{28,20},{1,9},{5... | collective-permute-start | bytes 36872 | tf_op jit(solution)/shard_map/ppermute | solution.py:663
  8.5 4.4 %collective-permute-start.3 = (f32[8,384]{1,0:T(8,128)}, f32[8,384]{1,0:T(8,128)S(1)}, u32[]{:S(2)}, u32[]{:S(2)}) collective-permute-start(f32[8,384]{1,0:T(8,128)} %get-tuple-element.77), channel_id=1, source_target_pairs={{0,4},{4,0},{8,12},{12,8},{16,20},{20,16},{24,28},{28,24},{1,5},{5... | collective-permute-start | bytes 36872 | tf_op jit(solution)/shard_map/ppermute | solution.py:663
  9.1 8.6 %collective-permute-start = (bf16[144,768]{1,0:T(8,128)(2,1)}, bf16[144,768]{1,0:T(8,128)(2,1)S(1)}, u32[]{:S(2)}, u32[]{:S(2)}) collective-permute-start(bf16[144,768]{1,0:T(8,128)(2,1)} %get-tuple-element.76.b0), channel_id=1, source_target_pairs={{0,1},{1,0},{2,3},{3,2},{4,5},{5,4},{6,7},{7,6},{8,9},{9,8},{10,11... | collective-permute-start | bytes 663560 | tf_op jit(solution)/shard_map/ppermute | solution.py:663
  11.2 8.9 %collective-permute-start.8 = (bf16[320,512]{1,0:T(8,128)(2,1)S(1)}, bf16[320,512]{1,0:T(8,128)(2,1)S(1)}, u32[]{:S(2)}, u32[]{:S(2)}) collective-permute-start(bf16[320,512]{1,0:T(8,128)(2,1)S(1)} %shard_map.239.refs_10_), channel_id=1, source_target_pairs={{0,2},{2,0},{1,3},{3,1},{4,6},{6,4},{5,7},{7,5},{8,10},{10,8},{9,1... | collective-permute-start | bytes 983048 | tf_op jit(solution)/shard_map/ppermute | solution.py:663
  13.0 4.7 %collective-permute-start.2 = (bf16[144,768]{1,0:T(8,128)(2,1)S(1)}, bf16[144,768]{1,0:T(8,128)(2,1)S(1)}, u32[]{:S(2)}, u32[]{:S(2)}) collective-permute-start(bf16[144,768]{1,0:T(8,128)(2,1)S(1)} %collective-permute-done.1.b2), channel_id=1, source_target_pairs={{0,1},{1,0},{2,3},{3,2},{4,5},{5,4},{6,7},{7,6},{8,9},{9,8},{10,11... | collective-permute-start | bytes 663560 | tf_op jit(solution)/shard_map/ppermute | solution.py:663
  13.0 4.7 %collective-permute-start.6 = (f32[8,384]{1,0:T(8,128)S(1)}, f32[8,384]{1,0:T(8,128)S(1)}, u32[]{:S(2)}, u32[]{:S(2)}) collective-permute-start(f32[8,384]{1,0:T(8,128)S(1)} %add_add_fusion), channel_id=1, source_target_pairs={{0,16},{4,20},{8,24},{12,28},{16,0},{20,4},{24,8},{28,12},{1,17},{... | collective-permute-start | bytes 36872 | tf_op jit(solution)/shard_map/ppermute | solution.py:663
  15.7 7.5 %collective-permute-start.7 = (bf16[320,512]{1,0:T(8,128)(2,1)S(1)}, bf16[320,512]{1,0:T(8,128)(2,1)S(1)}, u32[]{:S(2)}, u32[]{:S(2)}) collective-permute-start(bf16[320,512]{1,0:T(8,128)(2,1)S(1)} %shard_map.239.refs_10_), channel_id=1, source_target_pairs={{0,1},{1,0},{2,3},{3,2},{4,5},{5,4},{6,7},{7,6},{8,9},{9,8},{10,11... | collective-permute-start | bytes 983048 | tf_op jit(solution)/shard_map/ppermute | solution.py:663
  17.7 10.3 %copy-start = (bf16[2,512,512]{2,1,0:T(8,128)(2,1)S(1)}, bf16[2,512,512]{2,1,0:T(8,128)(2,1)}, u32[]{:S(2)}) copy-start(bf16[2,512,512]{2,1,0:T(8,128)(2,1)} %param.15) | copy-start | bytes 3145732
  20.1 7.9 %collective-permute-start.9 = (bf16[320,512]{1,0:T(8,128)(2,1)S(1)}, bf16[320,512]{1,0:T(8,128)(2,1)S(1)}, u32[]{:S(2)}, u32[]{:S(2)}) collective-permute-start(bf16[320,512]{1,0:T(8,128)(2,1)S(1)} %collective-permute-done.8.refs_12_), channel_id=1, source_target_pairs={{0,1},{1,0},{2,3},{3,2},{4,5},{5,4},{6,7},{7,6},{8,9},{9,8},{10,11... | collective-permute-start | bytes 983048 | tf_op jit(solution)/shard_map/ppermute | solution.py:663
  20.1 5.4 %collective-permute-start.11 = (f32[2,896]{1,0:T(2,128)S(1)}, f32[2,896]{1,0:T(2,128)S(1)}, u32[]{:S(2)}, u32[]{:S(2)}) collective-permute-start(f32[2,896]{1,0:T(2,128)S(1)} %get-tuple-element.87), channel_id=1, source_target_pairs={{0,8},{4,12},{8,16},{12,20},{16,24},{20,28},{24,0},{28,4},{1,9},{5... | collective-permute-start | bytes 21512 | tf_op jit(solution)/shard_map/ppermute | solution.py:705
  21.7 6.3 %collective-permute-start.10 = (f32[2,896]{1,0:T(2,128)S(1)}, f32[2,896]{1,0:T(2,128)S(1)}, u32[]{:S(2)}, u32[]{:S(2)}) collective-permute-start(f32[2,896]{1,0:T(2,128)S(1)} %get-tuple-element.87), channel_id=1, source_target_pairs={{0,4},{4,8},{8,12},{12,16},{16,20},{20,24},{24,28},{28,0},{1,5},{5... | collective-permute-start | bytes 21512 | tf_op jit(solution)/shard_map/ppermute | solution.py:705
  36.9 2.4 %collective-permute-start.14 = (bf16[2,320,512]{2,1,0:T(8,128)(2,1)S(1)}, bf16[2,320,512]{2,1,0:T(8,128)(2,1)S(1)}, u32[]{:S(2)}, u32[]{:S(2)}) collective-permute-start(bf16[2,320,512]{2,1,0:T(8,128)(2,1)S(1)} %get-tuple-element.99), channel_id=1, source_target_pairs={{0,1},{1,0},{2,3},{3,2},{4,5},{5,4},{6,7},{7,6},{8,9},{9,8},{10,11... | collective-permute-start | bytes 1966088 | tf_op jit(solution)/shard_map/ppermute | solution.py:663
  37.0 3.7 %collective-permute-start.13 = (f32[2,896]{1,0:T(2,128)S(1)}, f32[2,896]{1,0:T(2,128)S(1)}, u32[]{:S(2)}, u32[]{:S(2)}) collective-permute-start(f32[2,896]{1,0:T(2,128)S(1)} %get-tuple-element.97), channel_id=1, source_target_pairs={{8,0},{12,4},{16,8},{20,12},{24,16},{28,20},{0,24},{4,28},{9,1},{1... | collective-permute-start | bytes 21512 | tf_op jit(solution)/shard_map/ppermute | solution.py:716
  37.5 3.6 %collective-permute-start.12 = (f32[2,896]{1,0:T(2,128)S(1)}, f32[2,896]{1,0:T(2,128)S(1)}, u32[]{:S(2)}, u32[]{:S(2)}) collective-permute-start(f32[2,896]{1,0:T(2,128)S(1)} %get-tuple-element.97), channel_id=1, source_target_pairs={{4,0},{8,4},{12,8},{16,12},{20,16},{24,20},{28,24},{0,28},{5,1},{9... | collective-permute-start | bytes 21512 | tf_op jit(solution)/shard_map/ppermute | solution.py:716
  39.5 7.0 %collective-permute-start.15 = (bf16[160,512]{1,0:T(8,128)(2,1)S(1)}, bf16[160,512]{1,0:T(8,128)(2,1)S(1)}, u32[]{:S(2)}, u32[]{:S(2)}) collective-permute-start(bf16[160,512]{1,0:T(8,128)(2,1)S(1)} %get-tuple-element.103), channel_id=1, source_target_pairs={{0,6},{2,4},{4,2},{6,0},{8,14},{10,12},{12,10},{14,8},{16,22},{18,... | collective-permute-start | bytes 491528 | tf_op jit(solution)/shard_map/ppermute | solution.py:718
  46.5 1.9 %collective-permute-start.16 = (bf16[2,208,512]{2,1,0:T(8,128)(2,1)S(1)}, bf16[2,208,512]{2,1,0:T(8,128)(2,1)S(1)}, u32[]{:S(2)}, u32[]{:S(2)}) collective-permute-start(bf16[2,208,512]{2,1,0:T(8,128)(2,1)S(1)} %get-tuple-element.108), channel_id=1, source_target_pairs={{0,1},{1,0},{2,3},{3,2},{4,5},{5,4},{6,7},{7,6},{8,9},{9,8},{10,11... | collective-permute-start | bytes 1277960 | tf_op jit(solution)/shard_map/ppermute | solution.py:663
  46.5 7.0 %collective-permute-start.20 = (bf16[160,512]{1,0:T(8,128)(2,1)S(1)}, bf16[160,512]{1,0:T(8,128)(2,1)S(1)}, u32[]{:S(2)}, u32[]{:S(2)}) collective-permute-start(bf16[160,512]{1,0:T(8,128)(2,1)S(1)} %get-tuple-element.101), channel_id=1, source_target_pairs={{0,2},{2,0},{4,6},{6,4},{8,10},{10,8},{12,14},{14,12},{16,18},{18,... | collective-permute-start | bytes 491528 | tf_op jit(solution)/shard_map/ppermute | solution.py:718
  47.9 7.0 %collective-permute-start.21 = (bf16[160,512]{1,0:T(8,128)(2,1)S(1)}, bf16[160,512]{1,0:T(8,128)(2,1)S(1)}, u32[]{:S(2)}, u32[]{:S(2)}) collective-permute-start(bf16[160,512]{1,0:T(8,128)(2,1)S(1)} %get-tuple-element.102), channel_id=1, source_target_pairs={{0,4},{2,6},{4,0},{6,2},{8,12},{10,14},{12,8},{14,10},{16,20},{18,... | collective-permute-start | bytes 491528 | tf_op jit(solution)/shard_map/ppermute | solution.py:718
  48.5 7.1 %collective-permute-start.17 = (bf16[112,512]{1,0:T(8,128)(2,1)S(1)}, bf16[112,512]{1,0:T(8,128)(2,1)S(1)}, u32[]{:S(2)}, u32[]{:S(2)}) collective-permute-start(bf16[112,512]{1,0:T(8,128)(2,1)S(1)} %get-tuple-element.110), channel_id=1, source_target_pairs={{0,2},{2,0},{4,6},{6,4},{8,10},{10,8},{12,14},{14,12},{16,18},{18,... | collective-permute-start | bytes 344072 | tf_op jit(solution)/shard_map/ppermute | solution.py:718
  49.9 7.5 %collective-permute-start.18 = (bf16[112,512]{1,0:T(8,128)(2,1)S(1)}, bf16[112,512]{1,0:T(8,128)(2,1)S(1)}, u32[]{:S(2)}, u32[]{:S(2)}) collective-permute-start(bf16[112,512]{1,0:T(8,128)(2,1)S(1)} %get-tuple-element.111), channel_id=1, source_target_pairs={{0,4},{2,6},{4,0},{6,2},{8,12},{10,14},{12,8},{14,10},{16,20},{18,... | collective-permute-start | bytes 344072 | tf_op jit(solution)/shard_map/ppermute | solution.py:718
  50.7 8.5 %collective-permute-start.19 = (bf16[112,512]{1,0:T(8,128)(2,1)S(1)}, bf16[112,512]{1,0:T(8,128)(2,1)S(1)}, u32[]{:S(2)}, u32[]{:S(2)}) collective-permute-start(bf16[112,512]{1,0:T(8,128)(2,1)S(1)} %get-tuple-element.112), channel_id=1, source_target_pairs={{0,6},{2,4},{4,2},{6,0},{8,14},{10,12},{12,10},{14,8},{16,22},{18,... | collective-permute-start | bytes 344072 | tf_op jit(solution)/shard_map/ppermute | solution.py:718
  59.3 4.6 %collective-permute-start.22 = (bf16[72,512]{1,0:T(8,128)(2,1)S(1)}, bf16[72,512]{1,0:T(8,128)(2,1)S(1)}, u32[]{:S(2)}, u32[]{:S(2)}) collective-permute-start(bf16[72,512]{1,0:T(8,128)(2,1)S(1)} %get-tuple-element.120), channel_id=1, source_target_pairs={{0,8},{4,12},{8,0},{12,4},{16,24},{20,28},{24,16},{28,20},{1,9},{5... | collective-permute-start | bytes 221192 | tf_op jit(solution)/shard_map/ppermute | solution.py:663
  59.7 7.6 %collective-permute-start.23 = (bf16[72,512]{1,0:T(8,128)(2,1)S(1)}, bf16[72,512]{1,0:T(8,128)(2,1)S(1)}, u32[]{:S(2)}, u32[]{:S(2)}) collective-permute-start(bf16[72,512]{1,0:T(8,128)(2,1)S(1)} %get-tuple-element.121), channel_id=1, source_target_pairs={{0,16},{4,20},{8,24},{12,28},{16,0},{20,4},{24,8},{28,12},{1,17},{... | collective-permute-start | bytes 221192 | tf_op jit(solution)/shard_map/ppermute | solution.py:663
  62.1 6.3 %collective-permute-start.24 = (bf16[72,512]{1,0:T(8,128)(2,1)S(1)}, bf16[72,512]{1,0:T(8,128)(2,1)S(1)}, u32[]{:S(2)}, u32[]{:S(2)}) collective-permute-start(bf16[72,512]{1,0:T(8,128)(2,1)S(1)} %get-tuple-element.122), channel_id=1, source_target_pairs={{0,24},{4,28},{8,16},{12,20},{16,8},{20,12},{24,0},{28,4},{1,25},{... | collective-permute-start | bytes 221192 | tf_op jit(solution)/shard_map/ppermute | solution.py:663
  68.4 4.4 %collective-permute-start.25 = (bf16[64,512]{1,0:T(8,128)(2,1)S(1)}, bf16[64,512]{1,0:T(8,128)(2,1)S(1)}, u32[]{:S(2)}, u32[]{:S(2)}) collective-permute-start(bf16[64,512]{1,0:T(8,128)(2,1)S(1)} %get-tuple-element.130.refs_0_), channel_id=1, source_target_pairs={{0,8},{4,12},{8,0},{12,4},{16,24},{20,28},{24,16},{28,20},{1,9},{5... | collective-permute-start | bytes 196616 | tf_op jit(solution)/shard_map/ppermute | solution.py:663
  69.5 6.1 %collective-permute-start.30 = (bf16[64,512]{1,0:T(8,128)(2,1)S(1)}, bf16[64,512]{1,0:T(8,128)(2,1)S(1)}, u32[]{:S(2)}, u32[]{:S(2)}) collective-permute-start(bf16[64,512]{1,0:T(8,128)(2,1)S(1)} %get-tuple-element.130.refs_0_), channel_id=1, source_target_pairs={{0,24},{4,28},{8,16},{12,20},{16,8},{20,12},{24,0},{28,4},{1,25},{... | collective-permute-start | bytes 196616 | tf_op jit(solution)/shard_map/ppermute | solution.py:663
  71.5 5.5 %collective-permute-start.28 = (bf16[64,512]{1,0:T(8,128)(2,1)S(1)}, bf16[64,512]{1,0:T(8,128)(2,1)S(1)}, u32[]{:S(2)}, u32[]{:S(2)}) collective-permute-start(bf16[64,512]{1,0:T(8,128)(2,1)S(1)} %get-tuple-element.130.refs_0_), channel_id=1, source_target_pairs={{0,16},{4,20},{8,24},{12,28},{16,0},{20,4},{24,8},{28,12},{1,17},{... | collective-permute-start | bytes 196616 | tf_op jit(solution)/shard_map/ppermute | solution.py:663
  72.8 8.5 %collective-permute-start.26 = (bf16[64,512]{1,0:T(8,128)(2,1)S(1)}, bf16[64,512]{1,0:T(8,128)(2,1)S(1)}, u32[]{:S(2)}, u32[]{:S(2)}) collective-permute-start(bf16[64,512]{1,0:T(8,128)(2,1)S(1)} %get-tuple-element.130.refs_0_), channel_id=1, source_target_pairs={{0,4},{4,0},{8,12},{12,8},{16,20},{20,16},{24,28},{28,24},{1,5},{5... | collective-permute-start | bytes 196616 | tf_op jit(solution)/shard_map/ppermute | solution.py:663
  74.5 6.8 %collective-permute-start.27 = (bf16[64,512]{1,0:T(8,128)(2,1)S(1)}, bf16[64,512]{1,0:T(8,128)(2,1)S(1)}, u32[]{:S(2)}, u32[]{:S(2)}) collective-permute-start(bf16[64,512]{1,0:T(8,128)(2,1)S(1)} %collective-permute-done.25.refs_2_), channel_id=1, source_target_pairs={{0,4},{4,0},{8,12},{12,8},{16,20},{20,16},{24,28},{28,24},{1,5},{5... | collective-permute-start | bytes 196616 | tf_op jit(solution)/shard_map/ppermute | solution.py:663
  75.6 4.3 %collective-permute-start.31 = (bf16[64,512]{1,0:T(8,128)(2,1)S(1)}, bf16[64,512]{1,0:T(8,128)(2,1)S(1)}, u32[]{:S(2)}, u32[]{:S(2)}) collective-permute-start(bf16[64,512]{1,0:T(8,128)(2,1)S(1)} %collective-permute-done.30.refs_6_), channel_id=1, source_target_pairs={{0,4},{4,0},{8,12},{12,8},{16,20},{20,16},{24,28},{28,24},{1,5},{5... | collective-permute-start | bytes 196616 | tf_op jit(solution)/shard_map/ppermute | solution.py:663
  77.0 4.3 %collective-permute-start.29 = (bf16[64,512]{1,0:T(8,128)(2,1)S(1)}, bf16[64,512]{1,0:T(8,128)(2,1)S(1)}, u32[]{:S(2)}, u32[]{:S(2)}) collective-permute-start(bf16[64,512]{1,0:T(8,128)(2,1)S(1)} %collective-permute-done.28.refs_4_), channel_id=1, source_target_pairs={{0,4},{4,0},{8,12},{12,8},{16,20},{20,16},{24,28},{28,24},{1,5},{5... | collective-permute-start | bytes 196616 | tf_op jit(solution)/shard_map/ppermute | solution.py:663
